TPU v7x, 32 devices: a whole 2x2x4 slice. The times are simulated.
32 devices in a mesh: dp: 8 (over y, x, core), tensor: 4 (over z).
Axes of the slice: x: 2, y: 2, z: 4, core: 2. Of those that a mesh axis runs over, the one named last changes fastest.
Arguments:
- tokens: bfloat16 [64, 256, 1152], P('dp', 'tensor'), may hold values from -8 to 8
- timesteps: int32 [64], P('dp'), may hold values from 0 to 999
- labels: int32 [64], P('dp'), may hold values from 0 to 999
- patch_cells: int32 [64, 256], P('dp'), may hold values from 0 to 255, each once within a row
- class_table: bfloat16 [1000, 1152], P(None, 'tensor'), may hold values from -6 to 6
- ada_weight: bfloat16 [1152, 6, 1152], P('tensor', None, 'dp'), may hold values from -0.1875 to 0.1875
- ada_bias: bfloat16 [6, 1152], replicated, may hold values from -4 to 4
- qkv_weight: bfloat16 [1152, 3, 1152], P('dp', None, 'tensor'), may hold values from -0.1875 to 0.1875
- qkv_bias: bfloat16 [3, 1152], P(None, 'tensor'), may hold values from -3 to 3
- q_gain: bfloat16 [72], replicated, may hold values from 0.796875 to 2
- k_gain: bfloat16 [72], replicated, may hold values from 0.796875 to 2
- out_weight: bfloat16 [1152, 1152], P('tensor', 'dp'), may hold values from -0.75 to 0.75
- out_bias: bfloat16 [1152], replicated, may hold values from -3 to 3
- gate_up_weight: bfloat16 [1152, 2, 3072], P('dp', None, 'tensor'), may hold values from -0.1875 to 0.1875
- gate_up_bias: bfloat16 [2, 3072], P(None, 'tensor'), may hold values from -3 to 3
- down_weight: bfloat16 [3072, 1152], P('tensor', 'dp'), may hold values from -0.109375 to 0.109375
- down_bias: bfloat16 [1152], replicated, may hold values from -3 to 3
- cotangent: bfloat16 [64, 256, 1152], P('dp', 'tensor'), may hold values from -8 to 8
Outputs:
- output: bfloat16 [64, 256, 1152], P('dp', 'tensor')
- tokens_grad: float32 [64, 256, 1152], P('dp', 'tensor')
- class_table_grad: float32 [1000, 1152], P(None, 'tensor')
- ada_weight_grad: float32 [1152, 6, 1152], P('tensor', None, 'dp')
- ada_bias_grad: float32 [6, 1152], replicated
- qkv_weight_grad: float32 [1152, 3, 1152], P('dp', None, 'tensor')
- qkv_bias_grad: float32 [3, 1152], P(None, 'tensor')
- q_gain_grad: float32 [72], replicated
- k_gain_grad: float32 [72], replicated
- out_weight_grad: float32 [1152, 1152], P('tensor', 'dp')
- out_bias_grad: float32 [1152], replicated
- gate_up_weight_grad: float32 [1152, 2, 3072], P('dp', None, 'tensor')
- gate_up_bias_grad: float32 [2, 3072], P(None, 'tensor')
- down_weight_grad: float32 [3072, 1152], P('tensor', 'dp')
- down_bias_grad: float32 [1152], replicated
Inputs may be any that keep to these rules, and one draw needn't show every extreme that they name: `patch_cells`: each image's row holds every cell of the 16 x 16 patch grid once.
All inputs are finite; a program needn't handle non-finite values.
Results may differ from a plain program's by a relative error of at most 0.02.
Values may be sent and summed in bfloat16 or wider, within the bound.
No kernel may reach another device: no remote copies, remote signals or barrier semaphores. Data moves between devices by JAX's collectives and lax.ppermute only.
A program may use at most 112 MiB of HBM per device.

v0:
```python
import math

import jax
import jax.numpy as jnp
from jax import lax
from jax.sharding import PartitionSpec as P

D = 1152
HEAD_DIM = 72
CLASSES = 1000
GRID = 16
MICRO = 2


def rms_rows(values):
    return values * lax.rsqrt(jnp.mean(values * values, axis=-1, keepdims=True) + 1e-06)


def modulate(values, shift_rows, scale_rows):
    return rms_rows(values) * (1.0 + scale_rows) + shift_rows


def rotate_pairs(values):
    paired = values.reshape(values.shape[:-1] + (values.shape[-1] // 2, 2))
    return jnp.stack((-paired[..., 1], paired[..., 0]), axis=-1).reshape(values.shape)


def rotary_tables(patch_cells):
    row_place = (patch_cells // GRID).astype(jnp.float32)
    col_place = (patch_cells % GRID).astype(jnp.float32)
    rates = 10000.0 ** (-4.0 * jnp.arange(HEAD_DIM // 4, dtype=jnp.float32) / HEAD_DIM)
    rates = jnp.repeat(rates, 2)
    angles = jnp.concatenate((row_place[..., None] * rates, col_place[..., None] * rates), axis=-1)
    return (jnp.cos(angles)[..., None, :], jnp.sin(angles)[..., None, :])


def timestep_wave(timesteps):
    half_width = D // 2
    rates = jnp.exp(-math.log(10000.0) * jnp.arange(half_width, dtype=jnp.float32) / half_width)
    phases = timesteps.astype(jnp.float32)[:, None] * rates[None, :]
    return jnp.concatenate((jnp.cos(phases), jnp.sin(phases)), axis=-1)


def prepare_heads(q_cols, k_cols, q_gain, k_gain, cosines, sines):
    head_shape = q_cols.shape[:-1] + (q_cols.shape[-1] // HEAD_DIM, HEAD_DIM)
    q_normed = rms_rows(q_cols.reshape(head_shape)) * q_gain
    k_normed = rms_rows(k_cols.reshape(head_shape)) * k_gain
    q_turned = q_normed * cosines + rotate_pairs(q_normed) * sines
    k_turned = k_normed * cosines + rotate_pairs(k_normed) * sines
    return (q_turned, k_turned)


def swiglu(gate_vals, up_vals):
    return jax.nn.silu(gate_vals) * up_vals


def add_tree(totals, fresh):
    if totals is None:
        return fresh
    return tuple((total + extra for total, extra in zip(totals, fresh)))


def on_device(
    tokens,
    timesteps,
    labels,
    patch_cells,
    class_table,
    ada_weight,
    ada_bias,
    qkv_weight,
    qkv_bias,
    q_gain,
    k_gain,
    out_weight,
    out_bias,
    gate_up_weight,
    gate_up_bias,
    down_weight,
    down_bias,
    cotangent,
):
    tensor_rank = lax.axis_index("tensor")
    column_width = class_table.shape[1]
    micro_images = tokens.shape[0] // MICRO
    inv_root = 1.0 / math.sqrt(HEAD_DIM)
    highest = lax.Precision.HIGHEST
    wave_all = timestep_wave(timesteps)
    wave_slice = lax.dynamic_slice_in_dim(wave_all, tensor_rank * column_width, column_width, 1)
    one_hot = (labels[:, None] == jnp.arange(CLASSES, dtype=jnp.int32)[None, :]).astype(
        jnp.bfloat16
    )
    cond_all = jnp.dot(one_hot, class_table, preferred_element_type=jnp.float32) + wave_slice
    cond_low_all = jax.nn.silu(cond_all).astype(jnp.bfloat16)
    cos_all, sin_all = rotary_tables(patch_cells)
    q_gain_f = q_gain.astype(jnp.float32)
    k_gain_f = k_gain.astype(jnp.float32)
    ada_bias_f = ada_bias.astype(jnp.float32)
    qkv_bias_f = qkv_bias.astype(jnp.float32)
    gate_up_bias_f = gate_up_bias.astype(jnp.float32)
    out_bias_f = out_bias.astype(jnp.float32)
    down_bias_f = down_bias.astype(jnp.float32)
    weight_totals = None
    table_total = jnp.zeros(class_table.shape, jnp.float32)
    ada_bias_total = jnp.zeros(ada_bias.shape, jnp.float32)
    qkv_bias_total = jnp.zeros(qkv_bias.shape, jnp.float32)
    gate_up_bias_total = jnp.zeros(gate_up_bias.shape, jnp.float32)
    out_bias_total = jnp.zeros(out_bias.shape, jnp.float32)
    down_bias_total = jnp.zeros(down_bias.shape, jnp.float32)
    q_gain_total = jnp.zeros(q_gain.shape, jnp.float32)
    k_gain_total = jnp.zeros(k_gain.shape, jnp.float32)
    output_parts = []
    grad_parts = []
    for micro_index in range(MICRO):
        first_image = micro_index * micro_images
        last_image = first_image + micro_images
        x_rows = tokens[first_image:last_image].astype(jnp.float32)
        cond_m = cond_all[first_image:last_image]
        cond_low = cond_low_all[first_image:last_image]
        cos_m = cos_all[first_image:last_image]
        sin_m = sin_all[first_image:last_image]
        w_qkv, w_out, w_gate_up, w_down, w_ada = (
            lax.all_gather(qkv_weight, "dp", axis=0, tiled=True),
            lax.all_gather(out_weight, "dp", axis=1, tiled=True),
            lax.all_gather(gate_up_weight, "dp", axis=0, tiled=True),
            lax.all_gather(down_weight, "dp", axis=1, tiled=True),
            lax.all_gather(ada_weight, "dp", axis=2, tiled=True),
        )
        mod_part = jnp.einsum("bc,cke->bke", cond_low, w_ada, preferred_element_type=jnp.float32)
        mod_values = lax.psum(mod_part, "tensor") + ada_bias_f
        shift_a = mod_values[:, 0:1]
        scale_a = mod_values[:, 1:2]
        gate_a = mod_values[:, 2:3]
        shift_f = mod_values[:, 3:4]
        scale_f = mod_values[:, 4:5]
        gate_f = mod_values[:, 5:6]
        attn_in = modulate(x_rows, shift_a, scale_a).astype(jnp.bfloat16)
        attn_all = lax.all_gather(attn_in, "tensor", axis=1, tiled=True)
        qkv_all = (
            jnp.einsum("bpd,dke->bpke", attn_all, w_qkv, preferred_element_type=jnp.float32)
            + qkv_bias_f
        )
        q_cols = qkv_all[:, :, 0]
        k_cols = qkv_all[:, :, 1]
        q_rot, k_rot = prepare_heads(q_cols, k_cols, q_gain_f, k_gain_f, cos_m, sin_m)
        q_low = q_rot.astype(jnp.bfloat16)
        k_low = k_rot.astype(jnp.bfloat16)
        v_low = qkv_all[:, :, 2].reshape(q_low.shape).astype(jnp.bfloat16)
        scores = (
            jnp.einsum("bqhe,bkhe->bhqk", q_low, k_low, preferred_element_type=jnp.float32)
            * inv_root
        )
        peak = jnp.max(scores, axis=-1, keepdims=True)
        expo = jnp.exp(scores - peak)
        totals_row = jnp.sum(expo, axis=-1, keepdims=True)
        log_total = peak + jnp.log(totals_row)
        probs_low = (expo / totals_row).astype(jnp.bfloat16)
        heads_out = jnp.einsum(
            "bhqk,bkhe->bqhe", probs_low, v_low, preferred_element_type=jnp.float32
        )
        heads_out = heads_out.astype(jnp.bfloat16).reshape(q_cols.shape)
        proj_part = jnp.einsum("bpc,cd->bpd", heads_out, w_out, preferred_element_type=jnp.float32)
        attn = lax.psum_scatter(proj_part, "tensor", scatter_dimension=1, tiled=True) + out_bias_f
        mid = x_rows + gate_a * attn
        ffn_in = modulate(mid, shift_f, scale_f).astype(jnp.bfloat16)
        ffn_all = lax.all_gather(ffn_in, "tensor", axis=1, tiled=True)
        gate_up = (
            jnp.einsum("bpd,dkf->bpkf", ffn_all, w_gate_up, preferred_element_type=jnp.float32)
            + gate_up_bias_f
        )
        hidden = swiglu(gate_up[:, :, 0], gate_up[:, :, 1]).astype(jnp.bfloat16)
        down_part = jnp.einsum("bpf,fd->bpd", hidden, w_down, preferred_element_type=jnp.float32)
        ffn = (
            lax.psum_scatter(
                down_part.astype(jnp.bfloat16), "tensor", scatter_dimension=1, tiled=True
            ).astype(jnp.float32)
            + down_bias_f
        )
        output_parts.append((mid + gate_f * ffn).astype(jnp.bfloat16))
        grad_out = cotangent[first_image:last_image].astype(jnp.float32)
        d_ffn_f = gate_f * grad_out
        down_bias_part = jnp.sum(d_ffn_f, axis=(0, 1))
        d_gate_f = jnp.sum(grad_out * ffn, axis=1, keepdims=True)
        d_ffn_low = d_ffn_f.astype(jnp.bfloat16)
        d_ffn_all = lax.all_gather(d_ffn_low, "tensor", axis=1, tiled=True)
        grad_down = jnp.einsum("bpf,bpd->fd", hidden, d_ffn_all, preferred_element_type=jnp.float32)
        d_hidden = jnp.einsum("bpd,fd->bpf", d_ffn_all, w_down, preferred_element_type=jnp.float32)
        swiglu_back = jax.vjp(swiglu, gate_up[:, :, 0], gate_up[:, :, 1])[1]
        d_gate_vals, d_up_vals = swiglu_back(d_hidden)
        d_gate_up = jnp.stack((d_gate_vals, d_up_vals), axis=2).astype(jnp.bfloat16)
        gate_up_bias_total = gate_up_bias_total + jnp.sum(d_gate_up, axis=(0, 1), dtype=jnp.float32)
        grad_gate_up = jnp.einsum(
            "bpd,bpkf->dkf", ffn_all, d_gate_up, preferred_element_type=jnp.float32
        )
        d_fin_part = jnp.einsum(
            "bpkf,dkf->bpd", d_gate_up, w_gate_up, preferred_element_type=jnp.float32
        )
        d_ffn_in = lax.psum_scatter(d_fin_part, "tensor", scatter_dimension=1, tiled=True)
        norm_back_f = jax.vjp(modulate, mid, shift_f, scale_f)[1]
        mid_grads = norm_back_f(d_ffn_in)
        d_mid = grad_out + mid_grads[0]
        d_shift_f = mid_grads[1]
        d_scale_f = mid_grads[2]
        d_attn_f = gate_a * d_mid
        out_bias_part = jnp.sum(d_attn_f, axis=(0, 1))
        d_gate_a = jnp.sum(d_mid * attn, axis=1, keepdims=True)
        d_attn_low = d_attn_f.astype(jnp.bfloat16)
        d_attn_all = lax.all_gather(d_attn_low, "tensor", axis=1, tiled=True)
        grad_out_w = jnp.einsum(
            "bpc,bpd->cd", heads_out, d_attn_all, preferred_element_type=jnp.float32
        )
        d_heads = jnp.einsum("bpd,cd->bpc", d_attn_all, w_out, preferred_element_type=jnp.float32)
        d_heads = d_heads.astype(jnp.bfloat16).reshape(q_low.shape)
        scores_again = (
            jnp.einsum("bqhe,bkhe->bhqk", q_low, k_low, preferred_element_type=jnp.float32)
            * inv_root
        )
        probs_f = jnp.exp(scores_again - log_total)
        probs_again = probs_f.astype(jnp.bfloat16)
        d_probs = jnp.einsum("bqhe,bkhe->bhqk", d_heads, v_low, preferred_element_type=jnp.float32)
        d_vals = jnp.einsum(
            "bhqk,bqhe->bkhe", probs_again, d_heads, preferred_element_type=jnp.float32
        )
        d_scores = probs_f * (d_probs - jnp.sum(d_probs * probs_f, axis=-1, keepdims=True))
        d_scores = d_scores.astype(jnp.bfloat16)
        d_qrot = (
            jnp.einsum("bhqk,bkhe->bqhe", d_scores, k_low, preferred_element_type=jnp.float32)
            * inv_root
        )
        d_krot = (
            jnp.einsum("bhqk,bqhe->bkhe", d_scores, q_low, preferred_element_type=jnp.float32)
            * inv_root
        )
        prepare_back = jax.vjp(prepare_heads, q_cols, k_cols, q_gain_f, k_gain_f, cos_m, sin_m)[1]
        head_grads = prepare_back((d_qrot, d_krot))
        d_qkv = jnp.stack(
            (head_grads[0], head_grads[1], d_vals.reshape(q_cols.shape)), axis=2
        ).astype(jnp.bfloat16)
        qkv_bias_total = qkv_bias_total + jnp.sum(d_qkv, axis=(0, 1), dtype=jnp.float32)
        grad_qkv = jnp.einsum("bpd,bpke->dke", attn_all, d_qkv, preferred_element_type=jnp.float32)
        d_ain_part = jnp.einsum("bpke,dke->bpd", d_qkv, w_qkv, preferred_element_type=jnp.float32)
        d_attn_in = lax.psum_scatter(
            d_ain_part.astype(jnp.bfloat16), "tensor", scatter_dimension=1, tiled=True
        ).astype(jnp.float32)
        norm_back_a = jax.vjp(modulate, x_rows, shift_a, scale_a)[1]
        row_grads = norm_back_a(d_attn_in)
        grad_parts.append(d_mid + row_grads[0])
        d_mod_part = jnp.concatenate(
            (row_grads[1], row_grads[2], d_gate_a, d_shift_f, d_scale_f, d_gate_f), axis=1
        )
        d_mod, out_bias_step, down_bias_step, q_gain_step, k_gain_step = (
            lax.psum(d_mod_part.astype(jnp.bfloat16), "tensor").astype(jnp.float32),
            lax.psum(out_bias_part.astype(jnp.bfloat16), "tensor").astype(jnp.float32),
            lax.psum(down_bias_part.astype(jnp.bfloat16), "tensor").astype(jnp.float32),
            lax.psum(head_grads[2].astype(jnp.bfloat16), "tensor").astype(jnp.float32),
            lax.psum(head_grads[3].astype(jnp.bfloat16), "tensor").astype(jnp.float32),
        )
        out_bias_total = out_bias_total + out_bias_step
        down_bias_total = down_bias_total + down_bias_step
        q_gain_total = q_gain_total + q_gain_step
        k_gain_total = k_gain_total + k_gain_step
        ada_bias_total = ada_bias_total + jnp.sum(d_mod, axis=0)
        d_mod_low = d_mod.astype(jnp.bfloat16)
        grad_ada = jnp.einsum(
            "bc,bke->cke", cond_low, d_mod_low, preferred_element_type=jnp.float32
        )
        d_silu = jnp.einsum("bke,cke->bc", d_mod_low, w_ada, preferred_element_type=jnp.float32)
        silu_back = jax.vjp(jax.nn.silu, cond_m)[1]
        d_cond = silu_back(d_silu)[0]
        one_hot_m = one_hot[first_image:last_image].astype(jnp.float32)
        table_total = table_total + jnp.dot(one_hot_m.T, d_cond, precision=highest)
        micro_grads = (grad_qkv, grad_out_w, grad_gate_up, grad_down, grad_ada)
        micro_shards = (
            lax.psum_scatter(micro_grads[0], "dp", scatter_dimension=0, tiled=True),
            lax.psum_scatter(micro_grads[1], "dp", scatter_dimension=1, tiled=True),
            lax.psum_scatter(micro_grads[2], "dp", scatter_dimension=0, tiled=True),
            lax.psum_scatter(micro_grads[3], "dp", scatter_dimension=1, tiled=True),
            lax.psum_scatter(micro_grads[4], "dp", scatter_dimension=2, tiled=True),
        )
        weight_totals = add_tree(weight_totals, micro_shards)
    small_sums = lax.psum(
        (
            table_total,
            ada_bias_total,
            qkv_bias_total,
            gate_up_bias_total,
            out_bias_total,
            down_bias_total,
            q_gain_total,
            k_gain_total,
        ),
        "dp",
    )
    output = jnp.concatenate(output_parts, axis=0)
    tokens_grad = jnp.concatenate(grad_parts, axis=0)
    return (
        output,
        tokens_grad,
        small_sums[0],
        weight_totals[4],
        small_sums[1],
        weight_totals[0],
        small_sums[2],
        small_sums[6],
        small_sums[7],
        weight_totals[1],
        small_sums[4],
        weight_totals[2],
        small_sums[3],
        weight_totals[3],
        small_sums[5],
    )


def solution(mesh):
    in_specs = (
        P("dp", "tensor", None),
        P("dp"),
        P("dp"),
        P("dp", None),
        P(None, "tensor"),
        P("tensor", None, "dp"),
        P(),
        P("dp", None, "tensor"),
        P(None, "tensor"),
        P(),
        P(),
        P("tensor", "dp"),
        P(),
        P("dp", None, "tensor"),
        P(None, "tensor"),
        P("tensor", "dp"),
        P(),
        P("dp", "tensor", None),
    )
    out_specs = (
        P("dp", "tensor", None),
        P("dp", "tensor", None),
        P(None, "tensor"),
        P("tensor", None, "dp"),
        P(),
        P("dp", None, "tensor"),
        P(None, "tensor"),
        P(),
        P(),
        P("tensor", "dp"),
        P(),
        P("dp", None, "tensor"),
        P(None, "tensor"),
        P("tensor", "dp"),
        P(),
    )
    return jax.shard_map(
        on_device, mesh=mesh, in_specs=in_specs, out_specs=out_specs, check_vma=False
    )
```

profile of v0, /device:TPU:0, one launch (start us, length us, event | category | flops | bytes accessed | tf_op | source)
XLA Modules:
  0.0 1730.3 jit_solution(16914580157209431154)
XLA Ops:
  10.4 43.7 %all-gather.13.cloned.1.call-done = bf16[288,6,1152]{0,2,1:T(8,128)(2,1)} async-done(((bf16[288,6,144]{0,2,1:T(8,128)(2,1)}), bf16[288,6,1152]{0,2,1:T(8,128)(2,1)}) %all-gather.13.cloned.1.call-update) | async-done | bytes 3981328 | tf_op jit(solution)/shard_map/all_gather | solution.py:127
  54.0 4.8 fusion.154
  62.2 34.1 %all-reduce.17.cloned.1.call-done = (f32[4,6,1152]{2,0,1:T(4,128)}, f32[4,6,1152]{2,0,1:T(4,128)}) async-done(((f32[4,6,1152]{2,0,1:T(4,128)}, f32[4,6,1152]{2,0,1:T(4,128)}), (f32[4,6,1152]{2,0,1:T(4,128)}, f32[4,6,1152]{2,0,1:T(4,128)})) %all-reduce.17.cloned.1.call-update) | async-done | bytes 221200 | tf_op jit(solution)/shard_map/psum | solution.py:130
  103.9 13.3 all_gather.47
  118.7 11.9 all-gather.17.cloned.1.call-done
  130.6 52.6 %all-gather.15.cloned.1.call-done = bf16[4,256,1152]{2,1,0:T(8,128)(2,1)} async-done(((bf16[4,64,1152]{2,1,0:T(8,128)(2,1)}), bf16[4,256,1152]{2,1,0:T(8,128)(2,1)}) %all-gather.15.cloned.1.call-update) | async-done | bytes 2359312 | tf_op jit(solution)/shard_map/all_gather | solution.py:138
  183.1 5.0 fusion.52
  191.1 43.4 %all-gather.25.cloned.1.call-done = bf16[4,256,1152]{2,1,0:T(8,128)(2,1)} async-done(((bf16[4,64,1152]{2,1,0:T(8,128)(2,1)}), bf16[4,256,1152]{2,1,0:T(8,128)(2,1)}) %all-gather.25.cloned.1.call-update) | async-done | bytes 2359312 | tf_op jit(solution)/shard_map/all_gather | solution.py:138
  234.5 5.0 fusion.57
  286.0 5.7 add_convert_fusion.2
  313.2 71.2 %reduce-scatter.14.cloned.1.call-done = f32[4,64,1152]{2,1,0:T(8,128)} async-done(((f32[4,256,1152]{2,1,0:T(8,128)}), f32[4,64,1152]{2,1,0:T(8,128)}) %reduce-scatter.14.cloned.1.call-update) | async-done | bytes 1179664 | tf_op jit(solution)/shard_map/reduce_scatter | solution.py:163
  384.3 88.2 %reduce-scatter.18.cloned.1.call-done = f32[4,64,1152]{2,1,0:T(8,128)} async-done(((f32[4,256,1152]{2,1,0:T(8,128)}), f32[4,64,1152]{2,1,0:T(8,128)}) %reduce-scatter.18.cloned.1.call-update) | async-done | bytes 1179664 | tf_op jit(solution)/shard_map/reduce_scatter | solution.py:163
  488.2 21.5 %all-gather.21.cloned.1.call-done = bf16[1152,2,768]{2,0,1:T(8,128)(2,1)} async-done(((bf16[144,2,768]{2,0,1:T(8,128)(2,1)}), bf16[1152,2,768]{2,0,1:T(8,128)(2,1)}) %all-gather.21.cloned.1.call-update) | async-done | bytes 3538960 | tf_op jit(solution)/shard_map/all_gather | solution.py:125
  509.7 52.1 %all-gather.19.cloned.1.call-done = bf16[4,256,1152]{2,1,0:T(8,128)(2,1)} async-done(((bf16[4,64,1152]{2,1,0:T(8,128)(2,1)}), bf16[4,256,1152]{2,1,0:T(8,128)(2,1)}) %all-gather.19.cloned.1.call-update) | async-done | bytes 2359312 | tf_op jit(solution)/shard_map/all_gather | solution.py:166
  561.8 9.6 broadcast_add_fusion
  571.4 17.7 %all-gather.23.cloned.1.call-done = bf16[768,1152]{0,1:T(8,128)(2,1)} async-done(((bf16[768,144]{0,1:T(8,128)(2,1)}), bf16[768,1152]{0,1:T(8,128)(2,1)}) %all-gather.23.cloned.1.call-update) | async-done | bytes 1769488 | tf_op jit(solution)/shard_map/all_gather | solution.py:126
  589.1 52.1 %all-gather.29.cloned.1.call-done = bf16[4,256,1152]{2,1,0:T(8,128)(2,1)} async-done(((bf16[4,64,1152]{2,1,0:T(8,128)(2,1)}), bf16[4,256,1152]{2,1,0:T(8,128)(2,1)}) %all-gather.29.cloned.1.call-update) | async-done | bytes 2359312 | tf_op jit(solution)/shard_map/all_gather | solution.py:185
  641.3 9.0 fusion.71
  655.1 9.4 convolution_bitcast_fusion.1
  664.9 27.7 %all-gather.27.cloned.1.call-done = bf16[4,256,1152]{2,1,0:T(8,128)(2,1)} async-done(((bf16[4,64,1152]{2,1,0:T(8,128)(2,1)}), bf16[4,256,1152]{2,1,0:T(8,128)(2,1)}) %all-gather.27.cloned.1.call-update) | async-done | bytes 2359312 | tf_op jit(solution)/shard_map/all_gather | solution.py:166
  692.7 9.6 broadcast_add_fusion.1
  702.2 41.4 %all-gather.33.cloned.1.call-done = bf16[4,256,1152]{2,1,0:T(8,128)(2,1)} async-done(((bf16[4,64,1152]{2,1,0:T(8,128)(2,1)}), bf16[4,256,1152]{2,1,0:T(8,128)(2,1)}) %all-gather.33.cloned.1.call-update) | async-done | bytes 2359312 | tf_op jit(solution)/shard_map/all_gather | solution.py:185
  743.6 8.9 fusion.70
  757.4 9.4 convolution_bitcast_fusion
  768.4 24.4 %reduce-scatter.16.cloned.1.call-done = bf16[4,64,1152]{2,1,0:T(8,128)(2,1)} async-done(((bf16[4,256,1152]{2,1,0:T(8,128)(2,1)}), bf16[4,64,1152]{2,1,0:T(8,128)(2,1)}) %reduce-scatter.16.cloned.1.call-update) | async-done | bytes 589840 | tf_op jit(solution)/shard_map/reduce_scatter | solution.py:174
  792.8 87.0 %reduce-scatter.22.cloned.1.call-done = f32[4,64,1152]{2,1,0:T(8,128)} async-done(((f32[4,256,1152]{2,1,0:T(8,128)}), f32[4,64,1152]{2,1,0:T(8,128)}) %reduce-scatter.22.cloned.1.call-update) | async-done | bytes 1179664 | tf_op jit(solution)/shard_map/reduce_scatter | solution.py:198
  884.2 47.1 %reduce-scatter.20.cloned.1.call-done = bf16[4,64,1152]{2,1,0:T(8,128)(2,1)} async-done(((bf16[4,256,1152]{2,1,0:T(8,128)(2,1)}), bf16[4,64,1152]{2,1,0:T(8,128)(2,1)}) %reduce-scatter.20.cloned.1.call-update) | async-done | bytes 589840 | tf_op jit(solution)/shard_map/reduce_scatter | solution.py:174
  931.3 87.0 %reduce-scatter.26.cloned.1.call-done = f32[4,64,1152]{2,1,0:T(8,128)} async-done(((f32[4,256,1152]{2,1,0:T(8,128)}), f32[4,64,1152]{2,1,0:T(8,128)}) %reduce-scatter.26.cloned.1.call-update) | async-done | bytes 1179664 | tf_op jit(solution)/shard_map/reduce_scatter | solution.py:198
  1018.4 4.8 multiply_reduce_fusion.8
  1023.3 5.3 multiply_reduce_fusion.25
  1035.6 46.1 %all-gather.31.cloned.1.call-done = bf16[4,256,1152]{2,1,0:T(8,128)(2,1)} async-done(((bf16[4,64,1152]{2,1,0:T(8,128)(2,1)}), bf16[4,256,1152]{2,1,0:T(8,128)(2,1)}) %all-gather.31.cloned.1.call-update) | async-done | bytes 2359312 | tf_op jit(solution)/shard_map/all_gather | solution.py:208
  1090.3 43.0 %all-gather.35.cloned.1.call-done = bf16[4,256,1152]{2,1,0:T(8,128)(2,1)} async-done(((bf16[4,64,1152]{2,1,0:T(8,128)(2,1)}), bf16[4,256,1152]{2,1,0:T(8,128)(2,1)}) %all-gather.35.cloned.1.call-update) | async-done | bytes 2359312 | tf_op jit(solution)/shard_map/all_gather | solution.py:208
  1205.4 5.1 bitcast_convert_fusion.1
  1216.5 4.9 bitcast_convert_fusion
  1222.9 8.8 fusion.36
  1231.7 25.9 %reduce-scatter.24.cloned.1.call-done = bf16[4,64,1152]{2,1,0:T(8,128)(2,1)} async-done(((bf16[4,256,1152]{2,1,0:T(8,128)(2,1)}), bf16[4,64,1152]{2,1,0:T(8,128)(2,1)}) %reduce-scatter.24.cloned.1.call-update) | async-done | bytes 589840 | tf_op jit(solution)/shard_map/reduce_scatter | solution.py:242
  1258.8 48.8 %reduce-scatter.28.cloned.1.call-done = bf16[4,64,1152]{2,1,0:T(8,128)(2,1)} async-done(((bf16[4,256,1152]{2,1,0:T(8,128)(2,1)}), bf16[4,64,1152]{2,1,0:T(8,128)(2,1)}) %reduce-scatter.28.cloned.1.call-update) | async-done | bytes 589840 | tf_op jit(solution)/shard_map/reduce_scatter | solution.py:242
  1312.9 11.4 bitcast_add_fusion
  1340.8 7.4 fusion.31
  1357.5 9.3 bitcast_add_fusion.1
  1369.2 5.6 convolution_add_fusion
  1381.5 35.4 %reduce-scatter.36.cloned.1.call-done = f32[144,2,768]{2,0,1:T(8,128)} async-done(((f32[1152,2,768]{2,0,1:T(8,128)}), f32[144,2,768]{2,0,1:T(8,128)}) %reduce-scatter.36.cloned.1.call-update) | async-done | bytes 884752 | tf_op jit(solution)/shard_map/reduce_scatter | solution.py:276
  1426.4 25.1 %all-reduce.8 = (f32[6,1152]{1,0:T(8,128)}, f32[3,288]{1,0:T(4,128)}, f32[72]{0:T(128)}, f32[72]{0:T(128)}, f32[1152]{0:T(1024)}, /*index=5*/f32[2,768]{1,0:T(2,128)}, f32[1152]{0:T(1024)}) all-reduce(f32[6,1152]{1,0:T(8,128)S(1)} %add.494, f32[3,288]{1,0:T(4,128)S(1)} %copy-done.133, ...), channel_id=1, replica_groups=mesh['dp'=8,'tensor'=4] {'dp'}, use_global_device_ids=true, to_apply=%region_51.52 | all-reduce | flops 11760 | bytes 94080 | tf_op jit(solution)/shard_map/psum | solution.py:281
  1451.5 18.2 %reduce-scatter.38.cloned.1.call-done = f32[768,144]{0,1:T(8,128)} async-done(((f32[768,1152]{0,1:T(8,128)}), f32[768,144]{0,1:T(8,128)}) %reduce-scatter.38.cloned.1.call-update) | async-done | bytes 442384 | tf_op jit(solution)/shard_map/reduce_scatter | solution.py:277
  1469.7 43.7 %reduce-scatter.34.cloned.1.call-done = f32[288,144]{0,1:T(8,128)} async-done(((f32[288,1152]{0,1:T(8,128)}), f32[288,144]{0,1:T(8,128)}) %reduce-scatter.34.cloned.1.call-update) | async-done | bytes 165904 | tf_op jit(solution)/shard_map/reduce_scatter | solution.py:275
  1513.4 60.5 %all-reduce.15.cloned.1.call-done = f32[1000,288]{0,1:T(8,128)} async-done(((f32[1000,288]{0,1:T(8,128)}), f32[1000,288]{0,1:T(8,128)}) %all-reduce.15.cloned.1.call-update) | async-done | bytes 1152016 | tf_op jit(solution)/shard_map/psum | solution.py:281
  1573.9 59.9 %reduce-scatter.32.cloned.1.call-done = f32[144,3,288]{2,0,1:T(8,128)} async-done(((f32[1152,3,288]{2,0,1:T(8,128)}), f32[144,3,288]{2,0,1:T(8,128)}) %reduce-scatter.32.cloned.1.call-update) | async-done | bytes 497680 | tf_op jit(solution)/shard_map/reduce_scatter | solution.py:274
  1633.8 86.7 %reduce-scatter.30.cloned.1.call-done = f32[288,6,144]{0,2,1:T(8,128)} async-done(((f32[288,6,1152]{0,2,1:T(8,128)}), f32[288,6,144]{0,2,1:T(8,128)}) %reduce-scatter.30.cloned.1.call-update) | async-done | bytes 995344 | tf_op jit(solution)/shard_map/reduce_scatter | solution.py:278
  (548 shorter events, 264.7 us)
Async XLA Ops:
  7.2 46.9 %all-gather.13.cloned.1.call-start = ((), (), s32[]{:S(2)}) async-start(), calls=%async_computation.13 | async-start | bytes 5971968 | tf_op jit(solution)/shard_map/all_gather | solution.py:127
  7.9 88.3 %all-reduce.17.cloned.1.call-start = ((), (), s32[]{:S(2)}) async-start(), calls=%async_computation.39 | async-start | bytes 442368 | tf_op jit(solution)/shard_map/psum | solution.py:130
  10.4 48.5 %copy-start.97 = (bf16[8,288]{1,0:T(8,128)(2,1)}, bf16[8,288]{1,0:T(8,128)(2,1)S(1)}, u32[]{:S(2)}) copy-start(bf16[8,288]{1,0:T(8,128)(2,1)S(1)} %get-tuple-element.200) | copy-start | bytes 13828
  61.0 69.5 %all-gather.17.cloned.1.call-start = ((), (), s32[]{:S(2)}) async-start(), calls=%async_computation.15 | async-start | bytes 2985984 | tf_op jit(solution)/shard_map/all_gather | solution.py:123
  61.8 121.4 %all-gather.15.cloned.1.call-start = ((), (), s32[]{:S(2)}) async-start(), calls=%async_computation.14 | async-start | bytes 2949120 | tf_op jit(solution)/shard_map/all_gather | solution.py:138
  62.2 35.1 %copy-start.137 = (f32[4,64]{1,0:T(4,128)}, f32[4,64]{1,0:T(4,128)S(1)}, u32[]{:S(2)}) copy-start(f32[4,64]{1,0:T(4,128)S(1)} %get-tuple-element.74) | copy-start | bytes 3076
  62.2 35.1 %copy-start.138 = (f32[4,64]{1,0:T(4,128)}, f32[4,64]{1,0:T(4,128)S(1)}, u32[]{:S(2)}) copy-start(f32[4,64]{1,0:T(4,128)S(1)} %get-tuple-element.73) | copy-start | bytes 3076
  62.2 37.3 %copy-start.129 = (f32[4,64]{1,0:T(4,128)}, f32[4,64]{1,0:T(4,128)S(1)}, u32[]{:S(2)}) copy-start(f32[4,64]{1,0:T(4,128)S(1)} %get-tuple-element.218) | copy-start | bytes 3076
  62.2 37.3 %copy-start.131 = (f32[4,64]{1,0:T(4,128)}, f32[4,64]{1,0:T(4,128)S(1)}, u32[]{:S(2)}) copy-start(f32[4,64]{1,0:T(4,128)S(1)} %get-tuple-element.219) | copy-start | bytes 3076
  99.6 135.0 %all-gather.25.cloned.1.call-start = ((), (), s32[]{:S(2)}) async-start(), calls=%async_computation.21 | async-start | bytes 2949120 | tf_op jit(solution)/shard_map/all_gather | solution.py:138
  100.2 284.2 %reduce-scatter.14.cloned.1.call-start = ((), (), s32[]{:S(2)}) async-start(), calls=%async_computation.16 | async-start | bytes 5898240 | tf_op jit(solution)/shard_map/reduce_scatter | solution.py:163
  191.1 48.4 %copy-start.102 = (f32[4,256,4]{1,2,0:T(4,128)}, f32[4,256,4]{1,2,0:T(4,128)S(1)}, u32[]{:S(2)}) copy-start(f32[4,256,4]{1,2,0:T(4,128)S(1)} %multiply_reduce_fusion.22) | copy-start | bytes 49156
  191.1 52.4 %copy-start.75 = (f32[4,256,4]{1,2,0:T(4,128)}, f32[4,256,4]{1,2,0:T(4,128)S(1)}, u32[]{:S(2)}) copy-start(f32[4,256,4]{1,2,0:T(4,128)S(1)} %fusion.122) | copy-start | bytes 49156
  300.1 172.5 %reduce-scatter.18.cloned.1.call-start = ((), (), s32[]{:S(2)}) async-start(), calls=%async_computation.22 | async-start | bytes 5898240 | tf_op jit(solution)/shard_map/reduce_scatter | solution.py:163
  309.9 199.8 %all-gather.21.cloned.1.call-start = ((), (), s32[]{:S(2)}) async-start(), calls=%async_computation.18 | async-start | bytes 3981312 | tf_op jit(solution)/shard_map/all_gather | solution.py:125
  311.8 250.0 %all-gather.19.cloned.1.call-start = ((), (), s32[]{:S(2)}) async-start(), calls=%async_computation.17 | async-start | bytes 2949120 | tf_op jit(solution)/shard_map/all_gather | solution.py:166
  478.9 110.2 %all-gather.23.cloned.1.call-start = ((), (), s32[]{:S(2)}) async-start(), calls=%async_computation.19 | async-start | bytes 1990656 | tf_op jit(solution)/shard_map/all_gather | solution.py:126
  479.5 161.8 %all-gather.29.cloned.1.call-start = ((), (), s32[]{:S(2)}) async-start(), calls=%async_computation.25 | async-start | bytes 2949120 | tf_op jit(solution)/shard_map/all_gather | solution.py:185
  482.1 210.5 %all-gather.27.cloned.1.call-start = ((), (), s32[]{:S(2)}) async-start(), calls=%async_computation.23 | async-start | bytes 2949120 | tf_op jit(solution)/shard_map/all_gather | solution.py:166
  485.9 257.7 %all-gather.33.cloned.1.call-start = ((), (), s32[]{:S(2)}) async-start(), calls=%async_computation.29 | async-start | bytes 2949120 | tf_op jit(solution)/shard_map/all_gather | solution.py:185
  486.7 306.2 %reduce-scatter.16.cloned.1.call-start = ((), (), s32[]{:S(2)}) async-start(), calls=%async_computation.20 | async-start | bytes 2949120 | tf_op jit(solution)/shard_map/reduce_scatter | solution.py:174
  641.2 10.1 copy-start.156
  655.0 224.8 %reduce-scatter.22.cloned.1.call-start = ((), (), s32[]{:S(2)}) async-start(), calls=%async_computation.26 | async-start | bytes 5898240 | tf_op jit(solution)/shard_map/reduce_scatter | solution.py:198
  664.5 266.8 %reduce-scatter.20.cloned.1.call-start = ((), (), s32[]{:S(2)}) async-start(), calls=%async_computation.24 | async-start | bytes 2949120 | tf_op jit(solution)/shard_map/reduce_scatter | solution.py:174
  757.4 260.9 %reduce-scatter.26.cloned.1.call-start = ((), (), s32[]{:S(2)}) async-start(), calls=%async_computation.30 | async-start | bytes 5898240 | tf_op jit(solution)/shard_map/reduce_scatter | solution.py:198
  766.9 314.9 %all-gather.31.cloned.1.call-start = ((), (), s32[]{:S(2)}) async-start(), calls=%async_computation.27 | async-start | bytes 2949120 | tf_op jit(solution)/shard_map/all_gather | solution.py:208
  1030.6 102.7 %all-gather.35.cloned.1.call-start = ((), (), s32[]{:S(2)}) async-start(), calls=%async_computation.31 | async-start | bytes 2949120 | tf_op jit(solution)/shard_map/all_gather | solution.py:208
  1032.9 224.7 %reduce-scatter.24.cloned.1.call-start = ((), (), s32[]{:S(2)}) async-start(), calls=%async_computation.28 | async-start | bytes 2949120 | tf_op jit(solution)/shard_map/reduce_scatter | solution.py:242
  1203.6 137.2 %copy-start.43 = (bf16[4,256,4,72]{1,3,2,0:T(8,128)(2,1)}, bf16[4,256,4,72]{1,3,2,0:T(8,128)(2,1)S(1)}, u32[]{:S(2)}) copy-start(bf16[4,256,4,72]{1,3,2,0:T(8,128)(2,1)S(1)} %get-tuple-element.196) | copy-start | bytes 1769476
  1203.6 154.0 %copy-start.41 = (bf16[4,256,4,72]{1,3,2,0:T(8,128)(2,1)}, bf16[4,256,4,72]{1,3,2,0:T(8,128)(2,1)S(1)}, u32[]{:S(2)}) copy-start(bf16[4,256,4,72]{1,3,2,0:T(8,128)(2,1)S(1)} %get-tuple-element.197) | copy-start | bytes 1769476
  1210.6 97.0 %reduce-scatter.28.cloned.1.call-start = ((), (), s32[]{:S(2)}) async-start(), calls=%async_computation.32 | async-start | bytes 2949120 | tf_op jit(solution)/shard_map/reduce_scatter | solution.py:242
  1216.3 141.3 %copy-start.55 = (bf16[4,4,72,256]{3,2,1,0:T(8,128)(2,1)}, bf16[4,4,72,256]{3,2,1,0:T(8,128)(2,1)S(1)}, u32[]{:S(2)}) copy-start(bf16[4,4,72,256]{3,2,1,0:T(8,128)(2,1)S(1)} %fusion.85) | copy-start | bytes 1769476
  1221.5 87.4 %copy-start.88 = (f32[4,1152]{1,0:T(4,128)S(1)}, f32[4,1152]{1,0:T(4,128)}, u32[]{:S(2)}) copy-start(f32[4,1152]{1,0:T(4,128)} %copy-done.87) | copy-start | bytes 55300
  1221.5 87.4 %copy-start.91 = (f32[4,1152]{1,0:T(4,128)S(1)}, f32[4,1152]{1,0:T(4,128)}, u32[]{:S(2)}) copy-start(f32[4,1152]{1,0:T(4,128)} %copy-done.90) | copy-start | bytes 55300
  1221.5 87.4 %copy-start.130 = (f32[4,64]{1,0:T(4,128)S(1)}, f32[4,64]{1,0:T(4,128)}, u32[]{:S(2)}) copy-start(f32[4,64]{1,0:T(4,128)} %copy-done.129) | copy-start | bytes 3076
  1221.5 87.4 %copy-start.132 = (f32[4,64]{1,0:T(4,128)S(1)}, f32[4,64]{1,0:T(4,128)}, u32[]{:S(2)}) copy-start(f32[4,64]{1,0:T(4,128)} %copy-done.131) | copy-start | bytes 3076
  1221.5 126.7 %all-reduce.19.cloned.1.call-start = ((), (), s32[]{:S(2)}) async-start(), calls=%async_computation.40 | async-start | bytes 258048 | tf_op jit(solution)/shard_map/psum | solution.py:252
  1231.7 77.2 %copy-start.11 = (bf16[8,64,1152]{2,1,0:T(8,128)(2,1)S(1)}, bf16[8,64,1152]{2,1,0:T(8,128)(2,1)}, u32[]{:S(2)}) copy-start(bf16[8,64,1152]{2,1,0:T(8,128)(2,1)} %param.18) | copy-start | bytes 3538948
  1312.7 104.3 %reduce-scatter.36.cloned.1.call-start = ((), (), s32[]{:S(2)}) async-start(), calls=%async_computation.37 | async-start | bytes 7962624 | tf_op jit(solution)/shard_map/reduce_scatter | solution.py:276
  1324.3 145.4 %reduce-scatter.38.cloned.1.call-start = ((), (), s32[]{:S(2)}) async-start(), calls=%async_computation.38 | async-start | bytes 3981312 | tf_op jit(solution)/shard_map/reduce_scatter | solution.py:277
  1332.6 180.8 %reduce-scatter.34.cloned.1.call-start = ((), (), s32[]{:S(2)}) async-start(), calls=%async_computation.36 | async-start | bytes 1990656 | tf_op jit(solution)/shard_map/reduce_scatter | solution.py:275
  1339.7 234.2 %all-reduce.15.cloned.1.call-start = ((), (), s32[]{:S(2)}) async-start(), calls=%async_computation.33 | async-start | bytes 2359296 | tf_op jit(solution)/shard_map/psum | solution.py:281
  1357.5 276.4 %reduce-scatter.32.cloned.1.call-start = ((), (), s32[]{:S(2)}) async-start(), calls=%async_computation.35 | async-start | bytes 5971968 | tf_op jit(solution)/shard_map/reduce_scatter | solution.py:274
  1366.9 353.7 %reduce-scatter.30.cloned.1.call-start = ((), (), s32[]{:S(2)}) async-start(), calls=%async_computation.34 | async-start | bytes 11943936 | tf_op jit(solution)/shard_map/reduce_scatter | solution.py:278
  1380.4 43.2 %copy-start.15 = (f32[4,64,1152]{2,1,0:T(8,128)S(1)}, f32[4,64,1152]{2,1,0:T(8,128)}, u32[]{:S(2)}) copy-start(f32[4,64,1152]{2,1,0:T(8,128)} %get-tuple-element.116) | copy-start | bytes 3538948
  1380.4 43.2 %copy-start.22 = (bf16[4,64,1152]{2,1,0:T(8,128)(2,1)S(1)}, bf16[4,64,1152]{2,1,0:T(8,128)(2,1)}, u32[]{:S(2)}) copy-start(bf16[4,64,1152]{2,1,0:T(8,128)(2,1)} %reduce-scatter.28.cloned.1.call-done) | copy-start | bytes 1769476
  1381.5 38.3 %copy-start.44 = (bf16[4,256,4,72]{1,3,2,0:T(8,128)(2,1)S(1)}, bf16[4,256,4,72]{1,3,2,0:T(8,128)(2,1)}, u32[]{:S(2)}) copy-start(bf16[4,256,4,72]{1,3,2,0:T(8,128)(2,1)} %copy-done.43) | copy-start | bytes 1769476
  1426.0 296.9 %copy-start.1 = (bf16[1000,288]{0,1:T(8,128)(2,1)S(1)}, bf16[1000,288]{0,1:T(8,128)(2,1)}, u32[]{:S(2)}) copy-start(bf16[1000,288]{0,1:T(8,128)(2,1)} %param.22) | copy-start | bytes 1728004
  (145 other events, 397.6 us)
Sparse Core Ops, SparseCore 0:
  9.9 44.0 all-gather.12
  61.2 35.0 all-reduce.16
  98.3 32.1 all-gather.16
  132.7 50.4 all-gather.14
  185.2 49.2 all-gather.24
  300.2 84.1 reduce-scatter.13
  386.7 85.7 reduce-scatter.17
  475.2 34.4 all-gather.20
  511.3 50.4 all-gather.18
  563.7 25.3 all-gather.22
  590.8 50.4 all-gather.28
  643.3 49.2 all-gather.26
  694.3 49.2 all-gather.32
  745.9 46.8 reduce-scatter.15
  795.1 84.7 reduce-scatter.21
  882.7 48.5 reduce-scatter.19
  933.5 84.7 reduce-scatter.25
  1030.7 50.9 all-gather.30
  1084.0 49.2 all-gather.34
  1210.7 46.8 reduce-scatter.23
  1260.0 47.5 reduce-scatter.27
  1312.8 35.4 all-reduce.18
  1351.8 65.1 reduce-scatter.35
  1421.3 48.3 reduce-scatter.37
  1474.0 39.3 reduce-scatter.33
  1516.8 57.0 all-reduce.14
  1577.7 56.0 reduce-scatter.31
  1638.3 82.1 reduce-scatter.29
where the time goes:
time: 1740 us; the launch traced here: 1730 us
  waiting for transfers between devices  1280 us (74%)
  matrix products  193 us (11%)
  other arithmetic  125 us (7%)
  local copies, waits for them, and re-layouts  79.1 us (5%)
  blocking collectives  38.4 us (2%)
    reduce_scatter x2, waiting for transfers between devices, on_device(): lax.psum_scatter(d_fin_part, 'tensor', scatter_dimension=1, tiled=True)  174 us
    reduce_scatter x2, waiting for transfers between devices, on_device(): lax.psum_scatter(proj_part, 'tensor', scatter_dimension=1, tiled=True)  159 us
    all_gather x2, waiting for transfers between devices, on_device(): attn_all = lax.all_gather(attn_in, 'tensor', axis=1, tiled=True)  96 us
    all_gather x2, waiting for transfers between devices, on_device(): d_ffn_all = lax.all_gather(d_ffn_low, 'tensor', axis=1, tiled=True)  93.6 us
    all_gather x2, waiting for transfers between devices, on_device(): d_attn_all = lax.all_gather(d_attn_low, 'tensor', axis=1, tiled=True)  89.1 us
    reduce_scatter x1, waiting for transfers between devices, on_device(): lax.psum_scatter(micro_grads[4], 'dp', scatter_dimension=2, tiled=True)  86.7 us
    all_gather x2, waiting for transfers between devices, on_device(): ffn_all = lax.all_gather(ffn_in, 'tensor', axis=1, tiled=True)  79.9 us
    reduce_scatter x2, waiting for transfers between devices, on_device(): lax.psum_scatter(d_ain_part.astype(jnp.bfloat16), 'tensor', scatter_dimen...  74.7 us
  transfers between devices with their start and end apart: 28, of which 28 were waited for; matrix products, arithmetic and copies ran while one was open for 12% of the time, Pallas kernels for 0%

commit v1 on v0

v1 whole, which is shorter than its diff:
```python
import math

import jax
import jax.numpy as jnp
from jax import lax
from jax.sharding import Mesh
from jax.sharding import PartitionSpec as P

D = 1152
HEAD_DIM = 72
CLASSES = 1000
GRID = 16
F32 = jnp.float32
BF16 = jnp.bfloat16
CHIPS = "p"
CORES = "c"
LINE = "t"
EVERY = (CHIPS, CORES, LINE)
DATA = (CHIPS, CORES)


def rms_rows(values):
    return values * lax.rsqrt(jnp.mean(values * values, axis=-1, keepdims=True) + 1e-06)


def modulate(values, shift_rows, scale_rows):
    return rms_rows(values) * (1.0 + scale_rows) + shift_rows


def rotate_pairs(values):
    paired = values.reshape(values.shape[:-1] + (values.shape[-1] // 2, 2))
    return jnp.stack((-paired[..., 1], paired[..., 0]), axis=-1).reshape(values.shape)


def rotary_tables(patch_cells):
    row_place = (patch_cells // GRID).astype(F32)
    col_place = (patch_cells % GRID).astype(F32)
    rates = 10000.0 ** (-4.0 * jnp.arange(HEAD_DIM // 4, dtype=F32) / HEAD_DIM)
    rates = jnp.repeat(rates, 2)
    angles = jnp.concatenate((row_place[..., None] * rates, col_place[..., None] * rates), axis=-1)
    return (jnp.cos(angles)[..., None, :], jnp.sin(angles)[..., None, :])


def wave_columns(timesteps, first, width):
    half_width = D // 2
    columns = first + jnp.arange(width, dtype=jnp.int32)
    is_cos = columns < half_width
    spot = jnp.where(is_cos, columns, columns - half_width).astype(F32)
    rates = jnp.exp(-math.log(10000.0) * spot / half_width)
    phases = timesteps.astype(F32)[:, None] * rates[None, :]
    return jnp.where(is_cos[None, :], jnp.cos(phases), jnp.sin(phases))


def prepare_heads(q_cols, k_cols, q_gain, k_gain, cosines, sines):
    q_normed = rms_rows(q_cols) * q_gain
    k_normed = rms_rows(k_cols) * k_gain
    q_turned = q_normed * cosines + rotate_pairs(q_normed) * sines
    k_turned = k_normed * cosines + rotate_pairs(k_normed) * sines
    return (q_turned, k_turned)


def swiglu(gate_vals, up_vals):
    return jax.nn.silu(gate_vals) * up_vals


def axis_len(name):
    return lax.axis_size(name)


def swap(values, name, bit=1):
    count = axis_len(name)
    return lax.ppermute(values, name, [(i, i ^ bit) for i in range(count)])


def sum_by_swaps(values, name):
    count = axis_len(name)
    bit = 1
    while bit < count:
        values = values + swap(values, name, bit)
        bit *= 2
    return values


def gather_weight(piece):
    held = lax.all_gather(piece, LINE, axis=0)
    line, rows, cols = held.shape
    chips = axis_len(CHIPS)
    if chips != 4:
        return lax.all_gather(held, CHIPS, axis=1, tiled=True)
    me = lax.axis_index(CHIPS)
    half = line // 2
    from_x = swap(held, CHIPS, 1)
    from_y = swap(held, CHIPS, 2)
    diag_a = swap(from_x[:half], CHIPS, 2)
    diag_b = swap(from_y[half:], CHIPS, 1)
    whole = jnp.zeros((line, chips * rows, cols), piece.dtype)
    for part, flip, top in (
        (held, 0, 0),
        (from_x, 1, 0),
        (from_y, 2, 0),
        (diag_a, 3, 0),
        (diag_b, 3, half),
    ):
        whole = lax.dynamic_update_slice(whole, part, (top, (me ^ flip) * rows, 0))
    return whole


def scatter_grad(grad):
    line, all_rows, cols = grad.shape
    chips = axis_len(CHIPS)
    if chips != 4:
        grad = lax.psum_scatter(grad, CHIPS, scatter_dimension=1, tiled=True)
        return lax.psum_scatter(grad, LINE, scatter_dimension=0, tiled=False)
    rows = all_rows // chips
    me = lax.axis_index(CHIPS)
    half = line // 2

    def part(flip, top, count):
        return lax.dynamic_slice(grad, (top, (me ^ flip) * rows, 0), (count, rows, cols))

    got_x = swap(part(3, 0, half), CHIPS, 1)
    got_y = swap(part(3, half, line - half), CHIPS, 2)
    to_y = jnp.concatenate((part(2, 0, half) + got_x, part(2, half, line - half)), axis=0)
    to_x = jnp.concatenate((part(1, 0, half), part(1, half, line - half) + got_y), axis=0)
    from_y = swap(to_y, CHIPS, 2)
    from_x = swap(to_x, CHIPS, 1)
    own = (part(0, 0, line).astype(F32) + from_x.astype(F32) + from_y.astype(F32)).astype(BF16)
    return lax.psum_scatter(own, LINE, scatter_dimension=0, tiled=False)


def with_peer(values):
    return jnp.concatenate((values, swap(values, CORES)), axis=0)


def fold_peer(values):
    own = values.shape[0] // 2
    sent = swap(values[own:].astype(BF16), CORES)
    return values[:own] + sent.astype(F32)


def on_device(
    tokens,
    timesteps,
    labels,
    patch_cells,
    class_table,
    ada_weight,
    ada_bias,
    qkv_weight,
    qkv_bias,
    q_gain,
    k_gain,
    out_weight,
    out_bias,
    gate_up_weight,
    gate_up_bias,
    down_weight,
    down_bias,
    cotangent,
):
    core = lax.axis_index(CORES)
    line_at = lax.axis_index(LINE)
    line = axis_len(LINE)
    data = axis_len(CHIPS) * axis_len(CORES)
    devices = data * line
    images = tokens.shape[0]
    own_images = images // line
    width = class_table.shape[1]
    chunk = ada_weight.shape[2]
    inv_root = 1.0 / math.sqrt(HEAD_DIM)
    highest = lax.Precision.HIGHEST

    rows_w = qkv_weight.shape[0]
    head_cols = qkv_weight.shape[2] // 2
    ff_cols = gate_up_weight.shape[2] // 2

    def column_halves(which):
        qkv_half = lax.dynamic_slice_in_dim(qkv_weight, which * head_cols, head_cols, 2)
        out_half = lax.dynamic_slice_in_dim(out_weight, which * head_cols, head_cols, 0)
        gu_half = lax.dynamic_slice_in_dim(gate_up_weight, which * ff_cols, ff_cols, 2)
        down_half = lax.dynamic_slice_in_dim(down_weight, which * ff_cols, ff_cols, 0)
        return jnp.concatenate(
            (
                qkv_half.reshape(rows_w, 3 * head_cols),
                out_half.T,
                gu_half.reshape(rows_w, 2 * ff_cols),
                down_half.T,
            ),
            axis=1,
        )

    kept = column_halves(core)
    got = swap(column_halves(1 - core), CORES)
    both = jnp.concatenate(
        (jnp.where(core == 0, kept, got), jnp.where(core == 0, got, kept)), axis=0
    )
    attn_cols = 4 * head_cols
    w_attn = gather_weight(both[:, :attn_cols])
    w_ffn = gather_weight(both[:, attn_cols:])
    w_qkv = w_attn[:, :, : 3 * head_cols]
    w_out = w_attn[:, :, 3 * head_cols :]
    w_gu = w_ffn[:, :, : 2 * ff_cols]
    w_down = w_ffn[:, :, 2 * ff_cols :]

    small_in = lax.all_gather(jnp.stack((labels, timesteps)), DATA, axis=0)
    labels_all = small_in[:, 0].reshape(data * images)
    steps_all = small_in[:, 1].reshape(data * images)
    bias_in = jnp.concatenate((qkv_bias.reshape(-1), gate_up_bias.reshape(-1)))
    bias_all = lax.all_gather(bias_in, LINE, axis=0).astype(F32)
    qkv_b = bias_all[:, : 6 * head_cols].reshape(line, 3, 2, head_cols)
    qkv_b = lax.dynamic_index_in_dim(qkv_b, core, 2, keepdims=False).reshape(line, 3 * head_cols)
    gu_b = bias_all[:, 6 * head_cols :].reshape(line, 2, 2, ff_cols)
    gu_b = lax.dynamic_index_in_dim(gu_b, core, 2, keepdims=False).reshape(line, 2 * ff_cols)

    one_hot = (labels_all[:, None] == jnp.arange(CLASSES, dtype=jnp.int32)[None, :]).astype(BF16)
    cond = jnp.dot(one_hot, class_table, preferred_element_type=F32)
    cond = cond + wave_columns(steps_all, line_at * width, width)
    cond_low = jax.nn.silu(cond).astype(BF16)
    ada_flat = ada_weight.reshape(width, 6 * chunk)
    mod_part = jnp.dot(cond_low, ada_flat, preferred_element_type=F32)
    mod_part = lax.all_to_all(
        mod_part.reshape(devices, own_images * 6 * chunk), EVERY, 0, 0, tiled=True
    )
    mod = jnp.sum(mod_part.reshape(data, line, own_images, 6, chunk), axis=1)
    mod = mod.transpose(1, 2, 0, 3).reshape(own_images, 6, D) + ada_bias.astype(F32)
    shift_a, scale_a, gate_a, shift_f, scale_f, gate_f = (mod[:, k : k + 1] for k in range(6))

    cells = lax.dynamic_slice_in_dim(patch_cells, line_at * own_images, own_images, 0)
    cosines, sines = rotary_tables(with_peer(cells))
    cosines, sines = cosines[:, :, None], sines[:, :, None]
    q_gain_f = q_gain.astype(F32)
    k_gain_f = k_gain.astype(F32)

    x_rows = lax.all_to_all(tokens, LINE, 0, 1, tiled=True).astype(F32)
    attn_in = with_peer(modulate(x_rows, shift_a, scale_a).astype(BF16))
    qkv = jnp.einsum("bpd,zdn->bpzn", attn_in, w_qkv, preferred_element_type=F32) + qkv_b
    pair, patches = qkv.shape[:2]
    qkv = qkv.reshape(pair, patches, line, 3, head_cols // HEAD_DIM, HEAD_DIM)
    q_cols, k_cols = qkv[:, :, :, 0], qkv[:, :, :, 1]
    q_rot, k_rot = prepare_heads(q_cols, k_cols, q_gain_f, k_gain_f, cosines, sines)
    q_low, k_low = q_rot.astype(BF16), k_rot.astype(BF16)
    v_low = qkv[:, :, :, 2].astype(BF16)
    scores = (
        jnp.einsum("bqzhe,bkzhe->bzhqk", q_low, k_low, preferred_element_type=F32) * inv_root
    )
    peak = jnp.max(scores, axis=-1, keepdims=True)
    expo = jnp.exp(scores - peak)
    totals_row = jnp.sum(expo, axis=-1, keepdims=True)
    log_total = peak + jnp.log(totals_row)
    probs_low = (expo / totals_row).astype(BF16)
    heads_out = jnp.einsum("bzhqk,bkzhe->bqzhe", probs_low, v_low, preferred_element_type=F32)
    heads_out = heads_out.astype(BF16).reshape(pair, patches, line, head_cols)
    attn = fold_peer(
        jnp.einsum("bpzc,zdc->bpd", heads_out, w_out, preferred_element_type=F32)
    ) + out_bias.astype(F32)
    mid = x_rows + gate_a * attn
    ffn_in = with_peer(modulate(mid, shift_f, scale_f).astype(BF16))
    gate_up = jnp.einsum("bpd,zdn->bpzn", ffn_in, w_gu, preferred_element_type=F32) + gu_b
    gate_vals, up_vals = gate_up[..., :ff_cols], gate_up[..., ff_cols:]
    hidden = swiglu(gate_vals, up_vals).astype(BF16)
    ffn = fold_peer(
        jnp.einsum("bpzf,zdf->bpd", hidden, w_down, preferred_element_type=F32)
    ) + down_bias.astype(F32)
    output = lax.all_to_all((mid + gate_f * ffn).astype(BF16), LINE, 1, 0, tiled=True)

    grad_out = lax.all_to_all(cotangent, LINE, 0, 1, tiled=True).astype(F32)
    d_ffn_f = gate_f * grad_out
    down_bias_part = jnp.sum(d_ffn_f, axis=(0, 1))
    d_gate_f = jnp.sum(grad_out * ffn, axis=1, keepdims=True)
    d_ffn = with_peer(d_ffn_f.astype(BF16))
    g_down = jnp.einsum("bpd,bpzf->zdf", d_ffn, hidden, preferred_element_type=F32)
    d_hidden = jnp.einsum("bpd,zdf->bpzf", d_ffn, w_down, preferred_element_type=F32)
    d_gate, d_up = jax.vjp(swiglu, gate_vals, up_vals)[1](d_hidden)
    d_gu = jnp.concatenate((d_gate, d_up), axis=-1).astype(BF16)
    gu_bias_part = jnp.sum(d_gu, axis=(0, 1), dtype=F32)
    g_gu = jnp.einsum("bpd,bpzn->zdn", ffn_in, d_gu, preferred_element_type=F32)
    g_ffn = scatter_grad(jnp.concatenate((g_gu.astype(BF16), g_down.astype(BF16)), axis=-1))
    d_ffn_in = fold_peer(jnp.einsum("bpzn,zdn->bpd", d_gu, w_gu, preferred_element_type=F32))
    mid_grad, d_shift_f, d_scale_f = jax.vjp(modulate, mid, shift_f, scale_f)[1](d_ffn_in)
    d_mid = grad_out + mid_grad
    d_attn_f = gate_a * d_mid
    out_bias_part = jnp.sum(d_attn_f, axis=(0, 1))
    d_gate_a = jnp.sum(d_mid * attn, axis=1, keepdims=True)
    d_attn = with_peer(d_attn_f.astype(BF16))
    g_out = jnp.einsum("bpd,bpzc->zdc", d_attn, heads_out, preferred_element_type=F32)
    d_heads = jnp.einsum("bpd,zdc->bpzc", d_attn, w_out, preferred_element_type=F32)
    d_heads = d_heads.astype(BF16).reshape(q_low.shape)
    scores = (
        jnp.einsum("bqzhe,bkzhe->bzhqk", q_low, k_low, preferred_element_type=F32) * inv_root
    )
    probs_f = jnp.exp(scores - log_total)
    d_probs = jnp.einsum("bqzhe,bkzhe->bzhqk", d_heads, v_low, preferred_element_type=F32)
    d_vals = jnp.einsum(
        "bzhqk,bqzhe->bkzhe", probs_f.astype(BF16), d_heads, preferred_element_type=F32
    )
    d_scores = probs_f * (d_probs - jnp.sum(d_probs * probs_f, axis=-1, keepdims=True))
    d_scores = d_scores.astype(BF16)
    d_qrot = (
        jnp.einsum("bzhqk,bkzhe->bqzhe", d_scores, k_low, preferred_element_type=F32) * inv_root
    )
    d_krot = (
        jnp.einsum("bzhqk,bqzhe->bkzhe", d_scores, q_low, preferred_element_type=F32) * inv_root
    )
    prepare_back = jax.vjp(prepare_heads, q_cols, k_cols, q_gain_f, k_gain_f, cosines, sines)[1]
    d_q, d_k, q_gain_part, k_gain_part = prepare_back((d_qrot, d_krot))[:4]
    d_qkv = jnp.stack((d_q, d_k, d_vals), axis=3).astype(BF16)
    d_qkv = d_qkv.reshape(pair, patches, line, 3 * head_cols)
    qkv_bias_part = jnp.sum(d_qkv, axis=(0, 1), dtype=F32)
    g_qkv = jnp.einsum("bpd,bpzn->zdn", attn_in, d_qkv, preferred_element_type=F32)
    g_attn = scatter_grad(jnp.concatenate((g_qkv.astype(BF16), g_out.astype(BF16)), axis=-1))
    d_attn_in = fold_peer(jnp.einsum("bpzn,zdn->bpd", d_qkv, w_qkv, preferred_element_type=F32))
    row_grad, d_shift_a, d_scale_a = jax.vjp(modulate, x_rows, shift_a, scale_a)[1](d_attn_in)
    tokens_grad = lax.all_to_all(
        (d_mid + row_grad).astype(BF16), LINE, 1, 0, tiled=True
    ).astype(F32)

    d_mod = jnp.concatenate(
        (d_shift_a, d_scale_a, d_gate_a, d_shift_f, d_scale_f, d_gate_f), axis=1
    )
    ada_bias_part = jnp.sum(d_mod, axis=0)
    d_mod_low = d_mod.astype(BF16).reshape(own_images, 6, data, chunk).transpose(2, 0, 1, 3)
    d_mod_low = jnp.broadcast_to(
        d_mod_low[:, None], (data, line, own_images, 6, chunk)
    ).reshape(devices, own_images * 6 * chunk)
    d_mod_all = lax.all_to_all(d_mod_low, EVERY, 0, 0, tiled=True)
    d_mod_all = d_mod_all.reshape(data * images, 6 * chunk)
    g_ada = jnp.einsum("bc,be->ce", cond_low, d_mod_all, preferred_element_type=F32)
    g_ada = g_ada.reshape(width, 6, chunk)
    d_silu = jnp.einsum("be,ce->bc", d_mod_all, ada_flat, preferred_element_type=F32)
    d_cond = jax.vjp(jax.nn.silu, cond)[1](d_silu)[0]

    def by_core(part, groups, cols):
        spread = jnp.zeros((line, groups, 2, cols), F32)
        return lax.dynamic_update_slice(
            spread, part.reshape(line, groups, 1, cols), (0, 0, core, 0)
        )

    parts = (
        by_core(qkv_bias_part, 3, head_cols),
        by_core(gu_bias_part, 2, ff_cols),
        ada_bias_part,
        out_bias_part,
        down_bias_part,
        q_gain_part,
        k_gain_part,
    )
    flat = jnp.concatenate([part.reshape(-1) for part in parts])
    count = flat.shape[0]
    flat = jnp.concatenate((flat, d_cond.reshape(-1)))
    flat = sum_by_swaps(sum_by_swaps(flat, CORES), CHIPS)
    d_cond = flat[count:].reshape(d_cond.shape)
    flat = sum_by_swaps(flat[:count], LINE)
    sums = []
    at = 0
    for part in parts:
        sums.append(flat[at : at + part.size].reshape(part.shape))
        at += part.size
    qkv_bias_grad = lax.dynamic_index_in_dim(sums[0], line_at, 0, keepdims=False)
    gu_bias_grad = lax.dynamic_index_in_dim(sums[1], line_at, 0, keepdims=False)
    table_grad = jnp.dot(one_hot.astype(F32).T, d_cond, precision=highest)

    g_both = jnp.concatenate((g_attn, g_ffn), axis=1)
    kept = lax.dynamic_slice_in_dim(g_both, core * rows_w, rows_w, 0)
    got = swap(lax.dynamic_slice_in_dim(g_both, (1 - core) * rows_w, rows_w, 0), CORES)
    low_half = jnp.where(core == 0, kept, got).astype(F32)
    high_half = jnp.where(core == 0, got, kept).astype(F32)

    def joined(first, groups, cols):
        last = first + groups * cols
        return jnp.concatenate(
            (
                low_half[:, first:last].reshape(rows_w, groups, cols),
                high_half[:, first:last].reshape(rows_w, groups, cols),
            ),
            axis=2,
        )

    g_qkv = joined(0, 3, head_cols)
    g_out = joined(3 * head_cols, 1, head_cols)[:, 0].T
    g_gu = joined(attn_cols, 2, ff_cols)
    g_down = joined(attn_cols + 2 * ff_cols, 1, ff_cols)[:, 0].T
    return (
        output,
        tokens_grad,
        table_grad,
        g_ada,
        sums[2],
        g_qkv,
        qkv_bias_grad.reshape(qkv_bias.shape),
        sums[5],
        sums[6],
        g_out,
        sums[3],
        g_gu,
        gu_bias_grad.reshape(gate_up_bias.shape),
        g_down,
        sums[4],
    )


def solution(mesh):
    chips = mesh.shape["dp"] // 2
    finer = Mesh(mesh.devices.reshape(chips, 2, mesh.shape["tensor"]), EVERY)
    in_specs = (
        P(DATA, LINE, None),
        P(DATA),
        P(DATA),
        P(DATA, None),
        P(None, LINE),
        P(LINE, None, DATA),
        P(),
        P(DATA, None, LINE),
        P(None, LINE),
        P(),
        P(),
        P(LINE, DATA),
        P(),
        P(DATA, None, LINE),
        P(None, LINE),
        P(LINE, DATA),
        P(),
        P(DATA, LINE, None),
    )
    out_specs = (
        P(DATA, LINE, None),
        P(DATA, LINE, None),
        P(None, LINE),
        P(LINE, None, DATA),
        P(),
        P(DATA, None, LINE),
        P(None, LINE),
        P(),
        P(),
        P(LINE, DATA),
        P(),
        P(DATA, None, LINE),
        P(None, LINE),
        P(LINE, DATA),
        P(),
    )
    return jax.shard_map(
        on_device, mesh=finer, in_specs=in_specs, out_specs=out_specs, check_vma=False
    )
```

time: 1740 us -> 867 us (0.50)
  waiting for transfers between devices: 1280 us -> 300 us
  local copies, waits for them, and re-layouts: 79.1 us -> 198 us
  matrix products: 193 us -> 111 us
  starting transfers between devices: 2.7 us -> 61.4 us
  blocking collectives: 38.4 us -> 57.3 us
    reduce_scatter x13 -> x2, waiting for transfers between devices: 724 us -> 0.01 us  [scatter_grad(): return lax.psum_scatter(own, LINE, scatter_dimension=0, tiled=False)]
    all_gather x12 -> x2, waiting for transfers between devices: 453 us -> 13.5 us  [gather_weight(): held = lax.all_gather(piece, LINE, axis=0)]
    ppermute x0 -> x32, waiting for transfers between devices: none -> 195 us  [swap(): return lax.ppermute(values, name, [(i, i ^ bit) for i in range(count)])]
    psum x3 -> x0, waiting for transfers between devices: 94.7 us -> none  [the longest x1 60.5 us: on_device(): lax.psum((table_total, ada_bias_total, qkv_bias_total, gate_up_bias_total...]
    all_to_all x0 -> x6, waiting for transfers between devices: none -> 91.7 us  [the longest x1 52.6 us: on_device(): lax.all_to_all((mid + gate_f * ffn).astype(BF16), LINE, 1, 0, tiled=True)]
    dynamic_update_slice x0 -> x12, local copies, waits for them, and re-layouts: none -> 89.8 us  [the longest x10 89.5 us: gather_weight(): whole = lax.dynamic_update_slice(whole, part, (top, (me ^ flip) * rows, 0))]
    dot_general x45 -> x23, matrix products: 193 us -> 111 us  [the longest x1 12 us: on_device(): jnp.einsum('bpd,zdf->bpzf', d_ffn, w_down, preferred_element_type=F32)]
    unnamed x0 -> x1, blocking collectives: none -> 47 us
  transfers between devices with their start and end apart: 28 -> 42, of which waited for: 28 -> 16; matrix products, arithmetic and copies ran while one was open for 12% -> 41% of each run, Pallas kernels for 0% -> 0%
where the time goes in v1:
time: 867 us; the launch traced here: 857 us
  waiting for transfers between devices  300 us (35%)
  local copies, waits for them, and re-layouts  198 us (23%)
  other arithmetic  112 us (13%)
  matrix products  111 us (13%)
  starting transfers between devices  61.4 us (7%)
  blocking collectives  57.3 us (7%)
  between operations  16.7 us (2%)
    ppermute x32, waiting for transfers between devices, swap(): return lax.ppermute(values, name, [(i, i ^ bit) for i in range(count)])  195 us
    dynamic_update_slice x10, local copies, waits for them, and re-layouts, gather_weight(): whole = lax.dynamic_update_slice(whole, part, (top, (me ^ flip) * rows, 0))  89.5 us
    all_to_all x1, waiting for transfers between devices, on_device(): lax.all_to_all((mid + gate_f * ffn).astype(BF16), LINE, 1, 0, tiled=True)  52.6 us
    unnamed x1, blocking collectives  47 us
    ppermute x32, starting transfers between devices, swap(): return lax.ppermute(values, name, [(i, i ^ bit) for i in range(count)])  33.7 us
    all_to_all x1, waiting for transfers between devices, on_device(): x_rows = lax.all_to_all(tokens, LINE, 0, 1, tiled=True).astype(F32)  26.4 us
    unnamed x207, local copies, waits for them, and re-layouts  19.8 us
  transfers between devices with their start and end apart: 42, of which 16 were waited for; matrix products, arithmetic and copies ran while one was open for 41% of the time, Pallas kernels for 0%

profile of v1, /device:TPU:0, one launch (start us, length us, event | category | flops | bytes accessed | tf_op | source)
XLA Modules:
  0.0 856.8 jit_solution(16375936913948829748)
XLA Ops:
  15.6 10.3 %all-gather.4 = s32[8,2,8]{2,1,0:T(2,128)S(1)} all-gather(s32[1,2,8]{2,1,0:T(2,128)S(1)} %add_bitcast_fusion), channel_id=2, replica_groups=mesh['p'=4,'c'=2,'t'=4] {'p','c'}, dimensions={0}, use_global_device_ids=true | all-gather | bytes 576 | tf_op jit(solution)/shard_map/all_gather | solution.py:205
  28.6 4.9 all-to-all-start.1
  34.7 12.7 %all-to-all-done.1 = f32[32,1,1728]{2,1,0:T(1,128)S(1)} async-done(((f32[32,1,1728]{2,1,0:T(1,128)}), f32[32,1,1728]{2,1,0:T(1,128)S(1)}, u32[]{:S(2)}, u32[]{:S(2)}) %all-to-all-start.1) | async-done | bytes 221216 | tf_op jit(solution)/shard_map/all_to_all | solution.py:221
  47.4 4.7 all-to-all-start
  53.3 13.5 %all-gather.8.cloned.1.call-done = bf16[1152,576]{1,0:T(8,128)(2,1)} async-done(((bf16[288,576]{1,0:T(8,128)(2,1)}), bf16[1152,576]{1,0:T(8,128)(2,1)}) %all-gather.8.cloned.1.call-update) | async-done | bytes 1327120 | tf_op jit(solution)/shard_map/all_gather | solution.py:85
  70.4 26.4 %all-to-all-done = bf16[8,64,1152]{2,1,0:T(8,128)(2,1)S(1)} async-done(((bf16[8,64,1152]{2,1,0:T(8,128)(2,1)}), bf16[8,64,1152]{2,1,0:T(8,128)(2,1)S(1)}, u32[]{:S(2)}, u32[]{:S(2)}) %all-to-all-start) | async-done | bytes 1179680 | tf_op jit(solution)/shard_map/all_to_all | solution.py:234
  100.3 4.3 all-to-all-start.3
  113.8 47.0 %all-reduce.4 = bf16[9600]{0:T(1024)(128)(2,1)S(1)} all-reduce(bf16[9600]{0:T(1024)(128)(2,1)S(1)} %dynamic-update-slice), channel_id=4, replica_groups=mesh['p'=4,'c'=2,'t'=4] {'t'}, use_global_device_ids=true, to_apply=%add.4 | all-reduce | flops 9600 | bytes 38400
  169.4 19.0 %dynamic_update_slice.36 = bf16[4,1152,576]{1,2,0:T(8,128)(2,1)} dynamic-update-slice(bf16[4,1152,576]{1,2,0:T(8,128)(2,1)} %broadcast_in_dim.35, bf16[4,288,576]{1,2,0:T(8,128)(2,1)S(1)} %copy.304, s32[]{:T(128)} %constant.111.clone.1, s32[]{:T(128)S(6)} %select_n.128, s32[]{:T(128)} %constant.111.clone.1) | dynamic-update-slice | bytes 2654212 | tf_op jit(solution)/shard_map/dynamic_update_slice | solution.py:104
  191.2 21.2 %dynamic_update_slice.37 = bf16[4,1152,576]{1,2,0:T(8,128)(2,1)} dynamic-update-slice(bf16[4,1152,576]{1,2,0:T(8,128)(2,1)} %dynamic_update_slice.36, bf16[4,288,576]{1,2,0:T(8,128)(2,1)S(1)} %copy.305, s32[]{:T(128)} %constant.111.clone.1, s32[]{:T(128)S(6)} %select_n.129, s32[]{:T(128)} %constant.111.clone.1) | dynamic-update-slice | bytes 2654212 | tf_op jit(solution)/shard_map/dynamic_update_slice | solution.py:104
  215.3 21.0 %dynamic_update_slice.38 = bf16[4,1152,576]{1,2,0:T(8,128)(2,1)} dynamic-update-slice(bf16[4,1152,576]{1,2,0:T(8,128)(2,1)} %dynamic_update_slice.37, bf16[4,288,576]{1,2,0:T(8,128)(2,1)S(1)} %copy.306, s32[]{:T(128)} %constant.111.clone.1, s32[]{:T(128)S(6)} %select_n.130, s32[]{:T(128)} %constant.111.clone.1) | dynamic-update-slice | bytes 2654212 | tf_op jit(solution)/shard_map/dynamic_update_slice | solution.py:104
  241.8 10.3 %dynamic_update_slice.39 = bf16[4,1152,576]{1,2,0:T(8,128)(2,1)} dynamic-update-slice(bf16[4,1152,576]{1,2,0:T(8,128)(2,1)} %dynamic_update_slice.38, bf16[2,288,576]{1,2,0:T(8,128)(2,1)S(1)} %copy.307, s32[]{:T(128)} %constant.111.clone.1, s32[]{:T(128)S(6)} %select_n.131, s32[]{:T(128)} %constant.111.clone.1) | dynamic-update-slice | bytes 1327108 | tf_op jit(solution)/shard_map/dynamic_update_slice | solution.py:104
  253.7 10.3 %dynamic_update_slice.40 = bf16[4,1152,576]{1,2,0:T(8,128)(2,1)} dynamic-update-slice(bf16[4,1152,576]{1,2,0:T(8,128)(2,1)} %dynamic_update_slice.39, bf16[2,288,576]{1,2,0:T(8,128)(2,1)S(1)} %copy.308, s32[]{:T(128)} %constant.117.clone.1, s32[]{:T(128)S(6)} %select_n.131, s32[]{:T(128)} %constant.111.clone.1) | dynamic-update-slice | bytes 1327108 | tf_op jit(solution)/shard_map/dynamic_update_slice | solution.py:104
  264.0 7.3 broadcast_add_fusion.1
  275.6 4.6 squeeze.28
  288.5 4.0 reshape.495
  303.2 4.2 reshape.496
  307.5 4.8 add_convert_fusion.4
  320.5 4.0 convolution_bitcast_fusion.2
  347.0 22.5 %collective-permute-done.11 = bf16[2,288,1152]{2,1,0:T(8,128)(2,1)S(1)} collective-permute-done((bf16[2,288,1152]{2,1,0:T(8,128)(2,1)S(1)}, bf16[2,288,1152]{2,1,0:T(8,128)(2,1)S(1)}, u32[]{:S(2)}, u32[]{:S(2)}) %collective-permute-start.11) | collective-permute-done | bytes 1327136 | tf_op jit(solution)/shard_map/ppermute | solution.py:72
  372.6 10.8 %broadcast_add_fusion = f32[4,256,4,768]{3,1,2,0:T(8,128)} fusion(f32[4,768]{1,0:T(4,128)S(1)} %bitcast.377, bf16[4,1152,1152]{2,1,0:T(8,128)(2,1)S(1)} %constant_dynamic-update-slice_fusion.12, bf16[2,256,1152]{2,1,0:T(8,128)(2,1)S(1)} %collective-permute-done.8, bf16[2,256,1152]{2,1,0:T(8,128)(2,1)S(1)} %add_convert_fusion.3), kind=kOutput, calls=%fused_computation.44 | convolution fusion | flops 7255621632 | bytes 22032384 | tf_op jit(solution)/shard_map/bpd,zdn->bpzn/dot_general | solution.py:258
  383.4 12.0 %fusion.3 = (bf16[4,256,4,384]{3,1,2,0:T(8,128)(2,1)}, bf16[4,256,4,384]{3,1,2,0:T(8,128)(2,1)}, bf16[4,256,4,384]{3,1,2,0:T(8,128)(2,1)}) fusion(f32[4,256,4,768]{3,1,2,0:T(8,128)} %broadcast_add_fusion, bf16[4,1152,1152]{2,1,0:T(8,128)(2,1)S(1)} %constant_dynamic-update-slice_fusion.12, bf16[2,256,1152]{2,1,0:T(8,128)(2,1)} %collective-permute-done.14, ...), kind=kOutput, calls=%fused_computation.38 | convolution fusion | flops 3653763072 | bytes 27918336 | tf_op jit(solution)/shard_map/bpd,zdf->bpzf/dot_general | solution.py:272
  395.4 11.8 %fusion.10 = f32[4,256,1152]{2,1,0:T(8,128)} fusion(bf16[4,1152,1152]{2,1,0:T(8,128)(2,1)S(1)} %constant_dynamic-update-slice_fusion.12, bf16[4,256,4,384]{3,1,2,0:T(8,128)(2,1)} %get-tuple-element.129, bf16[4,256,4,384]{3,1,2,0:T(8,128)(2,1)} %get-tuple-element.128), kind=kOutput, calls=%fused_computation.59 | convolution fusion | flops 7260340224 | bytes 18087936 | tf_op jit(solution)/shard_map/bpzn,zdn->bpd/dot_general | solution.py:278
  409.3 6.2 convolution_bitcast_fusion.1
  418.7 5.8 fusion.31
  427.6 9.9 %fusion.8 = bf16[4,1152,768]{2,1,0:T(8,128)(2,1)S(1)} fusion(bf16[4,256,4,384]{3,1,2,0:T(8,128)(2,1)S(1)} %copy-done.25, bf16[4,256,4,384]{3,1,2,0:T(8,128)(2,1)S(1)} %copy-done.24, bf16[2,256,1152]{2,1,0:T(8,128)(2,1)} %copy-done.81, bf16[2,256,1152]{2,1,0:T(8,128)(2,1)S(1)} %copy-done.33), kind=kOutput, calls=%fused_computation.48 | convolution fusion | flops 7265058816 | bytes 15728640 | tf_op jit(solution)/shard_map/bpd,bpzn->zdn/dot_general | solution.py:276
  437.5 9.0 %fusion.16 = bf16[4,1152,384]{2,1,0:T(8,128)(2,1)S(1)} fusion(bf16[4,256,4,384]{3,1,2,0:T(8,128)(2,1)} %get-tuple-element.130, bf16[2,256,1152]{2,1,0:T(8,128)(2,1)} %collective-permute-done.14, bf16[2,256,1152]{2,1,0:T(8,128)(2,1)} %fusion.30), kind=kOutput, calls=%fused_computation.68 | convolution fusion | flops 3626827776 | bytes 9043968 | tf_op jit(solution)/shard_map/bpd,bpzf->zdf/dot_general | solution.py:271
  465.6 3.9 reshape.500
  469.5 4.8 fusion.111
  477.5 4.0 reshape.501
  484.1 4.8 fusion.112
  492.2 4.2 reshape.503
  496.4 6.3 multiply_reduce_fusion.3
  504.7 4.3 fusion.17
  510.7 7.2 fusion.9
  525.8 10.8 %collective-permute-done.25 = bf16[2,288,576]{2,1,0:T(8,128)(2,1)S(1)} collective-permute-done((bf16[2,288,576]{2,1,0:T(8,128)(2,1)S(1)}, bf16[2,288,576]{2,1,0:T(8,128)(2,1)S(1)}, u32[]{:S(2)}, u32[]{:S(2)}) %collective-permute-start.25) | collective-permute-done | bytes 663584 | tf_op jit(solution)/shard_map/ppermute | solution.py:72
  539.1 5.2 convolution_bitcast_fusion
  547.4 79.4 %collective-permute-done.23 = bf16[2,288,576]{2,1,0:T(8,128)(2,1)S(1)} collective-permute-done((bf16[2,288,576]{2,1,0:T(8,128)(2,1)S(1)}, bf16[2,288,576]{2,1,0:T(8,128)(2,1)S(1)}, u32[]{:S(2)}, u32[]{:S(2)}) %collective-permute-start.23) | collective-permute-done | bytes 663584 | tf_op jit(solution)/shard_map/ppermute | solution.py:72
  633.6 23.8 %collective-permute-done.26 = bf16[4,288,576]{2,1,0:T(8,128)(2,1)S(1)} collective-permute-done((bf16[4,288,576]{2,1,0:T(8,128)(2,1)S(1)}, bf16[4,288,576]{2,1,0:T(8,128)(2,1)S(1)}, u32[]{:S(2)}, u32[]{:S(2)}) %collective-permute-start.26) | collective-permute-done | bytes 1327136 | tf_op jit(solution)/shard_map/ppermute | solution.py:72
  657.4 5.1 collective-permute-done.24
  668.4 3.8 copy.313
  685.4 32.5 %collective-permute-done.28 = bf16[4,288,1152]{2,1,0:T(8,128)(2,1)} collective-permute-done((bf16[4,288,1152]{2,1,0:T(8,128)(2,1)}, bf16[4,288,1152]{2,1,0:T(8,128)(2,1)}, u32[]{:S(2)}, u32[]{:S(2)}) %collective-permute-start.28) | collective-permute-done | bytes 2654240 | tf_op jit(solution)/shard_map/ppermute | solution.py:72
  717.9 5.7 add_convert_fusion
  724.3 4.4 all-to-all-start.2
  732.8 52.6 %all-to-all-done.2 = bf16[2,256,1152]{2,0,1:T(2,128)(2,1)} async-done(((bf16[2,256,1152]{2,0,1:T(2,128)(2,1)}), bf16[2,256,1152]{2,0,1:T(2,128)(2,1)}, u32[]{:S(2)}, u32[]{:S(2)}) %all-to-all-start.2) | async-done | bytes 1179680 | tf_op jit(solution)/shard_map/all_to_all | solution.py:264
  801.0 5.7 all-to-all-start.4
  811.7 9.4 %collective-permute-done.21 = f32[18960]{0:T(1024)S(1)} collective-permute-done((f32[18960]{0:T(1024)S(1)}, f32[18960]{0:T(1024)S(1)}, u32[]{:S(2)}, u32[]{:S(2)}) %collective-permute-start.21) | collective-permute-done | bytes 75872 | tf_op jit(solution)/shard_map/ppermute | solution.py:72
  821.1 4.6 collective-permute-start.22
  (497 shorter events, 235.2 us)
Async XLA Ops:
  7.2 59.6 %all-gather.8.cloned.1.call-start = ((), (), s32[]{:S(2)}) async-start(), calls=%async_computation.10 | async-start | bytes 1843200 | tf_op jit(solution)/shard_map/all_gather | solution.py:85
  12.5 2.2 collective-permute-start.1
  28.6 18.8 %all-to-all-start.1 = ((f32[32,1,1728]{2,1,0:T(1,128)}), f32[32,1,1728]{2,1,0:T(1,128)S(1)}, u32[]{:S(2)}, u32[]{:S(2)}) async-start(f32[32,1,1728]{2,1,0:T(1,128)} %all_to_all.57), calls=%async_computation.1 | async-start | bytes 458752 | tf_op jit(solution)/shard_map/all_to_all | solution.py:221
  33.5 202.8 %all-gather.10.cloned.1.call-start = ((), (), s32[]{:S(2)}) async-start(), calls=%async_computation.11 | async-start | bytes 3317760 | tf_op jit(solution)/shard_map/all_gather | solution.py:85
  47.4 49.3 %all-to-all-start = ((bf16[8,64,1152]{2,1,0:T(8,128)(2,1)}), bf16[8,64,1152]{2,1,0:T(8,128)(2,1)S(1)}, u32[]{:S(2)}, u32[]{:S(2)}) async-start(bf16[8,64,1152]{2,1,0:T(8,128)(2,1)} %param.18), calls=%async_computation | async-start | bytes 2359296 | tf_op jit(solution)/shard_map/all_to_all | solution.py:234
  66.8 39.1 %collective-permute-start.3 = (bf16[4,288,576]{2,1,0:T(8,128)(2,1)}, bf16[4,288,576]{2,1,0:T(8,128)(2,1)S(1)}, u32[]{:S(2)}, u32[]{:S(2)}) collective-permute-start(bf16[4,288,576]{2,1,0:T(8,128)(2,1)} %bitcast.355), channel_id=1, source_target_pairs={{0,16},{8,24},{16,0},{24,8},{1,17},{9,25},{17,1},{25,9},{2,18},{10... | collective-permute-start | bytes 3981320 | tf_op jit(solution)/shard_map/ppermute | solution.py:72
  68.3 40.2 %collective-permute-start.2 = (bf16[4,288,576]{2,1,0:T(8,128)(2,1)}, bf16[4,288,576]{2,1,0:T(8,128)(2,1)}, u32[]{:S(2)}, u32[]{:S(2)}) collective-permute-start(bf16[4,288,576]{2,1,0:T(8,128)(2,1)} %bitcast.356), channel_id=1, source_target_pairs={{0,8},{8,0},{16,24},{24,16},{1,9},{9,1},{17,25},{25,17},{2,10},{10... | collective-permute-start | bytes 3981320 | tf_op jit(solution)/shard_map/ppermute | solution.py:72
  100.1 61.0 %copy-start.80 = (bf16[72]{0:T(256)(128)(2,1)S(1)}, bf16[72]{0:T(256)(128)(2,1)}, u32[]{:S(2)}) copy-start(bf16[72]{0:T(256)(128)(2,1)} %param.28) | copy-start | bytes 436
  100.2 61.2 %copy-start.73 = (bf16[1152]{0:T(1024)(128)(2,1)S(1)}, bf16[1152]{0:T(1024)(128)(2,1)}, u32[]{:S(2)}) copy-start(bf16[1152]{0:T(1024)(128)(2,1)} %param.30) | copy-start | bytes 6916
  100.2 163.9 %collective-permute-start = (bf16[2,256,1152]{2,1,0:T(8,128)(2,1)}, bf16[2,256,1152]{2,1,0:T(8,128)(2,1)}, u32[]{:S(2)}, u32[]{:S(2)}) collective-permute-start(bf16[2,256,1152]{2,1,0:T(8,128)(2,1)} %add_convert_fusion.6), channel_id=1, source_target_pairs={{0,4},{4,0},{1,5},{5,1},{2,6},{6,2},{3,7},{7,3},{8,12},{12,8},{9,1... | collective-permute-start | bytes 3538952 | tf_op jit(solution)/shard_map/ppermute | solution.py:72
  100.3 227.5 %all-to-all-start.3 = ((bf16[8,64,1152]{2,1,0:T(8,128)(2,1)}), bf16[8,64,1152]{2,1,0:T(8,128)(2,1)}, u32[]{:S(2)}, u32[]{:S(2)}) async-start(bf16[8,64,1152]{2,1,0:T(8,128)(2,1)} %param.35), calls=%async_computation.3 | async-start | bytes 2359296 | tf_op jit(solution)/shard_map/all_to_all | solution.py:266
  104.5 730.0 %reduce-scatter.3.cloned.1.call-start = ((), (), s32[]{:S(2)}) async-start(), calls=%async_computation.8 | async-start | bytes 1843200 | tf_op jit(solution)/shard_map/reduce_scatter | solution.py:128
  105.3 56.5 %collective-permute-start.6 = (s32[2,256]{1,0:T(2,128)S(1)}, s32[2,256]{1,0:T(2,128)S(1)}, u32[]{:S(2)}, u32[]{:S(2)}) collective-permute-start(s32[2,256]{1,0:T(2,128)S(1)} %constant_dynamic-slice_fusion.3), channel_id=1, source_target_pairs={{0,4},{4,0},{1,5},{5,1},{2,6},{6,2},{3,7},{7,3},{8,12},{12,8},{9,1... | collective-permute-start | bytes 6152 | tf_op jit(solution)/shard_map/ppermute | solution.py:72
  107.0 145.2 %collective-permute-start.5 = (bf16[2,288,576]{2,1,0:T(8,128)(2,1)}, bf16[2,288,576]{2,1,0:T(8,128)(2,1)}, u32[]{:S(2)}, u32[]{:S(2)}) collective-permute-start(bf16[2,288,576]{2,1,0:T(8,128)(2,1)} %slice.227), channel_id=1, source_target_pairs={{0,8},{8,0},{16,24},{24,16},{1,9},{9,1},{17,25},{25,17},{2,10},{10... | collective-permute-start | bytes 1990664 | tf_op jit(solution)/shard_map/ppermute | solution.py:72
  110.5 129.8 %collective-permute-start.4 = (bf16[2,288,576]{2,1,0:T(8,128)(2,1)}, bf16[2,288,576]{2,1,0:T(8,128)(2,1)}, u32[]{:S(2)}, u32[]{:S(2)}) collective-permute-start(bf16[2,288,576]{2,1,0:T(8,128)(2,1)} %slice.226), channel_id=1, source_target_pairs={{0,16},{8,24},{16,0},{24,8},{1,17},{9,25},{17,1},{25,9},{2,18},{10... | collective-permute-start | bytes 1990664 | tf_op jit(solution)/shard_map/ppermute | solution.py:72
  112.2 195.2 %copy-start.67 = (f32[72]{0:T(128)}, f32[72]{0:T(128)S(1)}, u32[]{:S(2)}) copy-start(f32[72]{0:T(128)S(1)} %convert_element_type.250) | copy-start | bytes 868
  161.2 146.2 %copy-start.69 = (f32[72]{0:T(128)}, f32[72]{0:T(128)S(1)}, u32[]{:S(2)}) copy-start(f32[72]{0:T(128)S(1)} %convert_element_type.254) | copy-start | bytes 868
  236.3 103.8 %collective-permute-start.10 = (bf16[4,288,1152]{2,1,0:T(8,128)(2,1)}, bf16[4,288,1152]{2,1,0:T(8,128)(2,1)}, u32[]{:S(2)}, u32[]{:S(2)}) collective-permute-start(bf16[4,288,1152]{2,1,0:T(8,128)(2,1)} %bitcast.347), channel_id=1, source_target_pairs={{0,16},{8,24},{16,0},{24,8},{1,17},{9,25},{17,1},{25,9},{2,18},{10... | collective-permute-start | bytes 7962632 | tf_op jit(solution)/shard_map/ppermute | solution.py:72
  236.7 100.3 %collective-permute-start.9 = (bf16[4,288,1152]{2,1,0:T(8,128)(2,1)}, bf16[4,288,1152]{2,1,0:T(8,128)(2,1)}, u32[]{:S(2)}, u32[]{:S(2)}) collective-permute-start(bf16[4,288,1152]{2,1,0:T(8,128)(2,1)} %bitcast.348), channel_id=1, source_target_pairs={{0,8},{8,0},{16,24},{24,16},{1,9},{9,1},{17,25},{25,17},{2,10},{10... | collective-permute-start | bytes 7962632 | tf_op jit(solution)/shard_map/ppermute | solution.py:72
  327.8 6.4 collective-permute-start.7
  330.6 52.8 %collective-permute-start.14 = (bf16[2,256,1152]{2,1,0:T(8,128)(2,1)}, bf16[2,256,1152]{2,1,0:T(8,128)(2,1)}, u32[]{:S(2)}, u32[]{:S(2)}) collective-permute-start(bf16[2,256,1152]{2,1,0:T(8,128)(2,1)} %fusion.30), channel_id=1, source_target_pairs={{0,4},{4,0},{1,5},{5,1},{2,6},{6,2},{3,7},{7,3},{8,12},{12,8},{9,1... | collective-permute-start | bytes 3538952 | tf_op jit(solution)/shard_map/ppermute | solution.py:72
  338.4 31.1 %collective-permute-start.11 = (bf16[2,288,1152]{2,1,0:T(8,128)(2,1)S(1)}, bf16[2,288,1152]{2,1,0:T(8,128)(2,1)S(1)}, u32[]{:S(2)}, u32[]{:S(2)}) collective-permute-start(bf16[2,288,1152]{2,1,0:T(8,128)(2,1)S(1)} %slice.243), channel_id=1, source_target_pairs={{0,16},{8,24},{16,0},{24,8},{1,17},{9,25},{17,1},{25,9},{2,18},{10... | collective-permute-start | bytes 3981320 | tf_op jit(solution)/shard_map/ppermute | solution.py:72
  341.6 30.8 %collective-permute-start.12 = (bf16[2,288,1152]{2,1,0:T(8,128)(2,1)S(1)}, bf16[2,288,1152]{2,1,0:T(8,128)(2,1)S(1)}, u32[]{:S(2)}, u32[]{:S(2)}) collective-permute-start(bf16[2,288,1152]{2,1,0:T(8,128)(2,1)S(1)} %slice.244), channel_id=1, source_target_pairs={{0,8},{8,0},{16,24},{24,16},{1,9},{9,1},{17,25},{25,17},{2,10},{10... | collective-permute-start | bytes 3981320 | tf_op jit(solution)/shard_map/ppermute | solution.py:72
  342.0 30.6 %collective-permute-start.8 = (bf16[2,256,1152]{2,1,0:T(8,128)(2,1)S(1)}, bf16[2,256,1152]{2,1,0:T(8,128)(2,1)S(1)}, u32[]{:S(2)}, u32[]{:S(2)}) collective-permute-start(bf16[2,256,1152]{2,1,0:T(8,128)(2,1)S(1)} %add_convert_fusion.3), channel_id=1, source_target_pairs={{0,4},{4,0},{1,5},{5,1},{2,6},{6,2},{3,7},{7,3},{8,12},{12,8},{9,1... | collective-permute-start | bytes 3538952 | tf_op jit(solution)/shard_map/ppermute | solution.py:72
  409.2 7.0 collective-permute-start.15
  415.7 3.0 collective-permute-start.13
  425.8 23.3 %collective-permute-start.16 = (bf16[2,256,1152]{2,1,0:T(8,128)(2,1)S(1)}, bf16[2,256,1152]{2,1,0:T(8,128)(2,1)}, u32[]{:S(2)}, u32[]{:S(2)}) collective-permute-start(bf16[2,256,1152]{2,1,0:T(8,128)(2,1)S(1)} %multiply_convert_fusion.3), channel_id=1, source_target_pairs={{0,4},{4,0},{1,5},{5,1},{2,6},{6,2},{3,7},{7,3},{8,12},{12,8},{9,1... | collective-permute-start | bytes 3538952 | tf_op jit(solution)/shard_map/ppermute | solution.py:72
  448.9 71.0 %collective-permute-start.29 = (bf16[2,288,1152]{2,1,0:T(8,128)(2,1)}, bf16[2,288,1152]{2,1,0:T(8,128)(2,1)}, u32[]{:S(2)}, u32[]{:S(2)}) collective-permute-start(bf16[2,288,1152]{2,1,0:T(8,128)(2,1)} %fusion.47), channel_id=1, source_target_pairs={{0,8},{8,0},{16,24},{24,16},{1,9},{9,1},{17,25},{25,17},{2,10},{10... | collective-permute-start | bytes 3981320 | tf_op jit(solution)/shard_map/ppermute | solution.py:72
  518.1 18.5 %collective-permute-start.25 = (bf16[2,288,576]{2,1,0:T(8,128)(2,1)S(1)}, bf16[2,288,576]{2,1,0:T(8,128)(2,1)S(1)}, u32[]{:S(2)}, u32[]{:S(2)}) collective-permute-start(bf16[2,288,576]{2,1,0:T(8,128)(2,1)S(1)} %fusion.56), channel_id=1, source_target_pairs={{0,8},{8,0},{16,24},{24,16},{1,9},{9,1},{17,25},{25,17},{2,10},{10... | collective-permute-start | bytes 1990664 | tf_op jit(solution)/shard_map/ppermute | solution.py:72
  522.0 107.0 %collective-permute-start.27 = (bf16[2,288,1152]{2,1,0:T(8,128)(2,1)S(1)}, bf16[2,288,1152]{2,1,0:T(8,128)(2,1)S(1)}, u32[]{:S(2)}, u32[]{:S(2)}) collective-permute-start(bf16[2,288,1152]{2,1,0:T(8,128)(2,1)S(1)} %get-tuple-element.132), channel_id=1, source_target_pairs={{0,16},{8,24},{16,0},{24,8},{1,17},{9,25},{17,1},{25,9},{2,18},{10... | collective-permute-start | bytes 3981320 | tf_op jit(solution)/shard_map/ppermute | solution.py:72
  525.2 160.2 %collective-permute-start.30 = (bf16[4,288,1152]{2,1,0:T(8,128)(2,1)}, bf16[4,288,1152]{2,1,0:T(8,128)(2,1)}, u32[]{:S(2)}, u32[]{:S(2)}) collective-permute-start(bf16[4,288,1152]{2,1,0:T(8,128)(2,1)} %pad_maximum_fusion.2), channel_id=1, source_target_pairs={{0,16},{8,24},{16,0},{24,8},{1,17},{9,25},{17,1},{25,9},{2,18},{10... | collective-permute-start | bytes 7962632 | tf_op jit(solution)/shard_map/ppermute | solution.py:72
  537.6 89.2 %collective-permute-start.23 = (bf16[2,288,576]{2,1,0:T(8,128)(2,1)S(1)}, bf16[2,288,576]{2,1,0:T(8,128)(2,1)S(1)}, u32[]{:S(2)}, u32[]{:S(2)}) collective-permute-start(bf16[2,288,576]{2,1,0:T(8,128)(2,1)S(1)} %get-tuple-element.136), channel_id=1, source_target_pairs={{0,16},{8,24},{16,0},{24,8},{1,17},{9,25},{17,1},{25,9},{2,18},{10... | collective-permute-start | bytes 1990664 | tf_op jit(solution)/shard_map/ppermute | solution.py:72
  545.6 128.1 %collective-permute-start.17 = (bf16[2,256,1152]{2,1,0:T(8,128)(2,1)}, bf16[2,256,1152]{2,1,0:T(8,128)(2,1)}, u32[]{:S(2)}, u32[]{:S(2)}) collective-permute-start(bf16[2,256,1152]{2,1,0:T(8,128)(2,1)} %slice.356), channel_id=1, source_target_pairs={{0,4},{4,0},{1,5},{5,1},{2,6},{6,2},{3,7},{7,3},{8,12},{12,8},{9,1... | collective-permute-start | bytes 3538952 | tf_op jit(solution)/shard_map/ppermute | solution.py:72
  546.8 110.6 %collective-permute-start.26 = (bf16[4,288,576]{2,1,0:T(8,128)(2,1)S(1)}, bf16[4,288,576]{2,1,0:T(8,128)(2,1)S(1)}, u32[]{:S(2)}, u32[]{:S(2)}) collective-permute-start(bf16[4,288,576]{2,1,0:T(8,128)(2,1)S(1)} %pad_maximum_fusion.8), channel_id=1, source_target_pairs={{0,16},{8,24},{16,0},{24,8},{1,17},{9,25},{17,1},{25,9},{2,18},{10... | collective-permute-start | bytes 3981320 | tf_op jit(solution)/shard_map/ppermute | solution.py:72
  627.2 35.3 %collective-permute-start.24 = (bf16[4,288,576]{2,1,0:T(8,128)(2,1)S(1)}, bf16[4,288,576]{2,1,0:T(8,128)(2,1)S(1)}, u32[]{:S(2)}, u32[]{:S(2)}) collective-permute-start(bf16[4,288,576]{2,1,0:T(8,128)(2,1)S(1)} %pad_maximum_fusion.7), channel_id=1, source_target_pairs={{0,8},{8,0},{16,24},{24,16},{1,9},{9,1},{17,25},{25,17},{2,10},{10... | collective-permute-start | bytes 3981320 | tf_op jit(solution)/shard_map/ppermute | solution.py:72
  631.1 86.7 %collective-permute-start.28 = (bf16[4,288,1152]{2,1,0:T(8,128)(2,1)}, bf16[4,288,1152]{2,1,0:T(8,128)(2,1)}, u32[]{:S(2)}, u32[]{:S(2)}) collective-permute-start(bf16[4,288,1152]{2,1,0:T(8,128)(2,1)} %pad_maximum_fusion.1), channel_id=1, source_target_pairs={{0,8},{8,0},{16,24},{24,16},{1,9},{9,1},{17,25},{25,17},{2,10},{10... | collective-permute-start | bytes 7962632 | tf_op jit(solution)/shard_map/ppermute | solution.py:72
  681.1 43.2 %all-to-all-start.5 = ((bf16[32,2,864]{2,1,0:T(2,128)(2,1)}), bf16[32,2,864]{2,1,0:T(2,128)(2,1)S(1)}, u32[]{:S(2)}, u32[]{:S(2)}) async-start(bf16[32,2,864]{2,1,0:T(2,128)(2,1)} %reshape.588), calls=%async_computation.5 | async-start | bytes 229376 | tf_op jit(solution)/shard_map/all_to_all | solution.py:325
  684.6 149.9 %reduce-scatter.5.cloned.1.call-start = ((), (), s32[]{:S(2)}) async-start(), calls=%async_computation.9 | async-start | bytes 3317760 | tf_op jit(solution)/shard_map/reduce_scatter | solution.py:128
  724.3 61.1 %all-to-all-start.2 = ((bf16[2,256,1152]{2,0,1:T(2,128)(2,1)}), bf16[2,256,1152]{2,0,1:T(2,128)(2,1)}, u32[]{:S(2)}, u32[]{:S(2)}) async-start(bf16[2,256,1152]{2,0,1:T(2,128)(2,1)} %copy.313), calls=%async_computation.2 | async-start | bytes 2359296 | tf_op jit(solution)/shard_map/all_to_all | solution.py:264
  730.4 60.4 %copy-start.65 = (f32[2,256]{1,0:T(2,128)S(1)}, f32[2,256]{1,0:T(2,128)}, u32[]{:S(2)}) copy-start(f32[2,256]{1,0:T(2,128)} %copy-done.64) | copy-start | bytes 6148
  730.4 60.4 %copy-start.66 = (f32[2,256]{1,0:T(2,128)S(1)}, f32[2,256]{1,0:T(2,128)}, u32[]{:S(2)}) copy-start(f32[2,256]{1,0:T(2,128)} %get-tuple-element.108) | copy-start | bytes 6148
  732.7 55.3 %collective-permute-start.18 = (f32[37392]{0:T(1024)S(1)}, f32[37392]{0:T(1024)}, u32[]{:S(2)}, u32[]{:S(2)}) collective-permute-start(f32[37392]{0:T(1024)S(1)} %concatenate.139), channel_id=1, source_target_pairs={{0,4},{4,0},{1,5},{5,1},{2,6},{6,2},{3,7},{7,3},{8,12},{12,8},{9,1... | collective-permute-start | bytes 448712 | tf_op jit(solution)/shard_map/ppermute | solution.py:72
  788.9 5.2 collective-permute-start.19
  794.2 12.8 %collective-permute-start.20 = (f32[37392]{0:T(1024)S(1)}, f32[37392]{0:T(1024)}, u32[]{:S(2)}, u32[]{:S(2)}) collective-permute-start(f32[37392]{0:T(1024)S(1)} %add.376), channel_id=1, source_target_pairs={{0,16},{8,24},{16,0},{24,8},{1,17},{9,25},{17,1},{25,9},{2,18},{10... | collective-permute-start | bytes 448712 | tf_op jit(solution)/shard_map/ppermute | solution.py:72
  801.0 34.8 %all-to-all-start.4 = ((bf16[2,256,1152]{2,0,1:T(2,128)(2,1)}), bf16[2,256,1152]{2,0,1:T(2,128)(2,1)S(1)}, u32[]{:S(2)}, u32[]{:S(2)}) async-start(bf16[2,256,1152]{2,0,1:T(2,128)(2,1)} %copy.320), calls=%async_computation.4 | async-start | bytes 2359296 | tf_op jit(solution)/shard_map/all_to_all | solution.py:313
  808.0 13.1 %collective-permute-start.21 = (f32[18960]{0:T(1024)S(1)}, f32[18960]{0:T(1024)S(1)}, u32[]{:S(2)}, u32[]{:S(2)}) collective-permute-start(f32[18960]{0:T(1024)S(1)} %slice.257), channel_id=1, source_target_pairs={{0,1},{1,0},{2,3},{3,2},{4,5},{5,4},{6,7},{7,6},{8,9},{9,8},{10,11... | collective-permute-start | bytes 227528 | tf_op jit(solution)/shard_map/ppermute | solution.py:72
  821.1 10.1 %collective-permute-start.22 = (f32[18960]{0:T(1024)S(1)}, f32[18960]{0:T(1024)S(1)}, u32[]{:S(2)}, u32[]{:S(2)}) collective-permute-start(f32[18960]{0:T(1024)S(1)} %slice_add_fusion.6), channel_id=1, source_target_pairs={{0,2},{1,3},{2,0},{3,1},{4,6},{5,7},{6,4},{7,5},{8,10},{9,11},{10,... | collective-permute-start | bytes 227528 | tf_op jit(solution)/shard_map/ppermute | solution.py:72
  835.7 2.5 collective-permute-start.31
  (87 other events, 708.9 us)
Sparse Core Ops, SparseCore 0:
  15.7 51.1 all-gather.7
  69.0 81.8 all-gather.9
  664.6 34.6 reduce-scatter.2
  723.7 70.3 reduce-scatter.4

commit v2 on v1

v2 whole, which is shorter than its diff:
```python
import functools
import math

import jax
import jax.numpy as jnp
from jax import lax
from jax.experimental import pallas as pl
from jax.experimental.pallas import tpu as pltpu
from jax.sharding import Mesh
from jax.sharding import PartitionSpec as P

D = 1152
HEAD_DIM = 72
CLASSES = 1000
GRID = 16
F32 = jnp.float32
BF16 = jnp.bfloat16
INV_ROOT = 1.0 / math.sqrt(HEAD_DIM)
CHIPS = "p"
CORES = "c"
LINE = "t"
PAD = 128
EVERY = (CHIPS, CORES, LINE)
DATA = (CHIPS, CORES)


def rms_rows(values):
    return values * lax.rsqrt(jnp.mean(values * values, axis=-1, keepdims=True) + 1e-06)


def modulate(values, shift_rows, scale_rows):
    return rms_rows(values) * (1.0 + scale_rows) + shift_rows


def rotary_tables(patch_cells, repeat):
    entry = jnp.arange(repeat * HEAD_DIM, dtype=jnp.int32) % HEAD_DIM
    half = HEAD_DIM // 2
    step = (entry % half // 2).astype(F32)
    rates = 10000.0 ** (-4.0 * step / HEAD_DIM)
    cells = patch_cells[..., None]
    place = jnp.where(entry < half, cells // GRID, cells % GRID).astype(F32)
    angles = place * rates
    return jnp.cos(angles), jnp.sin(angles)


def wave_columns(timesteps, first, width):
    half_width = D // 2
    columns = first + jnp.arange(width, dtype=jnp.int32)
    is_cos = columns < half_width
    spot = jnp.where(is_cos, columns, columns - half_width).astype(F32)
    rates = jnp.exp(-math.log(10000.0) * spot / half_width)
    phases = timesteps.astype(F32)[:, None] * rates[None, :]
    return jnp.where(is_cos[None, :], jnp.cos(phases), jnp.sin(phases))


def dot_rows(a, b):
    return lax.dot_general(a, b, (((1,), (0,)), ((), ())), preferred_element_type=F32)


def dot_last(a, b):
    return lax.dot_general(a, b, (((1,), (1,)), ((), ())), preferred_element_type=F32)


def dot_first(a, b):
    return lax.dot_general(a, b, (((0,), (0,)), ((), ())), preferred_element_type=F32)


def head_tables(cols):
    lane = lax.broadcasted_iota(jnp.int32, (cols, cols), 0)
    other = lax.broadcasted_iota(jnp.int32, (cols, cols), 1)
    same = jnp.where(lane // HEAD_DIM == other // HEAD_DIM, 1.0, 0.0).astype(BF16)
    even = other % 2 == 0
    turn = jnp.where(even & (lane == other + 1), -1.0, 0.0)
    turn = jnp.where(jnp.logical_not(even) & (lane == other - 1), 1.0, turn).astype(BF16)
    return same, turn


def unit_heads(values, same):
    mean_sq = dot_rows((values * values).astype(BF16), same) * (1.0 / HEAD_DIM)
    scale = lax.rsqrt(mean_sq + 1e-06)
    return values * scale, scale


def turn_heads(values, cosines, sines, turn):
    return values * cosines + dot_rows(values.astype(BF16), turn) * sines


def head_masks(cols):
    lane = lax.broadcasted_iota(jnp.int32, (1, cols), 1)
    return [
        (lane >= h * HEAD_DIM) & (lane < (h + 1) * HEAD_DIM) for h in range(cols // HEAD_DIM)
    ]


def attn_forward_kernel(
    own_ref, peer_ref, w_ref, b_ref, g_ref, cos_ref, sin_ref, same_ref, turn_ref,
    qkv_ref, heads_ref, own_out, peer_out, total,
):
    _, chips, rows, cols = w_ref.shape
    hc = cols // 4
    images, patches, width = own_ref.shape
    same, turn = same_ref[...], turn_ref[...]
    masks = head_masks(hc)
    at = pl.program_id(0)
    w = w_ref[0].reshape(chips * rows, cols)
    for side, x_ref in enumerate((own_ref, peer_ref)):
        x = x_ref[...].reshape(images * patches, width)
        qkv = dot_rows(x, w[:, : 3 * hc]) + b_ref[0]
        first = side * images * patches
        qkv_ref[0, first : first + images * patches] = qkv.astype(BF16)
        tables = [
            ref[side * images : (side + 1) * images].reshape(images * patches, hc)
            for ref in (cos_ref, sin_ref)
        ]
        q_rot = unit_heads(qkv[:, :hc], same)[0] * g_ref[0]
        q_rot = turn_heads(q_rot, *tables, turn).astype(BF16)
        k_rot = unit_heads(qkv[:, hc : 2 * hc], same)[0] * g_ref[1]
        k_rot = turn_heads(k_rot, *tables, turn).astype(BF16)
        v_all = qkv[:, 2 * hc :].astype(BF16)
        outs = []
        for image in range(images):
            rows_at = slice(image * patches, (image + 1) * patches)
            q, k, v = q_rot[rows_at], k_rot[rows_at], v_all[rows_at]
            heads = None
            for mine in masks:
                scores = dot_last(jnp.where(mine, q, jnp.zeros_like(q)), k)
                expo = jnp.exp(scores * INV_ROOT)
                probs = expo * (1.0 / jnp.sum(expo, axis=1, keepdims=True))
                part = dot_rows(probs.astype(BF16), v)
                heads = part if heads is None else jnp.where(mine, part, heads)
            outs.append(heads.astype(BF16))
        heads = jnp.concatenate(outs, axis=0)
        heads_ref[0, first : first + images * patches] = heads
        step = dot_last(heads, w[:, 3 * hc :])

        @pl.when(at == 0)
        def _():
            total[side] = step

        @pl.when(at > 0)
        def _():
            total[side] += step

    @pl.when(at == pl.num_programs(0) - 1)
    def _():
        own_out[...] = total[0].reshape(images, patches, width).astype(BF16)
        peer_out[...] = total[1].reshape(images, patches, width).astype(BF16)


def attn_backward_kernel(
    own_ref, peer_ref, w_ref, qkv_in_ref, g_ref, cos_ref, sin_ref, same_ref, turn_ref,
    dqkv_ref, own_out, peer_out, bias_ref, gain_ref, total,
):
    _, chips, rows, cols = w_ref.shape
    hc = cols // 4
    images, patches, width = own_ref.shape
    same, turn = same_ref[...], turn_ref[...]
    masks = head_masks(hc)
    at = pl.program_id(0)

    @pl.when(at == 0)
    def _():
        gain_ref[...] = jnp.zeros_like(gain_ref)

    w = w_ref[0].reshape(chips * rows, cols)
    bias = None
    for side, dy_ref in enumerate((own_ref, peer_ref)):
        first = side * images * patches
        rows_here = slice(first, first + images * patches)
        tables = [
            ref[side * images : (side + 1) * images].reshape(images * patches, hc)
            for ref in (cos_ref, sin_ref)
        ]
        dy = dy_ref[...].reshape(images * patches, width)
        d_heads_all = dot_rows(dy, w[:, 3 * hc :]).astype(BF16)
        qkv = qkv_in_ref[0, rows_here]
        v_all = qkv[:, 2 * hc :]
        uq, rq = unit_heads(qkv[:, :hc].astype(F32), same)
        uk, rk = unit_heads(qkv[:, hc : 2 * hc].astype(F32), same)
        q_rot = turn_heads(uq * g_ref[0], *tables, turn).astype(BF16)
        k_rot = turn_heads(uk * g_ref[1], *tables, turn).astype(BF16)
        grads = ([], [], [])
        for image in range(images):
            rows_at = slice(image * patches, (image + 1) * patches)
            q, k, v, d_heads = q_rot[rows_at], k_rot[rows_at], v_all[rows_at], d_heads_all[rows_at]
            zero = jnp.zeros_like(q)
            here = [None, None, None]
            for mine in masks:
                scores = dot_last(jnp.where(mine, q, zero), k)
                expo = jnp.exp(scores * INV_ROOT)
                probs = expo * (1.0 / jnp.sum(expo, axis=1, keepdims=True))
                d_probs = dot_last(jnp.where(mine, d_heads, zero), v)
                mean = jnp.sum(d_probs * probs, axis=1, keepdims=True)
                d_scores = (probs * (d_probs - mean)).astype(BF16)
                parts = (
                    dot_rows(d_scores, k),
                    dot_first(d_scores, q),
                    dot_first(probs.astype(BF16), d_heads),
                )
                here = [
                    new if old is None else jnp.where(mine, new, old)
                    for new, old in zip(parts, here)
                ]
            for which in range(3):
                grads[which].append(here[which])
        d_q, d_k, d_v = (jnp.concatenate(part, axis=0) for part in grads)
        sides = []
        for which, (grad, unit, scale) in enumerate(((d_q, uq, rq), (d_k, uk, rk))):
            grad = grad * INV_ROOT
            back = grad * tables[0] + dot_last((grad * tables[1]).astype(BF16), turn)
            gain_ref[which : which + 1] += jnp.sum(back * unit, axis=0, keepdims=True)
            back = back * g_ref[which]
            mean = dot_rows((back * unit).astype(BF16), same) * (1.0 / HEAD_DIM)
            sides.append((back - unit * mean) * scale)
        d_qkv = jnp.concatenate((sides[0], sides[1], d_v), axis=1)
        part = jnp.sum(d_qkv, axis=0, keepdims=True)
        bias = part if bias is None else bias + part
        d_qkv = d_qkv.astype(BF16)
        dqkv_ref[0, rows_here] = d_qkv
        step = dot_last(d_qkv, w[:, : 3 * hc])

        @pl.when(at == 0)
        def _():
            total[side] = step

        @pl.when(at > 0)
        def _():
            total[side] += step

    bias_ref[0] = bias

    @pl.when(at == pl.num_programs(0) - 1)
    def _():
        own_out[...] = total[0].reshape(images, patches, width).astype(BF16)
        peer_out[...] = total[1].reshape(images, patches, width).astype(BF16)


def resident(shape):
    return pl.BlockSpec(shape, lambda i: (0,) * len(shape))


def by_line(shape):
    return pl.BlockSpec((1,) + shape, lambda i: (i,) + (0,) * len(shape))


def attn_cost(x, w, products):
    images, patches, width = x.shape
    line, _, _, cols = w.shape
    pairs = 2 * images * line * (cols // (4 * HEAD_DIM)) * patches * patches
    return pl.CostEstimate(
        flops=4 * images * patches * width * line * cols + products * 2 * pairs * 256,
        bytes_accessed=w.size * 2 + x.size * 16,
        transcendentals=pairs,
    )


def attn_forward(own, peer, w, b, *tables):
    images, patches, width = own.shape
    line, _, _, cols = w.shape
    hc = cols // 4
    rows = 2 * images * patches
    return pl.pallas_call(
        attn_forward_kernel,
        grid=(line,),
        in_specs=[resident(own.shape)] * 2
        + [by_line(w.shape[1:]), by_line(b.shape[1:])]
        + [resident(table.shape) for table in tables],
        out_specs=[by_line((rows, 3 * hc)), by_line((rows, hc))] + [resident(own.shape)] * 2,
        out_shape=[
            jax.ShapeDtypeStruct((line, rows, 3 * hc), BF16),
            jax.ShapeDtypeStruct((line, rows, hc), BF16),
        ]
        + [jax.ShapeDtypeStruct(own.shape, BF16)] * 2,
        scratch_shapes=[pltpu.VMEM((2, images * patches, width), F32)],
        compiler_params=pltpu.CompilerParams(vmem_limit_bytes=50 << 20),
        cost_estimate=attn_cost(own, w, 2),
    )(own, peer, w, b, *tables)


def attn_backward(own, peer, w, qkv, *tables):
    images, patches, width = own.shape
    line, _, _, cols = w.shape
    hc = cols // 4
    rows = 2 * images * patches
    return pl.pallas_call(
        attn_backward_kernel,
        grid=(line,),
        in_specs=[resident(own.shape)] * 2
        + [by_line(w.shape[1:]), by_line(qkv.shape[1:])]
        + [resident(table.shape) for table in tables],
        out_specs=[by_line((rows, 3 * hc))]
        + [resident(own.shape)] * 2
        + [by_line((1, 3 * hc)), resident((2, hc))],
        out_shape=[jax.ShapeDtypeStruct((line, rows, 3 * hc), BF16)]
        + [jax.ShapeDtypeStruct(own.shape, BF16)] * 2
        + [jax.ShapeDtypeStruct((line, 1, 3 * hc), F32), jax.ShapeDtypeStruct((2, hc), F32)],
        scratch_shapes=[pltpu.VMEM((2, images * patches, width), F32)],
        compiler_params=pltpu.CompilerParams(vmem_limit_bytes=50 << 20),
        cost_estimate=attn_cost(own, w, 5),
    )(own, peer, w, qkv, *tables)


def swiglu(gate_vals, up_vals):
    return jax.nn.silu(gate_vals) * up_vals


def after(values, *others):
    return lax.optimization_barrier((values, others))[0]


def axis_len(name):
    return lax.axis_size(name)


def swap(values, name, bit=1):
    count = axis_len(name)
    return lax.ppermute(values, name, [(i, i ^ bit) for i in range(count)])


def sum_by_swaps(values, name):
    count = axis_len(name)
    bit = 1
    while bit < count:
        values = values + swap(values, name, bit)
        bit *= 2
    return values


def place_kernel(half, spot_ref, own_ref, x_ref, y_ref, da_ref, db_ref, out_ref):
    at = pl.program_id(0)
    out_ref[0, spot_ref[0]] = own_ref[0]
    out_ref[0, spot_ref[1]] = x_ref[0]
    out_ref[0, spot_ref[2]] = y_ref[0]

    @pl.when(at < half)
    def _():
        out_ref[0, spot_ref[3]] = da_ref[0]

    @pl.when(at >= half)
    def _():
        out_ref[0, spot_ref[3]] = db_ref[0]


def place_parts(own, from_x, from_y, diag_a, diag_b):
    line, rows, cols = own.shape
    half = diag_a.shape[0]
    spots = lax.axis_index(CHIPS) ^ jnp.arange(4, dtype=jnp.int32)
    straight = pl.BlockSpec((1, rows, cols), lambda i: (i, 0, 0))
    early = pl.BlockSpec((1, rows, cols), lambda i: (jnp.minimum(i, half - 1), 0, 0))
    late = pl.BlockSpec((1, rows, cols), lambda i: (jnp.maximum(i - half, 0), 0, 0))
    return pl.pallas_call(
        functools.partial(place_kernel, half),
        grid=(line,),
        in_specs=[pl.BlockSpec(memory_space=pltpu.SMEM)] + [straight] * 3 + [early, late],
        out_specs=pl.BlockSpec((1, 4, rows, cols), lambda i: (i, 0, 0, 0)),
        out_shape=jax.ShapeDtypeStruct((line, 4, rows, cols), own.dtype),
        compiler_params=pltpu.CompilerParams(vmem_limit_bytes=40 << 20),
        cost_estimate=pl.CostEstimate(flops=0, bytes_accessed=16 * own.size, transcendentals=0),
    )(spots, own, from_x, from_y, diag_a, diag_b)


def gather_line(piece):
    return lax.all_gather(piece, LINE, axis=0)


def first_hop(held):
    if axis_len(CHIPS) != 4:
        return (held,)
    return swap(held, CHIPS, 1), swap(held, CHIPS, 2)


def second_hop(arrived):
    if len(arrived) == 1:
        return arrived, arrived
    half = arrived[0].shape[0] // 2
    low, high = arrived[0][:half], arrived[1][half:]
    return (low, high), (swap(low, CHIPS, 2), swap(high, CHIPS, 1))


def whole_weight(held, arrived, last):
    if len(arrived) == 1:
        return lax.all_gather(held, CHIPS, axis=1, tiled=True)[:, None]
    return place_parts(held, *arrived, *last)


def weight_product(lefts, right):
    left = jnp.concatenate(lefts, axis=0)
    return jnp.einsum("rd,zrn->zdn", left, right, preferred_element_type=F32).astype(BF16)


def grad_kernel(counts, spot_ref, *refs):
    lefts, refs = refs[: sum(counts)], refs[sum(counts) :]
    rights, refs = refs[: len(counts)], refs[len(counts) :]
    outs, scratch = refs[:5], refs[5:]
    plain, turned = scratch[0], scratch[1:]
    rows = outs[4].shape[1]
    half = rows // 2

    @pl.when(pl.program_id(0) == 0)
    def _():
        for pair, count in enumerate(counts):
            at = 0
            for left in lefts[sum(counts[:pair]) : sum(counts[:pair]) + count]:
                plain[:, at : at + left.shape[0]] = left[...].T
                at += left.shape[0]
            for place in range(4):
                turned[pair][place * rows : (place + 1) * rows] = plain[
                    pl.ds(pl.multiple_of(spot_ref[place] * rows, rows), rows)
                ]

    first = 0
    for pair, right in enumerate(rights):
        last = first + right.shape[-1]
        made = dot_rows(turned[pair][...], right[0]).astype(BF16)
        top = 0
        for out, count in zip(outs, (half, rows - half, rows, rows, rows)):
            out[0, :, first:last] = made[top : top + count]
            top += count
        first = last


def chip_products(pairs):
    line, total_rows, _ = pairs[0][1].shape
    width = pairs[0][0][0].shape[1]
    cols = sum(right.shape[-1] for _, right in pairs)
    rows = width // 4
    half = rows // 2
    spots = lax.axis_index(CHIPS) ^ jnp.array((3, 2, 1, 0), dtype=jnp.int32)
    lefts = [left for group, _ in pairs for left in group]
    rights = [right for _, right in pairs]
    cut = (half, rows - half, rows, rows, rows)
    return pl.pallas_call(
        functools.partial(grad_kernel, tuple(len(group) for group, _ in pairs)),
        grid=(line,),
        in_specs=[pl.BlockSpec(memory_space=pltpu.SMEM)]
        + [resident(left.shape) for left in lefts]
        + [by_line(right.shape[1:]) for right in rights],
        out_specs=[by_line((count, cols)) for count in cut],
        out_shape=[jax.ShapeDtypeStruct((line, count, cols), BF16) for count in cut],
        scratch_shapes=[pltpu.VMEM((width, total_rows), BF16)] * (1 + len(pairs)),
        compiler_params=pltpu.CompilerParams(vmem_limit_bytes=50 << 20),
        cost_estimate=pl.CostEstimate(
            flops=2 * line * width * total_rows * cols,
            bytes_accessed=2 * line * (width + total_rows) * cols,
            transcendentals=0,
        ),
    )(spots, *lefts, *rights)


def send_diagonal(pairs):
    if axis_len(CHIPS) != 4:
        grad = jnp.concatenate([weight_product(*pair) for pair in pairs], axis=-1)
        return (grad,), None
    parts = chip_products(pairs)
    return parts, (swap(parts[0], CHIPS, 1), swap(parts[1], CHIPS, 2))


def send_blocks(parts, got):
    if got is None:
        return parts, None
    _, _, to_y, to_x, _ = parts
    half = got[0].shape[1]
    to_y = jnp.concatenate((to_y[:, :half] + got[0], to_y[:, half:]), axis=1)
    to_x = jnp.concatenate((to_x[:, :half], to_x[:, half:] + got[1]), axis=1)
    return (to_y, to_x), (swap(to_y, CHIPS, 2), swap(to_x, CHIPS, 1))


def add_blocks(parts, got):
    if got is None:
        return lax.psum_scatter(parts[0], CHIPS, scatter_dimension=1, tiled=True)
    return (parts[4].astype(F32) + got[0].astype(F32) + got[1].astype(F32)).astype(BF16)


def scatter_line(part):
    return lax.psum_scatter(part, LINE, scatter_dimension=0, tiled=False)


def with_peer(values):
    return jnp.concatenate((values, swap(values, CORES)), axis=0)


def fold_peer(values):
    own = values.shape[0] // 2
    sent = swap(values[own:].astype(BF16), CORES)
    return values[:own] + sent.astype(F32)


def on_device(
    tokens,
    timesteps,
    labels,
    patch_cells,
    class_table,
    ada_weight,
    ada_bias,
    qkv_weight,
    qkv_bias,
    q_gain,
    k_gain,
    out_weight,
    out_bias,
    gate_up_weight,
    gate_up_bias,
    down_weight,
    down_bias,
    cotangent,
):
    core = lax.axis_index(CORES)
    line_at = lax.axis_index(LINE)
    line = axis_len(LINE)
    data = axis_len(CHIPS) * axis_len(CORES)
    devices = data * line
    images = tokens.shape[0]
    own_images = images // line
    width = class_table.shape[1]
    chunk = ada_weight.shape[2]
    highest = lax.Precision.HIGHEST

    rows_w = qkv_weight.shape[0]
    head_cols = qkv_weight.shape[2] // 2
    ff_cols = gate_up_weight.shape[2] // 2

    def column_halves(which):
        qkv_half = lax.dynamic_slice_in_dim(qkv_weight, which * head_cols, head_cols, 2)
        out_half = lax.dynamic_slice_in_dim(out_weight, which * head_cols, head_cols, 0)
        gu_half = lax.dynamic_slice_in_dim(gate_up_weight, which * ff_cols, ff_cols, 2)
        down_half = lax.dynamic_slice_in_dim(down_weight, which * ff_cols, ff_cols, 0)
        return jnp.concatenate(
            (
                qkv_half.reshape(rows_w, 3 * head_cols),
                out_half.T,
                gu_half.reshape(rows_w, 2 * ff_cols),
                down_half.T,
            ),
            axis=1,
        )

    kept = column_halves(core)
    got = swap(column_halves(1 - core), CORES)
    both = jnp.concatenate(
        (jnp.where(core == 0, kept, got), jnp.where(core == 0, got, kept)), axis=0
    )
    attn_cols = 4 * head_cols
    held_attn = gather_line(both[:, :attn_cols])
    held_gu = gather_line(both[:, attn_cols : attn_cols + 2 * ff_cols])
    down_piece = both[:, attn_cols + 2 * ff_cols :]
    held_down = gather_line(jnp.pad(down_piece, ((0, 0), (0, PAD))))

    small_in = jnp.stack((labels, timesteps))
    small_in = lax.all_to_all(
        jnp.broadcast_to(small_in, (data,) + small_in.shape), DATA, 0, 0, tiled=True
    )
    labels_all = small_in[:, 0].reshape(data * images)
    steps_all = small_in[:, 1].reshape(data * images)
    one_hot = (labels_all[:, None] == jnp.arange(CLASSES, dtype=jnp.int32)[None, :]).astype(BF16)
    cond = jnp.dot(one_hot, class_table, preferred_element_type=F32)
    cond = cond + wave_columns(steps_all, line_at * width, width)
    cond_low = jax.nn.silu(cond).astype(BF16)
    ada_flat = ada_weight.reshape(width, 6 * chunk)
    mod_part = jnp.dot(cond_low, ada_flat, preferred_element_type=F32)
    bias_in = jnp.concatenate((qkv_bias.reshape(-1), gate_up_bias.reshape(-1))).astype(F32)
    bias_len = bias_in.shape[0]
    share = -(-bias_len // data)
    bias_in = jnp.pad(bias_in, (0, share * data - bias_len)).reshape(data, share)
    data_at = lax.axis_index(CHIPS) * axis_len(CORES) + core
    bias_in = lax.dynamic_index_in_dim(bias_in, data_at, 0, keepdims=True)
    mod_part = mod_part.reshape(devices, own_images * 6 * chunk)
    mod_part = jnp.concatenate((mod_part, jnp.broadcast_to(bias_in, (devices, share))), axis=1)
    mod_part = lax.all_to_all(mod_part, EVERY, 0, 0, tiled=True)
    bias_all = mod_part[:, own_images * 6 * chunk :].reshape(data, line, share)
    bias_all = bias_all.transpose(1, 0, 2).reshape(line, data * share)[:, :bias_len]
    mod_part = mod_part[:, : own_images * 6 * chunk]
    mod = jnp.sum(mod_part.reshape(data, line, own_images, 6, chunk), axis=1)
    mod = mod.transpose(1, 2, 0, 3).reshape(own_images, 6, D) + ada_bias.astype(F32)
    shift_a, scale_a, gate_a, shift_f, scale_f, gate_f = (mod[:, k : k + 1] for k in range(6))

    cells = lax.dynamic_slice_in_dim(patch_cells, line_at * own_images, own_images, 0)
    repeat = head_cols // HEAD_DIM
    cosines, sines = rotary_tables(with_peer(cells), repeat)
    gains = jnp.tile(jnp.stack((q_gain, k_gain)).astype(F32)[:, None], (1, 1, repeat))
    same, turn = head_tables(head_cols)

    x_rows = lax.all_to_all(after(tokens, held_attn), LINE, 0, 1, tiled=True)
    attn_arrived = after(first_hop(held_attn), cosines, sines)
    _, attn_last = second_hop(attn_arrived)
    x_rows = after(x_rows, attn_last).astype(F32)
    held_gu = after(held_gu, attn_last)
    gu_arrived = first_hop(held_gu)
    qkv_b = bias_all[:, : 6 * head_cols].reshape(line, 3, 2, head_cols)
    qkv_b = lax.dynamic_index_in_dim(qkv_b, core, 2, keepdims=False).reshape(line, 1, 3 * head_cols)
    gu_b = bias_all[:, 6 * head_cols :].reshape(line, 2, 2, ff_cols)
    gu_b = lax.dynamic_index_in_dim(gu_b, core, 2, keepdims=False).reshape(line, 2 * ff_cols)
    attn_own = modulate(x_rows, shift_a, scale_a).astype(BF16)
    attn_peer = swap(attn_own, CORES)
    w_attn = whole_weight(held_attn, attn_arrived, attn_last)
    tables = (gains, cosines, sines, same, turn)
    qkv, heads_out, part_own, part_peer = attn_forward(
        after(attn_own, held_gu), attn_peer, w_attn, qkv_b, *tables
    )
    part_peer = swap(part_peer, CORES)
    gu_passed, gu_last = second_hop(gu_arrived)
    part_own = after(part_own, gu_passed)
    held_down = after(held_down[:, :, :ff_cols], gu_last)
    down_arrived = first_hop(held_down)
    attn = part_own.astype(F32) + part_peer.astype(F32) + out_bias.astype(F32)
    patches = x_rows.shape[1]
    rows_all = 2 * own_images * patches

    def as_rows(*values):
        return [value.reshape(own_images * patches, D) for value in values]

    mid = x_rows + gate_a * attn
    ffn_in = with_peer(modulate(mid, shift_f, scale_f).astype(BF16))
    ffn_in = ffn_in.reshape(rows_all, D)
    w_gu = whole_weight(held_gu, gu_arrived, after(gu_last, ffn_in)).reshape(line, D, 2 * ff_cols)
    gate_up = jnp.einsum("rd,zdn->zrn", ffn_in, w_gu, preferred_element_type=F32) + gu_b[:, None]
    down_passed, down_last = second_hop(after(down_arrived, gate_up))
    gate_up = after(gate_up, down_passed)
    gate_vals, up_vals = gate_up[..., :ff_cols], gate_up[..., ff_cols:]
    hidden = swiglu(gate_vals, up_vals).astype(BF16)
    grad_out = lax.all_to_all(after(cotangent, heads_out), LINE, 0, 1, tiled=True).astype(F32)
    d_ffn_f = gate_f * grad_out
    d_ffn_own = d_ffn_f.astype(BF16)
    d_ffn = jnp.concatenate(as_rows(d_ffn_own, swap(d_ffn_own, CORES)), axis=0)
    down_parts, down_got = send_diagonal([([d_ffn], hidden)])
    hidden, d_ffn = after((hidden, d_ffn), down_parts)
    w_down = whole_weight(held_down, down_arrived, down_last).reshape(line, D, ff_cols)
    ffn = jnp.einsum("zrf,zdf->rd", hidden, w_down, preferred_element_type=F32)
    ffn = fold_peer(ffn.reshape(2 * own_images, patches, D)) + down_bias.astype(F32)
    output = lax.all_to_all((mid + gate_f * ffn).astype(BF16), LINE, 1, 0, tiled=True)

    down_bias_part = jnp.sum(d_ffn_f, axis=(0, 1))
    d_gate_f = jnp.sum(grad_out * ffn, axis=1, keepdims=True)
    d_hidden = jnp.einsum("rd,zdf->zrf", d_ffn, w_down, preferred_element_type=F32)
    d_gate, d_up = jax.vjp(swiglu, gate_vals, up_vals)[1](d_hidden)
    d_gu = jnp.concatenate((d_gate, d_up), axis=-1).astype(BF16)
    gu_bias_part = jnp.sum(d_gu, axis=1, dtype=F32)
    down_sent, down_blocks = send_blocks(down_parts, down_got)
    gu_parts, gu_got = send_diagonal([([ffn_in], after(d_gu, down_sent))])
    d_gu = after(d_gu, gu_parts)
    d_ffn_in = jnp.einsum("zrn,zdn->rd", d_gu, w_gu, preferred_element_type=F32)
    d_ffn_in = fold_peer(d_ffn_in.reshape(2 * own_images, patches, D))
    d_ffn_in = after(d_ffn_in, down_blocks)
    g_down = add_blocks(down_parts if down_blocks is not None else down_sent, down_blocks)
    g_down = scatter_line(g_down)
    mid_grad, d_shift_f, d_scale_f = jax.vjp(modulate, mid, shift_f, scale_f)[1](d_ffn_in)
    d_mid = grad_out + mid_grad
    d_attn_f = gate_a * d_mid
    out_bias_part = jnp.sum(d_attn_f, axis=(0, 1))
    d_gate_a = jnp.sum(d_mid * attn, axis=1, keepdims=True)
    d_attn_own = d_attn_f.astype(BF16)
    d_attn_peer = swap(d_attn_own, CORES)
    gu_sent, gu_blocks = send_blocks(gu_parts, gu_got)
    d_qkv, d_in_own, d_in_peer, qkv_bias_part, gain_part = attn_backward(
        after(d_attn_own, gu_sent), d_attn_peer, w_attn, qkv, *tables
    )
    d_in_peer = swap(d_in_peer, CORES)
    g_gu = add_blocks(gu_parts if gu_blocks is not None else gu_sent, after(gu_blocks, d_qkv))
    attn_parts, attn_got = send_diagonal(
        [
            (as_rows(attn_own, attn_peer), after(d_qkv, g_gu, output)),
            (as_rows(d_attn_own, d_attn_peer), heads_out),
        ]
    )
    g_gu = scatter_line(after(g_gu, g_down))
    gain_part = gain_part.reshape(2, repeat, HEAD_DIM).sum(axis=1)
    d_attn_in = d_in_own.astype(F32) + d_in_peer.astype(F32)
    row_grad, d_shift_a, d_scale_a = jax.vjp(modulate, x_rows, shift_a, scale_a)[1](d_attn_in)
    tokens_sent = (d_mid + row_grad).astype(BF16)

    d_mod = jnp.concatenate(
        (d_shift_a, d_scale_a, d_gate_a, d_shift_f, d_scale_f, d_gate_f), axis=1
    )
    ada_bias_part = jnp.sum(d_mod, axis=0)
    d_mod_low = d_mod.astype(BF16).reshape(own_images, 6, data, chunk).transpose(2, 0, 1, 3)
    d_mod_low = jnp.broadcast_to(
        d_mod_low[:, None], (data, line, own_images, 6, chunk)
    ).reshape(devices, own_images * 6 * chunk)
    attn_got, tokens_sent = lax.optimization_barrier((attn_got, tokens_sent))
    tokens_grad = lax.all_to_all(tokens_sent, LINE, 1, 0, tiled=True)
    attn_sent, attn_blocks = send_blocks(attn_parts, attn_got)
    d_mod_all = lax.all_to_all(d_mod_low, EVERY, 0, 0, tiled=True)
    d_mod_all = d_mod_all.reshape(data * images, 6 * chunk)
    g_ada = jnp.einsum("bc,be->ce", cond_low, d_mod_all, preferred_element_type=F32)
    g_ada = g_ada.reshape(width, 6, chunk)
    d_silu = jnp.einsum("be,ce->bc", d_mod_all, ada_flat, preferred_element_type=F32)
    d_cond = jax.vjp(jax.nn.silu, cond)[1](d_silu)[0]

    def by_core(part, groups, cols):
        spread = jnp.zeros((line, groups, 2, cols), F32)
        return lax.dynamic_update_slice(
            spread, part.reshape(line, groups, 1, cols), (0, 0, core, 0)
        )

    parts = (
        by_core(qkv_bias_part, 3, head_cols),
        by_core(gu_bias_part, 2, ff_cols),
        ada_bias_part,
        out_bias_part,
        down_bias_part,
        gain_part[0],
        gain_part[1],
    )
    flat = jnp.concatenate([part.reshape(-1) for part in parts])
    count = flat.shape[0]
    flat = jnp.concatenate((flat, d_cond.reshape(-1)))
    flat = sum_by_swaps(sum_by_swaps(flat, CORES), CHIPS)
    g_attn = add_blocks(attn_parts, after(attn_blocks, flat))
    g_attn, tokens_grad = lax.optimization_barrier((after(g_attn, g_gu), tokens_grad))
    g_attn = scatter_line(g_attn)
    d_cond = flat[count:].reshape(d_cond.shape)
    flat = sum_by_swaps(flat[:count], LINE)
    sums = []
    at = 0
    for part in parts:
        sums.append(flat[at : at + part.size].reshape(part.shape))
        at += part.size
    qkv_bias_grad = lax.dynamic_index_in_dim(sums[0], line_at, 0, keepdims=False)
    gu_bias_grad = lax.dynamic_index_in_dim(sums[1], line_at, 0, keepdims=False)
    tokens_grad = tokens_grad.astype(F32)
    table_grad = jnp.dot(one_hot.astype(F32).T, d_cond, precision=highest)

    def own_rows(part):
        kept = lax.dynamic_slice_in_dim(part, core * rows_w, rows_w, 0)
        got = swap(lax.dynamic_slice_in_dim(part, (1 - core) * rows_w, rows_w, 0), CORES)
        low_half = jnp.where(core == 0, kept, got).astype(F32)
        high_half = jnp.where(core == 0, got, kept).astype(F32)

        def joined(first, groups, cols):
            halves = [
                half[:, first : first + groups * cols].reshape(rows_w, groups, cols)
                for half in (low_half, high_half)
            ]
            return jnp.concatenate(halves, axis=2)

        return joined

    joined = own_rows(g_gu)
    g_gu = joined(0, 2, ff_cols)
    joined = own_rows(g_down)
    g_down = joined(0, 1, ff_cols)[:, 0].T
    joined = own_rows(g_attn)
    g_qkv = joined(0, 3, head_cols)
    g_out = joined(3 * head_cols, 1, head_cols)[:, 0].T
    return (
        output,
        tokens_grad,
        table_grad,
        g_ada,
        sums[2],
        g_qkv,
        qkv_bias_grad.reshape(qkv_bias.shape),
        sums[5],
        sums[6],
        g_out,
        sums[3],
        g_gu,
        gu_bias_grad.reshape(gate_up_bias.shape),
        g_down,
        sums[4],
    )


def solution(mesh):
    chips = mesh.shape["dp"] // 2
    finer = Mesh(mesh.devices.reshape(chips, 2, mesh.shape["tensor"]), EVERY)
    in_specs = (
        P(DATA, LINE, None),
        P(DATA),
        P(DATA),
        P(DATA, None),
        P(None, LINE),
        P(LINE, None, DATA),
        P(),
        P(DATA, None, LINE),
        P(None, LINE),
        P(),
        P(),
        P(LINE, DATA),
        P(),
        P(DATA, None, LINE),
        P(None, LINE),
        P(LINE, DATA),
        P(),
        P(DATA, LINE, None),
    )
    out_specs = (
        P(DATA, LINE, None),
        P(DATA, LINE, None),
        P(None, LINE),
        P(LINE, None, DATA),
        P(),
        P(DATA, None, LINE),
        P(None, LINE),
        P(),
        P(),
        P(LINE, DATA),
        P(),
        P(DATA, None, LINE),
        P(None, LINE),
        P(LINE, DATA),
        P(),
    )
    return jax.shard_map(
        on_device, mesh=finer, in_specs=in_specs, out_specs=out_specs, check_vma=False
    )
```

time: 867 us -> 537 us (0.62)
  local copies, waits for them, and re-layouts: 198 us -> 60.9 us
  waiting for transfers between devices: 300 us -> 163 us
  Pallas kernels: 0 us -> 110 us
  matrix products: 111 us -> 40.1 us
  blocking collectives: 57.3 us -> 0 us
  other arithmetic: 112 us -> 74.1 us
    pallas_call x0 -> x8, Pallas kernels: none -> 110 us  [the longest x1 40 us: attn_backward(): pl.pallas_call(attn_backward_kernel, grid=(line,), in_specs=[resident(own...]
    dynamic_update_slice x10 -> x0, local copies, waits for them, and re-layouts: 89.5 us -> none  [gather_weight(): whole = lax.dynamic_update_slice(whole, part, (top, (me ^ flip) * rows, 0))]
    ppermute x32 -> x42, waiting for transfers between devices: 195 us -> 110 us  [swap(): return lax.ppermute(values, name, [(i, i ^ bit) for i in range(count)])]
    dot_general x18 -> x4, matrix products: 107 us -> 35.8 us  [the longest x1 12.7 us: on_device(): jnp.einsum('rd,zdf->zrf', d_ffn, w_down, preferred_element_type=F32)]
    all_to_all x1, waiting for transfers between devices: 52.6 us -> 0.01 us  [on_device(): lax.all_to_all((mid + gate_f * ffn).astype(BF16), LINE, 1, 0, tiled=True)]
    unnamed x1 -> x0, blocking collectives: 47 us -> none
    reshape x14 -> x11, local copies, waits for them, and re-layouts: 25.9 us -> 2.05 us  [the longest x1 0.71 us: on_device(): bias_all.transpose(1, 0, 2).reshape(line, data * share)[:, :bias_len]]
    all_to_all x4 -> x5, waiting for transfers between devices: 39.1 us -> 16.1 us  [the longest x1 11.8 us: on_device(): x_rows = lax.all_to_all(after(tokens, held_attn), LINE, 0, 1, tiled=True)]
  transfers between devices with their start and end apart: 42 -> 55, of which waited for: 16 -> 26; matrix products, arithmetic and copies ran while one was open for 41% -> 26% of each run, Pallas kernels for 0% -> 17%
where the time goes in v2:
time: 537 us; the launch traced here: 531 us
  waiting for transfers between devices  163 us (30%)
  Pallas kernels  110 us (20%)
  other arithmetic  74.1 us (14%)
  starting transfers between devices  67.1 us (12%)
  local copies, waits for them, and re-layouts  60.9 us (11%)
  matrix products  40.1 us (7%)
  between operations  16 us (3%)
    ppermute x42, waiting for transfers between devices, swap(): return lax.ppermute(values, name, [(i, i ^ bit) for i in range(count)])  110 us
    pallas_call x1, Pallas kernels, attn_backward(): pl.pallas_call(attn_backward_kernel, grid=(line,), in_specs=[resident(own...  40 us
    pallas_call x3, Pallas kernels, chip_products(): pl.pallas_call(functools.partial(grad_kernel, tuple((len(group) for group...  34.6 us
    ppermute x42, starting transfers between devices, swap(): return lax.ppermute(values, name, [(i, i ^ bit) for i in range(count)])  34 us
    all_gather x3, waiting for transfers between devices, gather_line(): return lax.all_gather(piece, LINE, axis=0)  27.5 us
    pallas_call x1, Pallas kernels, attn_forward(): pl.pallas_call(attn_forward_kernel, grid=(line,), in_specs=[resident(own....  26.3 us
    unnamed x149, local copies, waits for them, and re-layouts  19.4 us
    dot_general x1, matrix products, on_device(): jnp.einsum('rd,zdf->zrf', d_ffn, w_down, preferred_element_type=F32)  12.7 us
  transfers between devices with their start and end apart: 55, of which 26 were waited for; matrix products, arithmetic and copies ran while one was open for 26% of the time, Pallas kernels for 17%

profile of v2, /device:TPU:0, one launch (start us, length us, event | category | flops | bytes accessed | tf_op | source)
XLA Modules:
  0.0 531.1 jit_solution(5958376006733714324)
XLA Ops:
  16.6 5.1 all-to-all-start.1
  22.1 4.3 all-to-all-done.1
  28.5 4.1 all-to-all-start.2
  32.6 27.2 %all-gather.7.cloned.1.call-done = bf16[1152,576]{1,0:T(8,128)(2,1)} async-done(((bf16[288,576]{1,0:T(8,128)(2,1)}), bf16[1152,576]{1,0:T(8,128)(2,1)}) %all-gather.7.cloned.1.call-update) | async-done | bytes 1327120 | tf_op jit(solution)/shard_map/all_gather | solution.py:363
  62.8 4.3 all-to-all-start
  69.0 5.7 %fusion.21 = (f32[4,256,144]{2,1,0:T(8,128)}, f32[4,256,144]{2,1,0:T(8,128)}) fusion(f32[144]{0:T(256)S(1)} %multiply_power_fusion, s32[4,256]{1,0:T(4,128)S(1)} %get-tuple-element.239, s32[4,256]{1,0:T(4,128)S(1)} %get-tuple-element.238, pred[144]{0:T(512)(128)(4,1)S(1)} %broadcast_compare_fusion.1), kind=kLoop, calls=%fused_computation.71 | loop fusion | flops 442368 | bytes 1188560 | tf_op jit(solution)/shard_map/sin | solution.py:43
  78.4 15.7 %collective-permute-done.2.y_ref = bf16[4,288,576]{2,1,0:T(8,128)(2,1)S(1)} collective-permute-done((bf16[4,288,576]{2,1,0:T(8,128)(2,1)}, bf16[4,288,576]{2,1,0:T(8,128)(2,1)S(1)}, u32[]{:S(2)}, u32[]{:S(2)}) %collective-permute-start.2) | collective-permute-done | bytes 1327136 | tf_op jit(solution)/shard_map/ppermute | solution.py:317
  95.4 2.0 slice.176
  101.0 11.8 %all-to-all-done = bf16[8,64,1152]{2,1,0:T(8,128)(2,1)} async-done(((bf16[8,64,1152]{2,1,0:T(8,128)(2,1)}), bf16[8,64,1152]{2,1,0:T(8,128)(2,1)}, u32[]{:S(2)}, u32[]{:S(2)}) %all-to-all-start) | async-done | bytes 1179680 | tf_op jit(solution)/shard_map/all_to_all | solution.py:583
  128.0 2.8 shard_map.316.w_ref
  130.8 2.5 copy-done.1
  133.3 26.3 %shard_map.317 = (bf16[4,1024,432]{2,1,0:T(8,128)(2,1)}, bf16[4,1024,144]{2,1,0:T(8,128)(2,1)}, bf16[2,256,1152]{2,1,0:T(8,128)(2,1)S(1)}, bf16[2,256,1152]{2,1,0:T(8,128)(2,1)}) custom-call(bf16[2,256,1152]{2,1,0:T(8,128)(2,1)} %copy-done.6, bf16[2,256,1152]{2,1,0:T(8,128)(2,1)} %collective-permute-done.6.peer_ref, bf16[4,4,288,576]{3,2,1,0:T(8,128)(2,1)} %copy-done.1, ...), custom_call_target="tpu_custom_call" | custom-call | flops 7583301632 | bytes 14745600 | tf_op jit(solution)/shard_map/pallas_call | solution.py:262
  159.8 4.3 all-to-all-start.3
  171.2 2.0 multiply_reduce_fusion.4
  175.0 14.1 %collective-permute-done.11.db_ref = bf16[2,288,768]{2,1,0:T(8,128)(2,1)S(1)} collective-permute-done((bf16[2,288,768]{2,1,0:T(8,128)(2,1)S(1)}, bf16[2,288,768]{2,1,0:T(8,128)(2,1)S(1)}, u32[]{:S(2)}, u32[]{:S(2)}) %collective-permute-start.11) | collective-permute-done | bytes 884768 | tf_op jit(solution)/shard_map/ppermute | solution.py:317
  197.5 2.0 pad_maximum_fusion.1
  200.1 3.5 shard_map.318
  203.7 8.3 %add_bitcast_fusion = f32[4,1024,768]{2,1,0:T(8,128)S(1)} fusion(f32[4,768]{1,0:T(4,128)S(1)} %bitcast.238, bf16[1024,1152,1]{1,0,2:T(8,128)(2,1)S(1)} %bitcast.216, bf16[4,1152,768]{2,1,0:T(8,128)(2,1)S(1)} %bitcast.197), kind=kOutput, calls=%fused_computation.1 | convolution fusion | flops 7250903040 | bytes 22032384 | tf_op jit(solution)/shard_map/rd,zdn->zrn/dot_general | solution.py:616
  218.8 3.0 multiply_convert_fusion.refs_1_
  221.8 6.2 %collective-permute-done.17.db_ref = bf16[2,288,384]{2,1,0:T(8,128)(2,1)S(1)} collective-permute-done((bf16[2,288,384]{2,1,0:T(8,128)(2,1)S(1)}, bf16[2,288,384]{2,1,0:T(8,128)(2,1)S(1)}, u32[]{:S(2)}, u32[]{:S(2)}) %collective-permute-start.17) | collective-permute-done | bytes 442400 | tf_op jit(solution)/shard_map/ppermute | solution.py:317
  228.2 2.6 shard_map.320
  234.3 8.5 %shard_map.319 = (bf16[4,144,384]{2,1,0:T(8,128)(2,1)S(1)}, bf16[4,144,384]{2,1,0:T(8,128)(2,1)S(1)}, bf16[4,288,384]{2,1,0:T(8,128)(2,1)S(1)}, bf16[4,288,384]{2,1,0:T(8,128)(2,1)S(1)}, bf16[4,288,384]{2,1,0:T(8,128)(2,1)S(1)}) custom-call(s32[4]{0:T(128)S(1)} %broadcast_xor_fusion.spot_ref, bf16[1024,1152]{1,0:T(8,128)(2,1)} %pad_maximum_fusion.2.refs_0_, ...), custom_call_target="tpu_custom_call" | custom-call | flops 3623878656 | bytes 6684672 | tf_op jit(solution)/shard_map/pallas_call | solution.py:432
  244.9 12.7 %fusion.2 = (bf16[4,1024,384]{2,1,0:T(8,128)(2,1)}, bf16[4,1024,384]{2,1,0:T(8,128)(2,1)}) fusion(f32[4,1024,768]{2,1,0:T(8,128)} %copy-done.29, bf16[4,1152,384]{2,1,0:T(8,128)(2,1)} %bitcast.199, bf16[1024,1152]{1,0:T(8,128)(2,1)} %pad_maximum_fusion.2.refs_0_), kind=kOutput, calls=%fused_computation.5 | convolution fusion | flops 3645898752 | bytes 24772608 | tf_op jit(solution)/shard_map/rd,zdf->zrf/dot_general | solution.py:634
  257.6 6.0 %pad_maximum_fusion.refs_1_ = bf16[4,1024,768]{2,1,0:T(8,128)(2,1)} fusion(bf16[4,1024,384]{2,1,0:T(8,128)(2,1)} %get-tuple-element.195, bf16[4,1024,384]{2,1,0:T(8,128)(2,1)} %get-tuple-element.194), kind=kLoop, calls=%fused_computation.6 | loop fusion | flops 12582912 | bytes 12582912 | tf_op jit(solution)/shard_map/concatenate | solution.py:636
  265.8 12.2 %shard_map.321 = (bf16[4,144,768]{2,1,0:T(8,128)(2,1)S(1)}, bf16[4,144,768]{2,1,0:T(8,128)(2,1)S(1)}, bf16[4,288,768]{2,1,0:T(8,128)(2,1)S(1)}, bf16[4,288,768]{2,1,0:T(8,128)(2,1)}, bf16[4,288,768]{2,1,0:T(8,128)(2,1)}) custom-call(s32[4]{0:T(128)S(1)} %broadcast_xor_fusion.spot_ref, bf16[1024,1152]{1,0:T(8,128)(2,1)} %bitcast.217, ...), custom_call_target="tpu_custom_call" | custom-call | flops 7247757312 | bytes 13369344 | tf_op jit(solution)/shard_map/pallas_call | solution.py:432
  278.0 10.6 %convolution_bitcast_fusion = f32[1024,1152]{1,0:T(8,128)S(1)} fusion(bf16[4,1024,768]{2,1,0:T(8,128)(2,1)} %pad_maximum_fusion.refs_1_, bf16[4,1152,768]{2,1,0:T(8,128)(2,1)S(1)} %bitcast.198), kind=kOutput, calls=%fused_computation.18 | convolution fusion | flops 7247757312 | bytes 18087936 | tf_op jit(solution)/shard_map/zrn,zdn->rd/dot_general | solution.py:641
  292.6 4.3 convolution_bitcast_fusion.1
  299.7 13.5 %collective-permute-done.23 = bf16[4,288,384]{2,1,0:T(8,128)(2,1)S(1)} collective-permute-done((bf16[4,288,384]{2,1,0:T(8,128)(2,1)}, bf16[4,288,384]{2,1,0:T(8,128)(2,1)S(1)}, u32[]{:S(2)}, u32[]{:S(2)}) %collective-permute-start.23) | collective-permute-done | bytes 884768 | tf_op jit(solution)/shard_map/ppermute | solution.py:317
  314.6 3.9 multiply_reduce_fusion.5
  319.8 12.1 %collective-permute-done.26 = bf16[4,144,768]{2,1,0:T(8,128)(2,1)S(1)} collective-permute-done((bf16[4,144,768]{2,1,0:T(8,128)(2,1)S(1)}, bf16[4,144,768]{2,1,0:T(8,128)(2,1)S(1)}, u32[]{:S(2)}, u32[]{:S(2)}) %collective-permute-start.26) | collective-permute-done | bytes 884768 | tf_op jit(solution)/shard_map/ppermute | solution.py:317
  339.2 2.2 copy.118
  341.4 4.3 all-to-all-start.4
  347.0 40.0 %shard_map.322 = (bf16[4,1024,432]{2,1,0:T(8,128)(2,1)}, bf16[2,256,1152]{2,1,0:T(8,128)(2,1)S(1)}, bf16[2,256,1152]{2,1,0:T(8,128)(2,1)}, f32[4,1,432]{2,1,0:T(1,128)S(1)}, f32[2,144]{1,0:T(2,128)S(1)}) custom-call(bf16[2,256,1152]{2,1,0:T(8,128)(2,1)} %multiply_convert_fusion.1.own_ref, bf16[2,256,1152]{2,1,0:T(8,128)(2,1)} %collective-permute-done.24.peer_ref, ...), custom_call_target="tpu_custom_call" | custom-call | flops 10804527104 | bytes 14745600 | tf_op jit(solution)/shard_map/pallas_call | solution.py:285
  388.9 4.4 add_convert_fusion
  393.4 2.6 copy.119
  395.9 13.9 %shard_map.323 = (bf16[4,144,576]{2,1,0:T(8,128)(2,1)}, bf16[4,144,576]{2,1,0:T(8,128)(2,1)}, bf16[4,288,576]{2,1,0:T(8,128)(2,1)}, bf16[4,288,576]{2,1,0:T(8,128)(2,1)}, bf16[4,288,576]{2,1,0:T(8,128)(2,1)}) custom-call(s32[4]{0:T(128)S(1)} %broadcast_xor_fusion.spot_ref, bf16[512,1152]{1,0:T(8,128)(2,1)S(1)} %bitcast.207, ...), custom_call_target="tpu_custom_call" | custom-call | flops 5435817984 | bytes 10027008 | tf_op jit(solution)/shard_map/pallas_call | solution.py:432
  411.2 2.5 fusion.9
  418.0 2.2 reduce.18
  421.0 5.8 %all-to-all-start.5 = ((bf16[32,2,864]{2,1,0:T(2,128)(2,1)}), bf16[32,2,864]{2,1,0:T(2,128)(2,1)S(1)}, u32[]{:S(2)}, u32[]{:S(2)}) async-start(bf16[32,2,864]{2,1,0:T(2,128)(2,1)} %reshape.579), calls=%async_computation.5 | async-start | bytes 229376 | tf_op jit(solution)/shard_map/all_to_all | solution.py:682
  426.8 2.8 fusion.12
  429.7 2.2 copy.125
  440.2 4.7 all-to-all-start.6
  450.9 21.5 %collective-permute-done.35 = f32[37392]{0:T(1024)S(1)} collective-permute-done((f32[37392]{0:T(1024)S(1)}, f32[37392]{0:T(1024)S(1)}, u32[]{:S(2)}, u32[]{:S(2)}) %collective-permute-start.35) | collective-permute-done | bytes 149600 | tf_op jit(solution)/shard_map/ppermute | solution.py:317
  474.1 3.7 collective-permute-done.36
  477.9 3.9 add_convert_fusion.1
  491.6 2.6 collective-permute-start.38
  495.8 7.0 %collective-permute-done.38 = f32[18960]{0:T(1024)S(1)} collective-permute-done((f32[18960]{0:T(1024)S(1)}, f32[18960]{0:T(1024)S(1)}, u32[]{:S(2)}, u32[]{:S(2)}) %collective-permute-start.38) | collective-permute-done | bytes 75872 | tf_op jit(solution)/shard_map/ppermute | solution.py:317
  508.9 9.8 %reduce-scatter.4.cloned.1.call-done = bf16[1,288,576]{2,1,0:T(8,128)(2,1)} async-done(((bf16[4,288,576]{2,1,0:T(8,128)(2,1)}), bf16[1,288,576]{2,1,0:T(8,128)(2,1)}) %reduce-scatter.4.cloned.1.call-update) | async-done | bytes 331792 | tf_op jit(solution)/shard_map/reduce_scatter | solution.py:475
  (431 shorter events, 137.5 us)
Async XLA Ops:
  7.2 52.6 %all-gather.7.cloned.1.call-start = ((), (), s32[]{:S(2)}) async-start(), calls=%async_computation.13 | async-start | bytes 1843200 | tf_op jit(solution)/shard_map/all_gather | solution.py:363
  16.6 9.8 %all-to-all-start.1 = ((s32[8,2,8]{2,1,0:T(2,128)}), s32[8,2,8]{2,1,0:T(2,128)S(1)}, u32[]{:S(2)}, u32[]{:S(2)}) async-start(s32[8,2,8]{2,1,0:T(2,128)} %broadcast_in_dim.92), calls=%async_computation.1 | async-start | bytes 16384 | tf_op jit(solution)/shard_map/all_to_all | solution.py:550
  28.5 34.2 %all-to-all-start.2 = ((f32[32,1,2028]{2,1,0:T(1,128)}), f32[32,1,2028]{2,1,0:T(1,128)}, u32[]{:S(2)}, u32[]{:S(2)}) async-start(f32[32,1,2028]{2,1,0:T(1,128)} %all_to_all.68), calls=%async_computation.2 | async-start | bytes 524288 | tf_op jit(solution)/shard_map/all_to_all | solution.py:569
  59.8 34.2 %collective-permute-start.2 = (bf16[4,288,576]{2,1,0:T(8,128)(2,1)}, bf16[4,288,576]{2,1,0:T(8,128)(2,1)S(1)}, u32[]{:S(2)}, u32[]{:S(2)}) collective-permute-start(bf16[4,288,576]{2,1,0:T(8,128)(2,1)} %bitcast.204), channel_id=1, source_target_pairs={{0,16},{8,24},{16,0},{24,8},{1,17},{9,25},{17,1},{25,9},{2,18},{10... | collective-permute-start | bytes 3981320 | tf_op jit(solution)/shard_map/ppermute | solution.py:317
  61.3 34.1 %collective-permute-start.1 = (bf16[4,288,576]{2,1,0:T(8,128)(2,1)}, bf16[4,288,576]{2,1,0:T(8,128)(2,1)}, u32[]{:S(2)}, u32[]{:S(2)}) collective-permute-start(bf16[4,288,576]{2,1,0:T(8,128)(2,1)} %bitcast.205), channel_id=1, source_target_pairs={{0,8},{8,0},{16,24},{24,16},{1,9},{9,1},{17,25},{25,17},{2,10},{10... | collective-permute-start | bytes 3981320 | tf_op jit(solution)/shard_map/ppermute | solution.py:317
  62.8 50.0 %all-to-all-start = ((bf16[8,64,1152]{2,1,0:T(8,128)(2,1)}), bf16[8,64,1152]{2,1,0:T(8,128)(2,1)}, u32[]{:S(2)}, u32[]{:S(2)}) async-start(bf16[8,64,1152]{2,1,0:T(8,128)(2,1)} %param.21), calls=%async_computation | async-start | bytes 2359296 | tf_op jit(solution)/shard_map/all_to_all | solution.py:583
  67.1 57.2 %all-gather.9.cloned.1.call-start = ((), (), s32[]{:S(2)}) async-start(), calls=%async_computation.14 | async-start | bytes 2211840 | tf_op jit(solution)/shard_map/all_gather | solution.py:363
  75.7 88.6 %all-gather.11.cloned.1.call-start = ((), (), s32[]{:S(2)}) async-start(), calls=%async_computation.15 | async-start | bytes 1474560 | tf_op jit(solution)/shard_map/all_gather | solution.py:363
  98.3 17.2 %collective-permute-start.5 = (bf16[2,288,576]{2,1,0:T(8,128)(2,1)}, bf16[2,288,576]{2,1,0:T(8,128)(2,1)S(1)}, u32[]{:S(2)}, u32[]{:S(2)}) collective-permute-start(bf16[2,288,576]{2,1,0:T(8,128)(2,1)} %slice.177), channel_id=1, source_target_pairs={{0,8},{8,0},{16,24},{24,16},{1,9},{9,1},{17,25},{25,17},{2,10},{10... | collective-permute-start | bytes 1990664 | tf_op jit(solution)/shard_map/ppermute | solution.py:317
  99.8 17.1 %collective-permute-start.4 = (bf16[2,288,576]{2,1,0:T(8,128)(2,1)}, bf16[2,288,576]{2,1,0:T(8,128)(2,1)}, u32[]{:S(2)}, u32[]{:S(2)}) collective-permute-start(bf16[2,288,576]{2,1,0:T(8,128)(2,1)} %slice.176), channel_id=1, source_target_pairs={{0,16},{8,24},{16,0},{24,8},{1,17},{9,25},{17,1},{25,9},{2,18},{10... | collective-permute-start | bytes 1990664 | tf_op jit(solution)/shard_map/ppermute | solution.py:317
  117.7 15.6 %collective-permute-start.6 = (bf16[2,256,1152]{2,1,0:T(8,128)(2,1)S(1)}, bf16[2,256,1152]{2,1,0:T(8,128)(2,1)}, u32[]{:S(2)}, u32[]{:S(2)}) collective-permute-start(bf16[2,256,1152]{2,1,0:T(8,128)(2,1)S(1)} %fusion.8.own_ref), channel_id=1, source_target_pairs={{0,4},{4,0},{1,5},{5,1},{2,6},{6,2},{3,7},{7,3},{8,12},{12,8},{9,1... | collective-permute-start | bytes 3538952 | tf_op jit(solution)/shard_map/ppermute | solution.py:317
  124.3 41.4 %collective-permute-start.8 = (bf16[4,288,768]{2,1,0:T(8,128)(2,1)}, bf16[4,288,768]{2,1,0:T(8,128)(2,1)}, u32[]{:S(2)}, u32[]{:S(2)}) collective-permute-start(bf16[4,288,768]{2,1,0:T(8,128)(2,1)} %bitcast.201), channel_id=1, source_target_pairs={{0,16},{8,24},{16,0},{24,8},{1,17},{9,25},{17,1},{25,9},{2,18},{10... | collective-permute-start | bytes 5308424 | tf_op jit(solution)/shard_map/ppermute | solution.py:317
  124.9 43.6 %collective-permute-start.7 = (bf16[4,288,768]{2,1,0:T(8,128)(2,1)}, bf16[4,288,768]{2,1,0:T(8,128)(2,1)}, u32[]{:S(2)}, u32[]{:S(2)}) collective-permute-start(bf16[4,288,768]{2,1,0:T(8,128)(2,1)} %bitcast.202), channel_id=1, source_target_pairs={{0,8},{8,0},{16,24},{24,16},{1,9},{9,1},{17,25},{25,17},{2,10},{10... | collective-permute-start | bytes 5308424 | tf_op jit(solution)/shard_map/ppermute | solution.py:317
  159.7 11.5 %collective-permute-start.9 = (bf16[2,256,1152]{2,1,0:T(8,128)(2,1)}, bf16[2,256,1152]{2,1,0:T(8,128)(2,1)}, u32[]{:S(2)}, u32[]{:S(2)}) collective-permute-start(bf16[2,256,1152]{2,1,0:T(8,128)(2,1)} %get-tuple-element.77), channel_id=1, source_target_pairs={{0,4},{4,0},{1,5},{5,1},{2,6},{6,2},{3,7},{7,3},{8,12},{12,8},{9,1... | collective-permute-start | bytes 3538952 | tf_op jit(solution)/shard_map/ppermute | solution.py:317
  159.8 34.7 %all-to-all-start.3 = ((bf16[8,64,1152]{2,1,0:T(8,128)(2,1)}), bf16[8,64,1152]{2,1,0:T(8,128)(2,1)}, u32[]{:S(2)}, u32[]{:S(2)}) async-start(bf16[8,64,1152]{2,1,0:T(8,128)(2,1)} %param.38), calls=%async_computation.3 | async-start | bytes 2359296 | tf_op jit(solution)/shard_map/all_to_all | solution.py:621
  164.1 318.0 %reduce-scatter.8.cloned.1.call-start = ((), (), s32[]{:S(2)}) async-start(), calls=%async_computation.12 | async-start | bytes 1105920 | tf_op jit(solution)/shard_map/reduce_scatter | solution.py:475
  167.0 22.1 %collective-permute-start.11 = (bf16[2,288,768]{2,1,0:T(8,128)(2,1)S(1)}, bf16[2,288,768]{2,1,0:T(8,128)(2,1)S(1)}, u32[]{:S(2)}, u32[]{:S(2)}) collective-permute-start(bf16[2,288,768]{2,1,0:T(8,128)(2,1)S(1)} %slice.245), channel_id=1, source_target_pairs={{0,8},{8,0},{16,24},{24,16},{1,9},{9,1},{17,25},{25,17},{2,10},{10... | collective-permute-start | bytes 2654216 | tf_op jit(solution)/shard_map/ppermute | solution.py:317
  169.6 21.8 %collective-permute-start.10 = (bf16[2,288,768]{2,1,0:T(8,128)(2,1)S(1)}, bf16[2,288,768]{2,1,0:T(8,128)(2,1)S(1)}, u32[]{:S(2)}, u32[]{:S(2)}) collective-permute-start(bf16[2,288,768]{2,1,0:T(8,128)(2,1)S(1)} %slice.244), channel_id=1, source_target_pairs={{0,16},{8,24},{16,0},{24,8},{1,17},{9,25},{17,1},{25,9},{2,18},{10... | collective-permute-start | bytes 2654216 | tf_op jit(solution)/shard_map/ppermute | solution.py:317
  175.0 22.5 %collective-permute-start.12 = (bf16[2,256,1152]{2,1,0:T(8,128)(2,1)}, bf16[2,256,1152]{2,1,0:T(8,128)(2,1)}, u32[]{:S(2)}, u32[]{:S(2)}) collective-permute-start(bf16[2,256,1152]{2,1,0:T(8,128)(2,1)} %add_convert_fusion.3), channel_id=1, source_target_pairs={{0,4},{4,0},{1,5},{5,1},{2,6},{6,2},{3,7},{7,3},{8,12},{12,8},{9,1... | collective-permute-start | bytes 3538952 | tf_op jit(solution)/shard_map/ppermute | solution.py:317
  192.4 21.1 %collective-permute-start.14 = (bf16[4,288,384]{2,1,0:T(8,128)(2,1)S(1)}, bf16[4,288,384]{2,1,0:T(8,128)(2,1)}, u32[]{:S(2)}, u32[]{:S(2)}) collective-permute-start(bf16[4,288,384]{2,1,0:T(8,128)(2,1)S(1)} %slice.250.own_ref), channel_id=1, source_target_pairs={{0,16},{8,24},{16,0},{24,8},{1,17},{9,25},{17,1},{25,9},{2,18},{10... | collective-permute-start | bytes 2654216 | tf_op jit(solution)/shard_map/ppermute | solution.py:317
  193.9 20.9 %collective-permute-start.13 = (bf16[4,288,384]{2,1,0:T(8,128)(2,1)S(1)}, bf16[4,288,384]{2,1,0:T(8,128)(2,1)}, u32[]{:S(2)}, u32[]{:S(2)}) collective-permute-start(bf16[4,288,384]{2,1,0:T(8,128)(2,1)S(1)} %slice.250.own_ref), channel_id=1, source_target_pairs={{0,8},{8,0},{16,24},{24,16},{1,9},{9,1},{17,25},{25,17},{2,10},{10... | collective-permute-start | bytes 2654216 | tf_op jit(solution)/shard_map/ppermute | solution.py:317
  197.5 35.2 %collective-permute-start.15 = (bf16[2,256,1152]{2,1,0:T(8,128)(2,1)S(1)}, bf16[2,256,1152]{2,1,0:T(8,128)(2,1)S(1)}, u32[]{:S(2)}, u32[]{:S(2)}) collective-permute-start(bf16[2,256,1152]{2,1,0:T(8,128)(2,1)S(1)} %fusion.18), channel_id=1, source_target_pairs={{0,4},{4,0},{1,5},{5,1},{2,6},{6,2},{3,7},{7,3},{8,12},{12,8},{9,1... | collective-permute-start | bytes 3538952 | tf_op jit(solution)/shard_map/ppermute | solution.py:317
  217.3 10.6 %collective-permute-start.17 = (bf16[2,288,384]{2,1,0:T(8,128)(2,1)S(1)}, bf16[2,288,384]{2,1,0:T(8,128)(2,1)S(1)}, u32[]{:S(2)}, u32[]{:S(2)}) collective-permute-start(bf16[2,288,384]{2,1,0:T(8,128)(2,1)S(1)} %slice.196), channel_id=1, source_target_pairs={{0,8},{8,0},{16,24},{24,16},{1,9},{9,1},{17,25},{25,17},{2,10},{10... | collective-permute-start | bytes 1327112 | tf_op jit(solution)/shard_map/ppermute | solution.py:317
  218.2 10.1 %collective-permute-start.16 = (bf16[2,288,384]{2,1,0:T(8,128)(2,1)S(1)}, bf16[2,288,384]{2,1,0:T(8,128)(2,1)S(1)}, u32[]{:S(2)}, u32[]{:S(2)}) collective-permute-start(bf16[2,288,384]{2,1,0:T(8,128)(2,1)S(1)} %slice.195), channel_id=1, source_target_pairs={{0,16},{8,24},{16,0},{24,8},{1,17},{9,25},{17,1},{25,9},{2,18},{10... | collective-permute-start | bytes 1327112 | tf_op jit(solution)/shard_map/ppermute | solution.py:317
  242.8 20.7 %collective-permute-start.19 = (bf16[4,144,384]{2,1,0:T(8,128)(2,1)S(1)}, bf16[4,144,384]{2,1,0:T(8,128)(2,1)S(1)}, u32[]{:S(2)}, u32[]{:S(2)}) collective-permute-start(bf16[4,144,384]{2,1,0:T(8,128)(2,1)S(1)} %get-tuple-element.86), channel_id=1, source_target_pairs={{0,8},{8,0},{16,24},{24,16},{1,9},{9,1},{17,25},{25,17},{2,10},{10... | collective-permute-start | bytes 1327112 | tf_op jit(solution)/shard_map/ppermute | solution.py:317
  244.3 20.3 %collective-permute-start.20 = (bf16[4,144,384]{2,1,0:T(8,128)(2,1)S(1)}, bf16[4,144,384]{2,1,0:T(8,128)(2,1)S(1)}, u32[]{:S(2)}, u32[]{:S(2)}) collective-permute-start(bf16[4,144,384]{2,1,0:T(8,128)(2,1)S(1)} %get-tuple-element.87), channel_id=1, source_target_pairs={{0,16},{8,24},{16,0},{24,8},{1,17},{9,25},{17,1},{25,9},{2,18},{10... | collective-permute-start | bytes 1327112 | tf_op jit(solution)/shard_map/ppermute | solution.py:317
  288.7 10.0 %collective-permute-start.21 = (bf16[2,256,1152]{2,1,0:T(8,128)(2,1)S(1)}, bf16[2,256,1152]{2,1,0:T(8,128)(2,1)S(1)}, u32[]{:S(2)}, u32[]{:S(2)}) collective-permute-start(bf16[2,256,1152]{2,1,0:T(8,128)(2,1)S(1)} %bitcast.222), channel_id=1, source_target_pairs={{0,4},{4,0},{1,5},{5,1},{2,6},{6,2},{3,7},{7,3},{8,12},{12,8},{9,1... | collective-permute-start | bytes 3538952 | tf_op jit(solution)/shard_map/ppermute | solution.py:317
  290.5 22.7 %collective-permute-start.23 = (bf16[4,288,384]{2,1,0:T(8,128)(2,1)}, bf16[4,288,384]{2,1,0:T(8,128)(2,1)S(1)}, u32[]{:S(2)}, u32[]{:S(2)}) collective-permute-start(bf16[4,288,384]{2,1,0:T(8,128)(2,1)} %pad_maximum_fusion.8), channel_id=1, source_target_pairs={{0,8},{8,0},{16,24},{24,16},{1,9},{9,1},{17,25},{25,17},{2,10},{10... | collective-permute-start | bytes 2654216 | tf_op jit(solution)/shard_map/ppermute | solution.py:317
  291.2 22.7 %collective-permute-start.22 = (bf16[4,288,384]{2,1,0:T(8,128)(2,1)}, bf16[4,288,384]{2,1,0:T(8,128)(2,1)S(1)}, u32[]{:S(2)}, u32[]{:S(2)}) collective-permute-start(bf16[4,288,384]{2,1,0:T(8,128)(2,1)} %pad_maximum_fusion.7), channel_id=1, source_target_pairs={{0,16},{8,24},{16,0},{24,8},{1,17},{9,25},{17,1},{25,9},{2,18},{10... | collective-permute-start | bytes 2654216 | tf_op jit(solution)/shard_map/ppermute | solution.py:317
  297.0 17.6 %collective-permute-start.18 = (bf16[2,256,1152]{2,1,0:T(8,128)(2,1)S(1)}, bf16[2,256,1152]{2,1,0:T(8,128)(2,1)S(1)}, u32[]{:S(2)}, u32[]{:S(2)}) collective-permute-start(bf16[2,256,1152]{2,1,0:T(8,128)(2,1)S(1)} %bitcast.221), channel_id=1, source_target_pairs={{0,4},{4,0},{1,5},{5,1},{2,6},{6,2},{3,7},{7,3},{8,12},{12,8},{9,1... | collective-permute-start | bytes 3538952 | tf_op jit(solution)/shard_map/ppermute | solution.py:317
  297.1 37.8 %collective-permute-start.25 = (bf16[4,144,768]{2,1,0:T(8,128)(2,1)S(1)}, bf16[4,144,768]{2,1,0:T(8,128)(2,1)S(1)}, u32[]{:S(2)}, u32[]{:S(2)}) collective-permute-start(bf16[4,144,768]{2,1,0:T(8,128)(2,1)S(1)} %get-tuple-element.94), channel_id=1, source_target_pairs={{0,8},{8,0},{16,24},{24,16},{1,9},{9,1},{17,25},{25,17},{2,10},{10... | collective-permute-start | bytes 2654216 | tf_op jit(solution)/shard_map/ppermute | solution.py:317
  298.7 33.2 %collective-permute-start.26 = (bf16[4,144,768]{2,1,0:T(8,128)(2,1)S(1)}, bf16[4,144,768]{2,1,0:T(8,128)(2,1)S(1)}, u32[]{:S(2)}, u32[]{:S(2)}) collective-permute-start(bf16[4,144,768]{2,1,0:T(8,128)(2,1)S(1)} %get-tuple-element.95), channel_id=1, source_target_pairs={{0,16},{8,24},{16,0},{24,8},{1,17},{9,25},{17,1},{25,9},{2,18},{10... | collective-permute-start | bytes 2654216 | tf_op jit(solution)/shard_map/ppermute | solution.py:317
  319.8 26.0 %collective-permute-start.24 = (bf16[2,256,1152]{2,1,0:T(8,128)(2,1)}, bf16[2,256,1152]{2,1,0:T(8,128)(2,1)}, u32[]{:S(2)}, u32[]{:S(2)}) collective-permute-start(bf16[2,256,1152]{2,1,0:T(8,128)(2,1)} %multiply_convert_fusion.1.own_ref), channel_id=1, source_target_pairs={{0,4},{4,0},{1,5},{5,1},{2,6},{6,2},{3,7},{7,3},{8,12},{12,8},{9,1... | collective-permute-start | bytes 3538952 | tf_op jit(solution)/shard_map/ppermute | solution.py:317
  333.5 55.4 %collective-permute-start.28 = (bf16[4,288,768]{2,1,0:T(8,128)(2,1)}, bf16[4,288,768]{2,1,0:T(8,128)(2,1)}, u32[]{:S(2)}, u32[]{:S(2)}) collective-permute-start(bf16[4,288,768]{2,1,0:T(8,128)(2,1)} %pad_maximum_fusion.4), channel_id=1, source_target_pairs={{0,8},{8,0},{16,24},{24,16},{1,9},{9,1},{17,25},{25,17},{2,10},{10... | collective-permute-start | bytes 5308424 | tf_op jit(solution)/shard_map/ppermute | solution.py:317
  336.5 52.4 %collective-permute-start.27 = (bf16[4,288,768]{2,1,0:T(8,128)(2,1)}, bf16[4,288,768]{2,1,0:T(8,128)(2,1)}, u32[]{:S(2)}, u32[]{:S(2)}) collective-permute-start(bf16[4,288,768]{2,1,0:T(8,128)(2,1)} %pad_maximum_fusion.3), channel_id=1, source_target_pairs={{0,16},{8,24},{16,0},{24,8},{1,17},{9,25},{17,1},{25,9},{2,18},{10... | collective-permute-start | bytes 5308424 | tf_op jit(solution)/shard_map/ppermute | solution.py:317
  341.4 51.9 %all-to-all-start.4 = ((bf16[2,256,1152]{2,0,1:T(2,128)(2,1)}), bf16[2,256,1152]{2,0,1:T(2,128)(2,1)}, u32[]{:S(2)}, u32[]{:S(2)}) async-start(bf16[2,256,1152]{2,0,1:T(2,128)(2,1)} %copy.118), calls=%async_computation.4 | async-start | bytes 2359296 | tf_op jit(solution)/shard_map/all_to_all | solution.py:630
  345.7 159.2 %reduce-scatter.6.cloned.1.call-start = ((), (), s32[]{:S(2)}) async-start(), calls=%async_computation.11 | async-start | bytes 2211840 | tf_op jit(solution)/shard_map/reduce_scatter | solution.py:475
  387.0 24.2 %collective-permute-start.31 = (bf16[2,256,1152]{2,1,0:T(8,128)(2,1)}, bf16[2,256,1152]{2,1,0:T(8,128)(2,1)}, u32[]{:S(2)}, u32[]{:S(2)}) collective-permute-start(bf16[2,256,1152]{2,1,0:T(8,128)(2,1)} %get-tuple-element.112), channel_id=1, source_target_pairs={{0,4},{4,0},{1,5},{5,1},{2,6},{6,2},{3,7},{7,3},{8,12},{12,8},{9,1... | collective-permute-start | bytes 3538952 | tf_op jit(solution)/shard_map/ppermute | solution.py:317
  409.9 19.8 %collective-permute-start.29 = (bf16[4,144,576]{2,1,0:T(8,128)(2,1)}, bf16[4,144,576]{2,1,0:T(8,128)(2,1)}, u32[]{:S(2)}, u32[]{:S(2)}) collective-permute-start(bf16[4,144,576]{2,1,0:T(8,128)(2,1)} %get-tuple-element.109), channel_id=1, source_target_pairs={{0,8},{8,0},{16,24},{24,16},{1,9},{9,1},{17,25},{25,17},{2,10},{10... | collective-permute-start | bytes 1990664 | tf_op jit(solution)/shard_map/ppermute | solution.py:317
  410.6 19.1 %collective-permute-start.30 = (bf16[4,144,576]{2,1,0:T(8,128)(2,1)}, bf16[4,144,576]{2,1,0:T(8,128)(2,1)}, u32[]{:S(2)}, u32[]{:S(2)}) collective-permute-start(bf16[4,144,576]{2,1,0:T(8,128)(2,1)} %get-tuple-element.110), channel_id=1, source_target_pairs={{0,16},{8,24},{16,0},{24,8},{1,17},{9,25},{17,1},{25,9},{2,18},{10... | collective-permute-start | bytes 1990664 | tf_op jit(solution)/shard_map/ppermute | solution.py:317
  421.0 19.2 %all-to-all-start.5 = ((bf16[32,2,864]{2,1,0:T(2,128)(2,1)}), bf16[32,2,864]{2,1,0:T(2,128)(2,1)S(1)}, u32[]{:S(2)}, u32[]{:S(2)}) async-start(bf16[32,2,864]{2,1,0:T(2,128)(2,1)} %reshape.579), calls=%async_computation.5 | async-start | bytes 229376 | tf_op jit(solution)/shard_map/all_to_all | solution.py:682
  434.5 43.4 %collective-permute-start.33 = (bf16[4,288,576]{2,1,0:T(8,128)(2,1)}, bf16[4,288,576]{2,1,0:T(8,128)(2,1)}, u32[]{:S(2)}, u32[]{:S(2)}) collective-permute-start(bf16[4,288,576]{2,1,0:T(8,128)(2,1)} %pad_maximum_fusion.6), channel_id=1, source_target_pairs={{0,8},{8,0},{16,24},{24,16},{1,9},{9,1},{17,25},{25,17},{2,10},{10... | collective-permute-start | bytes 3981320 | tf_op jit(solution)/shard_map/ppermute | solution.py:317
  438.8 39.1 %collective-permute-start.32 = (bf16[4,288,576]{2,1,0:T(8,128)(2,1)}, bf16[4,288,576]{2,1,0:T(8,128)(2,1)}, u32[]{:S(2)}, u32[]{:S(2)}) collective-permute-start(bf16[4,288,576]{2,1,0:T(8,128)(2,1)} %pad_maximum_fusion.5), channel_id=1, source_target_pairs={{0,16},{8,24},{16,0},{24,8},{1,17},{9,25},{17,1},{25,9},{2,18},{10... | collective-permute-start | bytes 3981320 | tf_op jit(solution)/shard_map/ppermute | solution.py:317
  440.2 41.6 %all-to-all-start.6 = ((bf16[2,256,1152]{2,0,1:T(2,128)(2,1)}), bf16[2,256,1152]{2,0,1:T(2,128)(2,1)S(1)}, u32[]{:S(2)}, u32[]{:S(2)}) async-start(bf16[2,256,1152]{2,0,1:T(2,128)(2,1)} %copy.125), calls=%async_computation.6 | async-start | bytes 2359296 | tf_op jit(solution)/shard_map/all_to_all | solution.py:680
  444.9 73.7 %reduce-scatter.4.cloned.1.call-start = ((), (), s32[]{:S(2)}) async-start(), calls=%async_computation.10 | async-start | bytes 1843200 | tf_op jit(solution)/shard_map/reduce_scatter | solution.py:475
  450.2 22.2 %collective-permute-start.35 = (f32[37392]{0:T(1024)S(1)}, f32[37392]{0:T(1024)S(1)}, u32[]{:S(2)}, u32[]{:S(2)}) collective-permute-start(f32[37392]{0:T(1024)S(1)} %add.365), channel_id=1, source_target_pairs={{0,8},{8,0},{16,24},{24,16},{1,9},{9,1},{17,25},{25,17},{2,10},{10... | collective-permute-start | bytes 448712 | tf_op jit(solution)/shard_map/ppermute | solution.py:317
  491.6 11.3 %collective-permute-start.38 = (f32[18960]{0:T(1024)S(1)}, f32[18960]{0:T(1024)S(1)}, u32[]{:S(2)}, u32[]{:S(2)}) collective-permute-start(f32[18960]{0:T(1024)S(1)} %slice_add_fusion.8), channel_id=1, source_target_pairs={{0,2},{1,3},{2,0},{3,1},{4,6},{5,7},{6,4},{7,5},{8,10},{9,11},{10,... | collective-permute-start | bytes 227528 | tf_op jit(solution)/shard_map/ppermute | solution.py:317
  506.0 13.8 %collective-permute-start.40 = (bf16[144,768]{1,0:T(8,128)(2,1)S(1)}, bf16[144,768]{1,0:T(8,128)(2,1)S(1)}, u32[]{:S(2)}, u32[]{:S(2)}) collective-permute-start(bf16[144,768]{1,0:T(8,128)(2,1)S(1)} %dynamic-slice_bitcast_fusion), channel_id=1, source_target_pairs={{0,4},{4,0},{1,5},{5,1},{2,6},{6,2},{3,7},{7,3},{8,12},{12,8},{9,1... | collective-permute-start | bytes 663560 | tf_op jit(solution)/shard_map/ppermute | solution.py:317
  (72 other events, 727.1 us)
Sparse Core Ops, SparseCore 0:
  16.1 43.7 all-gather.6
  75.8 48.4 all-gather.8
  126.5 27.6 all-gather.10
  339.3 36.1 reduce-scatter.7
  393.5 38.2 reduce-scatter.5
  482.2 36.4 reduce-scatter.3

commit v3 on v2

--- a/solution.py
+++ b/solution.py
@@ -94,66 +94,66 @@
 
 def attn_forward_kernel(
     own_ref, peer_ref, w_ref, b_ref, g_ref, cos_ref, sin_ref, same_ref, turn_ref,
-    qkv_ref, heads_ref, own_out, peer_out, total,
+    qkv_ref, heads_ref, own_out, peer_out, x_all, total,
 ):
-    _, chips, rows, cols = w_ref.shape
-    hc = cols // 4
+    hc = w_ref.shape[2] // 4
     images, patches, width = own_ref.shape
+    side = images * patches
     same, turn = same_ref[...], turn_ref[...]
     masks = head_masks(hc)
     at = pl.program_id(0)
-    w = w_ref[0].reshape(chips * rows, cols)
-    for side, x_ref in enumerate((own_ref, peer_ref)):
-        x = x_ref[...].reshape(images * patches, width)
-        qkv = dot_rows(x, w[:, : 3 * hc]) + b_ref[0]
-        first = side * images * patches
-        qkv_ref[0, first : first + images * patches] = qkv.astype(BF16)
-        tables = [
-            ref[side * images : (side + 1) * images].reshape(images * patches, hc)
-            for ref in (cos_ref, sin_ref)
-        ]
-        q_rot = unit_heads(qkv[:, :hc], same)[0] * g_ref[0]
-        q_rot = turn_heads(q_rot, *tables, turn).astype(BF16)
-        k_rot = unit_heads(qkv[:, hc : 2 * hc], same)[0] * g_ref[1]
-        k_rot = turn_heads(k_rot, *tables, turn).astype(BF16)
-        v_all = qkv[:, 2 * hc :].astype(BF16)
-        outs = []
-        for image in range(images):
-            rows_at = slice(image * patches, (image + 1) * patches)
-            q, k, v = q_rot[rows_at], k_rot[rows_at], v_all[rows_at]
-            heads = None
-            for mine in masks:
-                scores = dot_last(jnp.where(mine, q, jnp.zeros_like(q)), k)
-                expo = jnp.exp(scores * INV_ROOT)
-                probs = expo * (1.0 / jnp.sum(expo, axis=1, keepdims=True))
-                part = dot_rows(probs.astype(BF16), v)
-                heads = part if heads is None else jnp.where(mine, part, heads)
-            outs.append(heads.astype(BF16))
-        heads = jnp.concatenate(outs, axis=0)
-        heads_ref[0, first : first + images * patches] = heads
-        step = dot_last(heads, w[:, 3 * hc :])
-
-        @pl.when(at == 0)
-        def _():
-            total[side] = step
-
-        @pl.when(at > 0)
-        def _():
-            total[side] += step
+
+    @pl.when(at == 0)
+    def _():
+        x_all[:side] = own_ref[...].reshape(side, width)
+        x_all[side:] = peer_ref[...].reshape(side, width)
+
+    qkv = dot_rows(x_all[...], w_ref[0, :, : 3 * hc]) + b_ref[0]
+    qkv_ref[0] = qkv.astype(BF16)
+    tables = (cos_ref[...], sin_ref[...])
+    q_rot = unit_heads(qkv[:, :hc], same)[0] * (g_ref[0] * INV_ROOT)
+    q_rot = turn_heads(q_rot, *tables, turn).astype(BF16)
+    k_rot = unit_heads(qkv[:, hc : 2 * hc], same)[0] * g_ref[1]
+    k_rot = turn_heads(k_rot, *tables, turn).astype(BF16)
+    v_all = qkv[:, 2 * hc :].astype(BF16)
+    v_all = jnp.concatenate((v_all, jnp.ones((2 * side, 256 - hc), BF16)), axis=1)
+    q_heads = [jnp.where(mine, q_rot, jnp.zeros_like(q_rot)) for mine in masks]
+    outs = []
+    for image in range(2 * images):
+        rows_at = slice(image * patches, (image + 1) * patches)
+        k, v = k_rot[rows_at], v_all[rows_at]
+        heads = None
+        for q, mine in zip(q_heads, masks):
+            expo = jnp.exp(dot_last(q[rows_at], k)).astype(BF16)
+            part = dot_rows(expo, v)
+            part = part[:, :hc] * (1.0 / part[:, hc : hc + 1])
+            heads = part if heads is None else jnp.where(mine, part, heads)
+        outs.append(heads.astype(BF16))
+    heads = jnp.concatenate(outs, axis=0)
+    heads_ref[0] = heads
+    step = dot_last(heads, w_ref[0, :, 3 * hc :])
+
+    @pl.when(at == 0)
+    def _():
+        total[...] = step
+
+    @pl.when(at > 0)
+    def _():
+        total[...] += step
 
     @pl.when(at == pl.num_programs(0) - 1)
     def _():
-        own_out[...] = total[0].reshape(images, patches, width).astype(BF16)
-        peer_out[...] = total[1].reshape(images, patches, width).astype(BF16)
+        own_out[...] = total[:side].reshape(images, patches, width).astype(BF16)
+        peer_out[...] = total[side:].reshape(images, patches, width).astype(BF16)
 
 
 def attn_backward_kernel(
     own_ref, peer_ref, w_ref, qkv_in_ref, g_ref, cos_ref, sin_ref, same_ref, turn_ref,
-    dqkv_ref, own_out, peer_out, bias_ref, gain_ref, total,
+    dqkv_ref, own_out, peer_out, bias_ref, gain_ref, x_all, total,
 ):
-    _, chips, rows, cols = w_ref.shape
-    hc = cols // 4
+    hc = w_ref.shape[2] // 4
     images, patches, width = own_ref.shape
+    side = images * patches
     same, turn = same_ref[...], turn_ref[...]
     masks = head_masks(hc)
     at = pl.program_id(0)
@@ -161,78 +161,68 @@
     @pl.when(at == 0)
     def _():
         gain_ref[...] = jnp.zeros_like(gain_ref)
-
-    w = w_ref[0].reshape(chips * rows, cols)
-    bias = None
-    for side, dy_ref in enumerate((own_ref, peer_ref)):
-        first = side * images * patches
-        rows_here = slice(first, first + images * patches)
-        tables = [
-            ref[side * images : (side + 1) * images].reshape(images * patches, hc)
-            for ref in (cos_ref, sin_ref)
-        ]
-        dy = dy_ref[...].reshape(images * patches, width)
-        d_heads_all = dot_rows(dy, w[:, 3 * hc :]).astype(BF16)
-        qkv = qkv_in_ref[0, rows_here]
-        v_all = qkv[:, 2 * hc :]
-        uq, rq = unit_heads(qkv[:, :hc].astype(F32), same)
-        uk, rk = unit_heads(qkv[:, hc : 2 * hc].astype(F32), same)
-        q_rot = turn_heads(uq * g_ref[0], *tables, turn).astype(BF16)
-        k_rot = turn_heads(uk * g_ref[1], *tables, turn).astype(BF16)
-        grads = ([], [], [])
-        for image in range(images):
-            rows_at = slice(image * patches, (image + 1) * patches)
-            q, k, v, d_heads = q_rot[rows_at], k_rot[rows_at], v_all[rows_at], d_heads_all[rows_at]
-            zero = jnp.zeros_like(q)
-            here = [None, None, None]
-            for mine in masks:
-                scores = dot_last(jnp.where(mine, q, zero), k)
-                expo = jnp.exp(scores * INV_ROOT)
-                probs = expo * (1.0 / jnp.sum(expo, axis=1, keepdims=True))
-                d_probs = dot_last(jnp.where(mine, d_heads, zero), v)
-                mean = jnp.sum(d_probs * probs, axis=1, keepdims=True)
-                d_scores = (probs * (d_probs - mean)).astype(BF16)
-                parts = (
-                    dot_rows(d_scores, k),
-                    dot_first(d_scores, q),
-                    dot_first(probs.astype(BF16), d_heads),
-                )
-                here = [
-                    new if old is None else jnp.where(mine, new, old)
-                    for new, old in zip(parts, here)
-                ]
-            for which in range(3):
-                grads[which].append(here[which])
-        d_q, d_k, d_v = (jnp.concatenate(part, axis=0) for part in grads)
-        sides = []
-        for which, (grad, unit, scale) in enumerate(((d_q, uq, rq), (d_k, uk, rk))):
-            grad = grad * INV_ROOT
-            back = grad * tables[0] + dot_last((grad * tables[1]).astype(BF16), turn)
-            gain_ref[which : which + 1] += jnp.sum(back * unit, axis=0, keepdims=True)
-            back = back * g_ref[which]
-            mean = dot_rows((back * unit).astype(BF16), same) * (1.0 / HEAD_DIM)
-            sides.append((back - unit * mean) * scale)
-        d_qkv = jnp.concatenate((sides[0], sides[1], d_v), axis=1)
-        part = jnp.sum(d_qkv, axis=0, keepdims=True)
-        bias = part if bias is None else bias + part
-        d_qkv = d_qkv.astype(BF16)
-        dqkv_ref[0, rows_here] = d_qkv
-        step = dot_last(d_qkv, w[:, : 3 * hc])
-
-        @pl.when(at == 0)
-        def _():
-            total[side] = step
-
-        @pl.when(at > 0)
-        def _():
-            total[side] += step
-
-    bias_ref[0] = bias
+        x_all[:side] = own_ref[...].reshape(side, width)
+        x_all[side:] = peer_ref[...].reshape(side, width)
+
+    tables = (cos_ref[...], sin_ref[...])
+    d_heads_all = dot_rows(x_all[...], w_ref[0, :, 3 * hc :]).astype(BF16)
+    qkv = qkv_in_ref[0]
+    v_all = qkv[:, 2 * hc :]
+    uq, rq = unit_heads(qkv[:, :hc].astype(F32), same)
+    uk, rk = unit_heads(qkv[:, hc : 2 * hc].astype(F32), same)
+    q_rot = turn_heads(uq * (g_ref[0] * INV_ROOT), *tables, turn).astype(BF16)
+    k_rot = turn_heads(uk * g_ref[1], *tables, turn).astype(BF16)
+    zero = jnp.zeros_like(q_rot)
+    q_heads = [jnp.where(mine, q_rot, zero) for mine in masks]
+    v_heads = [jnp.where(mine, v_all, zero) for mine in masks]
+    grads = ([], [], [])
+    for image in range(2 * images):
+        rows_at = slice(image * patches, (image + 1) * patches)
+        q, k, d_heads = q_rot[rows_at], k_rot[rows_at], d_heads_all[rows_at]
+        here = [None, None, None]
+        for head, mine in enumerate(masks):
+            expo = jnp.exp(dot_last(k, q_heads[head][rows_at]))
+            probs = expo * (1.0 / jnp.sum(expo, axis=0, keepdims=True))
+            d_probs = dot_last(v_heads[head][rows_at], d_heads)
+            mean = jnp.sum(d_probs * probs, axis=0, keepdims=True)
+            d_scores = (probs * (d_probs - mean)).astype(BF16)
+            parts = (
+                dot_first(d_scores, k),
+                dot_rows(d_scores, q),
+                dot_rows(probs.astype(BF16), d_heads),
+            )
+            here = [
+                new if old is None else jnp.where(mine, new, old)
+                for new, old in zip(parts, here)
+            ]
+        for which in range(3):
+            grads[which].append(here[which])
+    d_q, d_k, d_v = (jnp.concatenate(part, axis=0) for part in grads)
+    sides = []
+    for which, (grad, unit, scale) in enumerate(((d_q * INV_ROOT, uq, rq), (d_k, uk, rk))):
+        back = grad * tables[0] + dot_last((grad * tables[1]).astype(BF16), turn)
+        gain_ref[which : which + 1] += jnp.sum(back * unit, axis=0, keepdims=True)
+        back = back * g_ref[which]
+        mean = dot_rows((back * unit).astype(BF16), same) * (1.0 / HEAD_DIM)
+        sides.append((back - unit * mean) * scale)
+    d_qkv = jnp.concatenate((sides[0], sides[1], d_v), axis=1)
+    bias_ref[0] = jnp.sum(d_qkv, axis=0, keepdims=True)
+    d_qkv = d_qkv.astype(BF16)
+    dqkv_ref[0] = d_qkv
+    step = dot_last(d_qkv, w_ref[0, :, : 3 * hc])
+
+    @pl.when(at == 0)
+    def _():
+        total[...] = step
+
+    @pl.when(at > 0)
+    def _():
+        total[...] += step
 
     @pl.when(at == pl.num_programs(0) - 1)
     def _():
-        own_out[...] = total[0].reshape(images, patches, width).astype(BF16)
-        peer_out[...] = total[1].reshape(images, patches, width).astype(BF16)
+        own_out[...] = total[:side].reshape(images, patches, width).astype(BF16)
+        peer_out[...] = total[side:].reshape(images, patches, width).astype(BF16)
 
 
 def resident(shape):
@@ -245,7 +235,7 @@
 
 def attn_cost(x, w, products):
     images, patches, width = x.shape
-    line, _, _, cols = w.shape
+    line, _, cols = w.shape
     pairs = 2 * images * line * (cols // (4 * HEAD_DIM)) * patches * patches
     return pl.CostEstimate(
         flops=4 * images * patches * width * line * cols + products * 2 * pairs * 256,
@@ -256,7 +246,7 @@
 
 def attn_forward(own, peer, w, b, *tables):
     images, patches, width = own.shape
-    line, _, _, cols = w.shape
+    line, _, cols = w.shape
     hc = cols // 4
     rows = 2 * images * patches
     return pl.pallas_call(
@@ -265,13 +255,14 @@
         in_specs=[resident(own.shape)] * 2
         + [by_line(w.shape[1:]), by_line(b.shape[1:])]
         + [resident(table.shape) for table in tables],
-        out_specs=[by_line((rows, 3 * hc)), by_line((rows, hc))] + [resident(own.shape)] * 2,
+        out_specs=[by_line((rows, 3 * hc)), by_line((rows, hc))]
+        + [resident(own.shape)] * 2,
         out_shape=[
             jax.ShapeDtypeStruct((line, rows, 3 * hc), BF16),
             jax.ShapeDtypeStruct((line, rows, hc), BF16),
         ]
         + [jax.ShapeDtypeStruct(own.shape, BF16)] * 2,
-        scratch_shapes=[pltpu.VMEM((2, images * patches, width), F32)],
+        scratch_shapes=[pltpu.VMEM((rows, width), BF16), pltpu.VMEM((rows, width), F32)],
         compiler_params=pltpu.CompilerParams(vmem_limit_bytes=50 << 20),
         cost_estimate=attn_cost(own, w, 2),
     )(own, peer, w, b, *tables)
@@ -279,7 +270,7 @@
 
 def attn_backward(own, peer, w, qkv, *tables):
     images, patches, width = own.shape
-    line, _, _, cols = w.shape
+    line, _, cols = w.shape
     hc = cols // 4
     rows = 2 * images * patches
     return pl.pallas_call(
@@ -294,14 +285,114 @@
         out_shape=[jax.ShapeDtypeStruct((line, rows, 3 * hc), BF16)]
         + [jax.ShapeDtypeStruct(own.shape, BF16)] * 2
         + [jax.ShapeDtypeStruct((line, 1, 3 * hc), F32), jax.ShapeDtypeStruct((2, hc), F32)],
-        scratch_shapes=[pltpu.VMEM((2, images * patches, width), F32)],
+        scratch_shapes=[pltpu.VMEM((rows, width), BF16), pltpu.VMEM((rows, width), F32)],
         compiler_params=pltpu.CompilerParams(vmem_limit_bytes=50 << 20),
         cost_estimate=attn_cost(own, w, 5),
     )(own, peer, w, qkv, *tables)
 
 
-def swiglu(gate_vals, up_vals):
-    return jax.nn.silu(gate_vals) * up_vals
+def ffn_forward_kernel(
+    own_ref, peer_ref, w_ref, b_ref, gu_ref, hidden_ref, x_all,
+):
+    ff = hidden_ref.shape[2]
+    images, patches, width = own_ref.shape
+    side = images * patches
+
+    @pl.when(pl.program_id(0) == 0)
+    def _():
+        x_all[:side] = own_ref[...].reshape(side, width)
+        x_all[side:] = peer_ref[...].reshape(side, width)
+
+    made = dot_rows(x_all[...], w_ref[0]) + b_ref[0]
+    gu_ref[0] = made.astype(BF16)
+    gate, up = made[:, :ff], made[:, ff:]
+    hidden_ref[0] = (gate * up / (1.0 + jnp.exp(-gate))).astype(BF16)
+
+
+def ffn_forward(own, peer, w, b):
+    images, patches, width = own.shape
+    line, _, cols = w.shape
+    rows = 2 * images * patches
+    return pl.pallas_call(
+        ffn_forward_kernel,
+        grid=(line,),
+        in_specs=[resident(own.shape)] * 2
+        + [by_line(w.shape[1:]), by_line(b.shape[1:])],
+        out_specs=[by_line((rows, cols)), by_line((rows, cols // 2))],
+        out_shape=[
+            jax.ShapeDtypeStruct((line, rows, cols), BF16),
+            jax.ShapeDtypeStruct((line, rows, cols // 2), BF16),
+        ],
+        scratch_shapes=[pltpu.VMEM((rows, width), BF16)],
+        compiler_params=pltpu.CompilerParams(vmem_limit_bytes=50 << 20),
+        cost_estimate=pl.CostEstimate(
+            flops=2 * rows * width * line * cols,
+            bytes_accessed=2 * line * cols * (width + 2 * rows),
+            transcendentals=line * rows * cols // 2,
+        ),
+    )(own, peer, w, b)
+
+
+def ffn_backward_kernel(
+    own_ref, peer_ref, down_ref, w_ref, gu_ref,
+    d_gu_ref, own_out, peer_out, bias_ref, x_all, total,
+):
+    ff = down_ref.shape[2]
+    images, patches, width = own_ref.shape
+    side = images * patches
+    at = pl.program_id(0)
+
+    @pl.when(at == 0)
+    def _():
+        x_all[:side] = own_ref[...].reshape(side, width)
+        x_all[side:] = peer_ref[...].reshape(side, width)
+
+    d_hidden = dot_rows(x_all[...], down_ref[0])
+    gate, up = gu_ref[0, :, :ff].astype(F32), gu_ref[0, :, ff:].astype(F32)
+    sig = 1.0 / (1.0 + jnp.exp(-gate))
+    silu = gate * sig
+    d_up = d_hidden * silu
+    d_gate = d_hidden * up * (sig + silu * (1.0 - sig))
+    bias_ref[0, :, :ff] = jnp.sum(d_gate, axis=0, keepdims=True)
+    bias_ref[0, :, ff:] = jnp.sum(d_up, axis=0, keepdims=True)
+    d_gu_ref[0, :, :ff] = d_gate.astype(BF16)
+    d_gu_ref[0, :, ff:] = d_up.astype(BF16)
+    step = dot_last(d_gu_ref[0], w_ref[0])
+
+    @pl.when(at == 0)
+    def _():
+        total[...] = step
+
+    @pl.when(at > 0)
+    def _():
+        total[...] += step
+
+    @pl.when(at == pl.num_programs(0) - 1)
+    def _():
+        own_out[...] = total[:side].reshape(images, patches, width).astype(BF16)
+        peer_out[...] = total[side:].reshape(images, patches, width).astype(BF16)
+
+
+def ffn_backward(own, peer, w_down, w_gu, gate_up):
+    images, patches, width = own.shape
+    line, rows, cols = gate_up.shape
+    return pl.pallas_call(
+        ffn_backward_kernel,
+        grid=(line,),
+        in_specs=[resident(own.shape)] * 2
+        + [by_line(w_down.shape[1:]), by_line(w_gu.shape[1:]), by_line((rows, cols))],
+        out_specs=[by_line((rows, cols))] + [resident(own.shape)] * 2 + [by_line((1, cols))],
+        out_shape=[jax.ShapeDtypeStruct((line, rows, cols), BF16)]
+        + [jax.ShapeDtypeStruct(own.shape, BF16)] * 2
+        + [jax.ShapeDtypeStruct((line, 1, cols), F32)],
+        scratch_shapes=[pltpu.VMEM((rows, width), BF16), pltpu.VMEM((rows, width), F32)],
+        compiler_params=pltpu.CompilerParams(vmem_limit_bytes=50 << 20),
+        cost_estimate=pl.CostEstimate(
+            flops=3 * rows * width * line * cols,
+            bytes_accessed=2 * line * cols * (2 * width + 2 * rows),
+            transcendentals=line * rows * cols // 2,
+        ),
+    )(own, peer, w_down, w_gu, gate_up)
 
 
 def after(values, *others):
@@ -357,6 +448,22 @@
         compiler_params=pltpu.CompilerParams(vmem_limit_bytes=40 << 20),
         cost_estimate=pl.CostEstimate(flops=0, bytes_accessed=16 * own.size, transcendentals=0),
     )(spots, own, from_x, from_y, diag_a, diag_b)
+
+
+def to_whole(values):
+    line = axis_len(LINE)
+    images, patches, width = values.shape
+    moved = values.reshape(line, images // line, patches, width)
+    moved = lax.all_to_all(moved, LINE, 0, 0, tiled=True)
+    return moved.transpose(1, 0, 2, 3).reshape(images // line, line * patches, width)
+
+
+def to_parts(values):
+    line = axis_len(LINE)
+    images, patches, width = values.shape
+    moved = values.reshape(images, line, patches // line, width).transpose(1, 0, 2, 3)
+    moved = lax.all_to_all(moved, LINE, 0, 0, tiled=True)
+    return moved.reshape(images * line, patches // line, width)
 
 
 def gather_line(piece):
@@ -580,8 +687,10 @@
     gains = jnp.tile(jnp.stack((q_gain, k_gain)).astype(F32)[:, None], (1, 1, repeat))
     same, turn = head_tables(head_cols)
 
-    x_rows = lax.all_to_all(after(tokens, held_attn), LINE, 0, 1, tiled=True)
-    attn_arrived = after(first_hop(held_attn), cosines, sines)
+    x_rows = to_whole(after(tokens, cond_low))
+    attn_arrived, cosines, sines = lax.optimization_barrier(
+        (first_hop(held_attn), cosines, sines)
+    )
     _, attn_last = second_hop(attn_arrived)
     x_rows = after(x_rows, attn_last).astype(F32)
     held_gu = after(held_gu, attn_last)
@@ -589,58 +698,56 @@
     qkv_b = bias_all[:, : 6 * head_cols].reshape(line, 3, 2, head_cols)
     qkv_b = lax.dynamic_index_in_dim(qkv_b, core, 2, keepdims=False).reshape(line, 1, 3 * head_cols)
     gu_b = bias_all[:, 6 * head_cols :].reshape(line, 2, 2, ff_cols)
-    gu_b = lax.dynamic_index_in_dim(gu_b, core, 2, keepdims=False).reshape(line, 2 * ff_cols)
+    gu_b = lax.dynamic_index_in_dim(gu_b, core, 2, keepdims=False).reshape(line, 1, 2 * ff_cols)
     attn_own = modulate(x_rows, shift_a, scale_a).astype(BF16)
     attn_peer = swap(attn_own, CORES)
     w_attn = whole_weight(held_attn, attn_arrived, attn_last)
-    tables = (gains, cosines, sines, same, turn)
+    w_attn = w_attn.reshape(line, D, attn_cols)
+    patches = x_rows.shape[1]
+    rows_all = 2 * own_images * patches
+    tables = (gains, cosines.reshape(rows_all, -1), sines.reshape(rows_all, -1), same, turn)
     qkv, heads_out, part_own, part_peer = attn_forward(
         after(attn_own, held_gu), attn_peer, w_attn, qkv_b, *tables
     )
     part_peer = swap(part_peer, CORES)
     gu_passed, gu_last = second_hop(gu_arrived)
-    part_own = after(part_own, gu_passed)
+    part_own = after(part_own, gu_passed, held_down)
     held_down = after(held_down[:, :, :ff_cols], gu_last)
     down_arrived = first_hop(held_down)
     attn = part_own.astype(F32) + part_peer.astype(F32) + out_bias.astype(F32)
-    patches = x_rows.shape[1]
-    rows_all = 2 * own_images * patches
 
     def as_rows(*values):
         return [value.reshape(own_images * patches, D) for value in values]
 
     mid = x_rows + gate_a * attn
-    ffn_in = with_peer(modulate(mid, shift_f, scale_f).astype(BF16))
-    ffn_in = ffn_in.reshape(rows_all, D)
-    w_gu = whole_weight(held_gu, gu_arrived, after(gu_last, ffn_in)).reshape(line, D, 2 * ff_cols)
-    gate_up = jnp.einsum("rd,zdn->zrn", ffn_in, w_gu, preferred_element_type=F32) + gu_b[:, None]
-    down_passed, down_last = second_hop(after(down_arrived, gate_up))
-    gate_up = after(gate_up, down_passed)
-    gate_vals, up_vals = gate_up[..., :ff_cols], gate_up[..., ff_cols:]
-    hidden = swiglu(gate_vals, up_vals).astype(BF16)
-    grad_out = lax.all_to_all(after(cotangent, heads_out), LINE, 0, 1, tiled=True).astype(F32)
+    ffn_own = modulate(mid, shift_f, scale_f).astype(BF16)
+    ffn_peer = swap(ffn_own, CORES)
+    grad_out = to_whole(after(cotangent, heads_out)).astype(F32)
     d_ffn_f = gate_f * grad_out
     d_ffn_own = d_ffn_f.astype(BF16)
-    d_ffn = jnp.concatenate(as_rows(d_ffn_own, swap(d_ffn_own, CORES)), axis=0)
-    down_parts, down_got = send_diagonal([([d_ffn], hidden)])
-    hidden, d_ffn = after((hidden, d_ffn), down_parts)
+    d_ffn_peer = swap(d_ffn_own, CORES)
+    w_gu = whole_weight(held_gu, gu_arrived, gu_last).reshape(line, D, 2 * ff_cols)
+    down_passed, down_last = second_hop(after(down_arrived, w_gu))
+    gate_up, hidden = ffn_forward(after(ffn_own, down_passed), ffn_peer, w_gu, gu_b)
+    down_parts, down_got = send_diagonal(
+        [(as_rows(d_ffn_own, d_ffn_peer), after(hidden, down_last))]
+    )
     w_down = whole_weight(held_down, down_arrived, down_last).reshape(line, D, ff_cols)
-    ffn = jnp.einsum("zrf,zdf->rd", hidden, w_down, preferred_element_type=F32)
+    d_gu, d_in_own, d_in_peer, gu_bias_part = ffn_backward(
+        after(d_ffn_own, down_parts), d_ffn_peer, w_down, w_gu, gate_up
+    )
+    d_in_peer = swap(d_in_peer, CORES)
+    down_sent, down_blocks = send_blocks(down_parts, after(down_got, d_gu))
+    gu_parts, gu_got = send_diagonal(
+        [(as_rows(ffn_own, ffn_peer), after(d_gu, down_sent))]
+    )
+    ffn = jnp.einsum("zrf,zdf->rd", after(hidden, gu_parts), w_down, preferred_element_type=F32)
     ffn = fold_peer(ffn.reshape(2 * own_images, patches, D)) + down_bias.astype(F32)
-    output = lax.all_to_all((mid + gate_f * ffn).astype(BF16), LINE, 1, 0, tiled=True)
+    output = to_parts((mid + gate_f * ffn).astype(BF16))
 
     down_bias_part = jnp.sum(d_ffn_f, axis=(0, 1))
     d_gate_f = jnp.sum(grad_out * ffn, axis=1, keepdims=True)
-    d_hidden = jnp.einsum("rd,zdf->zrf", d_ffn, w_down, preferred_element_type=F32)
-    d_gate, d_up = jax.vjp(swiglu, gate_vals, up_vals)[1](d_hidden)
-    d_gu = jnp.concatenate((d_gate, d_up), axis=-1).astype(BF16)
-    gu_bias_part = jnp.sum(d_gu, axis=1, dtype=F32)
-    down_sent, down_blocks = send_blocks(down_parts, down_got)
-    gu_parts, gu_got = send_diagonal([([ffn_in], after(d_gu, down_sent))])
-    d_gu = after(d_gu, gu_parts)
-    d_ffn_in = jnp.einsum("zrn,zdn->rd", d_gu, w_gu, preferred_element_type=F32)
-    d_ffn_in = fold_peer(d_ffn_in.reshape(2 * own_images, patches, D))
-    d_ffn_in = after(d_ffn_in, down_blocks)
+    d_ffn_in = after(d_in_own.astype(F32) + d_in_peer.astype(F32), down_blocks)
     g_down = add_blocks(down_parts if down_blocks is not None else down_sent, down_blocks)
     g_down = scatter_line(g_down)
     mid_grad, d_shift_f, d_scale_f = jax.vjp(modulate, mid, shift_f, scale_f)[1](d_ffn_in)
@@ -655,13 +762,13 @@
         after(d_attn_own, gu_sent), d_attn_peer, w_attn, qkv, *tables
     )
     d_in_peer = swap(d_in_peer, CORES)
-    g_gu = add_blocks(gu_parts if gu_blocks is not None else gu_sent, after(gu_blocks, d_qkv))
     attn_parts, attn_got = send_diagonal(
         [
-            (as_rows(attn_own, attn_peer), after(d_qkv, g_gu, output)),
+            (as_rows(attn_own, attn_peer), after(d_qkv, output)),
             (as_rows(d_attn_own, d_attn_peer), heads_out),
         ]
     )
+    g_gu = add_blocks(gu_parts if gu_blocks is not None else gu_sent, after(gu_blocks, attn_parts))
     g_gu = scatter_line(after(g_gu, g_down))
     gain_part = gain_part.reshape(2, repeat, HEAD_DIM).sum(axis=1)
     d_attn_in = d_in_own.astype(F32) + d_in_peer.astype(F32)
@@ -677,7 +784,7 @@
         d_mod_low[:, None], (data, line, own_images, 6, chunk)
     ).reshape(devices, own_images * 6 * chunk)
     attn_got, tokens_sent = lax.optimization_barrier((attn_got, tokens_sent))
-    tokens_grad = lax.all_to_all(tokens_sent, LINE, 1, 0, tiled=True)
+    tokens_grad = to_parts(tokens_sent)
     attn_sent, attn_blocks = send_blocks(attn_parts, attn_got)
     d_mod_all = lax.all_to_all(d_mod_low, EVERY, 0, 0, tiled=True)
     d_mod_all = d_mod_all.reshape(data * images, 6 * chunk)
@@ -705,7 +812,7 @@
     count = flat.shape[0]
     flat = jnp.concatenate((flat, d_cond.reshape(-1)))
     flat = sum_by_swaps(sum_by_swaps(flat, CORES), CHIPS)
-    g_attn = add_blocks(attn_parts, after(attn_blocks, flat))
+    g_attn = add_blocks(attn_parts, attn_blocks)
     g_attn, tokens_grad = lax.optimization_barrier((after(g_attn, g_gu), tokens_grad))
     g_attn = scatter_line(g_attn)
     d_cond = flat[count:].reshape(d_cond.shape)

time: 537 us -> 511 us (0.952)
  Pallas kernels: 110 us -> 139 us
  matrix products: 40.1 us -> 13.8 us
  waiting for transfers between devices: 163 us -> 137 us
  local copies, waits for them, and re-layouts: 60.9 us -> 68.7 us
  other arithmetic: 74.1 us -> 66.9 us
    pallas_call x0 -> x2, Pallas kernels: none -> 37.3 us  [the longest x1 24.3 us: ffn_backward(): pl.pallas_call(ffn_backward_kernel, grid=(line,), in_specs=[resident(own....]
    dot_general x4 -> x1, matrix products: 35.8 us -> 6.14 us  [on_device(): jnp.einsum('zrf,zdf->rd', after(hidden, gu_parts), w_down, preferred_elem...]
    ppermute x42, waiting for transfers between devices: 110 us -> 93.1 us  [swap(): return lax.ppermute(values, name, [(i, i ^ bit) for i in range(count)])]
    reduce_scatter x3, waiting for transfers between devices: 9.8 us -> 0.01 us  [scatter_line(): return lax.psum_scatter(part, LINE, scatter_dimension=0, tiled=False)]
    concatenate x3 -> x0, other arithmetic: 9.61 us -> none  [the longest x1 5.97 us: on_device(): d_gu = jnp.concatenate((d_gate, d_up), axis=-1).astype(BF16)]
    unnamed x149 -> x151, local copies, waits for them, and re-layouts: 19.4 us -> 28.6 us
  transfers between devices with their start and end apart: 55 -> 55, of which waited for: 26 -> 25; matrix products, arithmetic and copies ran while one was open for 26% -> 23% of each run, Pallas kernels for 17% -> 26%
where the time goes in v3:
time: 511 us; the launch traced here: 505 us
  Pallas kernels  139 us (27%)
  waiting for transfers between devices  137 us (27%)
  local copies, waits for them, and re-layouts  68.7 us (13%)
  other arithmetic  66.9 us (13%)
  starting transfers between devices  62.5 us (12%)
  between operations  16 us (3%)
  matrix products  13.8 us (3%)
    ppermute x42, waiting for transfers between devices, swap(): return lax.ppermute(values, name, [(i, i ^ bit) for i in range(count)])  93.1 us
    pallas_call x1, Pallas kernels, attn_backward(): pl.pallas_call(attn_backward_kernel, grid=(line,), in_specs=[resident(own...  36.3 us
    pallas_call x3, Pallas kernels, chip_products(): pl.pallas_call(functools.partial(grad_kernel, tuple((len(group) for group...  35 us
    ppermute x42, starting transfers between devices, swap(): return lax.ppermute(values, name, [(i, i ^ bit) for i in range(count)])  30 us
    unnamed x151, local copies, waits for them, and re-layouts  28.6 us
    all_gather x3, waiting for transfers between devices, gather_line(): return lax.all_gather(piece, LINE, axis=0)  25.1 us
    pallas_call x1, Pallas kernels, ffn_backward(): pl.pallas_call(ffn_backward_kernel, grid=(line,), in_specs=[resident(own....  24.3 us
    pallas_call x1, Pallas kernels, attn_forward(): pl.pallas_call(attn_forward_kernel, grid=(line,), in_specs=[resident(own....  22.2 us
  transfers between devices with their start and end apart: 55, of which 25 were waited for; matrix products, arithmetic and copies ran while one was open for 23% of the time, Pallas kernels for 26%

profile of v3, /device:TPU:0, one launch (start us, length us, event | category | flops | bytes accessed | tf_op | source)
XLA Modules:
  0.0 504.5 jit_solution(2594519695150318587)
XLA Ops:
  15.4 5.1 %all-to-all-start = ((s32[8,2,8]{2,1,0:T(2,128)}), s32[8,2,8]{2,1,0:T(2,128)S(1)}, u32[]{:S(2)}, u32[]{:S(2)}) async-start(s32[8,2,8]{2,1,0:T(2,128)} %broadcast_in_dim.89), calls=%async_computation | async-start | bytes 16384 | tf_op jit(solution)/shard_map/all_to_all | solution.py:657
  20.9 4.3 all-to-all-done
  25.4 2.3 multiply_convert_fusion.1
  29.7 4.1 all-to-all-start.2
  33.8 24.8 %all-gather.7.cloned.1.call-done = bf16[1152,576]{1,0:T(8,128)(2,1)} async-done(((bf16[288,576]{1,0:T(8,128)(2,1)}), bf16[1152,576]{1,0:T(8,128)(2,1)}) %all-gather.7.cloned.1.call-update) | async-done | bytes 1327120 | tf_op jit(solution)/shard_map/all_gather | solution.py:470
  61.6 4.3 all-to-all-start.1
  67.8 5.7 %fusion.15 = (f32[4,256,144]{2,1,0:T(8,128)}, f32[4,256,144]{2,1,0:T(8,128)}) fusion(f32[144]{0:T(256)S(1)} %multiply_power_fusion, s32[4,256]{1,0:T(4,128)S(1)} %get-tuple-element.249, s32[4,256]{1,0:T(4,128)S(1)} %get-tuple-element.248, pred[144]{0:T(512)(128)(4,1)S(1)} %broadcast_compare_fusion.1), kind=kLoop, calls=%fused_computation.56 | loop fusion | flops 442368 | bytes 1188560 | tf_op jit(solution)/shard_map/sin | solution.py:43
  77.1 15.8 %collective-permute-done.2.y_ref = bf16[4,288,576]{2,1,0:T(8,128)(2,1)S(1)} collective-permute-done((bf16[4,288,576]{2,1,0:T(8,128)(2,1)}, bf16[4,288,576]{2,1,0:T(8,128)(2,1)S(1)}, u32[]{:S(2)}, u32[]{:S(2)}) %collective-permute-start.2) | collective-permute-done | bytes 1327136 | tf_op jit(solution)/shard_map/ppermute | solution.py:408
  94.2 2.0 slice.161
  99.8 11.8 %all-to-all-done.1 = bf16[4,2,64,1152]{3,2,1,0:T(8,128)(2,1)} async-done(((bf16[4,2,64,1152]{3,2,1,0:T(8,128)(2,1)}), bf16[4,2,64,1152]{3,2,1,0:T(8,128)(2,1)}, u32[]{:S(2)}, u32[]{:S(2)}) %all-to-all-start.1) | async-done | bytes 1179680 | tf_op jit(solution)/shard_map/all_to_all | solution.py:457
  126.8 2.8 shard_map.316
  129.7 2.5 copy-done.2
  132.2 22.2 %shard_map.317 = (bf16[4,1024,432]{2,1,0:T(8,128)(2,1)}, bf16[4,1024,144]{2,1,0:T(8,128)(2,1)}, bf16[2,256,1152]{2,1,0:T(8,128)(2,1)S(1)}, bf16[2,256,1152]{2,1,0:T(8,128)(2,1)}) custom-call(bf16[2,256,1152]{2,1,0:T(8,128)(2,1)} %copy-done.7, bf16[2,256,1152]{2,1,0:T(8,128)(2,1)} %collective-permute-done.6.peer_ref, bf16[4,1152,576]{2,1,0:T(8,128)(2,1)} %bitcast.177, ...), custom_call_target="tpu_custom_call" | custom-call | flops 7583301632 | bytes 14745600 | tf_op jit(solution)/shard_map/pallas_call | solution.py:252
  154.5 4.3 all-to-all-start.3
  160.3 3.9 collective-permute-done.8.y_ref
  168.1 2.1 multiply_reduce_fusion.3
  171.9 14.6 %collective-permute-done.11.db_ref = bf16[2,288,768]{2,1,0:T(8,128)(2,1)S(1)} collective-permute-done((bf16[2,288,768]{2,1,0:T(8,128)(2,1)S(1)}, bf16[2,288,768]{2,1,0:T(8,128)(2,1)S(1)}, u32[]{:S(2)}, u32[]{:S(2)}) %collective-permute-start.11) | collective-permute-done | bytes 884768 | tf_op jit(solution)/shard_map/ppermute | solution.py:408
  198.6 3.2 shard_map.318
  201.8 2.8 copy-done.1
  205.9 3.6 collective-permute-done.13.y_ref
  214.5 12.9 %shard_map.319 = (bf16[4,1024,768]{2,1,0:T(8,128)(2,1)}, bf16[4,1024,384]{2,1,0:T(8,128)(2,1)}) custom-call(bf16[2,256,1152]{2,1,0:T(8,128)(2,1)} %add_convert_fusion.3.own_ref, bf16[2,256,1152]{2,1,0:T(8,128)(2,1)} %collective-permute-done.14.peer_ref, bf16[4,1152,768]{2,1,0:T(8,128)(2,1)} %bitcast.175, f32[4,1,768]{2,1,0:T(1,128)S(1)} %bitcast.192), custom_call_target="tpu_custom_call" | custom-call | flops 7247757312 | bytes 19660800 | tf_op jit(solution)/shard_map/pallas_call | solution.py:316
  227.4 2.6 shard_map.321
  231.8 8.4 %shard_map.320 = (bf16[4,144,384]{2,1,0:T(8,128)(2,1)S(1)}, bf16[4,144,384]{2,1,0:T(8,128)(2,1)S(1)}, bf16[4,288,384]{2,1,0:T(8,128)(2,1)S(1)}, bf16[4,288,384]{2,1,0:T(8,128)(2,1)S(1)}, bf16[4,288,384]{2,1,0:T(8,128)(2,1)S(1)}) custom-call(s32[4]{0:T(128)S(1)} %broadcast_xor_fusion.spot_ref, bf16[512,1152]{1,0:T(8,128)(2,1)} %fusion.11.refs_0_, ...), custom_call_target="tpu_custom_call" | custom-call | flops 3623878656 | bytes 6684672 | tf_op jit(solution)/shard_map/pallas_call | solution.py:539
  241.7 24.3 %shard_map.322 = (bf16[4,1024,768]{2,1,0:T(8,128)(2,1)}, bf16[2,256,1152]{2,1,0:T(8,128)(2,1)S(1)}, bf16[2,256,1152]{2,1,0:T(8,128)(2,1)S(1)}, f32[4,1,768]{2,1,0:T(1,128)S(1)}) custom-call(bf16[2,256,1152]{2,1,0:T(8,128)(2,1)} %fusion.12.own_ref, bf16[2,256,1152]{2,1,0:T(8,128)(2,1)} %collective-permute-done.15.peer_ref, bf16[4,1152,384]{2,1,0:T(8,128)(2,1)} %bitcast.179, ...), custom_call_target="tpu_custom_call" | custom-call | flops 10871635968 | bytes 26738688 | tf_op jit(solution)/shard_map/pallas_call | solution.py:379
  270.9 12.7 %shard_map.323 = (bf16[4,144,768]{2,1,0:T(8,128)(2,1)}, bf16[4,144,768]{2,1,0:T(8,128)(2,1)}, bf16[4,288,768]{2,1,0:T(8,128)(2,1)}, bf16[4,288,768]{2,1,0:T(8,128)(2,1)}, bf16[4,288,768]{2,1,0:T(8,128)(2,1)}) custom-call(s32[4]{0:T(128)S(1)} %broadcast_xor_fusion.spot_ref, bf16[512,1152]{1,0:T(8,128)(2,1)} %bitcast.30.refs_0_, ...), custom_call_target="tpu_custom_call" | custom-call | flops 7247757312 | bytes 13369344 | tf_op jit(solution)/shard_map/pallas_call | solution.py:539
  285.1 6.1 %convolution_bitcast_fusion = f32[1024,1152]{1,0:T(8,128)S(1)} fusion(bf16[4,1024,384]{2,1,0:T(8,128)(2,1)} %get-tuple-element.110.refs_2_, bf16[4,1152,384]{2,1,0:T(8,128)(2,1)S(1)} %bitcast.180), kind=kOutput, calls=%fused_computation.5 | convolution fusion | flops 3623878656 | bytes 11403264 | tf_op jit(solution)/shard_map/zrf,zdf->rd/dot_general | solution.py:744
  294.3 3.7 multiply_reduce_fusion.4
  300.8 2.7 add_convert_fusion.4
  303.5 7.2 %collective-permute-done.26 = bf16[4,144,768]{2,1,0:T(8,128)(2,1)} collective-permute-done((bf16[4,144,768]{2,1,0:T(8,128)(2,1)}, bf16[4,144,768]{2,1,0:T(8,128)(2,1)}, u32[]{:S(2)}, u32[]{:S(2)}) %collective-permute-start.26) | collective-permute-done | bytes 884768 | tf_op jit(solution)/shard_map/ppermute | solution.py:408
  315.7 4.3 all-to-all-start.4
  320.0 1.9 slice_add_fusion.1
  324.9 36.3 %shard_map.324 = (bf16[4,1024,432]{2,1,0:T(8,128)(2,1)}, bf16[2,256,1152]{2,1,0:T(8,128)(2,1)S(1)}, bf16[2,256,1152]{2,1,0:T(8,128)(2,1)}, f32[4,1,432]{2,1,0:T(1,128)S(1)}, f32[2,144]{1,0:T(2,128)S(1)}) custom-call(bf16[2,256,1152]{2,1,0:T(8,128)(2,1)} %multiply_convert_fusion.own_ref, bf16[2,256,1152]{2,1,0:T(8,128)(2,1)} %collective-permute-done.24.peer_ref, ...), custom_call_target="tpu_custom_call" | custom-call | flops 10804527104 | bytes 14745600 | tf_op jit(solution)/shard_map/pallas_call | solution.py:276
  361.3 2.1 fusion.5
  366.1 13.8 %shard_map.325 = (bf16[4,144,576]{2,1,0:T(8,128)(2,1)}, bf16[4,144,576]{2,1,0:T(8,128)(2,1)}, bf16[4,288,576]{2,1,0:T(8,128)(2,1)}, bf16[4,288,576]{2,1,0:T(8,128)(2,1)}, bf16[4,288,576]{2,1,0:T(8,128)(2,1)}) custom-call(s32[4]{0:T(128)S(1)} %broadcast_xor_fusion.spot_ref, bf16[512,1152]{1,0:T(8,128)(2,1)S(1)} %bitcast.187, ...), custom_call_target="tpu_custom_call" | custom-call | flops 5435817984 | bytes 10027008 | tf_op jit(solution)/shard_map/pallas_call | solution.py:539
  381.7 4.0 add_convert_fusion
  387.0 2.4 fusion.4
  391.3 2.3 reduce.16
  394.5 5.2 %all-to-all-start.6 = ((bf16[32,2,864]{2,1,0:T(2,128)(2,1)}), bf16[32,2,864]{2,1,0:T(2,128)(2,1)S(1)}, u32[]{:S(2)}, u32[]{:S(2)}) async-start(bf16[32,2,864]{2,1,0:T(2,128)(2,1)} %reshape.610), calls=%async_computation.6 | async-start | bytes 229376 | tf_op jit(solution)/shard_map/all_to_all | solution.py:789
  399.7 2.9 fusion.8
  413.1 4.6 all-to-all-start.5
  426.0 16.8 %collective-permute-done.31 = bf16[4,288,576]{2,1,0:T(8,128)(2,1)} collective-permute-done((bf16[4,288,576]{2,1,0:T(8,128)(2,1)}, bf16[4,288,576]{2,1,0:T(8,128)(2,1)}, u32[]{:S(2)}, u32[]{:S(2)}) %collective-permute-start.31) | collective-permute-done | bytes 1327136 | tf_op jit(solution)/shard_map/ppermute | solution.py:408
  442.7 2.6 collective-permute-done.30
  445.4 3.5 add_convert_fusion.1
  448.8 2.8 all-to-all-done.5
  455.2 3.2 collective-permute-done.33
  465.4 6.8 %collective-permute-done.35 = f32[18960]{0:T(1024)S(1)} collective-permute-done((f32[18960]{0:T(1024)S(1)}, f32[18960]{0:T(1024)S(1)}, u32[]{:S(2)}, u32[]{:S(2)}) %collective-permute-start.35) | collective-permute-done | bytes 75872 | tf_op jit(solution)/shard_map/ppermute | solution.py:408
  474.0 9.2 %collective-permute-done.36 = f32[18960]{0:T(1024)S(1)} collective-permute-done((f32[18960]{0:T(1024)S(1)}, f32[18960]{0:T(1024)S(1)}, u32[]{:S(2)}, u32[]{:S(2)}) %collective-permute-start.36) | collective-permute-done | bytes 75872 | tf_op jit(solution)/shard_map/ppermute | solution.py:408
  495.1 2.4 copy.138
  (422 shorter events, 138.3 us)
Async XLA Ops:
  7.2 51.4 %all-gather.7.cloned.1.call-start = ((), (), s32[]{:S(2)}) async-start(), calls=%async_computation.13 | async-start | bytes 1843200 | tf_op jit(solution)/shard_map/all_gather | solution.py:470
  15.4 9.8 %all-to-all-start = ((s32[8,2,8]{2,1,0:T(2,128)}), s32[8,2,8]{2,1,0:T(2,128)S(1)}, u32[]{:S(2)}, u32[]{:S(2)}) async-start(s32[8,2,8]{2,1,0:T(2,128)} %broadcast_in_dim.89), calls=%async_computation | async-start | bytes 16384 | tf_op jit(solution)/shard_map/all_to_all | solution.py:657
  29.7 31.9 %all-to-all-start.2 = ((f32[32,1,2028]{2,1,0:T(1,128)}), f32[32,1,2028]{2,1,0:T(1,128)}, u32[]{:S(2)}, u32[]{:S(2)}) async-start(f32[32,1,2028]{2,1,0:T(1,128)} %all_to_all.31), calls=%async_computation.2 | async-start | bytes 524288 | tf_op jit(solution)/shard_map/all_to_all | solution.py:676
  58.7 34.2 %collective-permute-start.2 = (bf16[4,288,576]{2,1,0:T(8,128)(2,1)}, bf16[4,288,576]{2,1,0:T(8,128)(2,1)S(1)}, u32[]{:S(2)}, u32[]{:S(2)}) collective-permute-start(bf16[4,288,576]{2,1,0:T(8,128)(2,1)} %bitcast.184), channel_id=1, source_target_pairs={{0,16},{8,24},{16,0},{24,8},{1,17},{9,25},{17,1},{25,9},{2,18},{10... | collective-permute-start | bytes 3981320 | tf_op jit(solution)/shard_map/ppermute | solution.py:408
  60.1 34.1 %collective-permute-start.1 = (bf16[4,288,576]{2,1,0:T(8,128)(2,1)}, bf16[4,288,576]{2,1,0:T(8,128)(2,1)}, u32[]{:S(2)}, u32[]{:S(2)}) collective-permute-start(bf16[4,288,576]{2,1,0:T(8,128)(2,1)} %bitcast.185), channel_id=1, source_target_pairs={{0,8},{8,0},{16,24},{24,16},{1,9},{9,1},{17,25},{25,17},{2,10},{10... | collective-permute-start | bytes 3981320 | tf_op jit(solution)/shard_map/ppermute | solution.py:408
  61.6 50.0 %all-to-all-start.1 = ((bf16[4,2,64,1152]{3,2,1,0:T(8,128)(2,1)}), bf16[4,2,64,1152]{3,2,1,0:T(8,128)(2,1)}, u32[]{:S(2)}, u32[]{:S(2)}) async-start(bf16[4,2,64,1152]{3,2,1,0:T(8,128)(2,1)} %bitcast.204), calls=%async_computation.1 | async-start | bytes 2359296 | tf_op jit(solution)/shard_map/all_to_all | solution.py:457
  65.9 57.3 %all-gather.9.cloned.1.call-start = ((), (), s32[]{:S(2)}) async-start(), calls=%async_computation.14 | async-start | bytes 2211840 | tf_op jit(solution)/shard_map/all_gather | solution.py:470
  74.5 84.4 %all-gather.11.cloned.1.call-start = ((), (), s32[]{:S(2)}) async-start(), calls=%async_computation.15 | async-start | bytes 1474560 | tf_op jit(solution)/shard_map/all_gather | solution.py:470
  97.2 17.2 %collective-permute-start.5 = (bf16[2,288,576]{2,1,0:T(8,128)(2,1)}, bf16[2,288,576]{2,1,0:T(8,128)(2,1)S(1)}, u32[]{:S(2)}, u32[]{:S(2)}) collective-permute-start(bf16[2,288,576]{2,1,0:T(8,128)(2,1)} %slice.162), channel_id=1, source_target_pairs={{0,8},{8,0},{16,24},{24,16},{1,9},{9,1},{17,25},{25,17},{2,10},{10... | collective-permute-start | bytes 1990664 | tf_op jit(solution)/shard_map/ppermute | solution.py:408
  98.6 17.1 %collective-permute-start.4 = (bf16[2,288,576]{2,1,0:T(8,128)(2,1)}, bf16[2,288,576]{2,1,0:T(8,128)(2,1)}, u32[]{:S(2)}, u32[]{:S(2)}) collective-permute-start(bf16[2,288,576]{2,1,0:T(8,128)(2,1)} %slice.161), channel_id=1, source_target_pairs={{0,16},{8,24},{16,0},{24,8},{1,17},{9,25},{17,1},{25,9},{2,18},{10... | collective-permute-start | bytes 1990664 | tf_op jit(solution)/shard_map/ppermute | solution.py:408
  116.5 15.7 %collective-permute-start.6 = (bf16[2,256,1152]{2,1,0:T(8,128)(2,1)S(1)}, bf16[2,256,1152]{2,1,0:T(8,128)(2,1)}, u32[]{:S(2)}, u32[]{:S(2)}) collective-permute-start(bf16[2,256,1152]{2,1,0:T(8,128)(2,1)S(1)} %fusion.3.own_ref), channel_id=1, source_target_pairs={{0,4},{4,0},{1,5},{5,1},{2,6},{6,2},{3,7},{7,3},{8,12},{12,8},{9,1... | collective-permute-start | bytes 3538952 | tf_op jit(solution)/shard_map/ppermute | solution.py:408
  123.1 41.1 %collective-permute-start.8 = (bf16[4,288,768]{2,1,0:T(8,128)(2,1)}, bf16[4,288,768]{2,1,0:T(8,128)(2,1)}, u32[]{:S(2)}, u32[]{:S(2)}) collective-permute-start(bf16[4,288,768]{2,1,0:T(8,128)(2,1)} %bitcast.181), channel_id=1, source_target_pairs={{0,16},{8,24},{16,0},{24,8},{1,17},{9,25},{17,1},{25,9},{2,18},{10... | collective-permute-start | bytes 5308424 | tf_op jit(solution)/shard_map/ppermute | solution.py:408
  123.7 42.6 %collective-permute-start.7 = (bf16[4,288,768]{2,1,0:T(8,128)(2,1)}, bf16[4,288,768]{2,1,0:T(8,128)(2,1)}, u32[]{:S(2)}, u32[]{:S(2)}) collective-permute-start(bf16[4,288,768]{2,1,0:T(8,128)(2,1)} %bitcast.182), channel_id=1, source_target_pairs={{0,8},{8,0},{16,24},{24,16},{1,9},{9,1},{17,25},{25,17},{2,10},{10... | collective-permute-start | bytes 5308424 | tf_op jit(solution)/shard_map/ppermute | solution.py:408
  154.4 13.7 %collective-permute-start.9 = (bf16[2,256,1152]{2,1,0:T(8,128)(2,1)}, bf16[2,256,1152]{2,1,0:T(8,128)(2,1)}, u32[]{:S(2)}, u32[]{:S(2)}) collective-permute-start(bf16[2,256,1152]{2,1,0:T(8,128)(2,1)} %get-tuple-element.85), channel_id=1, source_target_pairs={{0,4},{4,0},{1,5},{5,1},{2,6},{6,2},{3,7},{7,3},{8,12},{12,8},{9,1... | collective-permute-start | bytes 3538952 | tf_op jit(solution)/shard_map/ppermute | solution.py:408
  154.5 36.7 %all-to-all-start.3 = ((bf16[4,2,64,1152]{3,2,1,0:T(8,128)(2,1)}), bf16[4,2,64,1152]{3,2,1,0:T(8,128)(2,1)}, u32[]{:S(2)}, u32[]{:S(2)}) async-start(bf16[4,2,64,1152]{3,2,1,0:T(8,128)(2,1)} %bitcast.32), calls=%async_computation.3 | async-start | bytes 2359296 | tf_op jit(solution)/shard_map/all_to_all | solution.py:457
  158.8 295.3 %reduce-scatter.8.cloned.1.call-start = ((), (), s32[]{:S(2)}) async-start(), calls=%async_computation.12 | async-start | bytes 1105920 | tf_op jit(solution)/shard_map/reduce_scatter | solution.py:582
  165.5 21.1 %collective-permute-start.11 = (bf16[2,288,768]{2,1,0:T(8,128)(2,1)S(1)}, bf16[2,288,768]{2,1,0:T(8,128)(2,1)S(1)}, u32[]{:S(2)}, u32[]{:S(2)}) collective-permute-start(bf16[2,288,768]{2,1,0:T(8,128)(2,1)S(1)} %slice.223), channel_id=1, source_target_pairs={{0,8},{8,0},{16,24},{24,16},{1,9},{9,1},{17,25},{25,17},{2,10},{10... | collective-permute-start | bytes 2654216 | tf_op jit(solution)/shard_map/ppermute | solution.py:408
  167.5 21.0 %collective-permute-start.10 = (bf16[2,288,768]{2,1,0:T(8,128)(2,1)S(1)}, bf16[2,288,768]{2,1,0:T(8,128)(2,1)S(1)}, u32[]{:S(2)}, u32[]{:S(2)}) collective-permute-start(bf16[2,288,768]{2,1,0:T(8,128)(2,1)S(1)} %slice.222), channel_id=1, source_target_pairs={{0,16},{8,24},{16,0},{24,8},{1,17},{9,25},{17,1},{25,9},{2,18},{10... | collective-permute-start | bytes 2654216 | tf_op jit(solution)/shard_map/ppermute | solution.py:408
  171.9 42.6 %collective-permute-start.14 = (bf16[2,256,1152]{2,1,0:T(8,128)(2,1)}, bf16[2,256,1152]{2,1,0:T(8,128)(2,1)}, u32[]{:S(2)}, u32[]{:S(2)}) collective-permute-start(bf16[2,256,1152]{2,1,0:T(8,128)(2,1)} %add_convert_fusion.3.own_ref), channel_id=1, source_target_pairs={{0,4},{4,0},{1,5},{5,1},{2,6},{6,2},{3,7},{7,3},{8,12},{12,8},{9,1... | collective-permute-start | bytes 3538952 | tf_op jit(solution)/shard_map/ppermute | solution.py:408
  189.4 20.2 %collective-permute-start.13 = (bf16[4,288,384]{2,1,0:T(8,128)(2,1)S(1)}, bf16[4,288,384]{2,1,0:T(8,128)(2,1)}, u32[]{:S(2)}, u32[]{:S(2)}) collective-permute-start(bf16[4,288,384]{2,1,0:T(8,128)(2,1)S(1)} %slice.227.own_ref), channel_id=1, source_target_pairs={{0,16},{8,24},{16,0},{24,8},{1,17},{9,25},{17,1},{25,9},{2,18},{10... | collective-permute-start | bytes 2654216 | tf_op jit(solution)/shard_map/ppermute | solution.py:408
  189.8 19.8 %collective-permute-start.12 = (bf16[4,288,384]{2,1,0:T(8,128)(2,1)S(1)}, bf16[4,288,384]{2,1,0:T(8,128)(2,1)}, u32[]{:S(2)}, u32[]{:S(2)}) collective-permute-start(bf16[4,288,384]{2,1,0:T(8,128)(2,1)S(1)} %slice.227.own_ref), channel_id=1, source_target_pairs={{0,8},{8,0},{16,24},{24,16},{1,9},{9,1},{17,25},{25,17},{2,10},{10... | collective-permute-start | bytes 2654216 | tf_op jit(solution)/shard_map/ppermute | solution.py:408
  194.1 37.6 %collective-permute-start.15 = (bf16[2,256,1152]{2,1,0:T(8,128)(2,1)}, bf16[2,256,1152]{2,1,0:T(8,128)(2,1)}, u32[]{:S(2)}, u32[]{:S(2)}) collective-permute-start(bf16[2,256,1152]{2,1,0:T(8,128)(2,1)} %fusion.12.own_ref), channel_id=1, source_target_pairs={{0,4},{4,0},{1,5},{5,1},{2,6},{6,2},{3,7},{7,3},{8,12},{12,8},{9,1... | collective-permute-start | bytes 3538952 | tf_op jit(solution)/shard_map/ppermute | solution.py:408
  211.8 15.6 %collective-permute-start.17 = (bf16[2,288,384]{2,1,0:T(8,128)(2,1)S(1)}, bf16[2,288,384]{2,1,0:T(8,128)(2,1)S(1)}, u32[]{:S(2)}, u32[]{:S(2)}) collective-permute-start(bf16[2,288,384]{2,1,0:T(8,128)(2,1)S(1)} %slice.178), channel_id=1, source_target_pairs={{0,8},{8,0},{16,24},{24,16},{1,9},{9,1},{17,25},{25,17},{2,10},{10... | collective-permute-start | bytes 1327112 | tf_op jit(solution)/shard_map/ppermute | solution.py:408
  213.2 14.2 %collective-permute-start.16 = (bf16[2,288,384]{2,1,0:T(8,128)(2,1)S(1)}, bf16[2,288,384]{2,1,0:T(8,128)(2,1)S(1)}, u32[]{:S(2)}, u32[]{:S(2)}) collective-permute-start(bf16[2,288,384]{2,1,0:T(8,128)(2,1)S(1)} %slice.177), channel_id=1, source_target_pairs={{0,16},{8,24},{16,0},{24,8},{1,17},{9,25},{17,1},{25,9},{2,18},{10... | collective-permute-start | bytes 1327112 | tf_op jit(solution)/shard_map/ppermute | solution.py:408
  240.2 25.8 %collective-permute-start.18 = (bf16[4,144,384]{2,1,0:T(8,128)(2,1)S(1)}, bf16[4,144,384]{2,1,0:T(8,128)(2,1)S(1)}, u32[]{:S(2)}, u32[]{:S(2)}) collective-permute-start(bf16[4,144,384]{2,1,0:T(8,128)(2,1)S(1)} %get-tuple-element.94), channel_id=1, source_target_pairs={{0,8},{8,0},{16,24},{24,16},{1,9},{9,1},{17,25},{25,17},{2,10},{10... | collective-permute-start | bytes 1327112 | tf_op jit(solution)/shard_map/ppermute | solution.py:408
  241.3 24.7 %collective-permute-start.19 = (bf16[4,144,384]{2,1,0:T(8,128)(2,1)S(1)}, bf16[4,144,384]{2,1,0:T(8,128)(2,1)S(1)}, u32[]{:S(2)}, u32[]{:S(2)}) collective-permute-start(bf16[4,144,384]{2,1,0:T(8,128)(2,1)S(1)} %get-tuple-element.95), channel_id=1, source_target_pairs={{0,16},{8,24},{16,0},{24,8},{1,17},{9,25},{17,1},{25,9},{2,18},{10... | collective-permute-start | bytes 1327112 | tf_op jit(solution)/shard_map/ppermute | solution.py:408
  266.1 25.3 %collective-permute-start.21 = (bf16[2,256,1152]{2,1,0:T(8,128)(2,1)S(1)}, bf16[2,256,1152]{2,1,0:T(8,128)(2,1)S(1)}, u32[]{:S(2)}, u32[]{:S(2)}) collective-permute-start(bf16[2,256,1152]{2,1,0:T(8,128)(2,1)S(1)} %get-tuple-element.112), channel_id=1, source_target_pairs={{0,4},{4,0},{1,5},{5,1},{2,6},{6,2},{3,7},{7,3},{8,12},{12,8},{9,1... | collective-permute-start | bytes 3538952 | tf_op jit(solution)/shard_map/ppermute | solution.py:408
  267.3 24.5 %collective-permute-start.23 = (bf16[4,288,384]{2,1,0:T(8,128)(2,1)}, bf16[4,288,384]{2,1,0:T(8,128)(2,1)}, u32[]{:S(2)}, u32[]{:S(2)}) collective-permute-start(bf16[4,288,384]{2,1,0:T(8,128)(2,1)} %pad_maximum_fusion.5), channel_id=1, source_target_pairs={{0,8},{8,0},{16,24},{24,16},{1,9},{9,1},{17,25},{25,17},{2,10},{10... | collective-permute-start | bytes 2654216 | tf_op jit(solution)/shard_map/ppermute | solution.py:408
  269.6 22.8 %collective-permute-start.22 = (bf16[4,288,384]{2,1,0:T(8,128)(2,1)}, bf16[4,288,384]{2,1,0:T(8,128)(2,1)}, u32[]{:S(2)}, u32[]{:S(2)}) collective-permute-start(bf16[4,288,384]{2,1,0:T(8,128)(2,1)} %pad_maximum_fusion.4), channel_id=1, source_target_pairs={{0,16},{8,24},{16,0},{24,8},{1,17},{9,25},{17,1},{25,9},{2,18},{10... | collective-permute-start | bytes 2654216 | tf_op jit(solution)/shard_map/ppermute | solution.py:408
  283.6 36.4 %collective-permute-start.25 = (bf16[4,144,768]{2,1,0:T(8,128)(2,1)}, bf16[4,144,768]{2,1,0:T(8,128)(2,1)}, u32[]{:S(2)}, u32[]{:S(2)}) collective-permute-start(bf16[4,144,768]{2,1,0:T(8,128)(2,1)} %get-tuple-element.105), channel_id=1, source_target_pairs={{0,8},{8,0},{16,24},{24,16},{1,9},{9,1},{17,25},{25,17},{2,10},{10... | collective-permute-start | bytes 2654216 | tf_op jit(solution)/shard_map/ppermute | solution.py:408
  284.7 26.0 %collective-permute-start.26 = (bf16[4,144,768]{2,1,0:T(8,128)(2,1)}, bf16[4,144,768]{2,1,0:T(8,128)(2,1)}, u32[]{:S(2)}, u32[]{:S(2)}) collective-permute-start(bf16[4,144,768]{2,1,0:T(8,128)(2,1)} %get-tuple-element.106), channel_id=1, source_target_pairs={{0,16},{8,24},{16,0},{24,8},{1,17},{9,25},{17,1},{25,9},{2,18},{10... | collective-permute-start | bytes 2654216 | tf_op jit(solution)/shard_map/ppermute | solution.py:408
  300.6 24.3 %collective-permute-start.24 = (bf16[2,256,1152]{2,1,0:T(8,128)(2,1)}, bf16[2,256,1152]{2,1,0:T(8,128)(2,1)}, u32[]{:S(2)}, u32[]{:S(2)}) collective-permute-start(bf16[2,256,1152]{2,1,0:T(8,128)(2,1)} %multiply_convert_fusion.own_ref), channel_id=1, source_target_pairs={{0,4},{4,0},{1,5},{5,1},{2,6},{6,2},{3,7},{7,3},{8,12},{12,8},{9,1... | collective-permute-start | bytes 3538952 | tf_op jit(solution)/shard_map/ppermute | solution.py:408
  313.8 67.8 %collective-permute-start.39 = (bf16[4,288,768]{2,1,0:T(8,128)(2,1)}, bf16[4,288,768]{2,1,0:T(8,128)(2,1)}, u32[]{:S(2)}, u32[]{:S(2)}) collective-permute-start(bf16[4,288,768]{2,1,0:T(8,128)(2,1)} %pad_maximum_fusion.1), channel_id=1, source_target_pairs={{0,8},{8,0},{16,24},{24,16},{1,9},{9,1},{17,25},{25,17},{2,10},{10... | collective-permute-start | bytes 5308424 | tf_op jit(solution)/shard_map/ppermute | solution.py:408
  315.7 50.4 %all-to-all-start.4 = ((bf16[4,2,64,1152]{3,2,1,0:T(8,128)(2,1)}), bf16[4,2,64,1152]{3,2,1,0:T(8,128)(2,1)}, u32[]{:S(2)}, u32[]{:S(2)}) async-start(bf16[4,2,64,1152]{3,2,1,0:T(8,128)(2,1)} %bitcast.171), calls=%async_computation.4 | async-start | bytes 2359296 | tf_op jit(solution)/shard_map/all_to_all | solution.py:465
  320.0 165.3 %reduce-scatter.6.cloned.1.call-start = ((), (), s32[]{:S(2)}) async-start(), calls=%async_computation.11 | async-start | bytes 2211840 | tf_op jit(solution)/shard_map/reduce_scatter | solution.py:582
  323.3 58.4 %collective-permute-start.38 = (bf16[4,288,768]{2,1,0:T(8,128)(2,1)}, bf16[4,288,768]{2,1,0:T(8,128)(2,1)}, u32[]{:S(2)}, u32[]{:S(2)}) collective-permute-start(bf16[4,288,768]{2,1,0:T(8,128)(2,1)} %pad_maximum_fusion), channel_id=1, source_target_pairs={{0,16},{8,24},{16,0},{24,8},{1,17},{9,25},{17,1},{25,9},{2,18},{10... | collective-permute-start | bytes 5308424 | tf_op jit(solution)/shard_map/ppermute | solution.py:408
  361.3 24.5 %collective-permute-start.29 = (bf16[2,256,1152]{2,1,0:T(8,128)(2,1)}, bf16[2,256,1152]{2,1,0:T(8,128)(2,1)}, u32[]{:S(2)}, u32[]{:S(2)}) collective-permute-start(bf16[2,256,1152]{2,1,0:T(8,128)(2,1)} %get-tuple-element.123), channel_id=1, source_target_pairs={{0,4},{4,0},{1,5},{5,1},{2,6},{6,2},{3,7},{7,3},{8,12},{12,8},{9,1... | collective-permute-start | bytes 3538952 | tf_op jit(solution)/shard_map/ppermute | solution.py:408
  379.9 22.7 %collective-permute-start.27 = (bf16[4,144,576]{2,1,0:T(8,128)(2,1)}, bf16[4,144,576]{2,1,0:T(8,128)(2,1)}, u32[]{:S(2)}, u32[]{:S(2)}) collective-permute-start(bf16[4,144,576]{2,1,0:T(8,128)(2,1)} %get-tuple-element.120), channel_id=1, source_target_pairs={{0,8},{8,0},{16,24},{24,16},{1,9},{9,1},{17,25},{25,17},{2,10},{10... | collective-permute-start | bytes 1990664 | tf_op jit(solution)/shard_map/ppermute | solution.py:408
  380.9 21.8 %collective-permute-start.28 = (bf16[4,144,576]{2,1,0:T(8,128)(2,1)}, bf16[4,144,576]{2,1,0:T(8,128)(2,1)}, u32[]{:S(2)}, u32[]{:S(2)}) collective-permute-start(bf16[4,144,576]{2,1,0:T(8,128)(2,1)} %get-tuple-element.121), channel_id=1, source_target_pairs={{0,16},{8,24},{16,0},{24,8},{1,17},{9,25},{17,1},{25,9},{2,18},{10... | collective-permute-start | bytes 1990664 | tf_op jit(solution)/shard_map/ppermute | solution.py:408
  394.5 18.0 %all-to-all-start.6 = ((bf16[32,2,864]{2,1,0:T(2,128)(2,1)}), bf16[32,2,864]{2,1,0:T(2,128)(2,1)S(1)}, u32[]{:S(2)}, u32[]{:S(2)}) async-start(bf16[32,2,864]{2,1,0:T(2,128)(2,1)} %reshape.610), calls=%async_computation.6 | async-start | bytes 229376 | tf_op jit(solution)/shard_map/all_to_all | solution.py:789
  407.9 34.8 %collective-permute-start.31 = (bf16[4,288,576]{2,1,0:T(8,128)(2,1)}, bf16[4,288,576]{2,1,0:T(8,128)(2,1)}, u32[]{:S(2)}, u32[]{:S(2)}) collective-permute-start(bf16[4,288,576]{2,1,0:T(8,128)(2,1)} %pad_maximum_fusion.3), channel_id=1, source_target_pairs={{0,8},{8,0},{16,24},{24,16},{1,9},{9,1},{17,25},{25,17},{2,10},{10... | collective-permute-start | bytes 3981320 | tf_op jit(solution)/shard_map/ppermute | solution.py:408
  411.0 34.4 %collective-permute-start.30 = (bf16[4,288,576]{2,1,0:T(8,128)(2,1)}, bf16[4,288,576]{2,1,0:T(8,128)(2,1)}, u32[]{:S(2)}, u32[]{:S(2)}) collective-permute-start(bf16[4,288,576]{2,1,0:T(8,128)(2,1)} %pad_maximum_fusion.2), channel_id=1, source_target_pairs={{0,16},{8,24},{16,0},{24,8},{1,17},{9,25},{17,1},{25,9},{2,18},{10... | collective-permute-start | bytes 3981320 | tf_op jit(solution)/shard_map/ppermute | solution.py:408
  413.1 38.6 %all-to-all-start.5 = ((bf16[4,2,64,1152]{3,2,1,0:T(8,128)(2,1)}), bf16[4,2,64,1152]{3,2,1,0:T(8,128)(2,1)S(1)}, u32[]{:S(2)}, u32[]{:S(2)}) async-start(bf16[4,2,64,1152]{3,2,1,0:T(8,128)(2,1)} %bitcast.170), calls=%async_computation.5 | async-start | bytes 2359296 | tf_op jit(solution)/shard_map/all_to_all | solution.py:465
  417.7 71.5 %reduce-scatter.4.cloned.1.call-start = ((), (), s32[]{:S(2)}) async-start(), calls=%async_computation.10 | async-start | bytes 1843200 | tf_op jit(solution)/shard_map/reduce_scatter | solution.py:582
  425.9 25.8 %collective-permute-start.32 = (f32[37392]{0:T(1024)S(1)}, f32[37392]{0:T(1024)}, u32[]{:S(2)}, u32[]{:S(2)}) collective-permute-start(f32[37392]{0:T(1024)S(1)} %concatenate.121), channel_id=1, source_target_pairs={{0,4},{4,0},{1,5},{5,1},{2,6},{6,2},{3,7},{7,3},{8,12},{12,8},{9,1... | collective-permute-start | bytes 448712 | tf_op jit(solution)/shard_map/ppermute | solution.py:408
  452.6 5.7 %collective-permute-start.33 = (f32[37392]{0:T(1024)S(1)}, f32[37392]{0:T(1024)S(1)}, u32[]{:S(2)}, u32[]{:S(2)}) collective-permute-start(f32[37392]{0:T(1024)S(1)} %add.341), channel_id=1, source_target_pairs={{0,8},{8,0},{16,24},{24,16},{1,9},{9,1},{17,25},{25,17},{2,10},{10... | collective-permute-start | bytes 448712 | tf_op jit(solution)/shard_map/ppermute | solution.py:408
  463.7 8.5 %collective-permute-start.35 = (f32[18960]{0:T(1024)S(1)}, f32[18960]{0:T(1024)S(1)}, u32[]{:S(2)}, u32[]{:S(2)}) collective-permute-start(f32[18960]{0:T(1024)S(1)} %slice.232), channel_id=1, source_target_pairs={{0,1},{1,0},{2,3},{3,2},{4,5},{5,4},{6,7},{7,6},{8,9},{9,8},{10,11... | collective-permute-start | bytes 227528 | tf_op jit(solution)/shard_map/ppermute | solution.py:408
  472.2 11.0 %collective-permute-start.36 = (f32[18960]{0:T(1024)S(1)}, f32[18960]{0:T(1024)S(1)}, u32[]{:S(2)}, u32[]{:S(2)}) collective-permute-start(f32[18960]{0:T(1024)S(1)} %slice_add_fusion.8), channel_id=1, source_target_pairs={{0,2},{1,3},{2,0},{3,1},{4,6},{5,7},{6,4},{7,5},{8,10},{9,11},{10,... | collective-permute-start | bytes 227528 | tf_op jit(solution)/shard_map/ppermute | solution.py:408
  (73 other events, 559.2 us)
Sparse Core Ops, SparseCore 0:
  14.9 43.7 all-gather.6
  74.6 48.4 all-gather.8
  125.3 27.6 all-gather.10
  303.6 26.2 reduce-scatter.7
  385.9 45.6 reduce-scatter.5
  451.8 36.1 reduce-scatter.3

commit v4 on v3

--- a/solution.py
+++ b/solution.py
@@ -131,15 +131,13 @@
         outs.append(heads.astype(BF16))
     heads = jnp.concatenate(outs, axis=0)
     heads_ref[0] = heads
-    step = dot_last(heads, w_ref[0, :, 3 * hc :])
-
     @pl.when(at == 0)
     def _():
-        total[...] = step
+        total[...] = dot_last(heads, w_ref[0, :, 3 * hc :])
 
     @pl.when(at > 0)
     def _():
-        total[...] += step
+        total[...] += dot_last(heads, w_ref[0, :, 3 * hc :])
 
     @pl.when(at == pl.num_programs(0) - 1)
     def _():
@@ -209,15 +207,13 @@
     bias_ref[0] = jnp.sum(d_qkv, axis=0, keepdims=True)
     d_qkv = d_qkv.astype(BF16)
     dqkv_ref[0] = d_qkv
-    step = dot_last(d_qkv, w_ref[0, :, : 3 * hc])
-
     @pl.when(at == 0)
     def _():
-        total[...] = step
+        total[...] = dot_last(d_qkv, w_ref[0, :, : 3 * hc])
 
     @pl.when(at > 0)
     def _():
-        total[...] += step
+        total[...] += dot_last(d_qkv, w_ref[0, :, : 3 * hc])
 
     @pl.when(at == pl.num_programs(0) - 1)
     def _():
@@ -357,15 +353,13 @@
     bias_ref[0, :, ff:] = jnp.sum(d_up, axis=0, keepdims=True)
     d_gu_ref[0, :, :ff] = d_gate.astype(BF16)
     d_gu_ref[0, :, ff:] = d_up.astype(BF16)
-    step = dot_last(d_gu_ref[0], w_ref[0])
-
     @pl.when(at == 0)
     def _():
-        total[...] = step
+        total[...] = dot_last(d_gu_ref[0], w_ref[0])
 
     @pl.when(at > 0)
     def _():
-        total[...] += step
+        total[...] += dot_last(d_gu_ref[0], w_ref[0])
 
     @pl.when(at == pl.num_programs(0) - 1)
     def _():
@@ -688,17 +682,18 @@
     same, turn = head_tables(head_cols)
 
     x_rows = to_whole(after(tokens, cond_low))
-    attn_arrived, cosines, sines = lax.optimization_barrier(
-        (first_hop(held_attn), cosines, sines)
-    )
+    qkv_b = bias_all[:, : 6 * head_cols].reshape(line, 3, 2, head_cols)
+    qkv_b = lax.dynamic_index_in_dim(qkv_b, core, 2, keepdims=False).reshape(line, 1, 3 * head_cols)
+    gu_b = bias_all[:, 6 * head_cols :].reshape(line, 2, 2, ff_cols)
+    gu_b = lax.dynamic_index_in_dim(gu_b, core, 2, keepdims=False).reshape(line, 1, 2 * ff_cols)
+    ready = (cosines, sines, qkv_b, gu_b)
+    attn_arrived, ready = lax.optimization_barrier((first_hop(held_attn), ready))
+    cosines, sines, qkv_b, gu_b = ready
     _, attn_last = second_hop(attn_arrived)
     x_rows = after(x_rows, attn_last).astype(F32)
     held_gu = after(held_gu, attn_last)
     gu_arrived = first_hop(held_gu)
-    qkv_b = bias_all[:, : 6 * head_cols].reshape(line, 3, 2, head_cols)
-    qkv_b = lax.dynamic_index_in_dim(qkv_b, core, 2, keepdims=False).reshape(line, 1, 3 * head_cols)
-    gu_b = bias_all[:, 6 * head_cols :].reshape(line, 2, 2, ff_cols)
-    gu_b = lax.dynamic_index_in_dim(gu_b, core, 2, keepdims=False).reshape(line, 1, 2 * ff_cols)
+
     attn_own = modulate(x_rows, shift_a, scale_a).astype(BF16)
     attn_peer = swap(attn_own, CORES)
     w_attn = whole_weight(held_attn, attn_arrived, attn_last)
@@ -729,27 +724,24 @@
     w_gu = whole_weight(held_gu, gu_arrived, gu_last).reshape(line, D, 2 * ff_cols)
     down_passed, down_last = second_hop(after(down_arrived, w_gu))
     gate_up, hidden = ffn_forward(after(ffn_own, down_passed), ffn_peer, w_gu, gu_b)
-    down_parts, down_got = send_diagonal(
-        [(as_rows(d_ffn_own, d_ffn_peer), after(hidden, down_last))]
-    )
     w_down = whole_weight(held_down, down_arrived, down_last).reshape(line, D, ff_cols)
     d_gu, d_in_own, d_in_peer, gu_bias_part = ffn_backward(
-        after(d_ffn_own, down_parts), d_ffn_peer, w_down, w_gu, gate_up
+        d_ffn_own, d_ffn_peer, w_down, w_gu, gate_up
     )
     d_in_peer = swap(d_in_peer, CORES)
-    down_sent, down_blocks = send_blocks(down_parts, after(down_got, d_gu))
     gu_parts, gu_got = send_diagonal(
-        [(as_rows(ffn_own, ffn_peer), after(d_gu, down_sent))]
-    )
-    ffn = jnp.einsum("zrf,zdf->rd", after(hidden, gu_parts), w_down, preferred_element_type=F32)
+        [(as_rows(ffn_own, ffn_peer), d_gu)]
+    )
+    down_parts, down_got = send_diagonal(
+        [(as_rows(d_ffn_own, d_ffn_peer), after(hidden, gu_parts))]
+    )
+    ffn = jnp.einsum("zrf,zdf->rd", after(hidden, down_parts), w_down, preferred_element_type=F32)
     ffn = fold_peer(ffn.reshape(2 * own_images, patches, D)) + down_bias.astype(F32)
     output = to_parts((mid + gate_f * ffn).astype(BF16))
 
     down_bias_part = jnp.sum(d_ffn_f, axis=(0, 1))
     d_gate_f = jnp.sum(grad_out * ffn, axis=1, keepdims=True)
-    d_ffn_in = after(d_in_own.astype(F32) + d_in_peer.astype(F32), down_blocks)
-    g_down = add_blocks(down_parts if down_blocks is not None else down_sent, down_blocks)
-    g_down = scatter_line(g_down)
+    d_ffn_in = after(d_in_own.astype(F32) + d_in_peer.astype(F32), gu_got)
     mid_grad, d_shift_f, d_scale_f = jax.vjp(modulate, mid, shift_f, scale_f)[1](d_ffn_in)
     d_mid = grad_out + mid_grad
     d_attn_f = gate_a * d_mid
@@ -758,34 +750,40 @@
     d_attn_own = d_attn_f.astype(BF16)
     d_attn_peer = swap(d_attn_own, CORES)
     gu_sent, gu_blocks = send_blocks(gu_parts, gu_got)
+    down_sent, down_blocks = send_blocks(down_parts, after(down_got, gu_sent))
     d_qkv, d_in_own, d_in_peer, qkv_bias_part, gain_part = attn_backward(
-        after(d_attn_own, gu_sent), d_attn_peer, w_attn, qkv, *tables
+        after(d_attn_own, gu_sent, down_sent), d_attn_peer, w_attn, qkv, *tables
     )
     d_in_peer = swap(d_in_peer, CORES)
+    g_gu = add_blocks(gu_parts if gu_blocks is not None else gu_sent, after(gu_blocks, d_qkv))
     attn_parts, attn_got = send_diagonal(
         [
-            (as_rows(attn_own, attn_peer), after(d_qkv, output)),
+            (as_rows(attn_own, attn_peer), after(d_qkv, output, g_gu)),
             (as_rows(d_attn_own, d_attn_peer), heads_out),
         ]
     )
-    g_gu = add_blocks(gu_parts if gu_blocks is not None else gu_sent, after(gu_blocks, attn_parts))
-    g_gu = scatter_line(after(g_gu, g_down))
+    g_gu = scatter_line(g_gu)
+    qkv_bias_part, gain_part = after((qkv_bias_part, gain_part), attn_parts)
     gain_part = gain_part.reshape(2, repeat, HEAD_DIM).sum(axis=1)
     d_attn_in = d_in_own.astype(F32) + d_in_peer.astype(F32)
     row_grad, d_shift_a, d_scale_a = jax.vjp(modulate, x_rows, shift_a, scale_a)[1](d_attn_in)
     tokens_sent = (d_mid + row_grad).astype(BF16)
 
+    g_down = add_blocks(down_parts if down_blocks is not None else down_sent, after(down_blocks, tokens_sent))
+    attn_got = after(attn_got, g_down)
+    g_down = scatter_line(g_down)
+    attn_got = after(attn_got, g_gu, tokens_sent)
+    tokens_grad = to_parts(tokens_sent)
+    attn_sent, attn_blocks = send_blocks(attn_parts, attn_got)
     d_mod = jnp.concatenate(
         (d_shift_a, d_scale_a, d_gate_a, d_shift_f, d_scale_f, d_gate_f), axis=1
     )
+    d_mod, tokens_grad = lax.optimization_barrier((after(d_mod, attn_sent), tokens_grad))
     ada_bias_part = jnp.sum(d_mod, axis=0)
     d_mod_low = d_mod.astype(BF16).reshape(own_images, 6, data, chunk).transpose(2, 0, 1, 3)
     d_mod_low = jnp.broadcast_to(
         d_mod_low[:, None], (data, line, own_images, 6, chunk)
     ).reshape(devices, own_images * 6 * chunk)
-    attn_got, tokens_sent = lax.optimization_barrier((attn_got, tokens_sent))
-    tokens_grad = to_parts(tokens_sent)
-    attn_sent, attn_blocks = send_blocks(attn_parts, attn_got)
     d_mod_all = lax.all_to_all(d_mod_low, EVERY, 0, 0, tiled=True)
     d_mod_all = d_mod_all.reshape(data * images, 6 * chunk)
     g_ada = jnp.einsum("bc,be->ce", cond_low, d_mod_all, preferred_element_type=F32)
@@ -813,7 +811,7 @@
     flat = jnp.concatenate((flat, d_cond.reshape(-1)))
     flat = sum_by_swaps(sum_by_swaps(flat, CORES), CHIPS)
     g_attn = add_blocks(attn_parts, attn_blocks)
-    g_attn, tokens_grad = lax.optimization_barrier((after(g_attn, g_gu), tokens_grad))
+    g_attn = after(g_attn, g_gu, g_down)
     g_attn = scatter_line(g_attn)
     d_cond = flat[count:].reshape(d_cond.shape)
     flat = sum_by_swaps(flat[:count], LINE)

time: 511 us -> 506 us (level)
  waiting for transfers between devices: 137 us -> 150 us
  local copies, waits for them, and re-layouts: 68.7 us -> 57.3 us
    reduce_scatter x3, waiting for transfers between devices: 0.01 us -> 27.7 us  [scatter_line(): return lax.psum_scatter(part, LINE, scatter_dimension=0, tiled=False)]
    ppermute x42, waiting for transfers between devices: 93.1 us -> 75.8 us  [swap(): return lax.ppermute(values, name, [(i, i ^ bit) for i in range(count)])]
    unnamed x151 -> x138, local copies, waits for them, and re-layouts: 28.6 us -> 24.8 us
  transfers between devices with their start and end apart: 55 -> 55, of which waited for: 25 -> 25; matrix products, arithmetic and copies ran while one was open for 23% -> 20% of each run, Pallas kernels for 26% -> 20%
where the time goes in v4:
time: 506 us; the launch traced here: 500 us
  waiting for transfers between devices  150 us (30%)
  Pallas kernels  137 us (27%)
  other arithmetic  65.1 us (13%)
  starting transfers between devices  62.8 us (12%)
  local copies, waits for them, and re-layouts  57.3 us (11%)
  between operations  15.9 us (3%)
  matrix products  12.2 us (2%)
    ppermute x42, waiting for transfers between devices, swap(): return lax.ppermute(values, name, [(i, i ^ bit) for i in range(count)])  75.8 us
    pallas_call x1, Pallas kernels, attn_backward(): pl.pallas_call(attn_backward_kernel, grid=(line,), in_specs=[resident(own...  36.5 us
    pallas_call x3, Pallas kernels, chip_products(): pl.pallas_call(functools.partial(grad_kernel, tuple((len(group) for group...  34.9 us
    ppermute x42, starting transfers between devices, swap(): return lax.ppermute(values, name, [(i, i ^ bit) for i in range(count)])  30.1 us
    reduce_scatter x3, waiting for transfers between devices, scatter_line(): return lax.psum_scatter(part, LINE, scatter_dimension=0, tiled=False)  27.7 us
    all_gather x3, waiting for transfers between devices, gather_line(): return lax.all_gather(piece, LINE, axis=0)  26.6 us
    unnamed x138, local copies, waits for them, and re-layouts  24.8 us
    pallas_call x1, Pallas kernels, ffn_backward(): pl.pallas_call(ffn_backward_kernel, grid=(line,), in_specs=[resident(own....  22.1 us
  transfers between devices with their start and end apart: 55, of which 25 were waited for; matrix products, arithmetic and copies ran while one was open for 20% of the time, Pallas kernels for 20%

profile of v4, /device:TPU:0, one launch (start us, length us, event | category | flops | bytes accessed | tf_op | source)
XLA Modules:
  0.0 500.2 jit_solution(1003685806651141693)
XLA Ops:
  15.5 5.2 %all-to-all-start = ((s32[8,2,8]{2,1,0:T(2,128)}), s32[8,2,8]{2,1,0:T(2,128)S(1)}, u32[]{:S(2)}, u32[]{:S(2)}) async-start(s32[8,2,8]{2,1,0:T(2,128)} %broadcast_in_dim.89), calls=%async_computation | async-start | bytes 16384 | tf_op jit(solution)/shard_map/all_to_all | solution.py:651
  21.1 4.3 all-to-all-done
  25.6 2.3 multiply_convert_fusion.1
  29.3 4.0 all-to-all-start.2
  33.3 25.6 %all-gather.7.cloned.1.call-done = bf16[1152,576]{1,0:T(8,128)(2,1)} async-done(((bf16[288,576]{1,0:T(8,128)(2,1)}), bf16[1152,576]{1,0:T(8,128)(2,1)}) %all-gather.7.cloned.1.call-update) | async-done | bytes 1327120 | tf_op jit(solution)/shard_map/all_gather | solution.py:464
  61.8 4.3 all-to-all-start.1
  68.0 5.7 %fusion.15 = (f32[4,256,144]{2,1,0:T(8,128)}, f32[4,256,144]{2,1,0:T(8,128)}) fusion(f32[144]{0:T(256)S(1)} %multiply_power_fusion, s32[4,256]{1,0:T(4,128)S(1)} %get-tuple-element.265, s32[4,256]{1,0:T(4,128)S(1)} %get-tuple-element.264, pred[144]{0:T(512)(128)(4,1)S(1)} %broadcast_compare_fusion.1), kind=kLoop, calls=%fused_computation.56 | loop fusion | flops 442368 | bytes 1188560 | tf_op jit(solution)/shard_map/sin | solution.py:43
  76.8 16.2 %collective-permute-done.1.x_ref = bf16[4,288,576]{2,1,0:T(8,128)(2,1)S(1)} collective-permute-done((bf16[4,288,576]{2,1,0:T(8,128)(2,1)}, bf16[4,288,576]{2,1,0:T(8,128)(2,1)S(1)}, u32[]{:S(2)}, u32[]{:S(2)}) %collective-permute-start.1) | collective-permute-done | bytes 1327136 | tf_op jit(solution)/shard_map/ppermute | solution.py:402
  96.8 2.0 slice.165
  100.0 11.8 %all-to-all-done.1 = bf16[4,2,64,1152]{3,2,1,0:T(8,128)(2,1)} async-done(((bf16[4,2,64,1152]{3,2,1,0:T(8,128)(2,1)}), bf16[4,2,64,1152]{3,2,1,0:T(8,128)(2,1)}, u32[]{:S(2)}, u32[]{:S(2)}) %all-to-all-start.1) | async-done | bytes 1179680 | tf_op jit(solution)/shard_map/all_to_all | solution.py:451
  111.8 2.4 copy.94
  127.0 2.9 shard_map.316
  129.9 2.5 copy-done.2
  132.4 21.9 %shard_map.317 = (bf16[4,1024,432]{2,1,0:T(8,128)(2,1)}, bf16[4,1024,144]{2,1,0:T(8,128)(2,1)}, bf16[2,256,1152]{2,1,0:T(8,128)(2,1)S(1)}, bf16[2,256,1152]{2,1,0:T(8,128)(2,1)}) custom-call(bf16[2,256,1152]{2,1,0:T(8,128)(2,1)} %copy-done.7, bf16[2,256,1152]{2,1,0:T(8,128)(2,1)} %collective-permute-done.6.peer_ref, bf16[4,1152,576]{2,1,0:T(8,128)(2,1)} %bitcast.182, ...), custom_call_target="tpu_custom_call" | custom-call | flops 7583301632 | bytes 14745600 | tf_op jit(solution)/shard_map/pallas_call | solution.py:248
  154.4 4.5 all-to-all-start.3
  160.2 4.0 collective-permute-done.7.x_ref
  168.0 2.4 multiply_reduce_fusion.3
  172.2 14.1 %collective-permute-done.10.da_ref = bf16[2,288,768]{2,1,0:T(8,128)(2,1)S(1)} collective-permute-done((bf16[2,288,768]{2,1,0:T(8,128)(2,1)S(1)}, bf16[2,288,768]{2,1,0:T(8,128)(2,1)S(1)}, u32[]{:S(2)}, u32[]{:S(2)}) %collective-permute-start.10) | collective-permute-done | bytes 884768 | tf_op jit(solution)/shard_map/ppermute | solution.py:402
  195.3 2.9 shard_map.318
  198.2 2.8 copy-done.1
  202.3 6.3 %collective-permute-done.12.x_ref = bf16[4,288,384]{2,1,0:T(8,128)(2,1)} collective-permute-done((bf16[4,288,384]{2,1,0:T(8,128)(2,1)S(1)}, bf16[4,288,384]{2,1,0:T(8,128)(2,1)}, u32[]{:S(2)}, u32[]{:S(2)}) %collective-permute-start.12) | collective-permute-done | bytes 884768 | tf_op jit(solution)/shard_map/ppermute | solution.py:402
  214.0 13.0 %shard_map.319 = (bf16[4,1024,768]{2,1,0:T(8,128)(2,1)}, bf16[4,1024,384]{2,1,0:T(8,128)(2,1)}) custom-call(bf16[2,256,1152]{2,1,0:T(8,128)(2,1)} %add_convert_fusion.3.own_ref, bf16[2,256,1152]{2,1,0:T(8,128)(2,1)} %collective-permute-done.14.peer_ref, bf16[4,1152,768]{2,1,0:T(8,128)(2,1)} %bitcast.180, f32[4,1,768]{2,1,0:T(1,128)S(1)} %bitcast.197), custom_call_target="tpu_custom_call" | custom-call | flops 7247757312 | bytes 19660800 | tf_op jit(solution)/shard_map/pallas_call | solution.py:312
  227.0 2.6 shard_map.320
  232.4 22.1 %shard_map.321 = (bf16[4,1024,768]{2,1,0:T(8,128)(2,1)}, bf16[2,256,1152]{2,1,0:T(8,128)(2,1)S(1)}, bf16[2,256,1152]{2,1,0:T(8,128)(2,1)S(1)}, f32[4,1,768]{2,1,0:T(1,128)S(1)}) custom-call(bf16[2,256,1152]{2,1,0:T(8,128)(2,1)S(1)} %fusion.11.own_ref, bf16[2,256,1152]{2,1,0:T(8,128)(2,1)} %copy-done.59, bf16[4,1152,384]{2,1,0:T(8,128)(2,1)} %bitcast.184, ...), custom_call_target="tpu_custom_call" | custom-call | flops 10871635968 | bytes 26738688 | tf_op jit(solution)/shard_map/pallas_call | solution.py:373
  254.4 12.5 %shard_map.322 = (bf16[4,144,768]{2,1,0:T(8,128)(2,1)S(1)}, bf16[4,144,768]{2,1,0:T(8,128)(2,1)S(1)}, bf16[4,288,768]{2,1,0:T(8,128)(2,1)}, bf16[4,288,768]{2,1,0:T(8,128)(2,1)}, bf16[4,288,768]{2,1,0:T(8,128)(2,1)}) custom-call(s32[4]{0:T(128)S(1)} %broadcast_xor_fusion.spot_ref, bf16[512,1152]{1,0:T(8,128)(2,1)} %bitcast.36.refs_0_, ...), custom_call_target="tpu_custom_call" | custom-call | flops 7247757312 | bytes 13369344 | tf_op jit(solution)/shard_map/pallas_call | solution.py:533
  268.1 8.6 %shard_map.323 = (bf16[4,144,384]{2,1,0:T(8,128)(2,1)S(1)}, bf16[4,144,384]{2,1,0:T(8,128)(2,1)S(1)}, bf16[4,288,384]{2,1,0:T(8,128)(2,1)S(1)}, bf16[4,288,384]{2,1,0:T(8,128)(2,1)S(1)}, bf16[4,288,384]{2,1,0:T(8,128)(2,1)S(1)}) custom-call(s32[4]{0:T(128)S(1)} %broadcast_xor_fusion.spot_ref, bf16[512,1152]{1,0:T(8,128)(2,1)} %fusion.13.refs_0_, ...), custom_call_target="tpu_custom_call" | custom-call | flops 3623878656 | bytes 6684672 | tf_op jit(solution)/shard_map/pallas_call | solution.py:533
  279.6 6.1 %convolution_bitcast_fusion = f32[1024,1152]{1,0:T(8,128)S(1)} fusion(bf16[4,1024,384]{2,1,0:T(8,128)(2,1)} %get-tuple-element.115.refs_2_, bf16[4,1152,384]{2,1,0:T(8,128)(2,1)S(1)} %bitcast.185), kind=kOutput, calls=%fused_computation.5 | convolution fusion | flops 3623878656 | bytes 11403264 | tf_op jit(solution)/shard_map/zrf,zdf->rd/dot_general | solution.py:738
  285.9 3.7 collective-permute-done.21
  295.5 3.1 multiply_reduce_fusion.4
  307.1 4.8 all-to-all-start.4
  313.1 36.5 %shard_map.324 = (bf16[4,1024,432]{2,1,0:T(8,128)(2,1)}, bf16[2,256,1152]{2,1,0:T(8,128)(2,1)S(1)}, bf16[2,256,1152]{2,1,0:T(8,128)(2,1)}, f32[4,1,432]{2,1,0:T(1,128)S(1)}, f32[2,144]{1,0:T(2,128)S(1)}) custom-call(bf16[2,256,1152]{2,1,0:T(8,128)(2,1)} %multiply_convert_fusion.own_ref, bf16[2,256,1152]{2,1,0:T(8,128)(2,1)} %collective-permute-done.24.peer_ref, ...), custom_call_target="tpu_custom_call" | custom-call | flops 10804527104 | bytes 14745600 | tf_op jit(solution)/shard_map/pallas_call | solution.py:272
  349.6 4.1 add_convert_fusion
  358.1 13.9 %shard_map.325 = (bf16[4,144,576]{2,1,0:T(8,128)(2,1)}, bf16[4,144,576]{2,1,0:T(8,128)(2,1)}, bf16[4,288,576]{2,1,0:T(8,128)(2,1)}, bf16[4,288,576]{2,1,0:T(8,128)(2,1)}, bf16[4,288,576]{2,1,0:T(8,128)(2,1)}) custom-call(s32[4]{0:T(128)S(1)} %broadcast_xor_fusion.spot_ref, bf16[512,1152]{1,0:T(8,128)(2,1)S(1)} %bitcast.192, ...), custom_call_target="tpu_custom_call" | custom-call | flops 5435817984 | bytes 10027008 | tf_op jit(solution)/shard_map/pallas_call | solution.py:533
  374.0 2.9 fusion.10
  377.0 2.5 fusion.8
  380.7 5.1 %all-to-all-start.5 = ((bf16[4,2,64,1152]{3,2,1,0:T(8,128)(2,1)}), bf16[4,2,64,1152]{3,2,1,0:T(8,128)(2,1)S(1)}, u32[]{:S(2)}, u32[]{:S(2)}) async-start(bf16[4,2,64,1152]{3,2,1,0:T(8,128)(2,1)} %bitcast.200), calls=%async_computation.6 | async-start | bytes 2359296 | tf_op jit(solution)/shard_map/all_to_all | solution.py:459
  385.8 2.7 add_convert_fusion.4
  388.5 5.2 %collective-permute-done.28 = bf16[4,144,576]{2,1,0:T(8,128)(2,1)} collective-permute-done((bf16[4,144,576]{2,1,0:T(8,128)(2,1)}, bf16[4,144,576]{2,1,0:T(8,128)(2,1)}, u32[]{:S(2)}, u32[]{:S(2)}) %collective-permute-start.28) | collective-permute-done | bytes 663584 | tf_op jit(solution)/shard_map/ppermute | solution.py:402
  397.9 2.6 collective-permute-start.38
  404.5 27.1 %reduce-scatter.8.cloned.1.call-done = bf16[1,288,384]{2,1,0:T(8,128)(2,1)} async-done(((bf16[4,288,384]{2,1,0:T(8,128)(2,1)}), bf16[1,288,384]{2,1,0:T(8,128)(2,1)}) %reduce-scatter.8.cloned.1.call-update) | async-done | bytes 221200 | tf_op jit(solution)/shard_map/reduce_scatter | solution.py:576
  436.0 4.3 all-to-all-start.6
  440.6 3.9 add_convert_fusion.1
  444.6 3.8 all-to-all-done.6
  457.1 3.7 collective-permute-done.33
  461.8 4.2 collective-permute-done.34
  468.4 6.3 %collective-permute-done.35 = f32[18960]{0:T(1024)S(1)} collective-permute-done((f32[18960]{0:T(1024)S(1)}, f32[18960]{0:T(1024)S(1)}, u32[]{:S(2)}, u32[]{:S(2)}) %collective-permute-start.35) | collective-permute-done | bytes 75872 | tf_op jit(solution)/shard_map/ppermute | solution.py:402
  476.5 5.4 %collective-permute-done.36 = f32[18960]{0:T(1024)S(1)} collective-permute-done((f32[18960]{0:T(1024)S(1)}, f32[18960]{0:T(1024)S(1)}, u32[]{:S(2)}, u32[]{:S(2)}) %collective-permute-start.36) | collective-permute-done | bytes 75872 | tf_op jit(solution)/shard_map/ppermute | solution.py:402
  490.8 2.4 copy.136
  (398 shorter events, 123.2 us)
Async XLA Ops:
  7.2 51.6 %all-gather.7.cloned.1.call-start = ((), (), s32[]{:S(2)}) async-start(), calls=%async_computation.13 | async-start | bytes 1843200 | tf_op jit(solution)/shard_map/all_gather | solution.py:464
  15.5 9.9 %all-to-all-start = ((s32[8,2,8]{2,1,0:T(2,128)}), s32[8,2,8]{2,1,0:T(2,128)S(1)}, u32[]{:S(2)}, u32[]{:S(2)}) async-start(s32[8,2,8]{2,1,0:T(2,128)} %broadcast_in_dim.89), calls=%async_computation | async-start | bytes 16384 | tf_op jit(solution)/shard_map/all_to_all | solution.py:651
  29.3 32.5 %all-to-all-start.2 = ((f32[32,1,2028]{2,1,0:T(1,128)}), f32[32,1,2028]{2,1,0:T(1,128)S(1)}, u32[]{:S(2)}, u32[]{:S(2)}) async-start(f32[32,1,2028]{2,1,0:T(1,128)} %all_to_all.31), calls=%async_computation.2 | async-start | bytes 524288 | tf_op jit(solution)/shard_map/all_to_all | solution.py:670
  58.8 34.2 %collective-permute-start.1 = (bf16[4,288,576]{2,1,0:T(8,128)(2,1)}, bf16[4,288,576]{2,1,0:T(8,128)(2,1)S(1)}, u32[]{:S(2)}, u32[]{:S(2)}) collective-permute-start(bf16[4,288,576]{2,1,0:T(8,128)(2,1)} %bitcast.189), channel_id=1, source_target_pairs={{0,8},{8,0},{16,24},{24,16},{1,9},{9,1},{17,25},{25,17},{2,10},{10... | collective-permute-start | bytes 3981320 | tf_op jit(solution)/shard_map/ppermute | solution.py:402
  60.3 34.1 %collective-permute-start.2 = (bf16[4,288,576]{2,1,0:T(8,128)(2,1)}, bf16[4,288,576]{2,1,0:T(8,128)(2,1)}, u32[]{:S(2)}, u32[]{:S(2)}) collective-permute-start(bf16[4,288,576]{2,1,0:T(8,128)(2,1)} %bitcast.190), channel_id=1, source_target_pairs={{0,16},{8,24},{16,0},{24,8},{1,17},{9,25},{17,1},{25,9},{2,18},{10... | collective-permute-start | bytes 3981320 | tf_op jit(solution)/shard_map/ppermute | solution.py:402
  61.8 50.0 %all-to-all-start.1 = ((bf16[4,2,64,1152]{3,2,1,0:T(8,128)(2,1)}), bf16[4,2,64,1152]{3,2,1,0:T(8,128)(2,1)}, u32[]{:S(2)}, u32[]{:S(2)}) async-start(bf16[4,2,64,1152]{3,2,1,0:T(8,128)(2,1)} %bitcast.205), calls=%async_computation.1 | async-start | bytes 2359296 | tf_op jit(solution)/shard_map/all_to_all | solution.py:451
  66.1 57.2 %all-gather.9.cloned.1.call-start = ((), (), s32[]{:S(2)}) async-start(), calls=%async_computation.14 | async-start | bytes 2211840 | tf_op jit(solution)/shard_map/all_gather | solution.py:464
  74.7 84.3 %all-gather.11.cloned.1.call-start = ((), (), s32[]{:S(2)}) async-start(), calls=%async_computation.15 | async-start | bytes 1474560 | tf_op jit(solution)/shard_map/all_gather | solution.py:464
  95.3 18.9 %collective-permute-start.4 = (bf16[2,288,576]{2,1,0:T(8,128)(2,1)}, bf16[2,288,576]{2,1,0:T(8,128)(2,1)S(1)}, u32[]{:S(2)}, u32[]{:S(2)}) collective-permute-start(bf16[2,288,576]{2,1,0:T(8,128)(2,1)} %slice.164), channel_id=1, source_target_pairs={{0,16},{8,24},{16,0},{24,8},{1,17},{9,25},{17,1},{25,9},{2,18},{10... | collective-permute-start | bytes 1990664 | tf_op jit(solution)/shard_map/ppermute | solution.py:402
  98.8 17.1 %collective-permute-start.5 = (bf16[2,288,576]{2,1,0:T(8,128)(2,1)}, bf16[2,288,576]{2,1,0:T(8,128)(2,1)}, u32[]{:S(2)}, u32[]{:S(2)}) collective-permute-start(bf16[2,288,576]{2,1,0:T(8,128)(2,1)} %slice.165), channel_id=1, source_target_pairs={{0,8},{8,0},{16,24},{24,16},{1,9},{9,1},{17,25},{25,17},{2,10},{10... | collective-permute-start | bytes 1990664 | tf_op jit(solution)/shard_map/ppermute | solution.py:402
  119.2 13.2 %collective-permute-start.6 = (bf16[2,256,1152]{2,1,0:T(8,128)(2,1)S(1)}, bf16[2,256,1152]{2,1,0:T(8,128)(2,1)}, u32[]{:S(2)}, u32[]{:S(2)}) collective-permute-start(bf16[2,256,1152]{2,1,0:T(8,128)(2,1)S(1)} %fusion.3.own_ref), channel_id=1, source_target_pairs={{0,4},{4,0},{1,5},{5,1},{2,6},{6,2},{3,7},{7,3},{8,12},{12,8},{9,1... | collective-permute-start | bytes 3538952 | tf_op jit(solution)/shard_map/ppermute | solution.py:402
  123.3 40.9 %collective-permute-start.7 = (bf16[4,288,768]{2,1,0:T(8,128)(2,1)}, bf16[4,288,768]{2,1,0:T(8,128)(2,1)}, u32[]{:S(2)}, u32[]{:S(2)}) collective-permute-start(bf16[4,288,768]{2,1,0:T(8,128)(2,1)} %bitcast.186), channel_id=1, source_target_pairs={{0,8},{8,0},{16,24},{24,16},{1,9},{9,1},{17,25},{25,17},{2,10},{10... | collective-permute-start | bytes 5308424 | tf_op jit(solution)/shard_map/ppermute | solution.py:402
  123.9 42.2 %collective-permute-start.8 = (bf16[4,288,768]{2,1,0:T(8,128)(2,1)}, bf16[4,288,768]{2,1,0:T(8,128)(2,1)}, u32[]{:S(2)}, u32[]{:S(2)}) collective-permute-start(bf16[4,288,768]{2,1,0:T(8,128)(2,1)} %bitcast.187), channel_id=1, source_target_pairs={{0,16},{8,24},{16,0},{24,8},{1,17},{9,25},{17,1},{25,9},{2,18},{10... | collective-permute-start | bytes 5308424 | tf_op jit(solution)/shard_map/ppermute | solution.py:402
  154.3 13.7 %collective-permute-start.9 = (bf16[2,256,1152]{2,1,0:T(8,128)(2,1)}, bf16[2,256,1152]{2,1,0:T(8,128)(2,1)}, u32[]{:S(2)}, u32[]{:S(2)}) collective-permute-start(bf16[2,256,1152]{2,1,0:T(8,128)(2,1)} %get-tuple-element.93), channel_id=1, source_target_pairs={{0,4},{4,0},{1,5},{5,1},{2,6},{6,2},{3,7},{7,3},{8,12},{12,8},{9,1... | collective-permute-start | bytes 3538952 | tf_op jit(solution)/shard_map/ppermute | solution.py:402
  154.4 36.4 %all-to-all-start.3 = ((bf16[4,2,64,1152]{3,2,1,0:T(8,128)(2,1)}), bf16[4,2,64,1152]{3,2,1,0:T(8,128)(2,1)}, u32[]{:S(2)}, u32[]{:S(2)}) async-start(bf16[4,2,64,1152]{3,2,1,0:T(8,128)(2,1)} %bitcast.31), calls=%async_computation.3 | async-start | bytes 2359296 | tf_op jit(solution)/shard_map/all_to_all | solution.py:451
  165.4 20.8 %collective-permute-start.10 = (bf16[2,288,768]{2,1,0:T(8,128)(2,1)S(1)}, bf16[2,288,768]{2,1,0:T(8,128)(2,1)S(1)}, u32[]{:S(2)}, u32[]{:S(2)}) collective-permute-start(bf16[2,288,768]{2,1,0:T(8,128)(2,1)S(1)} %slice.223), channel_id=1, source_target_pairs={{0,16},{8,24},{16,0},{24,8},{1,17},{9,25},{17,1},{25,9},{2,18},{10... | collective-permute-start | bytes 2654216 | tf_op jit(solution)/shard_map/ppermute | solution.py:402
  167.3 20.6 %collective-permute-start.11 = (bf16[2,288,768]{2,1,0:T(8,128)(2,1)S(1)}, bf16[2,288,768]{2,1,0:T(8,128)(2,1)S(1)}, u32[]{:S(2)}, u32[]{:S(2)}) collective-permute-start(bf16[2,288,768]{2,1,0:T(8,128)(2,1)S(1)} %slice.224), channel_id=1, source_target_pairs={{0,8},{8,0},{16,24},{24,16},{1,9},{9,1},{17,25},{25,17},{2,10},{10... | collective-permute-start | bytes 2654216 | tf_op jit(solution)/shard_map/ppermute | solution.py:402
  172.2 41.8 %collective-permute-start.14 = (bf16[2,256,1152]{2,1,0:T(8,128)(2,1)}, bf16[2,256,1152]{2,1,0:T(8,128)(2,1)}, u32[]{:S(2)}, u32[]{:S(2)}) collective-permute-start(bf16[2,256,1152]{2,1,0:T(8,128)(2,1)} %add_convert_fusion.3.own_ref), channel_id=1, source_target_pairs={{0,4},{4,0},{1,5},{5,1},{2,6},{6,2},{3,7},{7,3},{8,12},{12,8},{9,1... | collective-permute-start | bytes 3538952 | tf_op jit(solution)/shard_map/ppermute | solution.py:402
  188.8 19.8 %collective-permute-start.12 = (bf16[4,288,384]{2,1,0:T(8,128)(2,1)S(1)}, bf16[4,288,384]{2,1,0:T(8,128)(2,1)}, u32[]{:S(2)}, u32[]{:S(2)}) collective-permute-start(bf16[4,288,384]{2,1,0:T(8,128)(2,1)S(1)} %slice.228.own_ref), channel_id=1, source_target_pairs={{0,8},{8,0},{16,24},{24,16},{1,9},{9,1},{17,25},{25,17},{2,10},{10... | collective-permute-start | bytes 2654216 | tf_op jit(solution)/shard_map/ppermute | solution.py:402
  189.4 19.5 %collective-permute-start.13 = (bf16[4,288,384]{2,1,0:T(8,128)(2,1)S(1)}, bf16[4,288,384]{2,1,0:T(8,128)(2,1)}, u32[]{:S(2)}, u32[]{:S(2)}) collective-permute-start(bf16[4,288,384]{2,1,0:T(8,128)(2,1)S(1)} %slice.228.own_ref), channel_id=1, source_target_pairs={{0,16},{8,24},{16,0},{24,8},{1,17},{9,25},{17,1},{25,9},{2,18},{10... | collective-permute-start | bytes 2654216 | tf_op jit(solution)/shard_map/ppermute | solution.py:402
  192.7 38.7 %collective-permute-start.15 = (bf16[2,256,1152]{2,1,0:T(8,128)(2,1)S(1)}, bf16[2,256,1152]{2,1,0:T(8,128)(2,1)S(1)}, u32[]{:S(2)}, u32[]{:S(2)}) collective-permute-start(bf16[2,256,1152]{2,1,0:T(8,128)(2,1)S(1)} %fusion.11.own_ref), channel_id=1, source_target_pairs={{0,4},{4,0},{1,5},{5,1},{2,6},{6,2},{3,7},{7,3},{8,12},{12,8},{9,1... | collective-permute-start | bytes 3538952 | tf_op jit(solution)/shard_map/ppermute | solution.py:402
  211.1 15.9 %collective-permute-start.16 = (bf16[2,288,384]{2,1,0:T(8,128)(2,1)S(1)}, bf16[2,288,384]{2,1,0:T(8,128)(2,1)S(1)}, u32[]{:S(2)}, u32[]{:S(2)}) collective-permute-start(bf16[2,288,384]{2,1,0:T(8,128)(2,1)S(1)} %slice.178), channel_id=1, source_target_pairs={{0,16},{8,24},{16,0},{24,8},{1,17},{9,25},{17,1},{25,9},{2,18},{10... | collective-permute-start | bytes 1327112 | tf_op jit(solution)/shard_map/ppermute | solution.py:402
  212.5 14.5 %collective-permute-start.17 = (bf16[2,288,384]{2,1,0:T(8,128)(2,1)S(1)}, bf16[2,288,384]{2,1,0:T(8,128)(2,1)S(1)}, u32[]{:S(2)}, u32[]{:S(2)}) collective-permute-start(bf16[2,288,384]{2,1,0:T(8,128)(2,1)S(1)} %slice.179), channel_id=1, source_target_pairs={{0,8},{8,0},{16,24},{24,16},{1,9},{9,1},{17,25},{25,17},{2,10},{10... | collective-permute-start | bytes 1327112 | tf_op jit(solution)/shard_map/ppermute | solution.py:402
  266.9 22.7 %collective-permute-start.21 = (bf16[4,144,768]{2,1,0:T(8,128)(2,1)S(1)}, bf16[4,144,768]{2,1,0:T(8,128)(2,1)}, u32[]{:S(2)}, u32[]{:S(2)}) collective-permute-start(bf16[4,144,768]{2,1,0:T(8,128)(2,1)S(1)} %get-tuple-element.105), channel_id=1, source_target_pairs={{0,16},{8,24},{16,0},{24,8},{1,17},{9,25},{17,1},{25,9},{2,18},{10... | collective-permute-start | bytes 2654216 | tf_op jit(solution)/shard_map/ppermute | solution.py:402
  267.5 25.6 %collective-permute-start.20 = (bf16[4,144,768]{2,1,0:T(8,128)(2,1)S(1)}, bf16[4,144,768]{2,1,0:T(8,128)(2,1)S(1)}, u32[]{:S(2)}, u32[]{:S(2)}) collective-permute-start(bf16[4,144,768]{2,1,0:T(8,128)(2,1)S(1)} %get-tuple-element.104), channel_id=1, source_target_pairs={{0,8},{8,0},{16,24},{24,16},{1,9},{9,1},{17,25},{25,17},{2,10},{10... | collective-permute-start | bytes 2654216 | tf_op jit(solution)/shard_map/ppermute | solution.py:402
  276.7 27.0 %collective-permute-start.22 = (bf16[4,144,384]{2,1,0:T(8,128)(2,1)S(1)}, bf16[4,144,384]{2,1,0:T(8,128)(2,1)S(1)}, u32[]{:S(2)}, u32[]{:S(2)}) collective-permute-start(bf16[4,144,384]{2,1,0:T(8,128)(2,1)S(1)} %get-tuple-element.110), channel_id=1, source_target_pairs={{0,8},{8,0},{16,24},{24,16},{1,9},{9,1},{17,25},{25,17},{2,10},{10... | collective-permute-start | bytes 1327112 | tf_op jit(solution)/shard_map/ppermute | solution.py:402
  278.2 25.6 %collective-permute-start.23 = (bf16[4,144,384]{2,1,0:T(8,128)(2,1)S(1)}, bf16[4,144,384]{2,1,0:T(8,128)(2,1)S(1)}, u32[]{:S(2)}, u32[]{:S(2)}) collective-permute-start(bf16[4,144,384]{2,1,0:T(8,128)(2,1)S(1)} %get-tuple-element.111), channel_id=1, source_target_pairs={{0,16},{8,24},{16,0},{24,8},{1,17},{9,25},{17,1},{25,9},{2,18},{10... | collective-permute-start | bytes 1327112 | tf_op jit(solution)/shard_map/ppermute | solution.py:402
  279.6 12.6 %collective-permute-start.19 = (bf16[2,256,1152]{2,1,0:T(8,128)(2,1)S(1)}, bf16[2,256,1152]{2,1,0:T(8,128)(2,1)S(1)}, u32[]{:S(2)}, u32[]{:S(2)}) collective-permute-start(bf16[2,256,1152]{2,1,0:T(8,128)(2,1)S(1)} %get-tuple-element.117), channel_id=1, source_target_pairs={{0,4},{4,0},{1,5},{5,1},{2,6},{6,2},{3,7},{7,3},{8,12},{12,8},{9,1... | collective-permute-start | bytes 3538952 | tf_op jit(solution)/shard_map/ppermute | solution.py:402
  292.3 57.3 %collective-permute-start.27 = (bf16[4,288,768]{2,1,0:T(8,128)(2,1)}, bf16[4,288,768]{2,1,0:T(8,128)(2,1)}, u32[]{:S(2)}, u32[]{:S(2)}) collective-permute-start(bf16[4,288,768]{2,1,0:T(8,128)(2,1)} %pad_maximum_fusion.1), channel_id=1, source_target_pairs={{0,8},{8,0},{16,24},{24,16},{1,9},{9,1},{17,25},{25,17},{2,10},{10... | collective-permute-start | bytes 5308424 | tf_op jit(solution)/shard_map/ppermute | solution.py:402
  299.9 12.0 %collective-permute-start.24 = (bf16[2,256,1152]{2,1,0:T(8,128)(2,1)}, bf16[2,256,1152]{2,1,0:T(8,128)(2,1)}, u32[]{:S(2)}, u32[]{:S(2)}) collective-permute-start(bf16[2,256,1152]{2,1,0:T(8,128)(2,1)} %multiply_convert_fusion.own_ref), channel_id=1, source_target_pairs={{0,4},{4,0},{1,5},{5,1},{2,6},{6,2},{3,7},{7,3},{8,12},{12,8},{9,1... | collective-permute-start | bytes 3538952 | tf_op jit(solution)/shard_map/ppermute | solution.py:402
  303.1 46.5 %collective-permute-start.26 = (bf16[4,288,768]{2,1,0:T(8,128)(2,1)}, bf16[4,288,768]{2,1,0:T(8,128)(2,1)}, u32[]{:S(2)}, u32[]{:S(2)}) collective-permute-start(bf16[4,288,768]{2,1,0:T(8,128)(2,1)} %pad_maximum_fusion), channel_id=1, source_target_pairs={{0,16},{8,24},{16,0},{24,8},{1,17},{9,25},{17,1},{25,9},{2,18},{10... | collective-permute-start | bytes 5308424 | tf_op jit(solution)/shard_map/ppermute | solution.py:402
  307.1 51.0 %all-to-all-start.4 = ((bf16[4,2,64,1152]{3,2,1,0:T(8,128)(2,1)}), bf16[4,2,64,1152]{3,2,1,0:T(8,128)(2,1)}, u32[]{:S(2)}, u32[]{:S(2)}) async-start(bf16[4,2,64,1152]{3,2,1,0:T(8,128)(2,1)} %bitcast.175), calls=%async_computation.4 | async-start | bytes 2359296 | tf_op jit(solution)/shard_map/all_to_all | solution.py:459
  311.9 83.1 %reduce-scatter.4.cloned.1.call-start = ((), (), s32[]{:S(2)}) async-start(), calls=%async_computation.10 | async-start | bytes 2211840 | tf_op jit(solution)/shard_map/reduce_scatter | solution.py:576
  353.7 20.2 %collective-permute-start.25 = (bf16[2,256,1152]{2,1,0:T(8,128)(2,1)}, bf16[2,256,1152]{2,1,0:T(8,128)(2,1)}, u32[]{:S(2)}, u32[]{:S(2)}) collective-permute-start(bf16[2,256,1152]{2,1,0:T(8,128)(2,1)} %get-tuple-element.124), channel_id=1, source_target_pairs={{0,4},{4,0},{1,5},{5,1},{2,6},{6,2},{3,7},{7,3},{8,12},{12,8},{9,1... | collective-permute-start | bytes 3538952 | tf_op jit(solution)/shard_map/ppermute | solution.py:402
  355.6 24.0 %collective-permute-start.31 = (bf16[4,288,384]{2,1,0:T(8,128)(2,1)}, bf16[4,288,384]{2,1,0:T(8,128)(2,1)}, u32[]{:S(2)}, u32[]{:S(2)}) collective-permute-start(bf16[4,288,384]{2,1,0:T(8,128)(2,1)} %pad_maximum_fusion.5), channel_id=1, source_target_pairs={{0,8},{8,0},{16,24},{24,16},{1,9},{9,1},{17,25},{25,17},{2,10},{10... | collective-permute-start | bytes 2654216 | tf_op jit(solution)/shard_map/ppermute | solution.py:402
  356.6 23.0 %collective-permute-start.30 = (bf16[4,288,384]{2,1,0:T(8,128)(2,1)}, bf16[4,288,384]{2,1,0:T(8,128)(2,1)}, u32[]{:S(2)}, u32[]{:S(2)}) collective-permute-start(bf16[4,288,384]{2,1,0:T(8,128)(2,1)} %pad_maximum_fusion.4), channel_id=1, source_target_pairs={{0,16},{8,24},{16,0},{24,8},{1,17},{9,25},{17,1},{25,9},{2,18},{10... | collective-permute-start | bytes 2654216 | tf_op jit(solution)/shard_map/ppermute | solution.py:402
  371.9 21.8 %collective-permute-start.28 = (bf16[4,144,576]{2,1,0:T(8,128)(2,1)}, bf16[4,144,576]{2,1,0:T(8,128)(2,1)}, u32[]{:S(2)}, u32[]{:S(2)}) collective-permute-start(bf16[4,144,576]{2,1,0:T(8,128)(2,1)} %get-tuple-element.130), channel_id=1, source_target_pairs={{0,8},{8,0},{16,24},{24,16},{1,9},{9,1},{17,25},{25,17},{2,10},{10... | collective-permute-start | bytes 1990664 | tf_op jit(solution)/shard_map/ppermute | solution.py:402
  372.5 21.9 %collective-permute-start.29 = (bf16[4,144,576]{2,1,0:T(8,128)(2,1)}, bf16[4,144,576]{2,1,0:T(8,128)(2,1)}, u32[]{:S(2)}, u32[]{:S(2)}) collective-permute-start(bf16[4,144,576]{2,1,0:T(8,128)(2,1)} %get-tuple-element.131), channel_id=1, source_target_pairs={{0,16},{8,24},{16,0},{24,8},{1,17},{9,25},{17,1},{25,9},{2,18},{10... | collective-permute-start | bytes 1990664 | tf_op jit(solution)/shard_map/ppermute | solution.py:402
  380.7 52.0 %all-to-all-start.5 = ((bf16[4,2,64,1152]{3,2,1,0:T(8,128)(2,1)}), bf16[4,2,64,1152]{3,2,1,0:T(8,128)(2,1)S(1)}, u32[]{:S(2)}, u32[]{:S(2)}) async-start(bf16[4,2,64,1152]{3,2,1,0:T(8,128)(2,1)} %bitcast.200), calls=%async_computation.6 | async-start | bytes 2359296 | tf_op jit(solution)/shard_map/all_to_all | solution.py:459
  385.8 45.9 %reduce-scatter.8.cloned.1.call-start = ((), (), s32[]{:S(2)}) async-start(), calls=%async_computation.12 | async-start | bytes 1105920 | tf_op jit(solution)/shard_map/reduce_scatter | solution.py:576
  397.9 42.7 %collective-permute-start.38 = (bf16[4,288,576]{2,1,0:T(8,128)(2,1)}, bf16[4,288,576]{2,1,0:T(8,128)(2,1)}, u32[]{:S(2)}, u32[]{:S(2)}) collective-permute-start(bf16[4,288,576]{2,1,0:T(8,128)(2,1)} %pad_maximum_fusion.3), channel_id=1, source_target_pairs={{0,8},{8,0},{16,24},{24,16},{1,9},{9,1},{17,25},{25,17},{2,10},{10... | collective-permute-start | bytes 3981320 | tf_op jit(solution)/shard_map/ppermute | solution.py:402
  403.0 37.6 %collective-permute-start.37 = (bf16[4,288,576]{2,1,0:T(8,128)(2,1)}, bf16[4,288,576]{2,1,0:T(8,128)(2,1)}, u32[]{:S(2)}, u32[]{:S(2)}) collective-permute-start(bf16[4,288,576]{2,1,0:T(8,128)(2,1)} %pad_maximum_fusion.2), channel_id=1, source_target_pairs={{0,16},{8,24},{16,0},{24,8},{1,17},{9,25},{17,1},{25,9},{2,18},{10... | collective-permute-start | bytes 3981320 | tf_op jit(solution)/shard_map/ppermute | solution.py:402
  432.6 12.0 %collective-permute-start.41 = (bf16[144,384]{1,0:T(8,128)(2,1)S(1)}, bf16[144,384]{1,0:T(8,128)(2,1)S(1)}, u32[]{:S(2)}, u32[]{:S(2)}) collective-permute-start(bf16[144,384]{1,0:T(8,128)(2,1)S(1)} %dynamic-slice_bitcast_fusion.2), channel_id=1, source_target_pairs={{0,4},{4,0},{1,5},{5,1},{2,6},{6,2},{3,7},{7,3},{8,12},{12,8},{9,1... | collective-permute-start | bytes 331784 | tf_op jit(solution)/shard_map/ppermute | solution.py:402
  436.0 12.5 %all-to-all-start.6 = ((bf16[32,2,864]{2,1,0:T(2,128)(2,1)}), bf16[32,2,864]{2,1,0:T(2,128)(2,1)S(1)}, u32[]{:S(2)}, u32[]{:S(2)}) async-start(bf16[32,2,864]{2,1,0:T(2,128)(2,1)} %reshape.594), calls=%async_computation.7 | async-start | bytes 229376 | tf_op jit(solution)/shard_map/all_to_all | solution.py:787
  440.3 44.4 %reduce-scatter.6.cloned.1.call-start = ((), (), s32[]{:S(2)}) async-start(), calls=%async_computation.11 | async-start | bytes 1843200 | tf_op jit(solution)/shard_map/reduce_scatter | solution.py:576
  451.5 10.1 %collective-permute-start.40 = (bf16[144,768]{1,0:T(8,128)(2,1)}, bf16[144,768]{1,0:T(8,128)(2,1)S(1)}, u32[]{:S(2)}, u32[]{:S(2)}) collective-permute-start(bf16[144,768]{1,0:T(8,128)(2,1)} %dynamic-slice_bitcast_fusion), channel_id=1, source_target_pairs={{0,4},{4,0},{1,5},{5,1},{2,6},{6,2},{3,7},{7,3},{8,12},{12,8},{9,1... | collective-permute-start | bytes 663560 | tf_op jit(solution)/shard_map/ppermute | solution.py:402
  466.1 8.6 %collective-permute-start.35 = (f32[18960]{0:T(1024)S(1)}, f32[18960]{0:T(1024)S(1)}, u32[]{:S(2)}, u32[]{:S(2)}) collective-permute-start(f32[18960]{0:T(1024)S(1)} %slice.232), channel_id=1, source_target_pairs={{0,1},{1,0},{2,3},{3,2},{4,5},{5,4},{6,7},{7,6},{8,9},{9,8},{10,11... | collective-permute-start | bytes 227528 | tf_op jit(solution)/shard_map/ppermute | solution.py:402
  474.7 7.2 %collective-permute-start.36 = (f32[18960]{0:T(1024)S(1)}, f32[18960]{0:T(1024)S(1)}, u32[]{:S(2)}, u32[]{:S(2)}) collective-permute-start(f32[18960]{0:T(1024)S(1)} %slice_add_fusion.8), channel_id=1, source_target_pairs={{0,2},{1,3},{2,0},{3,1},{4,6},{5,7},{6,4},{7,5},{8,10},{9,11},{10,... | collective-permute-start | bytes 227528 | tf_op jit(solution)/shard_map/ppermute | solution.py:402
  (69 other events, 548.3 us)
Sparse Core Ops, SparseCore 0:
  15.0 43.7 all-gather.6
  74.8 48.4 all-gather.8
  125.5 27.6 all-gather.10
  353.9 41.0 reduce-scatter.3
  397.8 33.8 reduce-scatter.7
  444.6 38.3 reduce-scatter.5

commit v5 on v4

--- a/solution.py
+++ b/solution.py
@@ -225,8 +225,8 @@
     return pl.BlockSpec(shape, lambda i: (0,) * len(shape))
 
 
-def by_line(shape):
-    return pl.BlockSpec((1,) + shape, lambda i: (i,) + (0,) * len(shape))
+def by_line(shape, first=0):
+    return pl.BlockSpec((1,) + shape, lambda i: (i + first,) + (0,) * len(shape))
 
 
 def attn_cost(x, w, products):
@@ -287,9 +287,9 @@
     )(own, peer, w, qkv, *tables)
 
 
-def ffn_forward_kernel(
-    own_ref, peer_ref, w_ref, b_ref, gu_ref, hidden_ref, x_all,
-):
+def ffn_forward_kernel(*refs):
+    own_ref, peer_ref, w_ref, b_ref = refs[:4]
+    gu_ref, hidden_ref, x_all = refs[-3:]
     ff = hidden_ref.shape[2]
     images, patches, width = own_ref.shape
     side = images * patches
@@ -305,28 +305,30 @@
     hidden_ref[0] = (gate * up / (1.0 + jnp.exp(-gate))).astype(BF16)
 
 
-def ffn_forward(own, peer, w, b):
+def ffn_forward(first, count, own, peer, w, b, *filled):
     images, patches, width = own.shape
     line, _, cols = w.shape
     rows = 2 * images * patches
     return pl.pallas_call(
         ffn_forward_kernel,
-        grid=(line,),
+        grid=(count,),
         in_specs=[resident(own.shape)] * 2
-        + [by_line(w.shape[1:]), by_line(b.shape[1:])],
-        out_specs=[by_line((rows, cols)), by_line((rows, cols // 2))],
+        + [by_line(w.shape[1:], first), by_line(b.shape[1:], first)]
+        + [pl.BlockSpec(memory_space=pl.ANY)] * len(filled),
+        out_specs=[by_line((rows, cols), first), by_line((rows, cols // 2), first)],
         out_shape=[
             jax.ShapeDtypeStruct((line, rows, cols), BF16),
             jax.ShapeDtypeStruct((line, rows, cols // 2), BF16),
         ],
         scratch_shapes=[pltpu.VMEM((rows, width), BF16)],
+        input_output_aliases={4: 0, 5: 1} if filled else {},
         compiler_params=pltpu.CompilerParams(vmem_limit_bytes=50 << 20),
         cost_estimate=pl.CostEstimate(
-            flops=2 * rows * width * line * cols,
-            bytes_accessed=2 * line * cols * (width + 2 * rows),
-            transcendentals=line * rows * cols // 2,
+            flops=2 * rows * width * count * cols,
+            bytes_accessed=2 * count * cols * (width + 2 * rows),
+            transcendentals=count * rows * cols // 2,
         ),
-    )(own, peer, w, b)
+    )(own, peer, w, b, *filled)
 
 
 def ffn_backward_kernel(
@@ -541,7 +543,7 @@
         scratch_shapes=[pltpu.VMEM((width, total_rows), BF16)] * (1 + len(pairs)),
         compiler_params=pltpu.CompilerParams(vmem_limit_bytes=50 << 20),
         cost_estimate=pl.CostEstimate(
-            flops=2 * line * width * total_rows * cols,
+            flops=line * width * total_rows * cols // 4,
             bytes_accessed=2 * line * (width + total_rows) * cols,
             transcendentals=0,
         ),
@@ -722,8 +724,12 @@
     d_ffn_own = d_ffn_f.astype(BF16)
     d_ffn_peer = swap(d_ffn_own, CORES)
     w_gu = whole_weight(held_gu, gu_arrived, gu_last).reshape(line, D, 2 * ff_cols)
-    down_passed, down_last = second_hop(after(down_arrived, w_gu))
-    gate_up, hidden = ffn_forward(after(ffn_own, down_passed), ffn_peer, w_gu, gu_b)
+    early = line // 2
+    begun = ffn_forward(0, early, ffn_own, ffn_peer, w_gu, gu_b)
+    down_passed, down_last = second_hop(after(down_arrived, begun))
+    gate_up, hidden = ffn_forward(
+        early, line - early, after(ffn_own, down_passed), ffn_peer, w_gu, gu_b, *begun
+    )
     w_down = whole_weight(held_down, down_arrived, down_last).reshape(line, D, ff_cols)
     d_gu, d_in_own, d_in_peer, gu_bias_part = ffn_backward(
         d_ffn_own, d_ffn_peer, w_down, w_gu, gate_up

time: 506 us -> 503 us (level)
  waiting for transfers between devices: 150 us -> 143 us
    ppermute x42, waiting for transfers between devices: 75.8 us -> 69 us  [swap(): return lax.ppermute(values, name, [(i, i ^ bit) for i in range(count)])]
    pallas_call x1 -> x2, Pallas kernels: 13 us -> 15.7 us  [ffn_forward(): pl.pallas_call(ffn_forward_kernel, grid=(count,), in_specs=[resident(own....]
    unnamed x138 -> x146, local copies, waits for them, and re-layouts: 24.8 us -> 26.2 us
  transfers between devices with their start and end apart: 55 -> 55, of which waited for: 25 -> 22; matrix products, arithmetic and copies ran while one was open for 20% -> 20% of each run, Pallas kernels for 20% -> 21%
where the time goes in v5:
time: 503 us; the launch traced here: 497 us
  waiting for transfers between devices  143 us (28%)
  Pallas kernels  140 us (28%)
  starting transfers between devices  63.4 us (13%)
  other arithmetic  63.1 us (13%)
  local copies, waits for them, and re-layouts  59.6 us (12%)
  between operations  16.2 us (3%)
  matrix products  12.2 us (2%)
    ppermute x42, waiting for transfers between devices, swap(): return lax.ppermute(values, name, [(i, i ^ bit) for i in range(count)])  69 us
    pallas_call x1, Pallas kernels, attn_backward(): pl.pallas_call(attn_backward_kernel, grid=(line,), in_specs=[resident(own...  36.5 us
    pallas_call x3, Pallas kernels, chip_products(): pl.pallas_call(functools.partial(grad_kernel, tuple((len(group) for group...  34.4 us
    ppermute x42, starting transfers between devices, swap(): return lax.ppermute(values, name, [(i, i ^ bit) for i in range(count)])  30.3 us
    reduce_scatter x3, waiting for transfers between devices, scatter_line(): return lax.psum_scatter(part, LINE, scatter_dimension=0, tiled=False)  27.5 us
    all_gather x3, waiting for transfers between devices, gather_line(): return lax.all_gather(piece, LINE, axis=0)  26.6 us
    unnamed x146, local copies, waits for them, and re-layouts  26.2 us
    pallas_call x1, Pallas kernels, ffn_backward(): pl.pallas_call(ffn_backward_kernel, grid=(line,), in_specs=[resident(own....  22.5 us
  transfers between devices with their start and end apart: 55, of which 22 were waited for; matrix products, arithmetic and copies ran while one was open for 20% of the time, Pallas kernels for 21%

profile of v5, /device:TPU:0, one launch (start us, length us, event | category | flops | bytes accessed | tf_op | source)
XLA Modules:
  0.0 497.1 jit_solution(13114818051250811576)
XLA Ops:
  15.5 5.2 %all-to-all-start = ((s32[8,2,8]{2,1,0:T(2,128)}), s32[8,2,8]{2,1,0:T(2,128)S(1)}, u32[]{:S(2)}, u32[]{:S(2)}) async-start(s32[8,2,8]{2,1,0:T(2,128)} %broadcast_in_dim.89), calls=%async_computation | async-start | bytes 16384 | tf_op jit(solution)/shard_map/all_to_all | solution.py:653
  21.1 4.3 all-to-all-done
  25.6 2.3 multiply_convert_fusion.1
  29.2 4.0 all-to-all-start.2
  33.2 25.6 %all-gather.7.cloned.1.call-done = bf16[1152,576]{1,0:T(8,128)(2,1)} async-done(((bf16[288,576]{1,0:T(8,128)(2,1)}), bf16[1152,576]{1,0:T(8,128)(2,1)}) %all-gather.7.cloned.1.call-update) | async-done | bytes 1327120 | tf_op jit(solution)/shard_map/all_gather | solution.py:466
  61.7 4.3 all-to-all-start.1
  68.0 5.7 %fusion.15 = (f32[4,256,144]{2,1,0:T(8,128)}, f32[4,256,144]{2,1,0:T(8,128)}) fusion(f32[144]{0:T(256)S(1)} %multiply_power_fusion, s32[4,256]{1,0:T(4,128)S(1)} %get-tuple-element.269, s32[4,256]{1,0:T(4,128)S(1)} %get-tuple-element.268, pred[144]{0:T(512)(128)(4,1)S(1)} %broadcast_compare_fusion.1), kind=kLoop, calls=%fused_computation.56 | loop fusion | flops 442368 | bytes 1188560 | tf_op jit(solution)/shard_map/sin | solution.py:43
  76.8 16.2 %collective-permute-done.1.x_ref = bf16[4,288,576]{2,1,0:T(8,128)(2,1)S(1)} collective-permute-done((bf16[4,288,576]{2,1,0:T(8,128)(2,1)}, bf16[4,288,576]{2,1,0:T(8,128)(2,1)S(1)}, u32[]{:S(2)}, u32[]{:S(2)}) %collective-permute-start.1) | collective-permute-done | bytes 1327136 | tf_op jit(solution)/shard_map/ppermute | solution.py:404
  100.0 11.8 %all-to-all-done.1 = bf16[4,2,64,1152]{3,2,1,0:T(8,128)(2,1)} async-done(((bf16[4,2,64,1152]{3,2,1,0:T(8,128)(2,1)}), bf16[4,2,64,1152]{3,2,1,0:T(8,128)(2,1)}, u32[]{:S(2)}, u32[]{:S(2)}) %all-to-all-start.1) | async-done | bytes 1179680 | tf_op jit(solution)/shard_map/all_to_all | solution.py:453
  111.7 2.4 copy.96
  127.0 2.9 shard_map.316
  129.9 2.5 copy-done.2
  132.4 21.9 %shard_map.317 = (bf16[4,1024,432]{2,1,0:T(8,128)(2,1)}, bf16[4,1024,144]{2,1,0:T(8,128)(2,1)}, bf16[2,256,1152]{2,1,0:T(8,128)(2,1)S(1)}, bf16[2,256,1152]{2,1,0:T(8,128)(2,1)}) custom-call(bf16[2,256,1152]{2,1,0:T(8,128)(2,1)} %copy-done.4, bf16[2,256,1152]{2,1,0:T(8,128)(2,1)} %collective-permute-done.6.peer_ref, bf16[4,1152,576]{2,1,0:T(8,128)(2,1)} %bitcast.184, ...), custom_call_target="tpu_custom_call" | custom-call | flops 7583301632 | bytes 14745600 | tf_op jit(solution)/shard_map/pallas_call | solution.py:248
  154.4 4.5 all-to-all-start.3
  161.2 3.0 collective-permute-done.7.x_ref
  168.0 2.5 multiply_reduce_fusion.3
  171.0 15.3 %collective-permute-done.10.da_ref = bf16[2,288,768]{2,1,0:T(8,128)(2,1)S(1)} collective-permute-done((bf16[2,288,768]{2,1,0:T(8,128)(2,1)S(1)}, bf16[2,288,768]{2,1,0:T(8,128)(2,1)S(1)}, u32[]{:S(2)}, u32[]{:S(2)}) %collective-permute-start.10) | collective-permute-done | bytes 884768 | tf_op jit(solution)/shard_map/ppermute | solution.py:404
  195.2 2.9 shard_map.318
  198.2 2.9 copy-done.1
  201.0 8.1 %shard_map.319 = (bf16[4,1024,768]{2,1,0:T(8,128)(2,1)}, bf16[4,1024,384]{2,1,0:T(8,128)(2,1)}) custom-call(bf16[2,256,1152]{2,1,0:T(8,128)(2,1)S(1)} %add_convert_fusion.3.refs_0_, bf16[2,256,1152]{2,1,0:T(8,128)(2,1)S(1)} %collective-permute-done.14.refs_1_, bf16[4,1152,768]{2,1,0:T(8,128)(2,1)} %bitcast.180, f32[4,1,768]{2,1,0:T(1,128)S(1)} %bitcast.200), custom_call_target="tpu_custom_call" | custom-call | flops 3623878656 | bytes 9830400 | tf_op jit(solution)/shard_map/pallas_call | solution.py:312
  215.4 7.7 %shard_map.320 = (bf16[4,1024,768]{2,1,0:T(8,128)(2,1)}, bf16[4,1024,384]{2,1,0:T(8,128)(2,1)}) custom-call(bf16[2,256,1152]{2,1,0:T(8,128)(2,1)S(1)} %add_convert_fusion.3.refs_0_, bf16[2,256,1152]{2,1,0:T(8,128)(2,1)S(1)} %collective-permute-done.14.refs_1_, bf16[4,1152,768]{2,1,0:T(8,128)(2,1)} %bitcast.181, ...), custom_call_target="tpu_custom_call", output_to_operand_aliasing={{0}: (4, {}), {1}: (5, {})} | custom-call | flops 3623878656 | bytes 9830400 | tf_op jit(solution)/shard_map/pallas_call | solution.py:312
  223.0 2.8 shard_map.321
  228.6 22.5 %shard_map.322 = (bf16[4,1024,768]{2,1,0:T(8,128)(2,1)}, bf16[2,256,1152]{2,1,0:T(8,128)(2,1)S(1)}, bf16[2,256,1152]{2,1,0:T(8,128)(2,1)S(1)}, f32[4,1,768]{2,1,0:T(1,128)S(1)}) custom-call(bf16[2,256,1152]{2,1,0:T(8,128)(2,1)S(1)} %fusion.11.own_ref, bf16[2,256,1152]{2,1,0:T(8,128)(2,1)} %copy-done.39, bf16[4,1152,384]{2,1,0:T(8,128)(2,1)} %bitcast.188, ...), custom_call_target="tpu_custom_call" | custom-call | flops 10871635968 | bytes 26738688 | tf_op jit(solution)/shard_map/pallas_call | solution.py:375
  251.1 11.7 %shard_map.323 = (bf16[4,144,768]{2,1,0:T(8,128)(2,1)S(1)}, bf16[4,144,768]{2,1,0:T(8,128)(2,1)S(1)}, bf16[4,288,768]{2,1,0:T(8,128)(2,1)}, bf16[4,288,768]{2,1,0:T(8,128)(2,1)}, bf16[4,288,768]{2,1,0:T(8,128)(2,1)}) custom-call(s32[4]{0:T(128)S(1)} %broadcast_xor_fusion.spot_ref, bf16[512,1152]{1,0:T(8,128)(2,1)S(1)} %bitcast.183, ...), custom_call_target="tpu_custom_call" | custom-call | flops 905969664 | bytes 13369344 | tf_op jit(solution)/shard_map/pallas_call | solution.py:535
  264.4 8.7 %shard_map.324 = (bf16[4,144,384]{2,1,0:T(8,128)(2,1)S(1)}, bf16[4,144,384]{2,1,0:T(8,128)(2,1)S(1)}, bf16[4,288,384]{2,1,0:T(8,128)(2,1)S(1)}, bf16[4,288,384]{2,1,0:T(8,128)(2,1)S(1)}, bf16[4,288,384]{2,1,0:T(8,128)(2,1)S(1)}) custom-call(s32[4]{0:T(128)S(1)} %broadcast_xor_fusion.spot_ref, bf16[512,1152]{1,0:T(8,128)(2,1)} %fusion.13.refs_0_, ...), custom_call_target="tpu_custom_call" | custom-call | flops 452984832 | bytes 6684672 | tf_op jit(solution)/shard_map/pallas_call | solution.py:535
  275.7 6.1 %convolution_bitcast_fusion = f32[1024,1152]{1,0:T(8,128)S(1)} fusion(bf16[4,1024,384]{2,1,0:T(8,128)(2,1)} %get-tuple-element.119.refs_2_, bf16[4,1152,384]{2,1,0:T(8,128)(2,1)S(1)} %bitcast.189), kind=kOutput, calls=%fused_computation.5 | convolution fusion | flops 3623878656 | bytes 11403264 | tf_op jit(solution)/shard_map/zrf,zdf->rd/dot_general | solution.py:744
  282.0 3.5 collective-permute-done.21
  291.9 2.2 multiply_reduce_fusion.4
  294.6 2.3 copy-done.36
  303.9 5.5 %all-to-all-start.4 = ((bf16[4,2,64,1152]{3,2,1,0:T(8,128)(2,1)}), bf16[4,2,64,1152]{3,2,1,0:T(8,128)(2,1)}, u32[]{:S(2)}, u32[]{:S(2)}) async-start(bf16[4,2,64,1152]{3,2,1,0:T(8,128)(2,1)} %bitcast.175), calls=%async_computation.4 | async-start | bytes 2359296 | tf_op jit(solution)/shard_map/all_to_all | solution.py:461
  310.6 36.5 %shard_map.325 = (bf16[4,1024,432]{2,1,0:T(8,128)(2,1)}, bf16[2,256,1152]{2,1,0:T(8,128)(2,1)S(1)}, bf16[2,256,1152]{2,1,0:T(8,128)(2,1)}, f32[4,1,432]{2,1,0:T(1,128)S(1)}, f32[2,144]{1,0:T(2,128)S(1)}) custom-call(bf16[2,256,1152]{2,1,0:T(8,128)(2,1)} %copy-done.32, bf16[2,256,1152]{2,1,0:T(8,128)(2,1)} %collective-permute-done.24.peer_ref, ...), custom_call_target="tpu_custom_call" | custom-call | flops 10804527104 | bytes 14745600 | tf_op jit(solution)/shard_map/pallas_call | solution.py:272
  347.2 4.1 add_convert_fusion
  354.7 13.9 %shard_map.326 = (bf16[4,144,576]{2,1,0:T(8,128)(2,1)}, bf16[4,144,576]{2,1,0:T(8,128)(2,1)}, bf16[4,288,576]{2,1,0:T(8,128)(2,1)}, bf16[4,288,576]{2,1,0:T(8,128)(2,1)}, bf16[4,288,576]{2,1,0:T(8,128)(2,1)}) custom-call(s32[4]{0:T(128)S(1)} %broadcast_xor_fusion.spot_ref, bf16[512,1152]{1,0:T(8,128)(2,1)S(1)} %bitcast.187, ...), custom_call_target="tpu_custom_call" | custom-call | flops 679477248 | bytes 10027008 | tf_op jit(solution)/shard_map/pallas_call | solution.py:535
  371.6 2.9 fusion.10
  374.6 2.6 fusion.8
  378.3 5.1 %all-to-all-start.5 = ((bf16[4,2,64,1152]{3,2,1,0:T(8,128)(2,1)}), bf16[4,2,64,1152]{3,2,1,0:T(8,128)(2,1)S(1)}, u32[]{:S(2)}, u32[]{:S(2)}) async-start(bf16[4,2,64,1152]{3,2,1,0:T(8,128)(2,1)} %bitcast.204), calls=%async_computation.6 | async-start | bytes 2359296 | tf_op jit(solution)/shard_map/all_to_all | solution.py:461
  383.4 2.7 add_convert_fusion.4
  386.1 5.2 %collective-permute-done.28 = bf16[4,144,576]{2,1,0:T(8,128)(2,1)} collective-permute-done((bf16[4,144,576]{2,1,0:T(8,128)(2,1)}, bf16[4,144,576]{2,1,0:T(8,128)(2,1)}, u32[]{:S(2)}, u32[]{:S(2)}) %collective-permute-start.28) | collective-permute-done | bytes 663584 | tf_op jit(solution)/shard_map/ppermute | solution.py:404
  398.5 2.6 collective-permute-start.37
  401.1 27.5 %reduce-scatter.8.cloned.1.call-done = bf16[1,288,384]{2,1,0:T(8,128)(2,1)} async-done(((bf16[4,288,384]{2,1,0:T(8,128)(2,1)}), bf16[1,288,384]{2,1,0:T(8,128)(2,1)}) %reduce-scatter.8.cloned.1.call-update) | async-done | bytes 221200 | tf_op jit(solution)/shard_map/reduce_scatter | solution.py:578
  432.9 3.9 all-to-all-start.6
  437.2 3.9 add_convert_fusion.1
  441.3 3.8 all-to-all-done.6
  453.7 3.7 collective-permute-done.33
  458.4 4.2 collective-permute-done.34
  465.0 6.3 %collective-permute-done.35 = f32[18960]{0:T(1024)S(1)} collective-permute-done((f32[18960]{0:T(1024)S(1)}, f32[18960]{0:T(1024)S(1)}, u32[]{:S(2)}, u32[]{:S(2)}) %collective-permute-start.35) | collective-permute-done | bytes 75872 | tf_op jit(solution)/shard_map/ppermute | solution.py:404
  473.1 5.5 %collective-permute-done.36 = f32[18960]{0:T(1024)S(1)} collective-permute-done((f32[18960]{0:T(1024)S(1)}, f32[18960]{0:T(1024)S(1)}, u32[]{:S(2)}, u32[]{:S(2)}) %collective-permute-start.36) | collective-permute-done | bytes 75872 | tf_op jit(solution)/shard_map/ppermute | solution.py:404
  487.4 2.4 copy.140
  (407 shorter events, 123.2 us)
Async XLA Ops:
  7.2 51.6 %all-gather.7.cloned.1.call-start = ((), (), s32[]{:S(2)}) async-start(), calls=%async_computation.13 | async-start | bytes 1843200 | tf_op jit(solution)/shard_map/all_gather | solution.py:466
  15.5 9.9 %all-to-all-start = ((s32[8,2,8]{2,1,0:T(2,128)}), s32[8,2,8]{2,1,0:T(2,128)S(1)}, u32[]{:S(2)}, u32[]{:S(2)}) async-start(s32[8,2,8]{2,1,0:T(2,128)} %broadcast_in_dim.89), calls=%async_computation | async-start | bytes 16384 | tf_op jit(solution)/shard_map/all_to_all | solution.py:653
  29.2 32.5 %all-to-all-start.2 = ((f32[32,1,2028]{2,1,0:T(1,128)}), f32[32,1,2028]{2,1,0:T(1,128)S(1)}, u32[]{:S(2)}, u32[]{:S(2)}) async-start(f32[32,1,2028]{2,1,0:T(1,128)} %all_to_all.31), calls=%async_computation.2 | async-start | bytes 524288 | tf_op jit(solution)/shard_map/all_to_all | solution.py:672
  58.8 34.2 %collective-permute-start.1 = (bf16[4,288,576]{2,1,0:T(8,128)(2,1)}, bf16[4,288,576]{2,1,0:T(8,128)(2,1)S(1)}, u32[]{:S(2)}, u32[]{:S(2)}) collective-permute-start(bf16[4,288,576]{2,1,0:T(8,128)(2,1)} %bitcast.193), channel_id=1, source_target_pairs={{0,8},{8,0},{16,24},{24,16},{1,9},{9,1},{17,25},{25,17},{2,10},{10... | collective-permute-start | bytes 3981320 | tf_op jit(solution)/shard_map/ppermute | solution.py:404
  60.3 34.1 %collective-permute-start.2 = (bf16[4,288,576]{2,1,0:T(8,128)(2,1)}, bf16[4,288,576]{2,1,0:T(8,128)(2,1)}, u32[]{:S(2)}, u32[]{:S(2)}) collective-permute-start(bf16[4,288,576]{2,1,0:T(8,128)(2,1)} %bitcast.194), channel_id=1, source_target_pairs={{0,16},{8,24},{16,0},{24,8},{1,17},{9,25},{17,1},{25,9},{2,18},{10... | collective-permute-start | bytes 3981320 | tf_op jit(solution)/shard_map/ppermute | solution.py:404
  61.7 50.0 %all-to-all-start.1 = ((bf16[4,2,64,1152]{3,2,1,0:T(8,128)(2,1)}), bf16[4,2,64,1152]{3,2,1,0:T(8,128)(2,1)}, u32[]{:S(2)}, u32[]{:S(2)}) async-start(bf16[4,2,64,1152]{3,2,1,0:T(8,128)(2,1)} %bitcast.210), calls=%async_computation.1 | async-start | bytes 2359296 | tf_op jit(solution)/shard_map/all_to_all | solution.py:453
  66.0 57.2 %all-gather.9.cloned.1.call-start = ((), (), s32[]{:S(2)}) async-start(), calls=%async_computation.14 | async-start | bytes 2211840 | tf_op jit(solution)/shard_map/all_gather | solution.py:466
  74.6 84.4 %all-gather.11.cloned.1.call-start = ((), (), s32[]{:S(2)}) async-start(), calls=%async_computation.15 | async-start | bytes 1474560 | tf_op jit(solution)/shard_map/all_gather | solution.py:466
  95.3 18.9 %collective-permute-start.4 = (bf16[2,288,576]{2,1,0:T(8,128)(2,1)}, bf16[2,288,576]{2,1,0:T(8,128)(2,1)S(1)}, u32[]{:S(2)}, u32[]{:S(2)}) collective-permute-start(bf16[2,288,576]{2,1,0:T(8,128)(2,1)} %slice.164), channel_id=1, source_target_pairs={{0,16},{8,24},{16,0},{24,8},{1,17},{9,25},{17,1},{25,9},{2,18},{10... | collective-permute-start | bytes 1990664 | tf_op jit(solution)/shard_map/ppermute | solution.py:404
  98.8 17.1 %collective-permute-start.5 = (bf16[2,288,576]{2,1,0:T(8,128)(2,1)}, bf16[2,288,576]{2,1,0:T(8,128)(2,1)}, u32[]{:S(2)}, u32[]{:S(2)}) collective-permute-start(bf16[2,288,576]{2,1,0:T(8,128)(2,1)} %slice.165), channel_id=1, source_target_pairs={{0,8},{8,0},{16,24},{24,16},{1,9},{9,1},{17,25},{25,17},{2,10},{10... | collective-permute-start | bytes 1990664 | tf_op jit(solution)/shard_map/ppermute | solution.py:404
  119.2 13.2 %collective-permute-start.6 = (bf16[2,256,1152]{2,1,0:T(8,128)(2,1)S(1)}, bf16[2,256,1152]{2,1,0:T(8,128)(2,1)}, u32[]{:S(2)}, u32[]{:S(2)}) collective-permute-start(bf16[2,256,1152]{2,1,0:T(8,128)(2,1)S(1)} %fusion.3.own_ref), channel_id=1, source_target_pairs={{0,4},{4,0},{1,5},{5,1},{2,6},{6,2},{3,7},{7,3},{8,12},{12,8},{9,1... | collective-permute-start | bytes 3538952 | tf_op jit(solution)/shard_map/ppermute | solution.py:404
  123.3 40.9 %collective-permute-start.7 = (bf16[4,288,768]{2,1,0:T(8,128)(2,1)}, bf16[4,288,768]{2,1,0:T(8,128)(2,1)}, u32[]{:S(2)}, u32[]{:S(2)}) collective-permute-start(bf16[4,288,768]{2,1,0:T(8,128)(2,1)} %bitcast.190), channel_id=1, source_target_pairs={{0,8},{8,0},{16,24},{24,16},{1,9},{9,1},{17,25},{25,17},{2,10},{10... | collective-permute-start | bytes 5308424 | tf_op jit(solution)/shard_map/ppermute | solution.py:404
  123.8 42.2 %collective-permute-start.8 = (bf16[4,288,768]{2,1,0:T(8,128)(2,1)}, bf16[4,288,768]{2,1,0:T(8,128)(2,1)}, u32[]{:S(2)}, u32[]{:S(2)}) collective-permute-start(bf16[4,288,768]{2,1,0:T(8,128)(2,1)} %bitcast.191), channel_id=1, source_target_pairs={{0,16},{8,24},{16,0},{24,8},{1,17},{9,25},{17,1},{25,9},{2,18},{10... | collective-permute-start | bytes 5308424 | tf_op jit(solution)/shard_map/ppermute | solution.py:404
  154.3 13.6 %collective-permute-start.9 = (bf16[2,256,1152]{2,1,0:T(8,128)(2,1)}, bf16[2,256,1152]{2,1,0:T(8,128)(2,1)S(1)}, u32[]{:S(2)}, u32[]{:S(2)}) collective-permute-start(bf16[2,256,1152]{2,1,0:T(8,128)(2,1)} %get-tuple-element.95), channel_id=1, source_target_pairs={{0,4},{4,0},{1,5},{5,1},{2,6},{6,2},{3,7},{7,3},{8,12},{12,8},{9,1... | collective-permute-start | bytes 3538952 | tf_op jit(solution)/shard_map/ppermute | solution.py:404
  154.4 36.4 %all-to-all-start.3 = ((bf16[4,2,64,1152]{3,2,1,0:T(8,128)(2,1)}), bf16[4,2,64,1152]{3,2,1,0:T(8,128)(2,1)}, u32[]{:S(2)}, u32[]{:S(2)}) async-start(bf16[4,2,64,1152]{3,2,1,0:T(8,128)(2,1)} %bitcast.211), calls=%async_computation.3 | async-start | bytes 2359296 | tf_op jit(solution)/shard_map/all_to_all | solution.py:453
  165.4 20.8 %collective-permute-start.10 = (bf16[2,288,768]{2,1,0:T(8,128)(2,1)S(1)}, bf16[2,288,768]{2,1,0:T(8,128)(2,1)S(1)}, u32[]{:S(2)}, u32[]{:S(2)}) collective-permute-start(bf16[2,288,768]{2,1,0:T(8,128)(2,1)S(1)} %slice.223), channel_id=1, source_target_pairs={{0,16},{8,24},{16,0},{24,8},{1,17},{9,25},{17,1},{25,9},{2,18},{10... | collective-permute-start | bytes 2654216 | tf_op jit(solution)/shard_map/ppermute | solution.py:404
  167.3 20.6 %collective-permute-start.11 = (bf16[2,288,768]{2,1,0:T(8,128)(2,1)S(1)}, bf16[2,288,768]{2,1,0:T(8,128)(2,1)S(1)}, u32[]{:S(2)}, u32[]{:S(2)}) collective-permute-start(bf16[2,288,768]{2,1,0:T(8,128)(2,1)S(1)} %slice.224), channel_id=1, source_target_pairs={{0,8},{8,0},{16,24},{24,16},{1,9},{9,1},{17,25},{25,17},{2,10},{10... | collective-permute-start | bytes 2654216 | tf_op jit(solution)/shard_map/ppermute | solution.py:404
  170.9 30.1 %collective-permute-start.14 = (bf16[2,256,1152]{2,1,0:T(8,128)(2,1)S(1)}, bf16[2,256,1152]{2,1,0:T(8,128)(2,1)S(1)}, u32[]{:S(2)}, u32[]{:S(2)}) collective-permute-start(bf16[2,256,1152]{2,1,0:T(8,128)(2,1)S(1)} %add_convert_fusion.3.refs_0_), channel_id=1, source_target_pairs={{0,4},{4,0},{1,5},{5,1},{2,6},{6,2},{3,7},{7,3},{8,12},{12,8},{9,1... | collective-permute-start | bytes 3538952 | tf_op jit(solution)/shard_map/ppermute | solution.py:404
  188.8 20.3 %collective-permute-start.12 = (bf16[4,288,384]{2,1,0:T(8,128)(2,1)}, bf16[4,288,384]{2,1,0:T(8,128)(2,1)}, u32[]{:S(2)}, u32[]{:S(2)}) collective-permute-start(bf16[4,288,384]{2,1,0:T(8,128)(2,1)} %slice.228.own_ref), channel_id=1, source_target_pairs={{0,8},{8,0},{16,24},{24,16},{1,9},{9,1},{17,25},{25,17},{2,10},{10... | collective-permute-start | bytes 2654216 | tf_op jit(solution)/shard_map/ppermute | solution.py:404
  189.4 19.7 %collective-permute-start.13 = (bf16[4,288,384]{2,1,0:T(8,128)(2,1)}, bf16[4,288,384]{2,1,0:T(8,128)(2,1)}, u32[]{:S(2)}, u32[]{:S(2)}) collective-permute-start(bf16[4,288,384]{2,1,0:T(8,128)(2,1)} %slice.228.own_ref), channel_id=1, source_target_pairs={{0,16},{8,24},{16,0},{24,8},{1,17},{9,25},{17,1},{25,9},{2,18},{10... | collective-permute-start | bytes 2654216 | tf_op jit(solution)/shard_map/ppermute | solution.py:404
  192.6 35.0 %collective-permute-start.15 = (bf16[2,256,1152]{2,1,0:T(8,128)(2,1)S(1)}, bf16[2,256,1152]{2,1,0:T(8,128)(2,1)S(1)}, u32[]{:S(2)}, u32[]{:S(2)}) collective-permute-start(bf16[2,256,1152]{2,1,0:T(8,128)(2,1)S(1)} %fusion.11.own_ref), channel_id=1, source_target_pairs={{0,4},{4,0},{1,5},{5,1},{2,6},{6,2},{3,7},{7,3},{8,12},{12,8},{9,1... | collective-permute-start | bytes 3538952 | tf_op jit(solution)/shard_map/ppermute | solution.py:404
  211.2 11.8 %collective-permute-start.16 = (bf16[2,288,384]{2,1,0:T(8,128)(2,1)S(1)}, bf16[2,288,384]{2,1,0:T(8,128)(2,1)S(1)}, u32[]{:S(2)}, u32[]{:S(2)}) collective-permute-start(bf16[2,288,384]{2,1,0:T(8,128)(2,1)S(1)} %slice.178), channel_id=1, source_target_pairs={{0,16},{8,24},{16,0},{24,8},{1,17},{9,25},{17,1},{25,9},{2,18},{10... | collective-permute-start | bytes 1327112 | tf_op jit(solution)/shard_map/ppermute | solution.py:404
  212.7 10.3 %collective-permute-start.17 = (bf16[2,288,384]{2,1,0:T(8,128)(2,1)S(1)}, bf16[2,288,384]{2,1,0:T(8,128)(2,1)S(1)}, u32[]{:S(2)}, u32[]{:S(2)}) collective-permute-start(bf16[2,288,384]{2,1,0:T(8,128)(2,1)S(1)} %slice.179), channel_id=1, source_target_pairs={{0,8},{8,0},{16,24},{24,16},{1,9},{9,1},{17,25},{25,17},{2,10},{10... | collective-permute-start | bytes 1327112 | tf_op jit(solution)/shard_map/ppermute | solution.py:404
  262.9 22.7 %collective-permute-start.21 = (bf16[4,144,768]{2,1,0:T(8,128)(2,1)S(1)}, bf16[4,144,768]{2,1,0:T(8,128)(2,1)}, u32[]{:S(2)}, u32[]{:S(2)}) collective-permute-start(bf16[4,144,768]{2,1,0:T(8,128)(2,1)S(1)} %get-tuple-element.109), channel_id=1, source_target_pairs={{0,16},{8,24},{16,0},{24,8},{1,17},{9,25},{17,1},{25,9},{2,18},{10... | collective-permute-start | bytes 2654216 | tf_op jit(solution)/shard_map/ppermute | solution.py:404
  263.5 25.6 %collective-permute-start.20 = (bf16[4,144,768]{2,1,0:T(8,128)(2,1)S(1)}, bf16[4,144,768]{2,1,0:T(8,128)(2,1)}, u32[]{:S(2)}, u32[]{:S(2)}) collective-permute-start(bf16[4,144,768]{2,1,0:T(8,128)(2,1)S(1)} %get-tuple-element.108), channel_id=1, source_target_pairs={{0,8},{8,0},{16,24},{24,16},{1,9},{9,1},{17,25},{25,17},{2,10},{10... | collective-permute-start | bytes 2654216 | tf_op jit(solution)/shard_map/ppermute | solution.py:404
  273.1 27.5 %collective-permute-start.22 = (bf16[4,144,384]{2,1,0:T(8,128)(2,1)S(1)}, bf16[4,144,384]{2,1,0:T(8,128)(2,1)S(1)}, u32[]{:S(2)}, u32[]{:S(2)}) collective-permute-start(bf16[4,144,384]{2,1,0:T(8,128)(2,1)S(1)} %get-tuple-element.114), channel_id=1, source_target_pairs={{0,8},{8,0},{16,24},{24,16},{1,9},{9,1},{17,25},{25,17},{2,10},{10... | collective-permute-start | bytes 1327112 | tf_op jit(solution)/shard_map/ppermute | solution.py:404
  274.3 26.3 %collective-permute-start.23 = (bf16[4,144,384]{2,1,0:T(8,128)(2,1)S(1)}, bf16[4,144,384]{2,1,0:T(8,128)(2,1)S(1)}, u32[]{:S(2)}, u32[]{:S(2)}) collective-permute-start(bf16[4,144,384]{2,1,0:T(8,128)(2,1)S(1)} %get-tuple-element.115), channel_id=1, source_target_pairs={{0,16},{8,24},{16,0},{24,8},{1,17},{9,25},{17,1},{25,9},{2,18},{10... | collective-permute-start | bytes 1327112 | tf_op jit(solution)/shard_map/ppermute | solution.py:404
  275.7 12.6 %collective-permute-start.19 = (bf16[2,256,1152]{2,1,0:T(8,128)(2,1)S(1)}, bf16[2,256,1152]{2,1,0:T(8,128)(2,1)S(1)}, u32[]{:S(2)}, u32[]{:S(2)}) collective-permute-start(bf16[2,256,1152]{2,1,0:T(8,128)(2,1)S(1)} %get-tuple-element.121), channel_id=1, source_target_pairs={{0,4},{4,0},{1,5},{5,1},{2,6},{6,2},{3,7},{7,3},{8,12},{12,8},{9,1... | collective-permute-start | bytes 3538952 | tf_op jit(solution)/shard_map/ppermute | solution.py:404
  288.3 58.9 %collective-permute-start.27 = (bf16[4,288,768]{2,1,0:T(8,128)(2,1)}, bf16[4,288,768]{2,1,0:T(8,128)(2,1)}, u32[]{:S(2)}, u32[]{:S(2)}) collective-permute-start(bf16[4,288,768]{2,1,0:T(8,128)(2,1)} %pad_maximum_fusion.1), channel_id=1, source_target_pairs={{0,8},{8,0},{16,24},{24,16},{1,9},{9,1},{17,25},{25,17},{2,10},{10... | collective-permute-start | bytes 5308424 | tf_op jit(solution)/shard_map/ppermute | solution.py:404
  294.4 15.0 %collective-permute-start.24 = (bf16[2,256,1152]{2,1,0:T(8,128)(2,1)S(1)}, bf16[2,256,1152]{2,1,0:T(8,128)(2,1)}, u32[]{:S(2)}, u32[]{:S(2)}) collective-permute-start(bf16[2,256,1152]{2,1,0:T(8,128)(2,1)S(1)} %multiply_convert_fusion.own_ref), channel_id=1, source_target_pairs={{0,4},{4,0},{1,5},{5,1},{2,6},{6,2},{3,7},{7,3},{8,12},{12,8},{9,1... | collective-permute-start | bytes 3538952 | tf_op jit(solution)/shard_map/ppermute | solution.py:404
  299.7 47.5 %collective-permute-start.26 = (bf16[4,288,768]{2,1,0:T(8,128)(2,1)}, bf16[4,288,768]{2,1,0:T(8,128)(2,1)}, u32[]{:S(2)}, u32[]{:S(2)}) collective-permute-start(bf16[4,288,768]{2,1,0:T(8,128)(2,1)} %pad_maximum_fusion), channel_id=1, source_target_pairs={{0,16},{8,24},{16,0},{24,8},{1,17},{9,25},{17,1},{25,9},{2,18},{10... | collective-permute-start | bytes 5308424 | tf_op jit(solution)/shard_map/ppermute | solution.py:404
  303.9 50.7 %all-to-all-start.4 = ((bf16[4,2,64,1152]{3,2,1,0:T(8,128)(2,1)}), bf16[4,2,64,1152]{3,2,1,0:T(8,128)(2,1)}, u32[]{:S(2)}, u32[]{:S(2)}) async-start(bf16[4,2,64,1152]{3,2,1,0:T(8,128)(2,1)} %bitcast.175), calls=%async_computation.4 | async-start | bytes 2359296 | tf_op jit(solution)/shard_map/all_to_all | solution.py:461
  309.4 82.5 %reduce-scatter.4.cloned.1.call-start = ((), (), s32[]{:S(2)}) async-start(), calls=%async_computation.10 | async-start | bytes 2211840 | tf_op jit(solution)/shard_map/reduce_scatter | solution.py:578
  351.3 20.3 %collective-permute-start.25 = (bf16[2,256,1152]{2,1,0:T(8,128)(2,1)}, bf16[2,256,1152]{2,1,0:T(8,128)(2,1)}, u32[]{:S(2)}, u32[]{:S(2)}) collective-permute-start(bf16[2,256,1152]{2,1,0:T(8,128)(2,1)} %get-tuple-element.128), channel_id=1, source_target_pairs={{0,4},{4,0},{1,5},{5,1},{2,6},{6,2},{3,7},{7,3},{8,12},{12,8},{9,1... | collective-permute-start | bytes 3538952 | tf_op jit(solution)/shard_map/ppermute | solution.py:404
  353.1 24.0 %collective-permute-start.31 = (bf16[4,288,384]{2,1,0:T(8,128)(2,1)}, bf16[4,288,384]{2,1,0:T(8,128)(2,1)}, u32[]{:S(2)}, u32[]{:S(2)}) collective-permute-start(bf16[4,288,384]{2,1,0:T(8,128)(2,1)} %pad_maximum_fusion.5), channel_id=1, source_target_pairs={{0,8},{8,0},{16,24},{24,16},{1,9},{9,1},{17,25},{25,17},{2,10},{10... | collective-permute-start | bytes 2654216 | tf_op jit(solution)/shard_map/ppermute | solution.py:404
  354.1 23.1 %collective-permute-start.30 = (bf16[4,288,384]{2,1,0:T(8,128)(2,1)}, bf16[4,288,384]{2,1,0:T(8,128)(2,1)}, u32[]{:S(2)}, u32[]{:S(2)}) collective-permute-start(bf16[4,288,384]{2,1,0:T(8,128)(2,1)} %pad_maximum_fusion.4), channel_id=1, source_target_pairs={{0,16},{8,24},{16,0},{24,8},{1,17},{9,25},{17,1},{25,9},{2,18},{10... | collective-permute-start | bytes 2654216 | tf_op jit(solution)/shard_map/ppermute | solution.py:404
  368.6 22.7 %collective-permute-start.28 = (bf16[4,144,576]{2,1,0:T(8,128)(2,1)}, bf16[4,144,576]{2,1,0:T(8,128)(2,1)}, u32[]{:S(2)}, u32[]{:S(2)}) collective-permute-start(bf16[4,144,576]{2,1,0:T(8,128)(2,1)} %get-tuple-element.134), channel_id=1, source_target_pairs={{0,8},{8,0},{16,24},{24,16},{1,9},{9,1},{17,25},{25,17},{2,10},{10... | collective-permute-start | bytes 1990664 | tf_op jit(solution)/shard_map/ppermute | solution.py:404
  369.7 22.2 %collective-permute-start.29 = (bf16[4,144,576]{2,1,0:T(8,128)(2,1)}, bf16[4,144,576]{2,1,0:T(8,128)(2,1)}, u32[]{:S(2)}, u32[]{:S(2)}) collective-permute-start(bf16[4,144,576]{2,1,0:T(8,128)(2,1)} %get-tuple-element.135), channel_id=1, source_target_pairs={{0,16},{8,24},{16,0},{24,8},{1,17},{9,25},{17,1},{25,9},{2,18},{10... | collective-permute-start | bytes 1990664 | tf_op jit(solution)/shard_map/ppermute | solution.py:404
  378.3 51.3 %all-to-all-start.5 = ((bf16[4,2,64,1152]{3,2,1,0:T(8,128)(2,1)}), bf16[4,2,64,1152]{3,2,1,0:T(8,128)(2,1)S(1)}, u32[]{:S(2)}, u32[]{:S(2)}) async-start(bf16[4,2,64,1152]{3,2,1,0:T(8,128)(2,1)} %bitcast.204), calls=%async_computation.6 | async-start | bytes 2359296 | tf_op jit(solution)/shard_map/all_to_all | solution.py:461
  383.4 45.2 %reduce-scatter.8.cloned.1.call-start = ((), (), s32[]{:S(2)}) async-start(), calls=%async_computation.12 | async-start | bytes 1105920 | tf_op jit(solution)/shard_map/reduce_scatter | solution.py:578
  394.8 42.4 %collective-permute-start.38 = (bf16[4,288,576]{2,1,0:T(8,128)(2,1)}, bf16[4,288,576]{2,1,0:T(8,128)(2,1)}, u32[]{:S(2)}, u32[]{:S(2)}) collective-permute-start(bf16[4,288,576]{2,1,0:T(8,128)(2,1)} %pad_maximum_fusion.3), channel_id=1, source_target_pairs={{0,8},{8,0},{16,24},{24,16},{1,9},{9,1},{17,25},{25,17},{2,10},{10... | collective-permute-start | bytes 3981320 | tf_op jit(solution)/shard_map/ppermute | solution.py:404
  398.5 38.7 %collective-permute-start.37 = (bf16[4,288,576]{2,1,0:T(8,128)(2,1)}, bf16[4,288,576]{2,1,0:T(8,128)(2,1)}, u32[]{:S(2)}, u32[]{:S(2)}) collective-permute-start(bf16[4,288,576]{2,1,0:T(8,128)(2,1)} %pad_maximum_fusion.2), channel_id=1, source_target_pairs={{0,16},{8,24},{16,0},{24,8},{1,17},{9,25},{17,1},{25,9},{2,18},{10... | collective-permute-start | bytes 3981320 | tf_op jit(solution)/shard_map/ppermute | solution.py:404
  429.5 11.7 %collective-permute-start.41 = (bf16[144,384]{1,0:T(8,128)(2,1)S(1)}, bf16[144,384]{1,0:T(8,128)(2,1)S(1)}, u32[]{:S(2)}, u32[]{:S(2)}) collective-permute-start(bf16[144,384]{1,0:T(8,128)(2,1)S(1)} %dynamic-slice_bitcast_fusion.2), channel_id=1, source_target_pairs={{0,4},{4,0},{1,5},{5,1},{2,6},{6,2},{3,7},{7,3},{8,12},{12,8},{9,1... | collective-permute-start | bytes 331784 | tf_op jit(solution)/shard_map/ppermute | solution.py:404
  432.9 12.1 %all-to-all-start.6 = ((bf16[32,2,864]{2,1,0:T(2,128)(2,1)}), bf16[32,2,864]{2,1,0:T(2,128)(2,1)S(1)}, u32[]{:S(2)}, u32[]{:S(2)}) async-start(bf16[32,2,864]{2,1,0:T(2,128)(2,1)} %reshape.594), calls=%async_computation.7 | async-start | bytes 229376 | tf_op jit(solution)/shard_map/all_to_all | solution.py:793
  436.9 44.4 %reduce-scatter.6.cloned.1.call-start = ((), (), s32[]{:S(2)}) async-start(), calls=%async_computation.11 | async-start | bytes 1843200 | tf_op jit(solution)/shard_map/reduce_scatter | solution.py:578
  448.1 10.1 %collective-permute-start.40 = (bf16[144,768]{1,0:T(8,128)(2,1)}, bf16[144,768]{1,0:T(8,128)(2,1)S(1)}, u32[]{:S(2)}, u32[]{:S(2)}) collective-permute-start(bf16[144,768]{1,0:T(8,128)(2,1)} %dynamic-slice_bitcast_fusion), channel_id=1, source_target_pairs={{0,4},{4,0},{1,5},{5,1},{2,6},{6,2},{3,7},{7,3},{8,12},{12,8},{9,1... | collective-permute-start | bytes 663560 | tf_op jit(solution)/shard_map/ppermute | solution.py:404
  462.7 8.6 %collective-permute-start.35 = (f32[18960]{0:T(1024)S(1)}, f32[18960]{0:T(1024)S(1)}, u32[]{:S(2)}, u32[]{:S(2)}) collective-permute-start(f32[18960]{0:T(1024)S(1)} %slice.232), channel_id=1, source_target_pairs={{0,1},{1,0},{2,3},{3,2},{4,5},{5,4},{6,7},{7,6},{8,9},{9,8},{10,11... | collective-permute-start | bytes 227528 | tf_op jit(solution)/shard_map/ppermute | solution.py:404
  471.3 7.3 %collective-permute-start.36 = (f32[18960]{0:T(1024)S(1)}, f32[18960]{0:T(1024)S(1)}, u32[]{:S(2)}, u32[]{:S(2)}) collective-permute-start(f32[18960]{0:T(1024)S(1)} %slice_add_fusion.8), channel_id=1, source_target_pairs={{0,2},{1,3},{2,0},{3,1},{4,6},{5,7},{6,4},{7,5},{8,10},{9,11},{10,... | collective-permute-start | bytes 227528 | tf_op jit(solution)/shard_map/ppermute | solution.py:404
  (73 other events, 624.8 us)
Sparse Core Ops, SparseCore 0:
  15.0 43.7 all-gather.6
  74.7 48.4 all-gather.8
  125.4 27.6 all-gather.10
  351.4 39.0 reduce-scatter.3
  393.4 35.1 reduce-scatter.7
  441.3 38.3 reduce-scatter.5

commit v6 on v5

--- a/solution.py
+++ b/solution.py
@@ -851,7 +851,7 @@
     joined = own_rows(g_down)
     g_down = joined(0, 1, ff_cols)[:, 0].T
     joined = own_rows(g_attn)
-    g_qkv = joined(0, 3, head_cols)
+    g_qkv = jnp.stack([joined(k * head_cols, 1, head_cols)[:, 0] for k in range(3)], axis=1)
     g_out = joined(3 * head_cols, 1, head_cols)[:, 0].T
     return (
         output,

time: 503 us -> 503 us (level)
    unnamed x146 -> x145, local copies, waits for them, and re-layouts: 26.2 us -> 25 us
where the time goes in v6:
time: 503 us; the launch traced here: 497 us
  waiting for transfers between devices  143 us (28%)
  Pallas kernels  140 us (28%)
  other arithmetic  64.1 us (13%)
  starting transfers between devices  63.3 us (13%)
  local copies, waits for them, and re-layouts  58.2 us (12%)
  between operations  16.1 us (3%)
  matrix products  12.2 us (2%)
    ppermute x42, waiting for transfers between devices, swap(): return lax.ppermute(values, name, [(i, i ^ bit) for i in range(count)])  69.1 us
    pallas_call x1, Pallas kernels, attn_backward(): pl.pallas_call(attn_backward_kernel, grid=(line,), in_specs=[resident(own...  36.6 us
    pallas_call x3, Pallas kernels, chip_products(): pl.pallas_call(functools.partial(grad_kernel, tuple((len(group) for group...  34.4 us
    ppermute x42, starting transfers between devices, swap(): return lax.ppermute(values, name, [(i, i ^ bit) for i in range(count)])  30.2 us
    reduce_scatter x3, waiting for transfers between devices, scatter_line(): return lax.psum_scatter(part, LINE, scatter_dimension=0, tiled=False)  27.5 us
    all_gather x3, waiting for transfers between devices, gather_line(): return lax.all_gather(piece, LINE, axis=0)  26.6 us
    unnamed x145, local copies, waits for them, and re-layouts  25 us
    pallas_call x1, Pallas kernels, ffn_backward(): pl.pallas_call(ffn_backward_kernel, grid=(line,), in_specs=[resident(own....  22.5 us
  transfers between devices with their start and end apart: 55, of which 22 were waited for; matrix products, arithmetic and copies ran while one was open for 20% of the time, Pallas kernels for 21%

profile of v6, /device:TPU:0, one launch (start us, length us, event | category | flops | bytes accessed | tf_op | source)
XLA Modules:
  0.0 496.6 jit_solution(3101522255768845800)
XLA Ops:
  15.5 5.2 %all-to-all-start = ((s32[8,2,8]{2,1,0:T(2,128)}), s32[8,2,8]{2,1,0:T(2,128)S(1)}, u32[]{:S(2)}, u32[]{:S(2)}) async-start(s32[8,2,8]{2,1,0:T(2,128)} %broadcast_in_dim.89), calls=%async_computation | async-start | bytes 16384 | tf_op jit(solution)/shard_map/all_to_all | solution.py:653
  21.1 4.3 all-to-all-done
  25.6 2.3 multiply_convert_fusion.1
  29.2 4.0 all-to-all-start.2
  33.2 25.6 %all-gather.7.cloned.1.call-done = bf16[1152,576]{1,0:T(8,128)(2,1)} async-done(((bf16[288,576]{1,0:T(8,128)(2,1)}), bf16[1152,576]{1,0:T(8,128)(2,1)}) %all-gather.7.cloned.1.call-update) | async-done | bytes 1327120 | tf_op jit(solution)/shard_map/all_gather | solution.py:466
  61.7 4.3 all-to-all-start.1
  68.0 5.7 %fusion.15 = (f32[4,256,144]{2,1,0:T(8,128)}, f32[4,256,144]{2,1,0:T(8,128)}) fusion(f32[144]{0:T(256)S(1)} %multiply_power_fusion, s32[4,256]{1,0:T(4,128)S(1)} %get-tuple-element.217, s32[4,256]{1,0:T(4,128)S(1)} %get-tuple-element.216, pred[144]{0:T(512)(128)(4,1)S(1)} %broadcast_compare_fusion.1), kind=kLoop, calls=%fused_computation.56 | loop fusion | flops 442368 | bytes 1188560 | tf_op jit(solution)/shard_map/sin | solution.py:43
  76.8 16.2 %collective-permute-done.1.x_ref = bf16[4,288,576]{2,1,0:T(8,128)(2,1)S(1)} collective-permute-done((bf16[4,288,576]{2,1,0:T(8,128)(2,1)}, bf16[4,288,576]{2,1,0:T(8,128)(2,1)S(1)}, u32[]{:S(2)}, u32[]{:S(2)}) %collective-permute-start.1) | collective-permute-done | bytes 1327136 | tf_op jit(solution)/shard_map/ppermute | solution.py:404
  100.0 11.8 %all-to-all-done.1 = bf16[4,2,64,1152]{3,2,1,0:T(8,128)(2,1)} async-done(((bf16[4,2,64,1152]{3,2,1,0:T(8,128)(2,1)}), bf16[4,2,64,1152]{3,2,1,0:T(8,128)(2,1)}, u32[]{:S(2)}, u32[]{:S(2)}) %all-to-all-start.1) | async-done | bytes 1179680 | tf_op jit(solution)/shard_map/all_to_all | solution.py:453
  111.8 2.4 copy.86
  126.9 2.9 shard_map.316
  129.8 2.5 copy-done.2
  132.4 21.9 %shard_map.317 = (bf16[4,1024,432]{2,1,0:T(8,128)(2,1)}, bf16[4,1024,144]{2,1,0:T(8,128)(2,1)}, bf16[2,256,1152]{2,1,0:T(8,128)(2,1)S(1)}, bf16[2,256,1152]{2,1,0:T(8,128)(2,1)}) custom-call(bf16[2,256,1152]{2,1,0:T(8,128)(2,1)} %copy-done.4, bf16[2,256,1152]{2,1,0:T(8,128)(2,1)} %collective-permute-done.6.peer_ref, bf16[4,1152,576]{2,1,0:T(8,128)(2,1)} %bitcast.194, ...), custom_call_target="tpu_custom_call" | custom-call | flops 7583301632 | bytes 14745600 | tf_op jit(solution)/shard_map/pallas_call | solution.py:248
  154.4 4.5 all-to-all-start.3
  161.1 3.0 collective-permute-done.7.x_ref
  168.0 2.5 multiply_reduce_fusion.3
  170.9 15.3 %collective-permute-done.10.da_ref = bf16[2,288,768]{2,1,0:T(8,128)(2,1)S(1)} collective-permute-done((bf16[2,288,768]{2,1,0:T(8,128)(2,1)S(1)}, bf16[2,288,768]{2,1,0:T(8,128)(2,1)S(1)}, u32[]{:S(2)}, u32[]{:S(2)}) %collective-permute-start.10) | collective-permute-done | bytes 884768 | tf_op jit(solution)/shard_map/ppermute | solution.py:404
  195.3 2.9 shard_map.318
  198.2 2.9 copy-done.1
  201.1 8.1 %shard_map.319 = (bf16[4,1024,768]{2,1,0:T(8,128)(2,1)}, bf16[4,1024,384]{2,1,0:T(8,128)(2,1)}) custom-call(bf16[2,256,1152]{2,1,0:T(8,128)(2,1)S(1)} %add_convert_fusion.3.refs_0_, bf16[2,256,1152]{2,1,0:T(8,128)(2,1)S(1)} %collective-permute-done.14.refs_1_, bf16[4,1152,768]{2,1,0:T(8,128)(2,1)} %bitcast.190, f32[4,1,768]{2,1,0:T(1,128)S(1)} %bitcast.210), custom_call_target="tpu_custom_call" | custom-call | flops 3623878656 | bytes 9830400 | tf_op jit(solution)/shard_map/pallas_call | solution.py:312
  215.4 7.7 %shard_map.320 = (bf16[4,1024,768]{2,1,0:T(8,128)(2,1)}, bf16[4,1024,384]{2,1,0:T(8,128)(2,1)}) custom-call(bf16[2,256,1152]{2,1,0:T(8,128)(2,1)S(1)} %add_convert_fusion.3.refs_0_, bf16[2,256,1152]{2,1,0:T(8,128)(2,1)S(1)} %collective-permute-done.14.refs_1_, bf16[4,1152,768]{2,1,0:T(8,128)(2,1)} %bitcast.191, ...), custom_call_target="tpu_custom_call", output_to_operand_aliasing={{0}: (4, {}), {1}: (5, {})} | custom-call | flops 3623878656 | bytes 9830400 | tf_op jit(solution)/shard_map/pallas_call | solution.py:312
  223.1 2.8 shard_map.321
  228.6 22.5 %shard_map.322 = (bf16[4,1024,768]{2,1,0:T(8,128)(2,1)}, bf16[2,256,1152]{2,1,0:T(8,128)(2,1)S(1)}, bf16[2,256,1152]{2,1,0:T(8,128)(2,1)S(1)}, f32[4,1,768]{2,1,0:T(1,128)S(1)}) custom-call(bf16[2,256,1152]{2,1,0:T(8,128)(2,1)S(1)} %fusion.11.own_ref, bf16[2,256,1152]{2,1,0:T(8,128)(2,1)} %copy-done.39, bf16[4,1152,384]{2,1,0:T(8,128)(2,1)} %bitcast.198, ...), custom_call_target="tpu_custom_call" | custom-call | flops 10871635968 | bytes 26738688 | tf_op jit(solution)/shard_map/pallas_call | solution.py:375
  251.2 11.7 %shard_map.323 = (bf16[4,144,768]{2,1,0:T(8,128)(2,1)S(1)}, bf16[4,144,768]{2,1,0:T(8,128)(2,1)S(1)}, bf16[4,288,768]{2,1,0:T(8,128)(2,1)}, bf16[4,288,768]{2,1,0:T(8,128)(2,1)}, bf16[4,288,768]{2,1,0:T(8,128)(2,1)}) custom-call(s32[4]{0:T(128)S(1)} %broadcast_xor_fusion.spot_ref, bf16[512,1152]{1,0:T(8,128)(2,1)S(1)} %bitcast.193, ...), custom_call_target="tpu_custom_call" | custom-call | flops 905969664 | bytes 13369344 | tf_op jit(solution)/shard_map/pallas_call | solution.py:535
  264.4 8.7 %shard_map.324 = (bf16[4,144,384]{2,1,0:T(8,128)(2,1)S(1)}, bf16[4,144,384]{2,1,0:T(8,128)(2,1)S(1)}, bf16[4,288,384]{2,1,0:T(8,128)(2,1)S(1)}, bf16[4,288,384]{2,1,0:T(8,128)(2,1)S(1)}, bf16[4,288,384]{2,1,0:T(8,128)(2,1)S(1)}) custom-call(s32[4]{0:T(128)S(1)} %broadcast_xor_fusion.spot_ref, bf16[512,1152]{1,0:T(8,128)(2,1)} %fusion.13.refs_0_, ...), custom_call_target="tpu_custom_call" | custom-call | flops 452984832 | bytes 6684672 | tf_op jit(solution)/shard_map/pallas_call | solution.py:535
  275.7 6.1 %convolution_bitcast_fusion = f32[1024,1152]{1,0:T(8,128)S(1)} fusion(bf16[4,1024,384]{2,1,0:T(8,128)(2,1)} %get-tuple-element.119.refs_2_, bf16[4,1152,384]{2,1,0:T(8,128)(2,1)S(1)} %bitcast.199), kind=kOutput, calls=%fused_computation.5 | convolution fusion | flops 3623878656 | bytes 11403264 | tf_op jit(solution)/shard_map/zrf,zdf->rd/dot_general | solution.py:744
  282.1 3.5 collective-permute-done.21
  291.9 2.2 multiply_reduce_fusion.4
  294.6 2.3 copy-done.36
  303.9 5.4 %all-to-all-start.4 = ((bf16[4,2,64,1152]{3,2,1,0:T(8,128)(2,1)}), bf16[4,2,64,1152]{3,2,1,0:T(8,128)(2,1)}, u32[]{:S(2)}, u32[]{:S(2)}) async-start(bf16[4,2,64,1152]{3,2,1,0:T(8,128)(2,1)} %bitcast.185), calls=%async_computation.4 | async-start | bytes 2359296 | tf_op jit(solution)/shard_map/all_to_all | solution.py:461
  310.6 36.6 %shard_map.325 = (bf16[4,1024,432]{2,1,0:T(8,128)(2,1)}, bf16[2,256,1152]{2,1,0:T(8,128)(2,1)S(1)}, bf16[2,256,1152]{2,1,0:T(8,128)(2,1)}, f32[4,1,432]{2,1,0:T(1,128)S(1)}, f32[2,144]{1,0:T(2,128)S(1)}) custom-call(bf16[2,256,1152]{2,1,0:T(8,128)(2,1)} %copy-done.32, bf16[2,256,1152]{2,1,0:T(8,128)(2,1)} %collective-permute-done.24.peer_ref, ...), custom_call_target="tpu_custom_call" | custom-call | flops 10804527104 | bytes 14745600 | tf_op jit(solution)/shard_map/pallas_call | solution.py:272
  347.2 4.1 add_convert_fusion
  354.7 13.9 %shard_map.326 = (bf16[4,144,576]{2,1,0:T(8,128)(2,1)}, bf16[4,144,576]{2,1,0:T(8,128)(2,1)}, bf16[4,288,576]{2,1,0:T(8,128)(2,1)}, bf16[4,288,576]{2,1,0:T(8,128)(2,1)}, bf16[4,288,576]{2,1,0:T(8,128)(2,1)}) custom-call(s32[4]{0:T(128)S(1)} %broadcast_xor_fusion.spot_ref, bf16[512,1152]{1,0:T(8,128)(2,1)S(1)} %bitcast.197, ...), custom_call_target="tpu_custom_call" | custom-call | flops 679477248 | bytes 10027008 | tf_op jit(solution)/shard_map/pallas_call | solution.py:535
  371.7 2.9 fusion.10
  374.6 2.6 fusion.8
  378.4 5.1 %all-to-all-start.5 = ((bf16[4,2,64,1152]{3,2,1,0:T(8,128)(2,1)}), bf16[4,2,64,1152]{3,2,1,0:T(8,128)(2,1)S(1)}, u32[]{:S(2)}, u32[]{:S(2)}) async-start(bf16[4,2,64,1152]{3,2,1,0:T(8,128)(2,1)} %bitcast.214), calls=%async_computation.6 | async-start | bytes 2359296 | tf_op jit(solution)/shard_map/all_to_all | solution.py:461
  383.5 2.7 add_convert_fusion.4
  386.2 5.1 %collective-permute-done.28 = bf16[4,144,576]{2,1,0:T(8,128)(2,1)} collective-permute-done((bf16[4,144,576]{2,1,0:T(8,128)(2,1)}, bf16[4,144,576]{2,1,0:T(8,128)(2,1)}, u32[]{:S(2)}, u32[]{:S(2)}) %collective-permute-start.28) | collective-permute-done | bytes 663584 | tf_op jit(solution)/shard_map/ppermute | solution.py:404
  398.6 2.6 collective-permute-start.37
  401.2 27.5 %reduce-scatter.8.cloned.1.call-done = bf16[1,288,384]{2,1,0:T(8,128)(2,1)} async-done(((bf16[4,288,384]{2,1,0:T(8,128)(2,1)}), bf16[1,288,384]{2,1,0:T(8,128)(2,1)}) %reduce-scatter.8.cloned.1.call-update) | async-done | bytes 221200 | tf_op jit(solution)/shard_map/reduce_scatter | solution.py:578
  432.9 3.9 all-to-all-start.6
  437.3 3.9 add_convert_fusion.1
  441.3 3.7 all-to-all-done.6
  453.7 3.7 collective-permute-done.33
  458.5 4.2 collective-permute-done.34
  465.0 6.3 %collective-permute-done.35 = f32[18960]{0:T(1024)S(1)} collective-permute-done((f32[18960]{0:T(1024)S(1)}, f32[18960]{0:T(1024)S(1)}, u32[]{:S(2)}, u32[]{:S(2)}) %collective-permute-start.35) | collective-permute-done | bytes 75872 | tf_op jit(solution)/shard_map/ppermute | solution.py:404
  473.2 5.5 %collective-permute-done.36 = f32[18960]{0:T(1024)S(1)} collective-permute-done((f32[18960]{0:T(1024)S(1)}, f32[18960]{0:T(1024)S(1)}, u32[]{:S(2)}, u32[]{:S(2)}) %collective-permute-start.36) | collective-permute-done | bytes 75872 | tf_op jit(solution)/shard_map/ppermute | solution.py:404
  486.9 2.4 copy.127
  (402 shorter events, 122.8 us)
Async XLA Ops:
  7.2 51.6 %all-gather.7.cloned.1.call-start = ((), (), s32[]{:S(2)}) async-start(), calls=%async_computation.13 | async-start | bytes 1843200 | tf_op jit(solution)/shard_map/all_gather | solution.py:466
  15.5 9.9 %all-to-all-start = ((s32[8,2,8]{2,1,0:T(2,128)}), s32[8,2,8]{2,1,0:T(2,128)S(1)}, u32[]{:S(2)}, u32[]{:S(2)}) async-start(s32[8,2,8]{2,1,0:T(2,128)} %broadcast_in_dim.89), calls=%async_computation | async-start | bytes 16384 | tf_op jit(solution)/shard_map/all_to_all | solution.py:653
  29.2 32.5 %all-to-all-start.2 = ((f32[32,1,2028]{2,1,0:T(1,128)}), f32[32,1,2028]{2,1,0:T(1,128)S(1)}, u32[]{:S(2)}, u32[]{:S(2)}) async-start(f32[32,1,2028]{2,1,0:T(1,128)} %all_to_all.31), calls=%async_computation.2 | async-start | bytes 524288 | tf_op jit(solution)/shard_map/all_to_all | solution.py:672
  58.8 34.2 %collective-permute-start.1 = (bf16[4,288,576]{2,1,0:T(8,128)(2,1)}, bf16[4,288,576]{2,1,0:T(8,128)(2,1)S(1)}, u32[]{:S(2)}, u32[]{:S(2)}) collective-permute-start(bf16[4,288,576]{2,1,0:T(8,128)(2,1)} %bitcast.203), channel_id=1, source_target_pairs={{0,8},{8,0},{16,24},{24,16},{1,9},{9,1},{17,25},{25,17},{2,10},{10... | collective-permute-start | bytes 3981320 | tf_op jit(solution)/shard_map/ppermute | solution.py:404
  60.3 34.1 %collective-permute-start.2 = (bf16[4,288,576]{2,1,0:T(8,128)(2,1)}, bf16[4,288,576]{2,1,0:T(8,128)(2,1)}, u32[]{:S(2)}, u32[]{:S(2)}) collective-permute-start(bf16[4,288,576]{2,1,0:T(8,128)(2,1)} %bitcast.204), channel_id=1, source_target_pairs={{0,16},{8,24},{16,0},{24,8},{1,17},{9,25},{17,1},{25,9},{2,18},{10... | collective-permute-start | bytes 3981320 | tf_op jit(solution)/shard_map/ppermute | solution.py:404
  61.7 50.0 %all-to-all-start.1 = ((bf16[4,2,64,1152]{3,2,1,0:T(8,128)(2,1)}), bf16[4,2,64,1152]{3,2,1,0:T(8,128)(2,1)}, u32[]{:S(2)}, u32[]{:S(2)}) async-start(bf16[4,2,64,1152]{3,2,1,0:T(8,128)(2,1)} %bitcast.218), calls=%async_computation.1 | async-start | bytes 2359296 | tf_op jit(solution)/shard_map/all_to_all | solution.py:453
  66.0 57.2 %all-gather.9.cloned.1.call-start = ((), (), s32[]{:S(2)}) async-start(), calls=%async_computation.14 | async-start | bytes 2211840 | tf_op jit(solution)/shard_map/all_gather | solution.py:466
  74.6 84.3 %all-gather.11.cloned.1.call-start = ((), (), s32[]{:S(2)}) async-start(), calls=%async_computation.15 | async-start | bytes 1474560 | tf_op jit(solution)/shard_map/all_gather | solution.py:466
  95.3 18.9 %collective-permute-start.4 = (bf16[2,288,576]{2,1,0:T(8,128)(2,1)}, bf16[2,288,576]{2,1,0:T(8,128)(2,1)S(1)}, u32[]{:S(2)}, u32[]{:S(2)}) collective-permute-start(bf16[2,288,576]{2,1,0:T(8,128)(2,1)} %slice.176), channel_id=1, source_target_pairs={{0,16},{8,24},{16,0},{24,8},{1,17},{9,25},{17,1},{25,9},{2,18},{10... | collective-permute-start | bytes 1990664 | tf_op jit(solution)/shard_map/ppermute | solution.py:404
  98.8 17.1 %collective-permute-start.5 = (bf16[2,288,576]{2,1,0:T(8,128)(2,1)}, bf16[2,288,576]{2,1,0:T(8,128)(2,1)}, u32[]{:S(2)}, u32[]{:S(2)}) collective-permute-start(bf16[2,288,576]{2,1,0:T(8,128)(2,1)} %slice.177), channel_id=1, source_target_pairs={{0,8},{8,0},{16,24},{24,16},{1,9},{9,1},{17,25},{25,17},{2,10},{10... | collective-permute-start | bytes 1990664 | tf_op jit(solution)/shard_map/ppermute | solution.py:404
  119.2 13.2 %collective-permute-start.6 = (bf16[2,256,1152]{2,1,0:T(8,128)(2,1)S(1)}, bf16[2,256,1152]{2,1,0:T(8,128)(2,1)}, u32[]{:S(2)}, u32[]{:S(2)}) collective-permute-start(bf16[2,256,1152]{2,1,0:T(8,128)(2,1)S(1)} %fusion.3.own_ref), channel_id=1, source_target_pairs={{0,4},{4,0},{1,5},{5,1},{2,6},{6,2},{3,7},{7,3},{8,12},{12,8},{9,1... | collective-permute-start | bytes 3538952 | tf_op jit(solution)/shard_map/ppermute | solution.py:404
  123.3 40.9 %collective-permute-start.7 = (bf16[4,288,768]{2,1,0:T(8,128)(2,1)}, bf16[4,288,768]{2,1,0:T(8,128)(2,1)}, u32[]{:S(2)}, u32[]{:S(2)}) collective-permute-start(bf16[4,288,768]{2,1,0:T(8,128)(2,1)} %bitcast.200), channel_id=1, source_target_pairs={{0,8},{8,0},{16,24},{24,16},{1,9},{9,1},{17,25},{25,17},{2,10},{10... | collective-permute-start | bytes 5308424 | tf_op jit(solution)/shard_map/ppermute | solution.py:404
  123.8 42.2 %collective-permute-start.8 = (bf16[4,288,768]{2,1,0:T(8,128)(2,1)}, bf16[4,288,768]{2,1,0:T(8,128)(2,1)}, u32[]{:S(2)}, u32[]{:S(2)}) collective-permute-start(bf16[4,288,768]{2,1,0:T(8,128)(2,1)} %bitcast.201), channel_id=1, source_target_pairs={{0,16},{8,24},{16,0},{24,8},{1,17},{9,25},{17,1},{25,9},{2,18},{10... | collective-permute-start | bytes 5308424 | tf_op jit(solution)/shard_map/ppermute | solution.py:404
  154.3 13.6 %collective-permute-start.9 = (bf16[2,256,1152]{2,1,0:T(8,128)(2,1)}, bf16[2,256,1152]{2,1,0:T(8,128)(2,1)S(1)}, u32[]{:S(2)}, u32[]{:S(2)}) collective-permute-start(bf16[2,256,1152]{2,1,0:T(8,128)(2,1)} %get-tuple-element.95), channel_id=1, source_target_pairs={{0,4},{4,0},{1,5},{5,1},{2,6},{6,2},{3,7},{7,3},{8,12},{12,8},{9,1... | collective-permute-start | bytes 3538952 | tf_op jit(solution)/shard_map/ppermute | solution.py:404
  154.4 36.4 %all-to-all-start.3 = ((bf16[4,2,64,1152]{3,2,1,0:T(8,128)(2,1)}), bf16[4,2,64,1152]{3,2,1,0:T(8,128)(2,1)}, u32[]{:S(2)}, u32[]{:S(2)}) async-start(bf16[4,2,64,1152]{3,2,1,0:T(8,128)(2,1)} %bitcast.219), calls=%async_computation.3 | async-start | bytes 2359296 | tf_op jit(solution)/shard_map/all_to_all | solution.py:453
  165.4 20.8 %collective-permute-start.10 = (bf16[2,288,768]{2,1,0:T(8,128)(2,1)S(1)}, bf16[2,288,768]{2,1,0:T(8,128)(2,1)S(1)}, u32[]{:S(2)}, u32[]{:S(2)}) collective-permute-start(bf16[2,288,768]{2,1,0:T(8,128)(2,1)S(1)} %slice.239), channel_id=1, source_target_pairs={{0,16},{8,24},{16,0},{24,8},{1,17},{9,25},{17,1},{25,9},{2,18},{10... | collective-permute-start | bytes 2654216 | tf_op jit(solution)/shard_map/ppermute | solution.py:404
  167.3 20.6 %collective-permute-start.11 = (bf16[2,288,768]{2,1,0:T(8,128)(2,1)S(1)}, bf16[2,288,768]{2,1,0:T(8,128)(2,1)S(1)}, u32[]{:S(2)}, u32[]{:S(2)}) collective-permute-start(bf16[2,288,768]{2,1,0:T(8,128)(2,1)S(1)} %slice.240), channel_id=1, source_target_pairs={{0,8},{8,0},{16,24},{24,16},{1,9},{9,1},{17,25},{25,17},{2,10},{10... | collective-permute-start | bytes 2654216 | tf_op jit(solution)/shard_map/ppermute | solution.py:404
  170.9 30.2 %collective-permute-start.14 = (bf16[2,256,1152]{2,1,0:T(8,128)(2,1)S(1)}, bf16[2,256,1152]{2,1,0:T(8,128)(2,1)S(1)}, u32[]{:S(2)}, u32[]{:S(2)}) collective-permute-start(bf16[2,256,1152]{2,1,0:T(8,128)(2,1)S(1)} %add_convert_fusion.3.refs_0_), channel_id=1, source_target_pairs={{0,4},{4,0},{1,5},{5,1},{2,6},{6,2},{3,7},{7,3},{8,12},{12,8},{9,1... | collective-permute-start | bytes 3538952 | tf_op jit(solution)/shard_map/ppermute | solution.py:404
  188.8 20.4 %collective-permute-start.12 = (bf16[4,288,384]{2,1,0:T(8,128)(2,1)}, bf16[4,288,384]{2,1,0:T(8,128)(2,1)}, u32[]{:S(2)}, u32[]{:S(2)}) collective-permute-start(bf16[4,288,384]{2,1,0:T(8,128)(2,1)} %slice.244.own_ref), channel_id=1, source_target_pairs={{0,8},{8,0},{16,24},{24,16},{1,9},{9,1},{17,25},{25,17},{2,10},{10... | collective-permute-start | bytes 2654216 | tf_op jit(solution)/shard_map/ppermute | solution.py:404
  189.4 19.8 %collective-permute-start.13 = (bf16[4,288,384]{2,1,0:T(8,128)(2,1)}, bf16[4,288,384]{2,1,0:T(8,128)(2,1)}, u32[]{:S(2)}, u32[]{:S(2)}) collective-permute-start(bf16[4,288,384]{2,1,0:T(8,128)(2,1)} %slice.244.own_ref), channel_id=1, source_target_pairs={{0,16},{8,24},{16,0},{24,8},{1,17},{9,25},{17,1},{25,9},{2,18},{10... | collective-permute-start | bytes 2654216 | tf_op jit(solution)/shard_map/ppermute | solution.py:404
  192.6 35.0 %collective-permute-start.15 = (bf16[2,256,1152]{2,1,0:T(8,128)(2,1)S(1)}, bf16[2,256,1152]{2,1,0:T(8,128)(2,1)S(1)}, u32[]{:S(2)}, u32[]{:S(2)}) collective-permute-start(bf16[2,256,1152]{2,1,0:T(8,128)(2,1)S(1)} %fusion.11.own_ref), channel_id=1, source_target_pairs={{0,4},{4,0},{1,5},{5,1},{2,6},{6,2},{3,7},{7,3},{8,12},{12,8},{9,1... | collective-permute-start | bytes 3538952 | tf_op jit(solution)/shard_map/ppermute | solution.py:404
  211.3 11.8 %collective-permute-start.16 = (bf16[2,288,384]{2,1,0:T(8,128)(2,1)S(1)}, bf16[2,288,384]{2,1,0:T(8,128)(2,1)S(1)}, u32[]{:S(2)}, u32[]{:S(2)}) collective-permute-start(bf16[2,288,384]{2,1,0:T(8,128)(2,1)S(1)} %slice.190), channel_id=1, source_target_pairs={{0,16},{8,24},{16,0},{24,8},{1,17},{9,25},{17,1},{25,9},{2,18},{10... | collective-permute-start | bytes 1327112 | tf_op jit(solution)/shard_map/ppermute | solution.py:404
  212.7 10.4 %collective-permute-start.17 = (bf16[2,288,384]{2,1,0:T(8,128)(2,1)S(1)}, bf16[2,288,384]{2,1,0:T(8,128)(2,1)S(1)}, u32[]{:S(2)}, u32[]{:S(2)}) collective-permute-start(bf16[2,288,384]{2,1,0:T(8,128)(2,1)S(1)} %slice.191), channel_id=1, source_target_pairs={{0,8},{8,0},{16,24},{24,16},{1,9},{9,1},{17,25},{25,17},{2,10},{10... | collective-permute-start | bytes 1327112 | tf_op jit(solution)/shard_map/ppermute | solution.py:404
  262.9 22.7 %collective-permute-start.21 = (bf16[4,144,768]{2,1,0:T(8,128)(2,1)S(1)}, bf16[4,144,768]{2,1,0:T(8,128)(2,1)}, u32[]{:S(2)}, u32[]{:S(2)}) collective-permute-start(bf16[4,144,768]{2,1,0:T(8,128)(2,1)S(1)} %get-tuple-element.109), channel_id=1, source_target_pairs={{0,16},{8,24},{16,0},{24,8},{1,17},{9,25},{17,1},{25,9},{2,18},{10... | collective-permute-start | bytes 2654216 | tf_op jit(solution)/shard_map/ppermute | solution.py:404
  263.5 25.6 %collective-permute-start.20 = (bf16[4,144,768]{2,1,0:T(8,128)(2,1)S(1)}, bf16[4,144,768]{2,1,0:T(8,128)(2,1)}, u32[]{:S(2)}, u32[]{:S(2)}) collective-permute-start(bf16[4,144,768]{2,1,0:T(8,128)(2,1)S(1)} %get-tuple-element.108), channel_id=1, source_target_pairs={{0,8},{8,0},{16,24},{24,16},{1,9},{9,1},{17,25},{25,17},{2,10},{10... | collective-permute-start | bytes 2654216 | tf_op jit(solution)/shard_map/ppermute | solution.py:404
  273.1 27.5 %collective-permute-start.22 = (bf16[4,144,384]{2,1,0:T(8,128)(2,1)S(1)}, bf16[4,144,384]{2,1,0:T(8,128)(2,1)S(1)}, u32[]{:S(2)}, u32[]{:S(2)}) collective-permute-start(bf16[4,144,384]{2,1,0:T(8,128)(2,1)S(1)} %get-tuple-element.114), channel_id=1, source_target_pairs={{0,8},{8,0},{16,24},{24,16},{1,9},{9,1},{17,25},{25,17},{2,10},{10... | collective-permute-start | bytes 1327112 | tf_op jit(solution)/shard_map/ppermute | solution.py:404
  274.4 26.3 %collective-permute-start.23 = (bf16[4,144,384]{2,1,0:T(8,128)(2,1)S(1)}, bf16[4,144,384]{2,1,0:T(8,128)(2,1)S(1)}, u32[]{:S(2)}, u32[]{:S(2)}) collective-permute-start(bf16[4,144,384]{2,1,0:T(8,128)(2,1)S(1)} %get-tuple-element.115), channel_id=1, source_target_pairs={{0,16},{8,24},{16,0},{24,8},{1,17},{9,25},{17,1},{25,9},{2,18},{10... | collective-permute-start | bytes 1327112 | tf_op jit(solution)/shard_map/ppermute | solution.py:404
  275.7 12.5 %collective-permute-start.19 = (bf16[2,256,1152]{2,1,0:T(8,128)(2,1)S(1)}, bf16[2,256,1152]{2,1,0:T(8,128)(2,1)S(1)}, u32[]{:S(2)}, u32[]{:S(2)}) collective-permute-start(bf16[2,256,1152]{2,1,0:T(8,128)(2,1)S(1)} %get-tuple-element.121), channel_id=1, source_target_pairs={{0,4},{4,0},{1,5},{5,1},{2,6},{6,2},{3,7},{7,3},{8,12},{12,8},{9,1... | collective-permute-start | bytes 3538952 | tf_op jit(solution)/shard_map/ppermute | solution.py:404
  288.3 58.9 %collective-permute-start.27 = (bf16[4,288,768]{2,1,0:T(8,128)(2,1)}, bf16[4,288,768]{2,1,0:T(8,128)(2,1)}, u32[]{:S(2)}, u32[]{:S(2)}) collective-permute-start(bf16[4,288,768]{2,1,0:T(8,128)(2,1)} %pad_maximum_fusion.1), channel_id=1, source_target_pairs={{0,8},{8,0},{16,24},{24,16},{1,9},{9,1},{17,25},{25,17},{2,10},{10... | collective-permute-start | bytes 5308424 | tf_op jit(solution)/shard_map/ppermute | solution.py:404
  294.4 15.0 %collective-permute-start.24 = (bf16[2,256,1152]{2,1,0:T(8,128)(2,1)S(1)}, bf16[2,256,1152]{2,1,0:T(8,128)(2,1)}, u32[]{:S(2)}, u32[]{:S(2)}) collective-permute-start(bf16[2,256,1152]{2,1,0:T(8,128)(2,1)S(1)} %multiply_convert_fusion.own_ref), channel_id=1, source_target_pairs={{0,4},{4,0},{1,5},{5,1},{2,6},{6,2},{3,7},{7,3},{8,12},{12,8},{9,1... | collective-permute-start | bytes 3538952 | tf_op jit(solution)/shard_map/ppermute | solution.py:404
  299.7 47.5 %collective-permute-start.26 = (bf16[4,288,768]{2,1,0:T(8,128)(2,1)}, bf16[4,288,768]{2,1,0:T(8,128)(2,1)}, u32[]{:S(2)}, u32[]{:S(2)}) collective-permute-start(bf16[4,288,768]{2,1,0:T(8,128)(2,1)} %pad_maximum_fusion), channel_id=1, source_target_pairs={{0,16},{8,24},{16,0},{24,8},{1,17},{9,25},{17,1},{25,9},{2,18},{10... | collective-permute-start | bytes 5308424 | tf_op jit(solution)/shard_map/ppermute | solution.py:404
  303.9 50.7 %all-to-all-start.4 = ((bf16[4,2,64,1152]{3,2,1,0:T(8,128)(2,1)}), bf16[4,2,64,1152]{3,2,1,0:T(8,128)(2,1)}, u32[]{:S(2)}, u32[]{:S(2)}) async-start(bf16[4,2,64,1152]{3,2,1,0:T(8,128)(2,1)} %bitcast.185), calls=%async_computation.4 | async-start | bytes 2359296 | tf_op jit(solution)/shard_map/all_to_all | solution.py:461
  309.4 82.5 %reduce-scatter.4.cloned.1.call-start = ((), (), s32[]{:S(2)}) async-start(), calls=%async_computation.10 | async-start | bytes 2211840 | tf_op jit(solution)/shard_map/reduce_scatter | solution.py:578
  351.3 20.3 %collective-permute-start.25 = (bf16[2,256,1152]{2,1,0:T(8,128)(2,1)}, bf16[2,256,1152]{2,1,0:T(8,128)(2,1)}, u32[]{:S(2)}, u32[]{:S(2)}) collective-permute-start(bf16[2,256,1152]{2,1,0:T(8,128)(2,1)} %get-tuple-element.128), channel_id=1, source_target_pairs={{0,4},{4,0},{1,5},{5,1},{2,6},{6,2},{3,7},{7,3},{8,12},{12,8},{9,1... | collective-permute-start | bytes 3538952 | tf_op jit(solution)/shard_map/ppermute | solution.py:404
  353.2 24.1 %collective-permute-start.31 = (bf16[4,288,384]{2,1,0:T(8,128)(2,1)}, bf16[4,288,384]{2,1,0:T(8,128)(2,1)}, u32[]{:S(2)}, u32[]{:S(2)}) collective-permute-start(bf16[4,288,384]{2,1,0:T(8,128)(2,1)} %pad_maximum_fusion.5), channel_id=1, source_target_pairs={{0,8},{8,0},{16,24},{24,16},{1,9},{9,1},{17,25},{25,17},{2,10},{10... | collective-permute-start | bytes 2654216 | tf_op jit(solution)/shard_map/ppermute | solution.py:404
  354.1 23.1 %collective-permute-start.30 = (bf16[4,288,384]{2,1,0:T(8,128)(2,1)}, bf16[4,288,384]{2,1,0:T(8,128)(2,1)}, u32[]{:S(2)}, u32[]{:S(2)}) collective-permute-start(bf16[4,288,384]{2,1,0:T(8,128)(2,1)} %pad_maximum_fusion.4), channel_id=1, source_target_pairs={{0,16},{8,24},{16,0},{24,8},{1,17},{9,25},{17,1},{25,9},{2,18},{10... | collective-permute-start | bytes 2654216 | tf_op jit(solution)/shard_map/ppermute | solution.py:404
  368.6 22.7 %collective-permute-start.28 = (bf16[4,144,576]{2,1,0:T(8,128)(2,1)}, bf16[4,144,576]{2,1,0:T(8,128)(2,1)}, u32[]{:S(2)}, u32[]{:S(2)}) collective-permute-start(bf16[4,144,576]{2,1,0:T(8,128)(2,1)} %get-tuple-element.134), channel_id=1, source_target_pairs={{0,8},{8,0},{16,24},{24,16},{1,9},{9,1},{17,25},{25,17},{2,10},{10... | collective-permute-start | bytes 1990664 | tf_op jit(solution)/shard_map/ppermute | solution.py:404
  369.7 22.2 %collective-permute-start.29 = (bf16[4,144,576]{2,1,0:T(8,128)(2,1)}, bf16[4,144,576]{2,1,0:T(8,128)(2,1)}, u32[]{:S(2)}, u32[]{:S(2)}) collective-permute-start(bf16[4,144,576]{2,1,0:T(8,128)(2,1)} %get-tuple-element.135), channel_id=1, source_target_pairs={{0,16},{8,24},{16,0},{24,8},{1,17},{9,25},{17,1},{25,9},{2,18},{10... | collective-permute-start | bytes 1990664 | tf_op jit(solution)/shard_map/ppermute | solution.py:404
  378.4 51.3 %all-to-all-start.5 = ((bf16[4,2,64,1152]{3,2,1,0:T(8,128)(2,1)}), bf16[4,2,64,1152]{3,2,1,0:T(8,128)(2,1)S(1)}, u32[]{:S(2)}, u32[]{:S(2)}) async-start(bf16[4,2,64,1152]{3,2,1,0:T(8,128)(2,1)} %bitcast.214), calls=%async_computation.6 | async-start | bytes 2359296 | tf_op jit(solution)/shard_map/all_to_all | solution.py:461
  383.4 45.2 %reduce-scatter.8.cloned.1.call-start = ((), (), s32[]{:S(2)}) async-start(), calls=%async_computation.12 | async-start | bytes 1105920 | tf_op jit(solution)/shard_map/reduce_scatter | solution.py:578
  394.9 42.4 %collective-permute-start.38 = (bf16[4,288,576]{2,1,0:T(8,128)(2,1)}, bf16[4,288,576]{2,1,0:T(8,128)(2,1)}, u32[]{:S(2)}, u32[]{:S(2)}) collective-permute-start(bf16[4,288,576]{2,1,0:T(8,128)(2,1)} %pad_maximum_fusion.3), channel_id=1, source_target_pairs={{0,8},{8,0},{16,24},{24,16},{1,9},{9,1},{17,25},{25,17},{2,10},{10... | collective-permute-start | bytes 3981320 | tf_op jit(solution)/shard_map/ppermute | solution.py:404
  398.6 38.7 %collective-permute-start.37 = (bf16[4,288,576]{2,1,0:T(8,128)(2,1)}, bf16[4,288,576]{2,1,0:T(8,128)(2,1)}, u32[]{:S(2)}, u32[]{:S(2)}) collective-permute-start(bf16[4,288,576]{2,1,0:T(8,128)(2,1)} %pad_maximum_fusion.2), channel_id=1, source_target_pairs={{0,16},{8,24},{16,0},{24,8},{1,17},{9,25},{17,1},{25,9},{2,18},{10... | collective-permute-start | bytes 3981320 | tf_op jit(solution)/shard_map/ppermute | solution.py:404
  429.5 11.7 %collective-permute-start.41 = (bf16[144,384]{1,0:T(8,128)(2,1)S(1)}, bf16[144,384]{1,0:T(8,128)(2,1)S(1)}, u32[]{:S(2)}, u32[]{:S(2)}) collective-permute-start(bf16[144,384]{1,0:T(8,128)(2,1)S(1)} %dynamic-slice_bitcast_fusion.2), channel_id=1, source_target_pairs={{0,4},{4,0},{1,5},{5,1},{2,6},{6,2},{3,7},{7,3},{8,12},{12,8},{9,1... | collective-permute-start | bytes 331784 | tf_op jit(solution)/shard_map/ppermute | solution.py:404
  432.9 12.1 %all-to-all-start.6 = ((bf16[32,2,864]{2,1,0:T(2,128)(2,1)}), bf16[32,2,864]{2,1,0:T(2,128)(2,1)S(1)}, u32[]{:S(2)}, u32[]{:S(2)}) async-start(bf16[32,2,864]{2,1,0:T(2,128)(2,1)} %reshape.610), calls=%async_computation.7 | async-start | bytes 229376 | tf_op jit(solution)/shard_map/all_to_all | solution.py:793
  436.9 44.4 %reduce-scatter.6.cloned.1.call-start = ((), (), s32[]{:S(2)}) async-start(), calls=%async_computation.11 | async-start | bytes 1843200 | tf_op jit(solution)/shard_map/reduce_scatter | solution.py:578
  448.2 10.1 %collective-permute-start.40 = (bf16[144,768]{1,0:T(8,128)(2,1)}, bf16[144,768]{1,0:T(8,128)(2,1)S(1)}, u32[]{:S(2)}, u32[]{:S(2)}) collective-permute-start(bf16[144,768]{1,0:T(8,128)(2,1)} %dynamic-slice_bitcast_fusion), channel_id=1, source_target_pairs={{0,4},{4,0},{1,5},{5,1},{2,6},{6,2},{3,7},{7,3},{8,12},{12,8},{9,1... | collective-permute-start | bytes 663560 | tf_op jit(solution)/shard_map/ppermute | solution.py:404
  462.7 8.6 %collective-permute-start.35 = (f32[18960]{0:T(1024)S(1)}, f32[18960]{0:T(1024)S(1)}, u32[]{:S(2)}, u32[]{:S(2)}) collective-permute-start(f32[18960]{0:T(1024)S(1)} %slice.248), channel_id=1, source_target_pairs={{0,1},{1,0},{2,3},{3,2},{4,5},{5,4},{6,7},{7,6},{8,9},{9,8},{10,11... | collective-permute-start | bytes 227528 | tf_op jit(solution)/shard_map/ppermute | solution.py:404
  471.3 7.3 %collective-permute-start.36 = (f32[18960]{0:T(1024)S(1)}, f32[18960]{0:T(1024)S(1)}, u32[]{:S(2)}, u32[]{:S(2)}) collective-permute-start(f32[18960]{0:T(1024)S(1)} %slice_add_fusion.8), channel_id=1, source_target_pairs={{0,2},{1,3},{2,0},{3,1},{4,6},{5,7},{6,4},{7,5},{8,10},{9,11},{10,... | collective-permute-start | bytes 227528 | tf_op jit(solution)/shard_map/ppermute | solution.py:404
  (73 other events, 624.9 us)
Sparse Core Ops, SparseCore 0:
  15.0 43.7 all-gather.6
  74.8 48.4 all-gather.8
  125.4 27.6 all-gather.10
  351.5 39.0 reduce-scatter.3
  393.4 35.2 reduce-scatter.7
  441.3 38.3 reduce-scatter.5
